TPU v7x, 32 devices: a whole 2x2x4 slice. The times are simulated.
32 devices in a mesh: gx: 16 (over z, x, core), gy: 2 (over y).
Axes of the slice: x: 2, y: 2, z: 4, core: 2. Of those that a mesh axis runs over, the one named last changes fastest.
Arguments:
- features: bfloat16 [16, 2, 3, 64, 256], P('gx', 'gy'), may hold values from -6 to 6
- block_coords: int32 [16, 2, 3], P('gx', 'gy'), may hold values from 0 to 31, as said below
- block_counts: int32 [16, 2], P('gx', 'gy'), may hold values from 2 to 3, as said below
- first_weight: bfloat16 [6912, 256], replicated, may hold values from -0.078125 to 0.078125
- second_weight: bfloat16 [6912, 256], replicated, may hold values from -0.078125 to 0.078125
- cotangent: bfloat16 [16, 2, 3, 64, 256], P('gx', 'gy'), may hold values from -6 to 6
Outputs:
- output_features: float32 [16, 2, 3, 64, 256], P('gx', 'gy')
- input_grad: float32 [16, 2, 3, 64, 256], P('gx', 'gy')
- first_weight_grad: float32 [6912, 256], P('gx', 'gy')
- second_weight_grad: float32 [6912, 256], P('gx', 'gy')
Inputs may be any that keep to these rules, and one draw needn't show every extreme that they name: `block_coords`: within a tile all 3 entries are distinct block positions, so slots at or past the tile's count name blocks that are not active. Slots 0 and 1 are always live and hold blocks of the lowest block layer in opposite corners of the tile's 2 x 2 block columns. `block_counts`: at least one tile holds 3 live slots in every draw.
All inputs are finite; a program needn't handle non-finite values.
Results may differ from a plain program's by a relative error of at most 0.0029.
Values may be sent and summed in bfloat16 or wider, within the bound.
No kernel may reach another device: no remote copies, remote signals or barrier semaphores. Data moves between devices by JAX's collectives and lax.ppermute only.
A program may use at most 128 MiB of HBM per device.

v0:
```python
import math

import jax
import jax.numpy as jnp
from jax import lax
from jax.sharding import PartitionSpec as P

C = 256
SLAB_BLOCKS = 8
MAX_BLOCKS = 3


def extended(cells, sides, width):
    for axis, dim in sides:
        count = lax.axis_size(axis)
        ends = count - 1
        head = lax.slice_in_dim(cells, 0, width, axis=dim)
        tail = lax.slice_in_dim(cells, cells.shape[dim] - width, cells.shape[dim], axis=dim)
        cells = jnp.concatenate(
            [
                lax.ppermute(tail, axis, [(i, (i + 1) % count) for i in range(ends)]),
                cells,
                lax.ppermute(head, axis, [((i + 1) % count, i) for i in range(ends)]),
            ],
            axis=dim,
        )
    return cells


def dense_grid(field, slot_blocks, slot_live):
    positions = jnp.arange(4 * SLAB_BLOCKS, dtype=jnp.int32)
    placing = ((slot_blocks[:, None] == positions[None, :]) & slot_live[:, None]).astype(
        jnp.bfloat16
    )
    flat_field = field.reshape(MAX_BLOCKS, 64 * C)
    blocks = lax.dot_general(
        placing, flat_field, (((0,), (0,)), ((), ())), preferred_element_type=jnp.float32
    )
    blocks = blocks.astype(jnp.bfloat16).reshape(2, 2, SLAB_BLOCKS, 4, 4, 4, C)
    return blocks.transpose(0, 3, 1, 4, 2, 5, 6).reshape(8, 8, 4 * SLAB_BLOCKS, C)


def extend(grid):
    widened = extended(grid, (("gx", 0), ("gy", 1)), 1)
    return jnp.pad(widened, ((0, 0), (0, 0), (1, 1), (0, 0)))


def columns(padded, slot_blocks):
    chan_width = padded.shape[3]
    start_x = slot_blocks // (2 * SLAB_BLOCKS)
    start_y = slot_blocks // SLAB_BLOCKS % 2
    start_z = slot_blocks % SLAB_BLOCKS

    def cut_cube(block_x, block_y, block_z):
        return lax.dynamic_slice(
            padded, (4 * block_x, 4 * block_y, 4 * block_z, block_x * 0), (6, 6, 6, chan_width)
        )

    cubes = jax.vmap(cut_cube)(start_x, start_y, start_z)
    tap_list = []
    for tap_index in range(27):
        shift_x = tap_index // 9
        shift_y = tap_index // 3 % 3
        shift_z = tap_index % 3
        piece = cubes[:, shift_x : shift_x + 4, shift_y : shift_y + 4, shift_z : shift_z + 4, :]
        tap_list.append(piece.reshape(-1, chan_width))
    return jnp.concatenate(tap_list, axis=1)


def transposed(cols, weight):
    chan_width = weight.shape[1]
    stacked = cols.reshape(cols.shape[0], 27, chan_width)
    flipped = weight.reshape(27, chan_width, chan_width)[::-1]
    return lax.dot_general(
        stacked, flipped, (((1, 2), (0, 2)), ((), ())), preferred_element_type=jnp.float32
    )


def contract_rows(cols, rows):
    return lax.dot_general(cols, rows, (((0,), (0,)), ((), ())), preferred_element_type=jnp.float32)


def reduce_weights(term):
    narrowed = lax.psum_scatter(term, "gx", scatter_dimension=0, tiled=True)
    return lax.psum_scatter(narrowed, "gy", scatter_dimension=1, tiled=True)


def per_device(features, block_coords, block_counts, first_weight, second_weight, cotangent):
    slot_blocks = block_coords.reshape(MAX_BLOCKS)
    slot_live = jnp.arange(MAX_BLOCKS, dtype=jnp.int32) < block_counts.reshape(())
    row_live = jnp.repeat(slot_live, 64)[:, None]
    zero_float = jnp.zeros((), jnp.float32)
    feature_cols = columns(extend(dense_grid(features, slot_blocks, slot_live)), slot_blocks)
    pre_first = jnp.dot(feature_cols, first_weight, preferred_element_type=jnp.float32)
    hidden = jnp.where(row_live, jax.nn.silu(pre_first), zero_float).astype(jnp.bfloat16)
    hidden_cols = columns(extend(dense_grid(hidden, slot_blocks, slot_live)), slot_blocks)
    output_rows = jnp.where(
        row_live,
        jnp.dot(hidden_cols, second_weight, preferred_element_type=jnp.float32),
        zero_float,
    )
    seed_rows = jnp.where(row_live, cotangent.reshape(-1, C), jnp.zeros((), jnp.bfloat16))
    seed_cols = columns(extend(dense_grid(cotangent, slot_blocks, slot_live)), slot_blocks)
    grad_scale = 1.0 / math.sqrt(64 * MAX_BLOCKS * lax.axis_size("gx") * lax.axis_size("gy"))
    second_term = contract_rows(hidden_cols, seed_rows) * grad_scale
    hidden_grad = transposed(seed_cols, second_weight)
    sigmoid_pre = jax.nn.sigmoid(pre_first)
    pre_grad = jnp.where(
        row_live, hidden_grad * sigmoid_pre * (1.0 + pre_first * (1.0 - sigmoid_pre)), zero_float
    ).astype(jnp.bfloat16)
    grad_cols = columns(extend(dense_grid(pre_grad, slot_blocks, slot_live)), slot_blocks)
    first_term = contract_rows(feature_cols, pre_grad) * grad_scale
    first_grad = reduce_weights(first_term)
    input_rows = jnp.where(row_live, transposed(grad_cols, first_weight), zero_float)
    second_grad = reduce_weights(second_term)
    return (
        output_rows.reshape(features.shape),
        input_rows.reshape(features.shape),
        first_grad,
        second_grad,
    )


def solution(mesh):
    placed = (
        P("gx", "gy", None, None, None),
        P("gx", "gy", None),
        P("gx", "gy"),
        P(),
        P(),
        P("gx", "gy", None, None, None),
    )
    return jax.shard_map(
        per_device,
        mesh=mesh,
        in_specs=placed,
        out_specs=(
            P("gx", "gy", None, None, None),
            P("gx", "gy", None, None, None),
            P("gx", "gy"),
            P("gx", "gy"),
        ),
        check_vma=False,
    )
```

profile of v0, /device:TPU:8, one launch (start us, length us, event | category | flops | bytes accessed | tf_op | source)
XLA Modules:
  0.0 499.8 jit_solution(167751732746583953)
XLA Ops:
  12.1 2.1 reshape.676
  15.9 1.9 collective-permute-start.8
  17.8 4.5 collective-permute-start.9
  25.4 2.2 reshape.614
  29.3 1.9 collective-permute-start
  31.2 4.5 collective-permute-start.1
  41.2 3.4 collective-permute-start.10
  49.7 5.2 %collective-permute-start.2 = (bf16[10,1,32,256]{3,2,1,0:T(8,128)(2,1)}, bf16[10,1,32,256]{3,2,1,0:T(8,128)(2,1)}, u32[]{:S(2)}, u32[]{:S(2)}) collective-permute-start(bf16[10,1,32,256]{3,2,1,0:T(8,128)(2,1)} %get-tuple-element.102), channel_id=1, source_target_pairs={{0,1},{2,3},{4,5},{6,7},{8,9},{10,11},{12,13},{14,15},{16,17},{18,... | collective-permute-start | bytes 491528 | tf_op jit(solution)/shard_map/ppermute | solution.py:21
  56.4 2.5 select_maximum_fusion.2
  59.7 12.5 %while.6 = (s32[]{:T(128)}, bf16[10,10,34,256]{3,2,1,0:T(8,128)(2,1)}, s32[3,4]{1,0:T(4,128)S(1)}, bf16[3,6,6,6,256]{4,3,2,1,0:T(8,128)(2,1)}, s32[]{:T(128)}) while((s32[]{:T(128)}, bf16[10,10,34,256]{3,2,1,0:T(8,128)(2,1)}, s32[3,4]{1,0:T(4,128)S(1)}, bf16[3,6,6,6,256]{4,3,2,1,0:T(8,128)(2,1)}, s32[]{:T(128)}) %tuple.190), condition=%wide.while_cond.2, body=%wide.while_body.2.sunk | while | flops 2 | bytes 297081 | solution.py:55
  60.3 3.5 bitcast_dynamic-update-slice_fusion.10
  64.5 3.5 bitcast_dynamic-update-slice_fusion.10
  68.6 3.5 bitcast_dynamic-update-slice_fusion.10
  72.2 5.3 %fusion.29 = (bf16[3,4,4,4,256]{4,3,2,1,0:T(4,128)(2,1)}, bf16[3,4,4,4,256]{4,3,2,1,0:T(4,128)(2,1)}, bf16[3,4,4,4,256]{4,3,2,1,0:T(4,128)(2,1)}, bf16[3,4,4,4,2...) fusion(bf16[3,6,6,6,256]{4,3,2,1,0:T(8,128)(2,1)} %get-tuple-el, ...), kind=kLoop, calls=%fused_computation.196 | loop fusion | bytes 3735552 | tf_op jit(solution)/shard_map/slice | solution.py:65
  78.7 3.5 fusion.5
  83.0 12.7 %while.4 = (s32[]{:T(128)}, bf16[10,10,34,256]{3,2,1,0:T(8,128)(2,1)}, s32[3,4]{1,0:T(4,128)S(1)}, bf16[3,6,6,6,256]{4,3,2,1,0:T(8,128)(2,1)}, s32[]{:T(128)}) while((s32[]{:T(128)}, bf16[10,10,34,256]{3,2,1,0:T(8,128)(2,1)}, s32[3,4]{1,0:T(4,128)S(1)}, bf16[3,6,6,6,256]{4,3,2,1,0:T(8,128)(2,1)}, s32[]{:T(128)}) %tuple.204), condition=%wide.while_cond, body=%wide.while_body.sunk | while | flops 2 | bytes 297081 | solution.py:55
  83.6 3.6 bitcast_dynamic-update-slice_fusion.8
  87.8 3.6 bitcast_dynamic-update-slice_fusion.8
  92.1 3.6 bitcast_dynamic-update-slice_fusion.8
  95.7 2.9 fusion.34
  227.6 4.0 convolution_multiply_fusion.1
  236.5 2.2 reshape.645
  240.5 1.9 collective-permute-start.4
  242.4 4.7 collective-permute-start.5
  250.4 5.1 %collective-permute-start.6 = (bf16[10,1,32,256]{3,2,1,0:T(8,128)(2,1)S(1)}, bf16[10,1,32,256]{3,2,1,0:T(8,128)(2,1)S(1)}, u32[]{:S(2)}, u32[]{:S(2)}) collective-permute-start(bf16[10,1,32,256]{3,2,1,0:T(8,128)(2,1)S(1)} %get-tuple-element.100), channel_id=1, source_target_pairs={{0,1},{2,3},{4,5},{6,7},{8,9},{10,11},{12,13},{14,15},{16,17},{18,... | collective-permute-start | bytes 491528 | tf_op jit(solution)/shard_map/ppermute | solution.py:21
  258.3 4.4 collective-permute-done.7
  262.7 2.6 select_maximum_fusion.4
  266.0 12.7 %while.5 = (s32[]{:T(128)}, bf16[10,10,34,256]{3,2,1,0:T(8,128)(2,1)}, s32[3,4]{1,0:T(4,128)S(1)}, bf16[3,6,6,6,256]{4,3,2,1,0:T(8,128)(2,1)}, s32[]{:T(128)}) while((s32[]{:T(128)}, bf16[10,10,34,256]{3,2,1,0:T(8,128)(2,1)}, s32[3,4]{1,0:T(4,128)S(1)}, bf16[3,6,6,6,256]{4,3,2,1,0:T(8,128)(2,1)}, s32[]{:T(128)}) %tuple.205), condition=%wide.while_cond.1, body=%wide.while_body.1.sunk | while | flops 2 | bytes 297081 | solution.py:55
  266.6 3.6 bitcast_dynamic-update-slice_fusion.9
  270.9 3.6 bitcast_dynamic-update-slice_fusion.9
  275.1 3.6 bitcast_dynamic-update-slice_fusion.9
  278.7 3.1 fusion.32
  294.3 5.2 %fusion.31 = (bf16[3,4,4,4,256]{4,3,2,1,0:T(4,128)(2,1)}, bf16[3,4,4,4,256]{4,3,2,1,0:T(4,128)(2,1)}, bf16[3,4,4,4,256]{4,3,2,1,0:T(4,128)(2,1)}, bf16[3,4,4,4,2...) fusion(bf16[3,6,6,6,256]{4,3,2,1,0:T(8,128)(2,1)} %get-tuple-el, ...), kind=kLoop, calls=%fused_computation.198 | loop fusion | bytes 3735552 | tf_op jit(solution)/shard_map/slice | solution.py:65
  343.8 4.1 convolution_multiply_fusion
  352.5 2.2 reshape.680
  355.7 1.9 collective-permute-start.12
  357.6 4.5 collective-permute-start.13
  369.3 4.1 collective-permute-done.15
  373.5 2.5 select_maximum_fusion
  376.8 12.7 %while.7 = (s32[]{:T(128)}, bf16[10,10,34,256]{3,2,1,0:T(8,128)(2,1)}, s32[3,4]{1,0:T(4,128)S(1)}, bf16[3,6,6,6,256]{4,3,2,1,0:T(8,128)(2,1)}, s32[]{:T(128)}) while((s32[]{:T(128)}, bf16[10,10,34,256]{3,2,1,0:T(8,128)(2,1)}, s32[3,4]{1,0:T(4,128)S(1)}, bf16[3,6,6,6,256]{4,3,2,1,0:T(8,128)(2,1)}, s32[]{:T(128)}) %tuple.206), condition=%wide.while_cond.3, body=%wide.while_body.3.sunk | while | flops 2 | bytes 297081 | solution.py:55
  377.4 3.7 bitcast_dynamic-update-slice_fusion.11
  381.6 3.6 bitcast_dynamic-update-slice_fusion.11
  385.9 3.6 bitcast_dynamic-update-slice_fusion.11
  389.5 3.0 fusion.28
  404.9 5.1 %fusion.27 = (bf16[3,4,4,4,256]{4,3,2,1,0:T(4,128)(2,1)}, bf16[3,4,4,4,256]{4,3,2,1,0:T(4,128)(2,1)}, bf16[3,4,4,4,256]{4,3,2,1,0:T(4,128)(2,1)}, bf16[3,4,4,4,2...) fusion(bf16[3,6,6,6,256]{4,3,2,1,0:T(8,128)(2,1)} %get-tuple-el, ...), kind=kLoop, calls=%fused_computation.194 | loop fusion | bytes 3735552 | tf_op jit(solution)/shard_map/slice | solution.py:65
  477.6 4.3 convolution_select_fusion
  482.0 3.7 fusion.9
  485.7 7.6 %reduce-scatter.11.cloned.1.call-done = f32[432,128]{1,0:T(8,128)} async-done(((f32[432,256]{1,0:T(8,128)}), f32[432,128]{1,0:T(8,128)}) %reduce-scatter.11.cloned.1.call-update) | async-done | bytes 221200 | tf_op jit(solution)/shard_map/reduce_scatter | solution.py:85
  (449 shorter events, 324.3 us)
Async XLA Ops:
  7.2 215.6 %copy-start = (bf16[6912,256]{1,0:T(8,128)(2,1)S(1)}, bf16[6912,256]{1,0:T(8,128)(2,1)}, u32[]{:S(2)}) copy-start(bf16[6912,256]{1,0:T(8,128)(2,1)} %param.9) | copy-start | bytes 10616836
  7.2 456.6 %reduce-scatter.5.cloned.1.call-start = ((), (), s32[]{:S(2)}) async-start(), calls=%async_computation.4 | async-start | bytes 7520256 | tf_op jit(solution)/shard_map/reduce_scatter | solution.py:84
  15.9 22.0 %collective-permute-start.8 = (bf16[1,8,32,256]{3,2,1,0:T(8,128)(2,1)}, bf16[1,8,32,256]{3,2,1,0:T(8,128)(2,1)}, u32[]{:S(2)}, u32[]{:S(2)}) collective-permute-start(bf16[1,8,32,256]{3,2,1,0:T(8,128)(2,1)} %get-tuple-element.107), channel_id=1, source_target_pairs={{0,2},{2,4},{4,6},{6,8},{8,10},{10,12},{12,14},{14,16},{16,18},{18... | collective-permute-start | bytes 393224 | tf_op jit(solution)/shard_map/ppermute | solution.py:21
  17.8 22.5 %collective-permute-start.9 = (bf16[1,8,32,256]{3,2,1,0:T(8,128)(2,1)}, bf16[1,8,32,256]{3,2,1,0:T(8,128)(2,1)}, u32[]{:S(2)}, u32[]{:S(2)}) collective-permute-start(bf16[1,8,32,256]{3,2,1,0:T(8,128)(2,1)} %get-tuple-element.106), channel_id=1, source_target_pairs={{2,0},{4,2},{6,4},{8,6},{10,8},{12,10},{14,12},{16,14},{18,16},{20... | collective-permute-start | bytes 393224 | tf_op jit(solution)/shard_map/ppermute | solution.py:23
  29.3 16.7 %collective-permute-start = (bf16[1,8,32,256]{3,2,1,0:T(8,128)(2,1)}, bf16[1,8,32,256]{3,2,1,0:T(8,128)(2,1)}, u32[]{:S(2)}, u32[]{:S(2)}) collective-permute-start(bf16[1,8,32,256]{3,2,1,0:T(8,128)(2,1)} %get-tuple-element.111), channel_id=1, source_target_pairs={{0,2},{2,4},{4,6},{6,8},{8,10},{10,12},{12,14},{14,16},{16,18},{18... | collective-permute-start | bytes 393224 | tf_op jit(solution)/shard_map/ppermute | solution.py:21
  31.2 15.8 %collective-permute-start.1 = (bf16[1,8,32,256]{3,2,1,0:T(8,128)(2,1)}, bf16[1,8,32,256]{3,2,1,0:T(8,128)(2,1)}, u32[]{:S(2)}, u32[]{:S(2)}) collective-permute-start(bf16[1,8,32,256]{3,2,1,0:T(8,128)(2,1)} %get-tuple-element.110), channel_id=1, source_target_pairs={{2,0},{4,2},{6,4},{8,6},{10,8},{12,10},{14,12},{16,14},{18,16},{20... | collective-permute-start | bytes 393224 | tf_op jit(solution)/shard_map/ppermute | solution.py:23
  41.2 15.2 %collective-permute-start.10 = (bf16[10,1,32,256]{3,2,1,0:T(8,128)(2,1)S(1)}, bf16[10,1,32,256]{3,2,1,0:T(8,128)(2,1)S(1)}, u32[]{:S(2)}, u32[]{:S(2)}) collective-permute-start(bf16[10,1,32,256]{3,2,1,0:T(8,128)(2,1)S(1)} %get-tuple-element.98), channel_id=1, source_target_pairs={{0,1},{2,3},{4,5},{6,7},{8,9},{10,11},{12,13},{14,15},{16,17},{18,... | collective-permute-start | bytes 491528 | tf_op jit(solution)/shard_map/ppermute | solution.py:21
  44.7 11.8 %collective-permute-start.11 = (bf16[10,1,32,256]{3,2,1,0:T(8,128)(2,1)S(1)}, bf16[10,1,32,256]{3,2,1,0:T(8,128)(2,1)S(1)}, u32[]{:S(2)}, u32[]{:S(2)}) collective-permute-start(bf16[10,1,32,256]{3,2,1,0:T(8,128)(2,1)S(1)} %get-tuple-element.99), channel_id=1, source_target_pairs={{1,0},{3,2},{5,4},{7,6},{9,8},{11,10},{13,12},{15,14},{17,16},{19,... | collective-permute-start | bytes 491528 | tf_op jit(solution)/shard_map/ppermute | solution.py:23
  49.7 29.0 %collective-permute-start.2 = (bf16[10,1,32,256]{3,2,1,0:T(8,128)(2,1)}, bf16[10,1,32,256]{3,2,1,0:T(8,128)(2,1)}, u32[]{:S(2)}, u32[]{:S(2)}) collective-permute-start(bf16[10,1,32,256]{3,2,1,0:T(8,128)(2,1)} %get-tuple-element.102), channel_id=1, source_target_pairs={{0,1},{2,3},{4,5},{6,7},{8,9},{10,11},{12,13},{14,15},{16,17},{18,... | collective-permute-start | bytes 491528 | tf_op jit(solution)/shard_map/ppermute | solution.py:21
  55.0 23.8 %collective-permute-start.3 = (bf16[10,1,32,256]{3,2,1,0:T(8,128)(2,1)}, bf16[10,1,32,256]{3,2,1,0:T(8,128)(2,1)}, u32[]{:S(2)}, u32[]{:S(2)}) collective-permute-start(bf16[10,1,32,256]{3,2,1,0:T(8,128)(2,1)} %get-tuple-element.103), channel_id=1, source_target_pairs={{1,0},{3,2},{5,4},{7,6},{9,8},{11,10},{13,12},{15,14},{17,16},{19,... | collective-permute-start | bytes 491528 | tf_op jit(solution)/shard_map/ppermute | solution.py:23
  187.5 30.0 %copy-start.44 = (bf16[192,1,256]{2,0,1:T(8,128)(2,1)S(1)}, bf16[192,1,256]{2,0,1:T(8,128)(2,1)}, u32[]{:S(2)}) copy-start(bf16[192,1,256]{2,0,1:T(8,128)(2,1)} %concatenate.181) | copy-start | bytes 294916
  187.5 30.7 %copy-start.43 = (bf16[192,1,256]{2,0,1:T(8,128)(2,1)S(1)}, bf16[192,1,256]{2,0,1:T(8,128)(2,1)}, u32[]{:S(2)}) copy-start(bf16[192,1,256]{2,0,1:T(8,128)(2,1)} %concatenate.182) | copy-start | bytes 294916
  187.5 31.3 %copy-start.42 = (bf16[192,1,256]{2,0,1:T(8,128)(2,1)S(1)}, bf16[192,1,256]{2,0,1:T(8,128)(2,1)}, u32[]{:S(2)}) copy-start(bf16[192,1,256]{2,0,1:T(8,128)(2,1)} %concatenate.183) | copy-start | bytes 294916
  187.5 32.0 %copy-start.39 = (bf16[192,1,256]{2,0,1:T(8,128)(2,1)S(1)}, bf16[192,1,256]{2,0,1:T(8,128)(2,1)}, u32[]{:S(2)}) copy-start(bf16[192,1,256]{2,0,1:T(8,128)(2,1)} %concatenate.184) | copy-start | bytes 294916
  187.5 32.6 %copy-start.37 = (bf16[192,1,256]{2,0,1:T(8,128)(2,1)S(1)}, bf16[192,1,256]{2,0,1:T(8,128)(2,1)}, u32[]{:S(2)}) copy-start(bf16[192,1,256]{2,0,1:T(8,128)(2,1)} %concatenate.185) | copy-start | bytes 294916
  187.5 33.2 %copy-start.34 = (bf16[192,1,256]{2,0,1:T(8,128)(2,1)S(1)}, bf16[192,1,256]{2,0,1:T(8,128)(2,1)}, u32[]{:S(2)}) copy-start(bf16[192,1,256]{2,0,1:T(8,128)(2,1)} %concatenate.186) | copy-start | bytes 294916
  187.5 33.9 %copy-start.35 = (bf16[192,1,256]{2,0,1:T(8,128)(2,1)S(1)}, bf16[192,1,256]{2,0,1:T(8,128)(2,1)}, u32[]{:S(2)}) copy-start(bf16[192,1,256]{2,0,1:T(8,128)(2,1)} %concatenate.187) | copy-start | bytes 294916
  187.5 34.5 %copy-start.5 = (bf16[192,6912]{1,0:T(8,128)(2,1)S(1)}, bf16[192,6912]{1,0:T(8,128)(2,1)}, u32[]{:S(2)}) copy-start(bf16[192,6912]{1,0:T(8,128)(2,1)} %constant_dynamic-update-slice_fusion.29) | copy-start | bytes 7962628
  187.5 34.5 %copy-start.40 = (bf16[192,256]{1,0:T(8,128)(2,1)S(1)}, bf16[192,256]{1,0:T(8,128)(2,1)}, u32[]{:S(2)}) copy-start(bf16[192,256]{1,0:T(8,128)(2,1)} %reshape.617) | copy-start | bytes 294916
  187.6 34.5 %copy-start.41 = (bf16[192,256]{1,0:T(8,128)(2,1)S(1)}, bf16[192,256]{1,0:T(8,128)(2,1)}, u32[]{:S(2)}) copy-start(bf16[192,256]{1,0:T(8,128)(2,1)} %reshape.618) | copy-start | bytes 294916
  189.3 32.8 %copy-start.38 = (bf16[192,256]{1,0:T(8,128)(2,1)S(1)}, bf16[192,256]{1,0:T(8,128)(2,1)}, u32[]{:S(2)}) copy-start(bf16[192,256]{1,0:T(8,128)(2,1)} %reshape.619) | copy-start | bytes 294916
  190.8 31.3 %copy-start.36 = (bf16[192,256]{1,0:T(8,128)(2,1)S(1)}, bf16[192,256]{1,0:T(8,128)(2,1)}, u32[]{:S(2)}) copy-start(bf16[192,256]{1,0:T(8,128)(2,1)} %reshape.620) | copy-start | bytes 294916
  192.4 29.8 %copy-start.33 = (bf16[192,256]{1,0:T(8,128)(2,1)S(1)}, bf16[192,256]{1,0:T(8,128)(2,1)}, u32[]{:S(2)}) copy-start(bf16[192,256]{1,0:T(8,128)(2,1)} %reshape.621) | copy-start | bytes 294916
  194.0 28.2 %copy-start.31 = (bf16[192,256]{1,0:T(8,128)(2,1)S(1)}, bf16[192,256]{1,0:T(8,128)(2,1)}, u32[]{:S(2)}) copy-start(bf16[192,256]{1,0:T(8,128)(2,1)} %reshape.622) | copy-start | bytes 294916
  195.5 26.7 %copy-start.32 = (bf16[192,256]{1,0:T(8,128)(2,1)S(1)}, bf16[192,256]{1,0:T(8,128)(2,1)}, u32[]{:S(2)}) copy-start(bf16[192,256]{1,0:T(8,128)(2,1)} %reshape.623) | copy-start | bytes 294916
  197.1 25.1 %copy-start.30 = (bf16[192,256]{1,0:T(8,128)(2,1)S(1)}, bf16[192,256]{1,0:T(8,128)(2,1)}, u32[]{:S(2)}) copy-start(bf16[192,256]{1,0:T(8,128)(2,1)} %reshape.624) | copy-start | bytes 294916
  198.7 23.6 %copy-start.29 = (bf16[192,256]{1,0:T(8,128)(2,1)S(1)}, bf16[192,256]{1,0:T(8,128)(2,1)}, u32[]{:S(2)}) copy-start(bf16[192,256]{1,0:T(8,128)(2,1)} %reshape.625) | copy-start | bytes 294916
  200.3 22.0 %copy-start.28 = (bf16[192,256]{1,0:T(8,128)(2,1)S(1)}, bf16[192,256]{1,0:T(8,128)(2,1)}, u32[]{:S(2)}) copy-start(bf16[192,256]{1,0:T(8,128)(2,1)} %reshape.626) | copy-start | bytes 294916
  201.8 20.5 %copy-start.27 = (bf16[192,256]{1,0:T(8,128)(2,1)S(1)}, bf16[192,256]{1,0:T(8,128)(2,1)}, u32[]{:S(2)}) copy-start(bf16[192,256]{1,0:T(8,128)(2,1)} %reshape.627) | copy-start | bytes 294916
  203.4 19.0 %copy-start.26 = (bf16[192,256]{1,0:T(8,128)(2,1)S(1)}, bf16[192,256]{1,0:T(8,128)(2,1)}, u32[]{:S(2)}) copy-start(bf16[192,256]{1,0:T(8,128)(2,1)} %reshape.628) | copy-start | bytes 294916
  205.0 17.4 %copy-start.25 = (bf16[192,256]{1,0:T(8,128)(2,1)S(1)}, bf16[192,256]{1,0:T(8,128)(2,1)}, u32[]{:S(2)}) copy-start(bf16[192,256]{1,0:T(8,128)(2,1)} %reshape.629) | copy-start | bytes 294916
  206.5 15.9 %copy-start.24 = (bf16[192,256]{1,0:T(8,128)(2,1)S(1)}, bf16[192,256]{1,0:T(8,128)(2,1)}, u32[]{:S(2)}) copy-start(bf16[192,256]{1,0:T(8,128)(2,1)} %reshape.630) | copy-start | bytes 294916
  231.7 244.4 %reduce-scatter.9.cloned.1.call-start = ((), (), s32[]{:S(2)}) async-start(), calls=%async_computation.6 | async-start | bytes 7520256 | tf_op jit(solution)/shard_map/reduce_scatter | solution.py:84
  240.5 7.5 %collective-permute-start.4 = (bf16[1,8,32,256]{3,2,1,0:T(8,128)(2,1)}, bf16[1,8,32,256]{3,2,1,0:T(8,128)(2,1)}, u32[]{:S(2)}, u32[]{:S(2)}) collective-permute-start(bf16[1,8,32,256]{3,2,1,0:T(8,128)(2,1)} %get-tuple-element.109), channel_id=1, source_target_pairs={{0,2},{2,4},{4,6},{6,8},{8,10},{10,12},{12,14},{14,16},{16,18},{18... | collective-permute-start | bytes 393224 | tf_op jit(solution)/shard_map/ppermute | solution.py:21
  242.4 8.0 %collective-permute-start.5 = (bf16[1,8,32,256]{3,2,1,0:T(8,128)(2,1)}, bf16[1,8,32,256]{3,2,1,0:T(8,128)(2,1)S(1)}, u32[]{:S(2)}, u32[]{:S(2)}) collective-permute-start(bf16[1,8,32,256]{3,2,1,0:T(8,128)(2,1)} %get-tuple-element.108), channel_id=1, source_target_pairs={{2,0},{4,2},{6,4},{8,6},{10,8},{12,10},{14,12},{16,14},{18,16},{20... | collective-permute-start | bytes 393224 | tf_op jit(solution)/shard_map/ppermute | solution.py:23
  250.4 7.9 %collective-permute-start.6 = (bf16[10,1,32,256]{3,2,1,0:T(8,128)(2,1)S(1)}, bf16[10,1,32,256]{3,2,1,0:T(8,128)(2,1)S(1)}, u32[]{:S(2)}, u32[]{:S(2)}) collective-permute-start(bf16[10,1,32,256]{3,2,1,0:T(8,128)(2,1)S(1)} %get-tuple-element.100), channel_id=1, source_target_pairs={{0,1},{2,3},{4,5},{6,7},{8,9},{10,11},{12,13},{14,15},{16,17},{18,... | collective-permute-start | bytes 491528 | tf_op jit(solution)/shard_map/ppermute | solution.py:21
  255.5 7.2 %collective-permute-start.7 = (bf16[10,1,32,256]{3,2,1,0:T(8,128)(2,1)S(1)}, bf16[10,1,32,256]{3,2,1,0:T(8,128)(2,1)S(1)}, u32[]{:S(2)}, u32[]{:S(2)}) collective-permute-start(bf16[10,1,32,256]{3,2,1,0:T(8,128)(2,1)S(1)} %get-tuple-element.101), channel_id=1, source_target_pairs={{1,0},{3,2},{5,4},{7,6},{9,8},{11,10},{13,12},{15,14},{17,16},{19,... | collective-permute-start | bytes 491528 | tf_op jit(solution)/shard_map/ppermute | solution.py:23
  329.2 14.6 %copy-start.10 = (bf16[192,256]{1,0:T(8,128)(2,1)S(1)}, bf16[192,256]{1,0:T(8,128)(2,1)}, u32[]{:S(2)}) copy-start(bf16[192,256]{1,0:T(8,128)(2,1)} %bitcast_select_fusion) | copy-start | bytes 294916
  347.9 137.8 %reduce-scatter.7.cloned.1.call-start = ((), (), s32[]{:S(2)}) async-start(), calls=%async_computation.5 | async-start | bytes 663552 | tf_op jit(solution)/shard_map/reduce_scatter | solution.py:85
  355.7 7.2 %collective-permute-start.12 = (bf16[1,8,32,256]{3,2,1,0:T(8,128)(2,1)S(1)}, bf16[1,8,32,256]{3,2,1,0:T(8,128)(2,1)S(1)}, u32[]{:S(2)}, u32[]{:S(2)}) collective-permute-start(bf16[1,8,32,256]{3,2,1,0:T(8,128)(2,1)S(1)} %get-tuple-element.105), channel_id=1, source_target_pairs={{0,2},{2,4},{4,6},{6,8},{8,10},{10,12},{12,14},{14,16},{16,18},{18... | collective-permute-start | bytes 393224 | tf_op jit(solution)/shard_map/ppermute | solution.py:21
  357.6 7.0 %collective-permute-start.13 = (bf16[1,8,32,256]{3,2,1,0:T(8,128)(2,1)S(1)}, bf16[1,8,32,256]{3,2,1,0:T(8,128)(2,1)S(1)}, u32[]{:S(2)}, u32[]{:S(2)}) collective-permute-start(bf16[1,8,32,256]{3,2,1,0:T(8,128)(2,1)S(1)} %get-tuple-element.104), channel_id=1, source_target_pairs={{2,0},{4,2},{6,4},{8,6},{10,8},{12,10},{14,12},{16,14},{18,16},{20... | collective-permute-start | bytes 393224 | tf_op jit(solution)/shard_map/ppermute | solution.py:23
  364.7 4.6 collective-permute-start.14
  366.1 7.4 %collective-permute-start.15 = (bf16[10,1,32,256]{3,2,1,0:T(8,128)(2,1)S(1)}, bf16[10,1,32,256]{3,2,1,0:T(8,128)(2,1)S(1)}, u32[]{:S(2)}, u32[]{:S(2)}) collective-permute-start(bf16[10,1,32,256]{3,2,1,0:T(8,128)(2,1)S(1)} %get-tuple-element.97), channel_id=1, source_target_pairs={{1,0},{3,2},{5,4},{7,6},{9,8},{11,10},{13,12},{15,14},{17,16},{19,... | collective-permute-start | bytes 491528 | tf_op jit(solution)/shard_map/ppermute | solution.py:23
  439.7 21.5 %copy-start.61 = (bf16[192,1,256]{2,0,1:T(8,128)(2,1)S(1)}, bf16[192,1,256]{2,0,1:T(8,128)(2,1)}, u32[]{:S(2)}) copy-start(bf16[192,1,256]{2,0,1:T(8,128)(2,1)} %concatenate.205) | copy-start | bytes 294916
  439.7 22.2 %copy-start.59 = (bf16[192,1,256]{2,0,1:T(8,128)(2,1)S(1)}, bf16[192,1,256]{2,0,1:T(8,128)(2,1)}, u32[]{:S(2)}) copy-start(bf16[192,1,256]{2,0,1:T(8,128)(2,1)} %concatenate.206) | copy-start | bytes 294916
  439.7 22.8 %copy-start.57 = (bf16[192,1,256]{2,0,1:T(8,128)(2,1)S(1)}, bf16[192,1,256]{2,0,1:T(8,128)(2,1)}, u32[]{:S(2)}) copy-start(bf16[192,1,256]{2,0,1:T(8,128)(2,1)} %concatenate.207) | copy-start | bytes 294916
  439.7 23.4 %copy-start.55 = (bf16[192,1,256]{2,0,1:T(8,128)(2,1)S(1)}, bf16[192,1,256]{2,0,1:T(8,128)(2,1)}, u32[]{:S(2)}) copy-start(bf16[192,1,256]{2,0,1:T(8,128)(2,1)} %concatenate.208) | copy-start | bytes 294916
  463.8 29.5 %reduce-scatter.11.cloned.1.call-start = ((), (), s32[]{:S(2)}) async-start(), calls=%async_computation.7 | async-start | bytes 663552 | tf_op jit(solution)/shard_map/reduce_scatter | solution.py:85
  (37 other events, 312.7 us)
Sparse Core Ops, SparseCore 0:
  231.8 91.9 reduce-scatter.4
  348.0 89.3 reduce-scatter.8
  463.9 12.8 reduce-scatter.6
  479.6 13.6 reduce-scatter.10
where the time goes:
time: 508 us; the launch traced here: 500 us
  local copies, waits for them, and re-layouts  380 us (75%)
  starting transfers between devices  47 us (9%)
  matrix products  22.9 us (5%)
  waiting for transfers between devices  20.6 us (4%)
  between operations  15.9 us (3%)
  other arithmetic  13.8 us (3%)
    unnamed x249, local copies, waits for them, and re-layouts  104 us
    concatenate x58, local copies, waits for them, and re-layouts, columns(): return jnp.concatenate(tap_list, axis=1)  86.2 us
    reshape x54, local copies, waits for them, and re-layouts, columns(): tap_list.append(piece.reshape(-1, chan_width))  84.1 us
    gather x36, local copies, waits for them, and re-layouts  50.5 us
    slice x8, local copies, waits for them, and re-layouts, columns(): cubes[:, shift_x:shift_x + 4, shift_y:shift_y + 4, shift_z:shift_z + 4, :]  27.6 us
    ppermute x8, starting transfers between devices, extended(): lax.ppermute(head, axis, [((i + 1) % count, i) for i in range(ends)])  23.9 us
    ppermute x8, starting transfers between devices, extended(): lax.ppermute(tail, axis, [(i, (i + 1) % count) for i in range(ends)])  22.7 us
    concatenate x4, other arithmetic, extended(): jnp.concatenate([lax.ppermute(tail, axis, [(i, (i + 1) % count) for i in...  11 us
  transfers between devices with their start and end apart: 20, of which 8 were waited for; matrix products, arithmetic and copies ran while one was open for 51% of the time, Pallas kernels for 0%

commit v1 on v0

v1 whole, which is shorter than its diff:
```python
import functools
import math

import jax
import jax.numpy as jnp
import numpy as np
from jax import lax
from jax.experimental import pallas as pl
from jax.experimental.pallas import tpu as pltpu
from jax.sharding import PartitionSpec as P

C = 256
TAPS = 27
PLANE = 16
STEP_Y = 64.0
STEP_X = 4096.0
NOWHERE = -1.0e7
META_ROWS = 16
VMEM = pltpu.MemorySpace.VMEM
SMEM = pltpu.MemorySpace.SMEM


def params(mib):
    return pltpu.CompilerParams(vmem_limit_bytes=mib * 2**20)


def dot(lhs, rhs, dims=((1,), (0,))):
    return lax.dot_general(lhs, rhs, (dims, ((), ())), preferred_element_type=jnp.float32)


def source_codes(metas, offsets, width):
    lane = lax.broadcasted_iota(jnp.int32, (1, 512), 1)
    total = jnp.full((1, 512), NOWHERE, jnp.float32)
    for place, (meta, offset) in enumerate(zip(metas, offsets)):
        rows = meta.astype(jnp.float32)
        parts = []
        for half in range(2):
            x, y, z, live = (rows[4 * half + i : 4 * half + i + 1] for i in range(4))
            parts.append(
                jnp.where(live > 0.5, x * STEP_X + y * STEP_Y + z + offset, NOWHERE)
            )
        code = jnp.concatenate(parts, axis=1)
        inside = (lane >= place * width) & (lane < (place + 1) * width)
        total = jnp.where(inside, code, total)
    return total


def selectors(metas, where_ref, own_code, sides, width):
    near = where_ref[0].astype(jnp.float32) * (2 * STEP_X)
    side_offsets = [where_ref[1 + i].astype(jnp.float32) * (8 * STEP_Y) for i in range(sides)]
    offsets = [0.0] + side_offsets + [near, -near]
    for side_offset in side_offsets:
        offsets += [near + side_offset, side_offset - near]
    codes = source_codes(metas, offsets, width)
    edge = codes[:, : 3 * (1 + sides) * width]
    middle = codes[:, : (1 + sides) * width]
    return tuple(
        (source == own_code + step).astype(jnp.float32).astype(jnp.bfloat16)
        for source, step in ((edge, -STEP_X), (middle, 0.0), (edge, STEP_X))
    )


def fill(cols_ref, tiles, faces, chosen, width):
    for plane in range(6):
        if plane == 0:
            pieces = [tile[3 * width : 4 * width] for tile in tiles] + faces
            select = chosen[0]
        elif plane == 5:
            pieces = [tile[0:width] for tile in tiles] + faces
            select = chosen[2]
        else:
            pieces = [tile[(plane - 1) * width : plane * width] for tile in tiles]
            select = chosen[1]
        moved = dot(select, jnp.concatenate(pieces, axis=0)).astype(jnp.bfloat16)
        for shift in range(9):
            cols_ref[shift, plane * width : (plane + 1) * width, :] = moved[
                shift * width : (shift + 1) * width
            ]


def tap_rows(cols_ref, tap, width):
    start = tap // 9 * width
    return cols_ref[tap % 9, start : start + 4 * width, :]


def conv(cols_ref, weight_ref, width):
    total = None
    for tap in range(TAPS):
        term = dot(tap_rows(cols_ref, tap, width), weight_ref[tap * C : (tap + 1) * C, :])
        total = term if total is None else total + term
    return total


def conv_back(cols_ref, weight_ref, width):
    total = None
    for tap in range(TAPS):
        weight = weight_ref[(26 - tap) * C : (27 - tap) * C, :]
        term = dot(tap_rows(cols_ref, tap, width), weight, ((1,), (1,)))
        total = term if total is None else total + term
    return total


def live_rows(where_ref, sides, slots):
    row = lax.broadcasted_iota(jnp.int32, (4 * slots * PLANE, 1), 0)
    slot = (row // PLANE) % slots
    return slot < where_ref[1 + sides]


def neighbourhood(own_ref, side_refs, far_ref, fdiag_refs, near_ref, rows, width):
    sides = len(side_refs)
    faced = 2 * width
    near_at = faced + META_ROWS
    metas = [own_ref[rows : rows + 8, :]]
    metas += [ref[rows : rows + 8, :] for ref in side_refs]
    metas += [near_ref[faced : faced + 8, :], far_ref[faced : faced + 8, :]]
    for i, ref in enumerate(fdiag_refs):
        start = (i + 1) * near_at + faced
        metas += [near_ref[start : start + 8, :], ref[faced : faced + 8, :]]
    fields = []
    for field in range(2):
        top = field * (rows // 2)
        tiles = [own_ref.at[top : top + rows // 2]]
        tiles += [ref.at[top : top + rows // 2] for ref in side_refs]
        face = field * width
        faces = [near_ref[face : face + width, :], far_ref[face : face + width, :]]
        for i, ref in enumerate(fdiag_refs):
            start = (i + 1) * near_at + face
            faces += [near_ref[start : start + width, :], ref[face : face + width, :]]
        fields.append((tiles, faces))
    return metas, fields


def first_kernel(slots, sides, *refs):
    where_ref, code_ref, own_ref = refs[:3]
    side_refs, refs = refs[3 : 3 + sides], refs[3 + sides :]
    far_ref, fdiag_refs, near_ref = refs[0], refs[1 : 1 + sides], refs[1 + sides]
    refs = refs[2 + sides :]
    first_ref, second_ref, out_ref, feature_cols_ref, seed_cols_ref = refs
    width = slots * PLANE
    rows = 8 * width
    metas, fields = neighbourhood(own_ref, side_refs, far_ref, fdiag_refs, near_ref, rows, width)
    chosen = selectors(metas, where_ref, code_ref[...], sides, width)
    fill(feature_cols_ref, *fields[0], chosen, width)
    pre_first = conv(feature_cols_ref, first_ref, width)
    live = live_rows(where_ref, sides, slots)
    sigmoid = 1.0 / (1.0 + jnp.exp(-pre_first))
    hidden = jnp.where(live, pre_first * sigmoid, 0.0)
    slope = jnp.where(live, sigmoid * (1.0 + pre_first * (1.0 - sigmoid)), 0.0)
    out_ref[: rows // 2, :] = hidden.astype(jnp.bfloat16)
    fill(seed_cols_ref, *fields[1], chosen, width)
    hidden_grad = conv_back(seed_cols_ref, second_ref, width)
    out_ref[rows // 2 : rows, :] = (hidden_grad * slope).astype(jnp.bfloat16)
    out_ref[rows:, :] = own_ref[rows:, :]


def last_kernel(slots, sides, *refs):
    where_ref, code_ref, own_ref = refs[:3]
    side_refs, refs = refs[3 : 3 + sides], refs[3 + sides :]
    far_ref, fdiag_refs, near_ref = refs[0], refs[1 : 1 + sides], refs[1 + sides]
    refs = refs[2 + sides :]
    first_ref, second_ref, output_ref, input_ref, hidden_cols_ref, grad_cols_ref = refs
    width = slots * PLANE
    rows = 8 * width
    metas, fields = neighbourhood(own_ref, side_refs, far_ref, fdiag_refs, near_ref, rows, width)
    chosen = selectors(metas, where_ref, code_ref[...], sides, width)
    live = live_rows(where_ref, sides, slots)

    def put(ref, total):
        total = jnp.where(live, total, 0.0)
        for x in range(4):
            for slot in range(slots):
                start = x * width + slot * PLANE
                ref[slot, x * PLANE : (x + 1) * PLANE, :] = total[start : start + PLANE]

    fill(hidden_cols_ref, *fields[0], chosen, width)
    put(output_ref, conv(hidden_cols_ref, second_ref, width))
    fill(grad_cols_ref, *fields[1], chosen, width)
    put(input_ref, conv_back(grad_cols_ref, first_ref, width))


def store_terms(place_ref, keep_ref, send_ref, total_ref, chunks, rows):
    core = place_ref[0]
    for i in range(chunks // 2):
        keep_at = pl.multiple_of((2 * i + core) * rows, 8)
        send_at = pl.multiple_of((2 * i + 1 - core) * rows, 8)
        keep_ref[i] = total_ref[pl.ds(keep_at, rows), :]
        send_ref[i] = total_ref[pl.ds(send_at, rows), :].astype(jnp.bfloat16)


def second_terms_kernel(slots, scale, place_ref, both_ref, cols_ref, keep_ref, send_ref, total_ref):
    width = slots * PLANE
    hidden = both_ref[: 4 * width, :].astype(jnp.float32).T.astype(jnp.bfloat16)
    for tap in range(TAPS):
        total_ref[tap * C : (tap + 1) * C, :] = dot(hidden, tap_rows(cols_ref, 26 - tap, width)) * scale
    store_terms(place_ref, keep_ref, send_ref, total_ref, 2 * keep_ref.shape[0], keep_ref.shape[1])


def first_terms_kernel(slots, scale, place_ref, both_ref, cols_ref, keep_ref, send_ref, total_ref):
    width = slots * PLANE
    grad = both_ref[4 * width : 8 * width, :]
    for tap in range(TAPS):
        total_ref[tap * C : (tap + 1) * C, :] = (
            dot(tap_rows(cols_ref, tap, width), grad, ((0,), (0,))) * scale
        )
    store_terms(place_ref, keep_ref, send_ref, total_ref, 2 * keep_ref.shape[0], keep_ref.shape[1])


def swap(cells, axis, bit):
    count = lax.axis_size(axis)
    return lax.ppermute(cells, axis, [(i, i ^ bit) for i in range(count)])


def side_steps(count):
    if count == 2:
        return [[(0, 1), (1, 0)]]
    ends = count - 1
    return [
        [(i, i + 1) for i in range(ends)],
        [(i + 1, i) for i in range(ends)],
    ]


def far_steps(count):
    pairs = [(i, i + 1) for i in range(1, count - 1, 2)]
    return pairs + [(b, a) for a, b in pairs]


def exchanged(own, rows, width, core):
    gx, gy = lax.axis_size("gx"), lax.axis_size("gy")
    steps = side_steps(gy)

    def faces(tile, low):
        half = rows // 2
        starts = (0, half) if low else (3 * width, half + 3 * width)
        return [tile[start : start + width] for start in starts] + [tile[rows : rows + META_ROWS]]

    def face(tile, low_core):
        low, high = (jnp.concatenate(faces(tile, low), axis=0) for low in (True, False))
        return jnp.where(core == low_core, low, high)

    far_face = face(own, 0)
    side = [lax.ppermute(own, "gy", step) for step in steps]
    far = lax.ppermute(far_face, "gx", far_steps(gx))
    fdiag = [
        lax.ppermute(
            far_face,
            ("gx", "gy"),
            [(a * gy + c, b * gy + d) for a, b in far_steps(gx) for c, d in step],
        )
        for step in steps
    ]
    near = swap(jnp.concatenate([face(tile, 1) for tile in [own] + side], axis=0), "gx", 1)
    return (own, *side, far, *fdiag, near)


def halved(keep, got, index, axis):
    def part(i):
        return (
            lax.dynamic_index_in_dim(keep, i, axis, keepdims=False)
            + lax.dynamic_index_in_dim(got, i, axis, keepdims=False).astype(jnp.float32)
        )

    return part(index), part(1 - index).astype(jnp.bfloat16)


def spread(whole, index, count, axis):
    return [
        lax.dynamic_index_in_dim(whole, index ^ m, axis, keepdims=False).astype(jnp.bfloat16)
        for m in range(1, count)
    ]


def per_device(features, block_coords, block_counts, first_weight, second_weight, cotangent):
    gx, gy = lax.axis_size("gx"), lax.axis_size("gy")
    ix, iy = lax.axis_index("gx"), lax.axis_index("gy")
    slots = features.shape[2]
    width = slots * PLANE
    rows = 8 * width
    core, half, deep = ix % 2, ix // 2 % 2, ix // 4
    deeps = gx // 4
    sides = 1 if gy == 2 else 2

    coords = block_coords.reshape(slots)
    count = block_counts.reshape(())
    lanes = np.arange(512)
    lane_slot = (lanes // PLANE) % slots
    position = sum(jnp.where(lane_slot == s, coords[s], 0) for s in range(slots))
    meta = jnp.stack(
        [
            position // 16,
            4 * (position // 8 % 2) + lanes % PLANE // 4,
            4 * (position % 8) + lanes % 4,
            (lane_slot < count).astype(jnp.int32),
        ]
    )
    meta = meta.reshape(4, 2, C).transpose(1, 0, 2).reshape(8, C).astype(jnp.bfloat16)
    meta = jnp.concatenate([meta, jnp.zeros((META_ROWS - 8, C), jnp.bfloat16)], axis=0)
    cells = np.arange(9 * width)
    shift, cell = cells // width, cells % PLANE
    cell_slot = cells // PLANE % slots
    position = sum(jnp.where(cell_slot == s, coords[s], 0) for s in range(slots))
    code = (
        (position // 16) * int(STEP_X)
        + (4 * (position // 8 % 2) + (cell // 4 + shift // 3 - 1)) * int(STEP_Y)
        + 4 * (position % 8)
        + (cell % 4 + shift % 3 - 1)
    ).astype(jnp.float32)[:, None]
    side_signs = [1 - 2 * iy] if sides == 1 else [-1, 1]
    where = jnp.stack([jnp.asarray(v, jnp.int32) for v in [1 - 2 * core, *side_signs, count]])
    place = core.astype(jnp.int32).reshape(1)

    def planes(field):
        return field.reshape(slots, 4, PLANE, C).transpose(1, 0, 2, 3).reshape(4 * width, C)

    own = jnp.concatenate([planes(features), planes(cotangent), meta], axis=0)
    around = exchanged(own, rows, width, core)
    in_specs = [pl.BlockSpec(memory_space=SMEM)] + [pl.BlockSpec(memory_space=VMEM)] * (
        len(around) + 3
    )
    out = pl.BlockSpec(memory_space=VMEM)
    cols = jax.ShapeDtypeStruct((9, 6 * width, C), jnp.bfloat16)
    both, feature_cols, seed_cols = pl.pallas_call(
        functools.partial(first_kernel, slots, sides),
        out_shape=(jax.ShapeDtypeStruct(own.shape, jnp.bfloat16), cols, cols),
        in_specs=in_specs,
        out_specs=(out, out, out),
        compiler_params=params(48),
        name="first_layer",
    )(where, code, *around, first_weight, second_weight)

    grad_scale = 1.0 / math.sqrt(64 * slots * gx * gy)
    chunk = TAPS * C // gx

    def terms(kernel, name, cols):
        return pl.pallas_call(
            functools.partial(kernel, slots, grad_scale),
            out_shape=(
                jax.ShapeDtypeStruct((gx // 2, chunk, C), jnp.float32),
                jax.ShapeDtypeStruct((gx // 2, chunk, C), jnp.bfloat16),
            ),
            in_specs=[pl.BlockSpec(memory_space=SMEM), out, out],
            out_specs=(out, out),
            scratch_shapes=[pltpu.VMEM((TAPS * C, C), jnp.float32)],
            compiler_params=params(48),
            name=name,
        )(place, both, cols)

    second_keep, second_send = terms(second_terms_kernel, "second_terms", seed_cols)
    first_keep, first_send = terms(first_terms_kernel, "first_terms", feature_cols)

    def shaped(cells):
        return cells.reshape(deeps, 2, chunk, gy, C // gy)

    def over_y(keep, axis):
        sent = spread(keep, iy, gy, axis)
        got = [swap(piece, "gy", m) for m, piece in enumerate(sent, 1)]
        own = lax.dynamic_index_in_dim(keep, iy, axis, keepdims=False)
        return own + sum(piece.astype(jnp.float32) for piece in got)

    def over_z(keep):
        sent = spread(keep, deep, deeps, 0)
        got = [swap(piece, "gx", 4 * m) for m, piece in enumerate(sent, 1)]
        own = lax.dynamic_index_in_dim(keep, deep, 0, keepdims=False)
        return own + sum(piece.astype(jnp.float32) for piece in got)

    second_got = shaped(swap(second_send, "gx", 1))
    second_keep, second_sent = halved(shaped(second_keep), second_got, half, 1)
    second_sum = second_keep + swap(second_sent, "gx", 2).astype(jnp.float32)
    second_grad = over_z(over_y(second_sum, 2))

    first_got = shaped(swap(first_send, "gx", 1))
    first_sum = over_y(shaped(first_keep) + first_got.astype(jnp.float32), 3)
    first_keep, first_sent = (
        lax.dynamic_index_in_dim(first_sum, half, 1, keepdims=False),
        lax.dynamic_index_in_dim(first_sum, 1 - half, 1, keepdims=False).astype(jnp.bfloat16),
    )
    first_sum = first_keep + swap(first_sent, "gx", 2).astype(jnp.float32)
    first_grad = over_z(first_sum)

    around = exchanged(both, rows, width, core)
    result = jax.ShapeDtypeStruct((slots, 64, C), jnp.float32)
    output, input_grad = pl.pallas_call(
        functools.partial(last_kernel, slots, sides),
        out_shape=(result, result),
        in_specs=in_specs,
        out_specs=(out, out),
        scratch_shapes=[pltpu.VMEM(cols.shape, jnp.bfloat16)] * 2,
        compiler_params=params(48),
        name="last_layer",
    )(where, code, *around, first_weight, second_weight)
    return (
        output.reshape(features.shape),
        input_grad.reshape(features.shape),
        first_grad,
        second_grad,
    )


def solution(mesh):
    placed = (
        P("gx", "gy", None, None, None),
        P("gx", "gy", None),
        P("gx", "gy"),
        P(),
        P(),
        P("gx", "gy", None, None, None),
    )
    return jax.shard_map(
        per_device,
        mesh=mesh,
        in_specs=placed,
        out_specs=(
            P("gx", "gy", None, None, None),
            P("gx", "gy", None, None, None),
            P("gx", "gy"),
            P("gx", "gy"),
        ),
        check_vma=False,
    )
```

time: 508 us -> 140 us (0.28); the launches traced: 500 us -> 138 us
  local copies, waits for them, and re-layouts: 380 us -> 34.3 us
  matrix products: 22.9 us -> 0 us
  Pallas kernels: 0 us -> 22.2 us
  starting transfers between devices: 47 us -> 30.2 us
  between operations: 15.9 us -> 1.75 us
  waiting for transfers between devices: 20.6 us -> 31.7 us
    unnamed x249 -> x45, local copies, waits for them, and re-layouts: 104 us -> 4.27 us
    concatenate x62 -> x0, local copies, waits for them, and re-layouts: 88.1 us -> none  [the longest x58 86.2 us: columns(): return jnp.concatenate(tap_list, axis=1)]
    reshape x60 -> x4, local copies, waits for them, and re-layouts: 96 us -> 11.6 us  [the longest x2 9.82 us: shaped(): return cells.reshape(deeps, 2, chunk, gy, C // gy)]
    gather x36 -> x0, local copies, waits for them, and re-layouts: 50.5 us -> none
    slice x16 -> x12, local copies, waits for them, and re-layouts: 34.5 us -> 1.4 us  [the longest x1 1.35 us: per_device(): coords[s]]
    dot_general x10 -> x0, matrix products: 22.9 us -> none  [the longest x2 8.12 us: contract_rows(): lax.dot_general(cols, rows, (((0,), (0,)), ((), ())), preferred_element_t...]
    pallas_call x0 -> x4, Pallas kernels: none -> 22.2 us  [the longest x1 7.69 us: per_device(): pl.pallas_call(functools.partial(first_kernel, slots, sides), out_shape=(...]
    ppermute x16 -> x20, waiting for transfers between devices: 12.9 us -> 31.7 us  [the longest x14 28.8 us: swap(): return lax.ppermute(cells, axis, [(i, i ^ bit) for i in range(count)])]
  transfers between devices with their start and end apart: 20 -> 20, of which waited for: 8 -> 8; matrix products, arithmetic and copies ran while one was open for 51% -> 29% of each run, Pallas kernels for 0% -> 8%
where the time goes in v1:
time: 140 us; the launch traced here: 138 us
  local copies, waits for them, and re-layouts  34.3 us (24%)
  waiting for transfers between devices  31.7 us (23%)
  starting transfers between devices  30.2 us (22%)
  Pallas kernels  22.2 us (16%)
  other arithmetic  17.5 us (12%)
  between operations  1.75 us (1%)
    ppermute x14, waiting for transfers between devices, swap(): return lax.ppermute(cells, axis, [(i, i ^ bit) for i in range(count)])  28.8 us
    ppermute x14, starting transfers between devices, swap(): return lax.ppermute(cells, axis, [(i, i ^ bit) for i in range(count)])  14 us
    reshape x2, local copies, waits for them, and re-layouts, shaped(): return cells.reshape(deeps, 2, chunk, gy, C // gy)  9.82 us
    ppermute x2, starting transfers between devices, exchanged(): lax.ppermute(far_face, ('gx', 'gy'), [(a * gy + c, b * gy + d) for a, b i...  9.68 us
    pallas_call x1, Pallas kernels, per_device(): pl.pallas_call(functools.partial(first_kernel, slots, sides), out_shape=(...  7.69 us
    pallas_call x1, Pallas kernels, per_device(): pl.pallas_call(functools.partial(last_kernel, slots, sides), out_shape=(r...  7.53 us
    pallas_call x2, Pallas kernels, terms(): pl.pallas_call(functools.partial(kernel, slots, grad_scale), out_shape=(j...  6.97 us
    ppermute x2, starting transfers between devices, exchanged(): far = lax.ppermute(far_face, 'gx', far_steps(gx))  4.35 us
  transfers between devices with their start and end apart: 20, of which 8 were waited for; matrix products, arithmetic and copies ran while one was open for 29% of the time, Pallas kernels for 8%

profile of v1, /device:TPU:8, one launch (start us, length us, event | category | flops | bytes accessed | tf_op | source)
XLA Modules:
  0.0 137.7 jit_solution(10394221771175800704)
XLA Ops:
  0.7 1.4 fusion.41
  2.0 2.7 %fusion.25 = (bf16[512]{0:T(512)(128)(2,1)S(1)}, bf16[512]{0:T(512)(128)(2,1)S(1)}, bf16[512]{0:T(512)(128)(2,1)S(1)}) fusion(pred[512]{0:T(512)(128)(4,1)} %constant.199.clone, s32[]{:T(128)} %bitcast.5, pred[512]{0:T(512)(128)(4,1)} %constant.198.clone, s32[]{:T(128)} %bitcast.4, pred[512]{0:T(512)(128)(4,1)} %constant.197.clone, s32[]{:T(128)} %bitcast.3, ...), kind=kLoop, calls=%fused_computation.86 | loop fusion | flops 26624 | bytes 8716 | tf_op jit(solution)/shard_map/convert.7
  6.2 0.9 copy.66
  7.1 0.9 copy.67
  8.0 1.6 %collective-permute-start = (bf16[400,256]{1,0:T(8,128)(2,1)S(1)}, bf16[400,256]{1,0:T(8,128)(2,1)S(1)}, u32[]{:S(2)}, u32[]{:S(2)}) collective-permute-start(bf16[400,256]{1,0:T(8,128)(2,1)S(1)} %pad_maximum_fusion.refs_2_), channel_id=1, source_target_pairs={{0,1},{1,0},{2,3},{3,2},{4,5},{5,4},{6,7},{7,6},{8,9},{9,8},{10,11... | collective-permute-start | bytes 614408 | tf_op jit(solution)/shard_map/ppermute | solution.py:242
  9.7 2.4 %collective-permute-start.1 = (bf16[112,256]{1,0:T(8,128)(2,1)S(1)}, bf16[112,256]{1,0:T(8,128)(2,1)S(1)}, u32[]{:S(2)}, u32[]{:S(2)}) collective-permute-start(bf16[112,256]{1,0:T(8,128)(2,1)S(1)} %get-tuple-element.44), channel_id=1, source_target_pairs={{2,4},{6,8},{10,12},{14,16},{18,20},{22,24},{26,28},{4,2},{8,6},{1... | collective-permute-start | bytes 172040 | tf_op jit(solution)/shard_map/ppermute | solution.py:243
  12.1 4.0 %collective-permute-start.2 = (bf16[112,256]{1,0:T(8,128)(2,1)S(1)}, bf16[112,256]{1,0:T(8,128)(2,1)S(1)}, u32[]{:S(2)}, u32[]{:S(2)}) collective-permute-start(bf16[112,256]{1,0:T(8,128)(2,1)S(1)} %get-tuple-element.44), channel_id=1, source_target_pairs={{2,5},{3,4},{6,9},{7,8},{10,13},{11,12},{14,17},{15,16},{18,21},{1... | collective-permute-start | bytes 172040 | tf_op jit(solution)/shard_map/ppermute | solution.py:245
  16.3 2.0 %fusion.18 = f32[432]{0:T(512)S(1)} fusion(s32[432]{0:T(512)S(1)} %copy-done.18, s32[432]{0:T(512)S(1)} %copy-done.17, pred[432]{0:T(512)(128)(4,1)S(1)} %copy-done.21, pred[432]{0:T(512)(128)(4,1)S(1)} %copy-done.20, pred[432]{0:T(512)(128)(4,1)S(1)} %copy-done.19, s32[]{:T(128)} %bitcast.5, s32[]{:T(128)} %bitcast.4, s32[]{:T(128)} %bitcast.3), kind=kLoop, calls=%fused_computation.79 | loop fusion | flops 23328 | bytes 6492 | tf_op jit(solution)/shard_map/convert_element_type | solution.py:307
  18.5 0.9 collective-permute-done.2.refs_5_
  19.5 7.7 %first_layer.1 = (bf16[400,256]{1,0:T(8,128)(2,1)S(1)}, bf16[9,288,256]{2,1,0:T(8,128)(2,1)S(1)}, bf16[9,288,256]{2,1,0:T(8,128)(2,1)S(1)}) custom-call(s32[3]{0:T(128)S(1)} %pad_add_fusion.refs_0_, f32[432,1]{1,0:T(8,128)S(1)} %copy.33.refs_1_, bf16[400,256]{1,0:T(8,128)(2,1)S(1)} %pad_maximum_fusion.refs_2_, ...), custom_call_target="tpu_custom_call" | custom-call | tf_op jit(solution)/shard_map/first_layer/pallas_call | solution.py:322
  27.2 3.6 %second_terms.1 = (f32[8,432,256]{2,1,0:T(8,128)}, bf16[8,432,256]{2,1,0:T(8,128)(2,1)}) custom-call(s32[1]{0:T(128)} %bitcast.21.place_ref, bf16[400,256]{1,0:T(8,128)(2,1)S(1)} %get-tuple-element.13.refs_2_.both_ref, bf16[9,288,256]{2,1,0:T(8,128)(2,1)S(1)} %get-tuple-element.19.cols_ref), custom_call_target="tpu_custom_call" | custom-call | tf_op jit(solution)/shard_map/second_terms/pallas_call | solution.py:335
  31.2 3.3 %first_terms.1 = (f32[8,432,256]{2,1,0:T(8,128)}, bf16[8,432,256]{2,1,0:T(8,128)(2,1)S(1)}) custom-call(s32[1]{0:T(128)} %bitcast.21.place_ref, bf16[400,256]{1,0:T(8,128)(2,1)S(1)} %get-tuple-element.13.refs_2_.both_ref, bf16[9,288,256]{2,1,0:T(8,128)(2,1)S(1)} %get-tuple-element.16.cols_ref), custom_call_target="tpu_custom_call" | custom-call | tf_op jit(solution)/shard_map/first_terms/pallas_call | solution.py:335
  36.0 5.4 %reshape.90 = f32[4,2,432,2,128]{4,3,2,1,0:T(2,128)} reshape(f32[8,432,256]{2,1,0:T(8,128)} %get-tuple-element.20) | data formatting | bytes 7077888 | tf_op jit(solution)/shard_map/reshape | solution.py:352
  41.3 4.0 %constant_dynamic-slice_fusion.1 = (f32[4,1,432,2,128]{4,3,2,1,0:T(2,128)}, f32[4,1,432,2,128]{4,3,2,1,0:T(2,128)}) fusion(f32[4,2,432,2,128]{4,3,2,1,0:T(2,128)} %reshape.90, s32[]{:T(128)S(6)} %select_n.172, s32[]{:T(128)S(6)} %select_n.171), kind=kLoop, calls=%fused_computation.46 | loop fusion | bytes 7077896 | tf_op jit(solution)/shard_map/jit(dynamic_index_in_dim)/dynamic_slice | solution.py:259
  46.1 4.5 %reshape.91 = bf16[4,2,432,2,128]{4,3,2,1,0:T(2,128)(2,1)} reshape(bf16[8,432,256]{2,1,0:T(8,128)(2,1)} %collective-permute-done.14) | data formatting | bytes 3538944 | tf_op jit(solution)/shard_map/reshape | solution.py:352
  50.5 3.7 %constant_dynamic-slice_fusion.2 = (bf16[4,1,432,2,128]{4,3,2,1,0:T(2,128)(2,1)}, bf16[4,1,432,2,128]{4,3,2,1,0:T(2,128)(2,1)S(1)}) fusion(bf16[4,2,432,2,128]{4,3,2,1,0:T(2,128)(2,1)} %reshape.91, s32[]{:T(128)S(6)} %select_n.171, s32[]{:T(128)S(6)} %select_n.172), kind=kLoop, calls=%fused_computation.47 | loop fusion | bytes 3538952 | tf_op jit(solution)/shard_map/jit(dynamic_index_in_dim)/dynamic_slice | solution.py:260
  54.2 1.1 fusion.4
  55.3 2.0 %collective-permute-start.15 = (bf16[4,432,2,128]{3,1,0,2:T(8,128)(2,1)}, bf16[4,432,2,128]{3,1,0,2:T(8,128)(2,1)}, u32[]{:S(2)}, u32[]{:S(2)}) collective-permute-start(bf16[4,432,2,128]{3,1,0,2:T(8,128)(2,1)} %fusion.4), channel_id=1, source_target_pairs={{0,4},{2,6},{4,0},{6,2},{8,12},{10,14},{12,8},{14,10},{16,20},{18,... | collective-permute-start | bytes 2654216 | tf_op jit(solution)/shard_map/ppermute | solution.py:210
  57.3 3.6 %convert_add_fusion = f32[8,432,256]{2,1,0:T(8,128)} fusion(f32[8,432,256]{2,1,0:T(8,128)S(1)} %copy-done.13, bf16[8,432,256]{2,1,0:T(8,128)(2,1)} %collective-permute-done.8), kind=kLoop, calls=%fused_computation | loop fusion | flops 1769472 | bytes 8847360 | tf_op jit(solution)/shard_map/add | solution.py:372
  60.9 3.7 %add.166 = f32[4,2,432,2,128]{4,3,2,1,0:T(2,128)S(1)} reshape(f32[8,432,256]{2,1,0:T(8,128)} %convert_add_fusion) | data formatting | bytes 7077888 | tf_op jit(solution)/shard_map/add | solution.py:372
  64.6 1.6 %constant_dynamic-slice_fusion.4 = bf16[4,2,432,1,128]{4,3,2,1,0:T(2,128)(2,1)S(1)} fusion(f32[4,2,432,2,128]{4,3,2,1,0:T(2,128)S(1)} %add.166, s32[]{:T(128)S(6)} %select_n.168), kind=kLoop, calls=%fused_computation.49 | loop fusion | bytes 1769476 | tf_op jit(solution)/shard_map/jit(dynamic_index_in_dim)/dynamic_slice | solution.py:268
  66.4 1.6 %collective-permute-start.9 = (bf16[4,2,432,128]{3,2,0,1:T(8,128)(2,1)S(1)}, bf16[4,2,432,128]{3,2,0,1:T(8,128)(2,1)S(1)}, u32[]{:S(2)}, u32[]{:S(2)}) collective-permute-start(bf16[4,2,432,128]{3,2,0,1:T(8,128)(2,1)S(1)} %bitcast.66), channel_id=1, source_target_pairs={{0,1},{1,0},{2,3},{3,2},{4,5},{5,4},{6,7},{7,6},{8,9},{9,8},{10,11... | collective-permute-start | bytes 2654216 | tf_op jit(solution)/shard_map/ppermute | solution.py:210
  68.6 1.8 %constant_dynamic-slice_fusion.5 = f32[4,2,432,1,128]{4,3,2,1,0:T(1,128)S(1)} fusion(f32[4,2,432,2,128]{4,3,2,1,0:T(2,128)S(1)} %add.166, s32[]{:T(128)S(6)} %select_n.167), kind=kLoop, calls=%fused_computation.50 | loop fusion | bytes 3538948 | tf_op jit(solution)/shard_map/jit(dynamic_index_in_dim)/dynamic_slice | solution.py:357
  70.5 7.2 %collective-permute-done.15 = bf16[4,432,2,128]{3,1,0,2:T(8,128)(2,1)} collective-permute-done((bf16[4,432,2,128]{3,1,0,2:T(8,128)(2,1)}, bf16[4,432,2,128]{3,1,0,2:T(8,128)(2,1)}, u32[]{:S(2)}, u32[]{:S(2)}) %collective-permute-start.15) | collective-permute-done | bytes 884768 | tf_op jit(solution)/shard_map/ppermute | solution.py:210
  77.7 1.4 %fusion.2 = f32[4,432,2,128]{3,1,0,2:T(8,128)S(1)} fusion(f32[4,1,432,2,128]{4,3,2,1,0:T(2,128)S(1)} %copy-done.8, bf16[4,432,2,128]{3,1,0,2:T(8,128)(2,1)} %collective-permute-done.15, bf16[4,1,432,2,128]{4,3,2,1,0:T(2,128)(2,1)S(1)} %copy-done.14), kind=kLoop, calls=%fused_computation.5 | loop fusion | flops 1769472 | bytes 5308416 | tf_op jit(solution)/shard_map/add | solution.py:368
  79.1 1.0 fusion.6
  80.0 1.5 %collective-permute-start.16 = (bf16[4,432,128]{2,1,0:T(8,128)(2,1)}, bf16[4,432,128]{2,1,0:T(8,128)(2,1)}, u32[]{:S(2)}, u32[]{:S(2)}) collective-permute-start(bf16[4,432,128]{2,1,0:T(8,128)(2,1)} %fusion.6), channel_id=1, source_target_pairs={{0,1},{1,0},{2,3},{3,2},{4,5},{5,4},{6,7},{7,6},{8,9},{9,8},{10,11... | collective-permute-start | bytes 1327112 | tf_op jit(solution)/shard_map/ppermute | solution.py:210
  81.5 7.4 %collective-permute-done.9 = bf16[4,2,432,128]{3,2,0,1:T(8,128)(2,1)S(1)} collective-permute-done((bf16[4,2,432,128]{3,2,0,1:T(8,128)(2,1)S(1)}, bf16[4,2,432,128]{3,2,0,1:T(8,128)(2,1)S(1)}, u32[]{:S(2)}, u32[]{:S(2)}) %collective-permute-start.9) | collective-permute-done | bytes 884768 | tf_op jit(solution)/shard_map/ppermute | solution.py:210
  89.1 1.3 copy-done.9
  90.4 0.9 fusion.5
  91.2 1.2 collective-permute-start.10
  92.4 1.9 %collective-permute-start.5 = (bf16[112,256]{1,0:T(8,128)(2,1)}, bf16[112,256]{1,0:T(8,128)(2,1)}, u32[]{:S(2)}, u32[]{:S(2)}) collective-permute-start(bf16[112,256]{1,0:T(8,128)(2,1)} %get-tuple-element.42), channel_id=1, source_target_pairs={{2,4},{6,8},{10,12},{14,16},{18,20},{22,24},{26,28},{4,2},{8,6},{1... | collective-permute-start | bytes 172040 | tf_op jit(solution)/shard_map/ppermute | solution.py:243
  94.4 5.7 %collective-permute-start.6 = (bf16[112,256]{1,0:T(8,128)(2,1)}, bf16[112,256]{1,0:T(8,128)(2,1)}, u32[]{:S(2)}, u32[]{:S(2)}) collective-permute-start(bf16[112,256]{1,0:T(8,128)(2,1)} %get-tuple-element.42), channel_id=1, source_target_pairs={{2,5},{3,4},{6,9},{7,8},{10,13},{11,12},{14,17},{15,16},{18,21},{1... | collective-permute-start | bytes 172040 | tf_op jit(solution)/shard_map/ppermute | solution.py:245
  100.1 2.0 %collective-permute-done.6.refs_5_ = bf16[112,256]{1,0:T(8,128)(2,1)} collective-permute-done((bf16[112,256]{1,0:T(8,128)(2,1)}, bf16[112,256]{1,0:T(8,128)(2,1)}, u32[]{:S(2)}, u32[]{:S(2)}) %collective-permute-start.6) | collective-permute-done | bytes 57376 | tf_op jit(solution)/shard_map/ppermute | solution.py:245
  102.1 0.9 copy-done.2
  103.1 0.9 copy-done.4
  104.0 0.9 copy-done.6
  104.9 7.5 %last_layer.1 = (f32[3,64,256]{2,1,0:T(8,128)}, f32[3,64,256]{2,1,0:T(8,128)}) custom-call(s32[3]{0:T(128)S(1)} %pad_add_fusion.refs_0_, f32[432,1]{1,0:T(8,128)S(1)} %copy-done.4, bf16[400,256]{1,0:T(8,128)(2,1)S(1)} %copy-done.2, bf16[400,256]{1,0:T(8,128)(2,1)S(1)} %copy-done.6, bf16[112,256]{1,0:T(8,128)(2,1)} %collective-permute-done.5.refs_4_, ...), custom_call_target="tpu_custom_call" | custom-call | tf_op jit(solution)/shard_map/last_layer/pallas_call | solution.py:382
  112.5 1.2 bitcast_add_fusion.1
  113.8 3.0 %collective-permute-start.18 = (bf16[432,128]{1,0:T(8,128)(2,1)S(1)}, bf16[432,128]{1,0:T(8,128)(2,1)S(1)}, u32[]{:S(2)}, u32[]{:S(2)}) collective-permute-start(bf16[432,128]{1,0:T(8,128)(2,1)S(1)} %get-tuple-element.28), channel_id=1, source_target_pairs={{0,16},{2,18},{4,20},{6,22},{8,24},{10,26},{12,28},{14,30},{16,0},... | collective-permute-start | bytes 331784 | tf_op jit(solution)/shard_map/ppermute | solution.py:210
  117.3 1.1 bitcast_add_fusion.2
  118.5 1.1 collective-permute-start.11
  119.6 2.0 %collective-permute-start.12 = (bf16[432,128]{1,0:T(8,128)(2,1)S(1)}, bf16[432,128]{1,0:T(8,128)(2,1)S(1)}, u32[]{:S(2)}, u32[]{:S(2)}) collective-permute-start(bf16[432,128]{1,0:T(8,128)(2,1)S(1)} %get-tuple-element.31), channel_id=1, source_target_pairs={{0,16},{2,18},{4,20},{6,22},{8,24},{10,26},{12,28},{14,30},{16,0},... | collective-permute-start | bytes 331784 | tf_op jit(solution)/shard_map/ppermute | solution.py:210
  122.4 8.7 %collective-permute-done.19 = bf16[432,128]{1,0:T(8,128)(2,1)S(1)} collective-permute-done((bf16[432,128]{1,0:T(8,128)(2,1)S(1)}, bf16[432,128]{1,0:T(8,128)(2,1)S(1)}, u32[]{:S(2)}, u32[]{:S(2)}) %collective-permute-start.19) | collective-permute-done | bytes 110624 | tf_op jit(solution)/shard_map/ppermute | solution.py:210
  131.1 0.7 bitcast_add_fusion.3
  131.8 1.8 %collective-permute-done.12 = bf16[432,128]{1,0:T(8,128)(2,1)S(1)} collective-permute-done((bf16[432,128]{1,0:T(8,128)(2,1)S(1)}, bf16[432,128]{1,0:T(8,128)(2,1)S(1)}, u32[]{:S(2)}, u32[]{:S(2)}) %collective-permute-start.12) | collective-permute-done | bytes 110624 | tf_op jit(solution)/shard_map/ppermute | solution.py:210
  133.6 3.3 %collective-permute-done.13 = bf16[432,128]{1,0:T(8,128)(2,1)S(1)} collective-permute-done((bf16[432,128]{1,0:T(8,128)(2,1)S(1)}, bf16[432,128]{1,0:T(8,128)(2,1)S(1)}, u32[]{:S(2)}, u32[]{:S(2)}) %collective-permute-start.13) | collective-permute-done | bytes 110624 | tf_op jit(solution)/shard_map/ppermute | solution.py:210
  136.9 0.7 bitcast_add_fusion.4
  (94 shorter events, 6.2 us)
Async XLA Ops:
  0.6 15.7 %copy-start.19 = (pred[432]{0:T(512)(128)(4,1)S(1)}, pred[432]{0:T(512)(128)(4,1)}, u32[]{:S(2)}) copy-start(pred[432]{0:T(512)(128)(4,1)} %constant.203.clone) | copy-start | bytes 1300
  0.6 15.6 %copy-start.20 = (pred[432]{0:T(512)(128)(4,1)S(1)}, pred[432]{0:T(512)(128)(4,1)}, u32[]{:S(2)}) copy-start(pred[432]{0:T(512)(128)(4,1)} %constant.204.clone) | copy-start | bytes 1300
  0.7 15.6 %copy-start.21 = (pred[432]{0:T(512)(128)(4,1)S(1)}, pred[432]{0:T(512)(128)(4,1)}, u32[]{:S(2)}) copy-start(pred[432]{0:T(512)(128)(4,1)} %constant.205.clone) | copy-start | bytes 1300
  0.7 15.6 %copy-start.17 = (s32[432]{0:T(512)S(1)}, s32[432]{0:T(512)}, u32[]{:S(2)}) copy-start(s32[432]{0:T(512)} %constant.206.clone) | copy-start | bytes 5188
  0.7 15.6 %copy-start.18 = (s32[432]{0:T(512)S(1)}, s32[432]{0:T(512)}, u32[]{:S(2)}) copy-start(s32[432]{0:T(512)} %constant.207.clone) | copy-start | bytes 5188
  8.0 8.1 %collective-permute-start = (bf16[400,256]{1,0:T(8,128)(2,1)S(1)}, bf16[400,256]{1,0:T(8,128)(2,1)S(1)}, u32[]{:S(2)}, u32[]{:S(2)}) collective-permute-start(bf16[400,256]{1,0:T(8,128)(2,1)S(1)} %pad_maximum_fusion.refs_2_), channel_id=1, source_target_pairs={{0,1},{1,0},{2,3},{3,2},{4,5},{5,4},{6,7},{7,6},{8,9},{9,8},{10,11... | collective-permute-start | bytes 614408 | tf_op jit(solution)/shard_map/ppermute | solution.py:242
  9.7 8.9 %collective-permute-start.1 = (bf16[112,256]{1,0:T(8,128)(2,1)S(1)}, bf16[112,256]{1,0:T(8,128)(2,1)S(1)}, u32[]{:S(2)}, u32[]{:S(2)}) collective-permute-start(bf16[112,256]{1,0:T(8,128)(2,1)S(1)} %get-tuple-element.44), channel_id=1, source_target_pairs={{2,4},{6,8},{10,12},{14,16},{18,20},{22,24},{26,28},{4,2},{8,6},{1... | collective-permute-start | bytes 172040 | tf_op jit(solution)/shard_map/ppermute | solution.py:243
  12.1 7.3 %collective-permute-start.2 = (bf16[112,256]{1,0:T(8,128)(2,1)S(1)}, bf16[112,256]{1,0:T(8,128)(2,1)S(1)}, u32[]{:S(2)}, u32[]{:S(2)}) collective-permute-start(bf16[112,256]{1,0:T(8,128)(2,1)S(1)} %get-tuple-element.44), channel_id=1, source_target_pairs={{2,5},{3,4},{6,9},{7,8},{10,13},{11,12},{14,17},{15,16},{18,21},{1... | collective-permute-start | bytes 172040 | tf_op jit(solution)/shard_map/ppermute | solution.py:245
  16.2 3.3 %collective-permute-start.3 = (bf16[224,256]{1,0:T(8,128)(2,1)S(1)}, bf16[224,256]{1,0:T(8,128)(2,1)S(1)}, u32[]{:S(2)}, u32[]{:S(2)}) collective-permute-start(bf16[224,256]{1,0:T(8,128)(2,1)S(1)} %pad_maximum_fusion.1), channel_id=1, source_target_pairs={{0,2},{2,0},{4,6},{6,4},{8,10},{10,8},{12,14},{14,12},{16,18},{18,... | collective-permute-start | bytes 344072 | tf_op jit(solution)/shard_map/ppermute | solution.py:210
  18.5 8.7 %copy-start.3 = (f32[432,1]{1,0:T(8,128)}, f32[432,1]{1,0:T(8,128)S(1)}, u32[]{:S(2)}) copy-start(f32[432,1]{1,0:T(8,128)S(1)} %copy.33.refs_1_) | copy-start | bytes 5188
  27.2 8.8 %copy-start.1 = (bf16[400,256]{1,0:T(8,128)(2,1)}, bf16[400,256]{1,0:T(8,128)(2,1)S(1)}, u32[]{:S(2)}) copy-start(bf16[400,256]{1,0:T(8,128)(2,1)S(1)} %get-tuple-element.13.refs_2_.both_ref) | copy-start | bytes 614404
  30.8 15.3 %collective-permute-start.14 = (bf16[8,432,256]{2,1,0:T(8,128)(2,1)}, bf16[8,432,256]{2,1,0:T(8,128)(2,1)}, u32[]{:S(2)}, u32[]{:S(2)}) collective-permute-start(bf16[8,432,256]{2,1,0:T(8,128)(2,1)} %get-tuple-element.21), channel_id=1, source_target_pairs={{0,2},{2,0},{4,6},{6,4},{8,10},{10,8},{12,14},{14,12},{16,18},{18,... | collective-permute-start | bytes 5308424 | tf_op jit(solution)/shard_map/ppermute | solution.py:210
  34.6 22.7 %collective-permute-start.8 = (bf16[8,432,256]{2,1,0:T(8,128)(2,1)S(1)}, bf16[8,432,256]{2,1,0:T(8,128)(2,1)}, u32[]{:S(2)}, u32[]{:S(2)}) collective-permute-start(bf16[8,432,256]{2,1,0:T(8,128)(2,1)S(1)} %get-tuple-element.18), channel_id=1, source_target_pairs={{0,2},{2,0},{4,6},{6,4},{8,10},{10,8},{12,14},{14,12},{16,18},{18,... | collective-permute-start | bytes 5308424 | tf_op jit(solution)/shard_map/ppermute | solution.py:210
  34.7 10.7 %collective-permute-start.4 = (bf16[400,256]{1,0:T(8,128)(2,1)S(1)}, bf16[400,256]{1,0:T(8,128)(2,1)S(1)}, u32[]{:S(2)}, u32[]{:S(2)}) collective-permute-start(bf16[400,256]{1,0:T(8,128)(2,1)S(1)} %get-tuple-element.13.refs_2_.both_ref), channel_id=1, source_target_pairs={{0,1},{1,0},{2,3},{3,2},{4,5},{5,4},{6,7},{7,6},{8,9},{9,8},{10,11... | collective-permute-start | bytes 614408 | tf_op jit(solution)/shard_map/ppermute | solution.py:242
  45.4 5.2 %copy-start.5 = (bf16[400,256]{1,0:T(8,128)(2,1)}, bf16[400,256]{1,0:T(8,128)(2,1)S(1)}, u32[]{:S(2)}) copy-start(bf16[400,256]{1,0:T(8,128)(2,1)S(1)} %collective-permute-done.4.refs_3_) | copy-start | bytes 614404
  50.5 3.7 %copy-start.7 = (f32[4,1,432,2,128]{4,3,2,1,0:T(2,128)S(1)}, f32[4,1,432,2,128]{4,3,2,1,0:T(2,128)}, u32[]{:S(2)}) copy-start(f32[4,1,432,2,128]{4,3,2,1,0:T(2,128)} %get-tuple-element.22) | copy-start | bytes 5308420
  54.2 3.1 %copy-start.13 = (f32[8,432,256]{2,1,0:T(8,128)S(1)}, f32[8,432,256]{2,1,0:T(8,128)}, u32[]{:S(2)}) copy-start(f32[8,432,256]{2,1,0:T(8,128)} %get-tuple-element.17) | copy-start | bytes 10616836
  55.3 22.3 %collective-permute-start.15 = (bf16[4,432,2,128]{3,1,0,2:T(8,128)(2,1)}, bf16[4,432,2,128]{3,1,0,2:T(8,128)(2,1)}, u32[]{:S(2)}, u32[]{:S(2)}) collective-permute-start(bf16[4,432,2,128]{3,1,0,2:T(8,128)(2,1)} %fusion.4), channel_id=1, source_target_pairs={{0,4},{2,6},{4,0},{6,2},{8,12},{10,14},{12,8},{14,10},{16,20},{18,... | collective-permute-start | bytes 2654216 | tf_op jit(solution)/shard_map/ppermute | solution.py:210
  66.2 1.7 %copy-start.15 = (bf16[112,256]{1,0:T(8,128)(2,1)S(1)}, bf16[112,256]{1,0:T(8,128)(2,1)}, u32[]{:S(2)}) copy-start(bf16[112,256]{1,0:T(8,128)(2,1)} %get-tuple-element.41) | copy-start | bytes 172036
  66.3 1.7 %copy-start.16 = (bf16[112,256]{1,0:T(8,128)(2,1)S(1)}, bf16[112,256]{1,0:T(8,128)(2,1)}, u32[]{:S(2)}) copy-start(bf16[112,256]{1,0:T(8,128)(2,1)} %maximum_select_fusion.1) | copy-start | bytes 172036
  66.4 22.6 %collective-permute-start.9 = (bf16[4,2,432,128]{3,2,0,1:T(8,128)(2,1)S(1)}, bf16[4,2,432,128]{3,2,0,1:T(8,128)(2,1)S(1)}, u32[]{:S(2)}, u32[]{:S(2)}) collective-permute-start(bf16[4,2,432,128]{3,2,0,1:T(8,128)(2,1)S(1)} %bitcast.66), channel_id=1, source_target_pairs={{0,1},{1,0},{2,3},{3,2},{4,5},{5,4},{6,7},{7,6},{8,9},{9,8},{10,11... | collective-permute-start | bytes 2654216 | tf_op jit(solution)/shard_map/ppermute | solution.py:210
  68.6 9.0 %copy-start.8 = (f32[4,1,432,2,128]{4,3,2,1,0:T(2,128)S(1)}, f32[4,1,432,2,128]{4,3,2,1,0:T(2,128)}, u32[]{:S(2)}) copy-start(f32[4,1,432,2,128]{4,3,2,1,0:T(2,128)} %get-tuple-element.23) | copy-start | bytes 5308420
  68.6 9.0 %copy-start.14 = (bf16[4,1,432,2,128]{4,3,2,1,0:T(2,128)(2,1)S(1)}, bf16[4,1,432,2,128]{4,3,2,1,0:T(2,128)(2,1)}, u32[]{:S(2)}) copy-start(bf16[4,1,432,2,128]{4,3,2,1,0:T(2,128)(2,1)} %get-tuple-element.24) | copy-start | bytes 2654212
  68.6 33.5 %collective-permute-start.7 = (bf16[224,256]{1,0:T(8,128)(2,1)}, bf16[224,256]{1,0:T(8,128)(2,1)}, u32[]{:S(2)}, u32[]{:S(2)}) collective-permute-start(bf16[224,256]{1,0:T(8,128)(2,1)} %pad_maximum_fusion.2), channel_id=1, source_target_pairs={{0,2},{2,0},{4,6},{6,4},{8,10},{10,8},{12,14},{14,12},{16,18},{18,... | collective-permute-start | bytes 344072 | tf_op jit(solution)/shard_map/ppermute | solution.py:210
  79.1 2.5 %copy-start.11 = (f32[4,432,2,128]{3,1,0,2:T(8,128)}, f32[4,432,2,128]{3,1,0,2:T(8,128)S(1)}, u32[]{:S(2)}) copy-start(f32[4,432,2,128]{3,1,0,2:T(8,128)S(1)} %fusion.2) | copy-start | bytes 5308420
  80.0 22.1 %copy-start = (bf16[6912,256]{1,0:T(8,128)(2,1)S(1)}, bf16[6912,256]{1,0:T(8,128)(2,1)}, u32[]{:S(2)}) copy-start(bf16[6912,256]{1,0:T(8,128)(2,1)} %refs_7_.3) | copy-start | bytes 10616836
  80.0 32.5 %collective-permute-start.16 = (bf16[4,432,128]{2,1,0:T(8,128)(2,1)}, bf16[4,432,128]{2,1,0:T(8,128)(2,1)}, u32[]{:S(2)}, u32[]{:S(2)}) collective-permute-start(bf16[4,432,128]{2,1,0:T(8,128)(2,1)} %fusion.6), channel_id=1, source_target_pairs={{0,1},{1,0},{2,3},{3,2},{4,5},{5,4},{6,7},{7,6},{8,9},{9,8},{10,11... | collective-permute-start | bytes 1327112 | tf_op jit(solution)/shard_map/ppermute | solution.py:210
  89.1 1.3 copy-start.9
  91.2 26.1 %collective-permute-start.10 = (bf16[4,432,128]{2,1,0:T(8,128)(2,1)}, bf16[4,432,128]{2,1,0:T(8,128)(2,1)}, u32[]{:S(2)}, u32[]{:S(2)}) collective-permute-start(bf16[4,432,128]{2,1,0:T(8,128)(2,1)} %fusion.5), channel_id=1, source_target_pairs={{0,4},{2,6},{4,0},{6,2},{8,12},{10,14},{12,8},{14,10},{16,20},{18,... | collective-permute-start | bytes 1327112 | tf_op jit(solution)/shard_map/ppermute | solution.py:210
  92.4 7.7 %collective-permute-start.5 = (bf16[112,256]{1,0:T(8,128)(2,1)}, bf16[112,256]{1,0:T(8,128)(2,1)}, u32[]{:S(2)}, u32[]{:S(2)}) collective-permute-start(bf16[112,256]{1,0:T(8,128)(2,1)} %get-tuple-element.42), channel_id=1, source_target_pairs={{2,4},{6,8},{10,12},{14,16},{18,20},{22,24},{26,28},{4,2},{8,6},{1... | collective-permute-start | bytes 172040 | tf_op jit(solution)/shard_map/ppermute | solution.py:243
  94.4 7.8 %collective-permute-start.6 = (bf16[112,256]{1,0:T(8,128)(2,1)}, bf16[112,256]{1,0:T(8,128)(2,1)}, u32[]{:S(2)}, u32[]{:S(2)}) collective-permute-start(bf16[112,256]{1,0:T(8,128)(2,1)} %get-tuple-element.42), channel_id=1, source_target_pairs={{2,5},{3,4},{6,9},{7,8},{10,13},{11,12},{14,17},{15,16},{18,21},{1... | collective-permute-start | bytes 172040 | tf_op jit(solution)/shard_map/ppermute | solution.py:245
  102.1 0.9 copy-start.2
  103.1 0.9 copy-start.4
  104.0 0.9 copy-start.6
  104.9 7.5 %copy-start.12 = (f32[4,432,2,128]{3,1,0,2:T(8,128)S(1)}, f32[4,432,2,128]{3,1,0,2:T(8,128)}, u32[]{:S(2)}) copy-start(f32[4,432,2,128]{3,1,0,2:T(8,128)} %copy-done.11) | copy-start | bytes 5308420
  112.5 4.9 %copy-start.10 = (f32[4,2,432,128]{3,2,0,1:T(8,128)S(1)}, f32[4,2,432,128]{3,2,0,1:T(8,128)}, u32[]{:S(2)}) copy-start(f32[4,2,432,128]{3,2,0,1:T(8,128)} %copy-done.9) | copy-start | bytes 5308420
  113.8 7.8 %collective-permute-start.17 = (bf16[432,128]{1,0:T(8,128)(2,1)S(1)}, bf16[432,128]{1,0:T(8,128)(2,1)S(1)}, u32[]{:S(2)}, u32[]{:S(2)}) collective-permute-start(bf16[432,128]{1,0:T(8,128)(2,1)S(1)} %get-tuple-element.26), channel_id=1, source_target_pairs={{0,8},{2,10},{4,12},{6,14},{8,0},{10,2},{12,4},{14,6},{16,24},{18,... | collective-permute-start | bytes 331784 | tf_op jit(solution)/shard_map/ppermute | solution.py:210
  113.8 8.6 %collective-permute-start.18 = (bf16[432,128]{1,0:T(8,128)(2,1)S(1)}, bf16[432,128]{1,0:T(8,128)(2,1)S(1)}, u32[]{:S(2)}, u32[]{:S(2)}) collective-permute-start(bf16[432,128]{1,0:T(8,128)(2,1)S(1)} %get-tuple-element.28), channel_id=1, source_target_pairs={{0,16},{2,18},{4,20},{6,22},{8,24},{10,26},{12,28},{14,30},{16,0},... | collective-permute-start | bytes 331784 | tf_op jit(solution)/shard_map/ppermute | solution.py:210
  116.9 14.2 %collective-permute-start.19 = (bf16[432,128]{1,0:T(8,128)(2,1)S(1)}, bf16[432,128]{1,0:T(8,128)(2,1)S(1)}, u32[]{:S(2)}, u32[]{:S(2)}) collective-permute-start(bf16[432,128]{1,0:T(8,128)(2,1)S(1)} %get-tuple-element.27), channel_id=1, source_target_pairs={{0,24},{2,26},{4,28},{6,30},{8,16},{10,18},{12,20},{14,22},{16,8},... | collective-permute-start | bytes 331784 | tf_op jit(solution)/shard_map/ppermute | solution.py:210
  118.5 13.4 %collective-permute-start.11 = (bf16[432,128]{1,0:T(8,128)(2,1)S(1)}, bf16[432,128]{1,0:T(8,128)(2,1)S(1)}, u32[]{:S(2)}, u32[]{:S(2)}) collective-permute-start(bf16[432,128]{1,0:T(8,128)(2,1)S(1)} %get-tuple-element.29), channel_id=1, source_target_pairs={{0,8},{2,10},{4,12},{6,14},{8,0},{10,2},{12,4},{14,6},{16,24},{18,... | collective-permute-start | bytes 331784 | tf_op jit(solution)/shard_map/ppermute | solution.py:210
  119.6 14.1 %collective-permute-start.12 = (bf16[432,128]{1,0:T(8,128)(2,1)S(1)}, bf16[432,128]{1,0:T(8,128)(2,1)S(1)}, u32[]{:S(2)}, u32[]{:S(2)}) collective-permute-start(bf16[432,128]{1,0:T(8,128)(2,1)S(1)} %get-tuple-element.31), channel_id=1, source_target_pairs={{0,16},{2,18},{4,20},{6,22},{8,24},{10,26},{12,28},{14,30},{16,0},... | collective-permute-start | bytes 331784 | tf_op jit(solution)/shard_map/ppermute | solution.py:210
  121.6 15.3 %collective-permute-start.13 = (bf16[432,128]{1,0:T(8,128)(2,1)S(1)}, bf16[432,128]{1,0:T(8,128)(2,1)S(1)}, u32[]{:S(2)}, u32[]{:S(2)}) collective-permute-start(bf16[432,128]{1,0:T(8,128)(2,1)S(1)} %get-tuple-element.30), channel_id=1, source_target_pairs={{0,24},{2,26},{4,28},{6,30},{8,16},{10,18},{12,20},{14,22},{16,8},... | collective-permute-start | bytes 331784 | tf_op jit(solution)/shard_map/ppermute | solution.py:210

commit v2 on v0

v2 whole, which is shorter than its diff:
```python
import functools
import math

import jax
import jax.numpy as jnp
from jax import lax
from jax.experimental import pallas as pl
from jax.experimental.pallas import tpu as pltpu
from jax.sharding import PartitionSpec as P

C = 256
TAPS = 27
PLANE = 16
META = 16
LANES = 512
STEP_Y = 64.0
STEP_X = 4096.0
NOWHERE = -1.0e7
VMEM = pl.BlockSpec(memory_space=pltpu.MemorySpace.VMEM)
SMEM = pl.BlockSpec(memory_space=pltpu.MemorySpace.SMEM)


def params(mib):
    return pltpu.CompilerParams(vmem_limit_bytes=mib * 2**20)


def dot(lhs, rhs, dims=((1,), (0,))):
    return lax.dot_general(lhs, rhs, (dims, ((), ())), preferred_element_type=jnp.float32)


def iota(shape, dim):
    return lax.broadcasted_iota(jnp.int32, shape, dim)


def place_codes(meta, offset, absent=NOWHERE):
    rows = meta.astype(jnp.float32)
    parts = []
    for half in range(2):
        x, y, z, live = (rows[4 * half + i : 4 * half + i + 1] for i in range(4))
        parts.append(jnp.where(live > 0.5, x * STEP_X + y * STEP_Y + z + offset, absent))
    return jnp.concatenate(parts, axis=1)


def source_codes(metas, near, side_offsets, width):
    offsets = [0.0, *side_offsets, near, -near]
    for side_offset in side_offsets:
        offsets += [near + side_offset, side_offset - near]
    lane = iota((1, LANES), 1)
    total = jnp.full((1, LANES), NOWHERE, jnp.float32)
    for place, (meta, offset) in enumerate(zip(metas, offsets)):
        inside = (lane >= place * width) & (lane < (place + 1) * width)
        total = jnp.where(inside, place_codes(meta, offset), total)
    return total


def target_codes(meta, width):
    codes = place_codes(meta, 0.0, 3 * NOWHERE)
    own = iota((width, LANES), 0) == iota((width, LANES), 1)
    column = jnp.sum(jnp.where(own, codes, 0.0), axis=1, keepdims=True)
    return jnp.concatenate(
        [column + ((s // 3 - 1) * STEP_Y + (s % 3 - 1)) for s in range(9)], axis=0
    )


def selectors(source, target, sides, width):
    edge = source[:, : 3 * (1 + sides) * width]
    middle = source[:, : (1 + sides) * width]
    return tuple(
        (codes == target + step).astype(jnp.float32).astype(jnp.bfloat16)
        for codes, step in ((edge, -STEP_X), (middle, 0.0), (edge, STEP_X))
    )


def fill(cols_ref, tiles, faces, chosen, width, columns=slice(None)):
    def load(source, start):
        ref, first = source
        return ref[pl.ds(first + start, width), columns]

    for plane in range(6):
        if plane in (0, 5):
            near = 3 * width if plane == 0 else 0
            pieces = [load(tile, near) for tile in tiles] + [load(face, 0) for face in faces]
        else:
            pieces = [load(tile, (plane - 1) * width) for tile in tiles]
        select = chosen[0 if plane == 0 else 2 if plane == 5 else 1]
        moved = dot(select, jnp.concatenate(pieces, axis=0)).astype(jnp.bfloat16)
        for shift in range(9):
            cols_ref[shift, plane * width : (plane + 1) * width, :] = moved[
                shift * width : (shift + 1) * width
            ]


def tap_rows(cols_ref, tap, width, columns=slice(None)):
    start = tap // 9 * width
    return cols_ref[tap % 9, start : start + 4 * width, columns]


def conv(cols_ref, weight_ref, width):
    total = None
    for tap in range(TAPS):
        term = dot(tap_rows(cols_ref, tap, width), weight_ref[tap * C : (tap + 1) * C, :])
        total = term if total is None else total + term
    return total


def conv_back(cols_ref, weight_ref, width):
    total = None
    for tap in range(TAPS):
        weight = weight_ref[(26 - tap) * C : (27 - tap) * C, :]
        term = dot(tap_rows(cols_ref, tap, width), weight, ((1,), (1,)))
        total = term if total is None else total + term
    return total


def live_rows(meta, width):
    codes = place_codes(meta, 0.0)
    own = iota((width, LANES), 0) == iota((width, LANES), 1)
    column = jnp.sum(jnp.where(own, codes, 0.0), axis=1, keepdims=True)
    return jnp.concatenate([column] * 4, axis=0) > 0.5 * NOWHERE


def near_sign(axis="gx"):
    return (1 - 2 * (lax.axis_index(axis) % 2)).astype(jnp.float32)


def near_row(width):
    return pl.multiple_of((lax.axis_index("gx") % 2) * (3 * width), PLANE)


def side_offsets(sides):
    if sides == 2:
        return [-8 * STEP_Y, 8 * STEP_Y]
    return [(1 - 2 * lax.axis_index("gy")).astype(jnp.float32) * (8 * STEP_Y)]


def pack_kernel(features_ref, cotangent_ref, coords_ref, counts_ref, own_ref, face_ref):
    slots = features_ref.shape[2]
    width = slots * PLANE
    core = lax.axis_index("gx") % 2
    for field, ref in enumerate((features_ref, cotangent_ref)):
        for x in range(4):
            for slot in range(slots):
                start = field * 4 * width + x * width + slot * PLANE
                own_ref[start : start + PLANE, :] = ref[0, 0, slot, x * PLANE : (x + 1) * PLANE, :]
    lane = iota((1, LANES), 1)
    lane_slot = (lane // PLANE) % slots
    position = jnp.zeros((1, LANES), jnp.int32)
    for slot in range(slots):
        position = jnp.where(lane_slot == slot, coords_ref[0, 0, slot], position)
    values = [
        position // 16,
        4 * (position // 8 % 2) + lane % PLANE // 4,
        4 * (position % 8) + lane % 4,
        (lane_slot < counts_ref[0, 0]).astype(jnp.int32),
    ]
    rows = [v[:, h * C : (h + 1) * C] for h in range(2) for v in values]
    rows.append(jnp.zeros((META - 8, C), jnp.int32))
    meta = jnp.concatenate(rows, axis=0).astype(jnp.float32).astype(jnp.bfloat16)
    own_ref[8 * width :, :] = meta
    for field in range(2):
        at = pl.multiple_of(4 * width * field + 3 * width * core, PLANE)
        face_ref[field * width : (field + 1) * width, :] = own_ref[pl.ds(at, width), :]
    face_ref[2 * width :, :] = meta


def around(refs, sides):
    own, refs = refs[0], refs[1:]
    side, far, fdiag = refs[:sides], refs[sides], refs[sides + 1 : 2 * sides + 1]
    near, ndiag = refs[2 * sides + 1], refs[2 * sides + 2 :]
    return own, side, far, fdiag, near, ndiag


def own_sources(refs, sides, width, field):
    own, side, far, fdiag, near, ndiag = around(refs, sides)
    top, at = field * 4 * width, near_row(width)
    tiles = [(own, top)] + [(ref, top) for ref in side]
    faces = [(near, top + at), (far, field * width)]
    for n, f in zip(ndiag, fdiag):
        faces += [(n, top + at), (f, field * width)]
    return tiles, faces


def side_sources(refs, width, field):
    own, (side,), far, (fdiag,), near, (ndiag,) = around(refs, 1)
    return own_sources((side, own, fdiag, far, ndiag, near), 1, width, field)


def hidden_kernel(sides, count, *refs):
    early, refs = refs[:count], refs[count:]
    weight_ref, hidden_ref, slope_ref, cols_ref, source_ref, target_ref = refs
    own, side, far, fdiag, near, ndiag = around(early, sides)
    width = own.shape[0] // 8 // PLANE * PLANE
    rows, faced = 8 * width, 2 * width
    metas = [own[rows : rows + 8, :]] + [ref[rows : rows + 8, :] for ref in side]
    edges = [near[rows : rows + 8, :], far[faced : faced + 8, :]]
    for n, f in zip(ndiag, fdiag):
        edges += [n[rows : rows + 8, :], f[faced : faced + 8, :]]
    sign = near_sign() * (2 * STEP_X)
    offsets = side_offsets(sides)
    source = source_codes(metas + edges, sign, offsets, width)
    target = target_codes(metas[0], width)
    source_ref[...] = jnp.zeros(source_ref.shape, jnp.float32)
    source_ref[0:1, :] = source
    target_ref[:, 0:1] = target
    if sides == 1:
        mirrored = [metas[1], metas[0], edges[2], edges[3], edges[0], edges[1]]
        source_ref[1:2, :] = source_codes(mirrored, sign, [-offsets[0]], width)
        target_ref[:, 1:2] = target_codes(metas[1], width)
    else:
        target_ref[:, 1:2] = target
    chosen = selectors(source, target, sides, width)
    fill(cols_ref, *own_sources(early, sides, width, 0), chosen, width)
    pre_first = conv(cols_ref, weight_ref, width)
    live = live_rows(metas[0], width)
    sigmoid = 1.0 / (1.0 + jnp.exp(-pre_first))
    hidden_ref[...] = jnp.where(live, pre_first * sigmoid, 0.0).astype(jnp.bfloat16)
    slope_ref[...] = jnp.where(live, sigmoid * (1.0 + pre_first * (1.0 - sigmoid)), 0.0)


def grad_kernel(sides, count, *refs):
    early, refs = refs[:count], refs[count:]
    weight_ref, hidden_ref, slope_ref, source_ref, target_ref = refs[:5]
    grad_ref, face_ref, cols_ref = refs[5:]
    width = hidden_ref.shape[0] // 4
    chosen = selectors(source_ref[0:1, :], target_ref[:, 0:1], sides, width)
    fill(cols_ref, *own_sources(early, sides, width, 1), chosen, width)
    hidden_grad = conv_back(cols_ref, weight_ref, width)
    grad_ref[...] = (hidden_grad * slope_ref[...]).astype(jnp.bfloat16)
    at = pl.multiple_of(3 * width * (lax.axis_index("gx") % 2), PLANE)
    face_ref[:width, :] = hidden_ref[pl.ds(at, width), :]
    face_ref[width:, :] = grad_ref[pl.ds(at, width), :]


def store_terms(keep_ref, send_ref, total_ref):
    core = lax.axis_index("gx") % 2
    pairs, rows = keep_ref.shape[0], keep_ref.shape[1]
    for i in range(pairs):
        keep_at = pl.multiple_of((2 * i + core) * rows, 8)
        send_at = pl.multiple_of((2 * i + 1 - core) * rows, 8)
        keep_ref[i] = total_ref[pl.ds(keep_at, rows), :]
        send_ref[i] = total_ref[pl.ds(send_at, rows), :].astype(jnp.bfloat16)


def my_columns(cols):
    if cols == C:
        return slice(None)
    return pl.ds(pl.multiple_of(lax.axis_index("gy") * cols, 128), cols)


def second_terms_kernel(count, grouped, *refs):
    early, refs = refs[:count], refs[count:]
    hiddens, refs = refs[: 1 + grouped], refs[1 + grouped :]
    cols_ref, source_ref, target_ref, keep_ref, send_ref, total_ref, side_ref = refs
    cols = keep_ref.shape[2]
    columns = my_columns(cols)
    width = hiddens[0].shape[0] // 4
    hidden = jnp.concatenate([ref[...] for ref in hiddens], axis=0)
    hidden = hidden.astype(jnp.float32).T.astype(jnp.bfloat16)
    if grouped:
        chosen = selectors(source_ref[1:2, :], target_ref[:, 1:2], 1, width)
        fill(side_ref, *side_sources(early, width, 1), chosen, width, columns)

    def rows(tap):
        pieces = [tap_rows(cols_ref, 26 - tap, width, columns)]
        if grouped:
            pieces.append(tap_rows(side_ref, 26 - tap, width))
        return jnp.concatenate(pieces, axis=0)

    step = C // cols
    for first in range(0, TAPS, step):
        taps = range(first, min(first + step, TAPS))
        result = dot(hidden, jnp.concatenate([rows(tap) for tap in taps], axis=1))
        for i, tap in enumerate(taps):
            total_ref[tap * C : (tap + 1) * C, :] = result[:, i * cols : (i + 1) * cols]
    store_terms(keep_ref, send_ref, total_ref)


def first_terms_kernel(count, grouped, *refs):
    early, refs = refs[:count], refs[count:]
    grads, refs = refs[: 1 + grouped], refs[1 + grouped :]
    cols_ref, source_ref, target_ref, keep_ref, send_ref, total_ref, side_ref = refs
    columns = my_columns(keep_ref.shape[2])
    width = grads[0].shape[0] // 4
    if grouped:
        chosen = selectors(source_ref[1:2, :], target_ref[:, 1:2], 1, width)
        fill(side_ref, *side_sources(early, width, 0), chosen, width)
    grad = jnp.concatenate([ref[:, columns] for ref in grads], axis=0)
    for tap in range(TAPS):
        pieces = [tap_rows(cols_ref, tap, width)]
        if grouped:
            pieces.append(tap_rows(side_ref, tap, width))
        total_ref[tap * C : (tap + 1) * C, :] = dot(
            jnp.concatenate(pieces, axis=0), grad, ((0,), (0,))
        )
    store_terms(keep_ref, send_ref, total_ref)


def last_kernel(sides, count, *refs):
    own_ref, refs = refs[0], refs[1:]
    hidden_around, refs = refs[: 1 + sides], refs[1 + sides :]
    grad_around, refs = refs[: 1 + sides], refs[1 + sides :]
    fars, refs = refs[: 1 + sides], refs[1 + sides :]
    hidden_near, refs = refs[: 1 + sides], refs[1 + sides :]
    grad_near, refs = refs[: 1 + sides], refs[1 + sides :]
    first_ref, second_ref, source_ref, target_ref, output_ref, input_ref = refs[:6]
    hidden_cols_ref, grad_cols_ref = refs[6:]
    width = hidden_around[0].shape[0] // 4
    slots = output_ref.shape[0]
    chosen = selectors(source_ref[0:1, :], target_ref[:, 0:1], sides, width)
    live = live_rows(own_ref[8 * width : 8 * width + 8, :], width)
    at = near_row(width)

    def sources(field, tiles, nears):
        faces = []
        for near, far in zip(nears, fars):
            faces += [(near, at), (far, field * width)]
        return [(ref, 0) for ref in tiles], faces

    def put(ref, total):
        total = jnp.where(live, total, 0.0)
        for x in range(4):
            for slot in range(slots):
                start = x * width + slot * PLANE
                ref[slot, x * PLANE : (x + 1) * PLANE, :] = total[start : start + PLANE]

    fill(hidden_cols_ref, *sources(0, hidden_around, hidden_near), chosen, width)
    put(output_ref, conv(hidden_cols_ref, second_ref, width))
    fill(grad_cols_ref, *sources(1, grad_around, grad_near), chosen, width)
    put(input_ref, conv_back(grad_cols_ref, first_ref, width))


def swap(cells, axis, bit):
    return lax.ppermute(cells, axis, [(i, i ^ bit) for i in range(lax.axis_size(axis))])


def side_steps(count):
    if count == 2:
        return [[(0, 1), (1, 0)]]
    ends = count - 1
    return [[(i, i + 1) for i in range(ends)], [(i + 1, i) for i in range(ends)]]


def far_steps(count):
    pairs = [(i, i + 1) for i in range(1, count - 1, 2)]
    return pairs + [(b, a) for a, b in pairs]


def from_sides(cells):
    return [lax.ppermute(cells, "gy", step) for step in side_steps(lax.axis_size("gy"))]


def from_far(face):
    gx, gy = lax.axis_size("gx"), lax.axis_size("gy")
    far = lax.ppermute(face, "gx", far_steps(gx))
    return [far] + [
        lax.ppermute(
            face,
            ("gx", "gy"),
            [(a * gy + c, b * gy + d) for a, b in far_steps(gx) for c, d in step],
        )
        for step in side_steps(gy)
    ]


def piece(cells, index, axis):
    return lax.dynamic_index_in_dim(cells, index, axis, keepdims=False)


def over_core(keep, send):
    return lambda part: part(keep) + part(swap(send, "gx", 1)).astype(jnp.float32)


def per_device(features, block_coords, block_counts, first_weight, second_weight, cotangent):
    gx, gy = lax.axis_size("gx"), lax.axis_size("gy")
    ix, iy = lax.axis_index("gx"), lax.axis_index("gy")
    slots = features.shape[2]
    width = slots * PLANE
    rows = 8 * width
    half, deep = ix // 2 % 2, ix // 4
    deeps = gx // 4
    sides = 1 if gy == 2 else 2
    grouped = gy == 2
    cols = C // gy if grouped else C
    chunk = TAPS * C // gx

    def shape(dims, kind=jnp.bfloat16):
        return jax.ShapeDtypeStruct(dims, kind)

    own, face = pl.pallas_call(
        pack_kernel,
        out_shape=(shape((rows + META, C)), shape((2 * width + META, C))),
        in_specs=[VMEM, VMEM, SMEM, SMEM],
        out_specs=(VMEM, VMEM),
        compiler_params=params(8),
        name="pack",
    )(features, cotangent, block_coords, block_counts)
    side = from_sides(own)
    fars = from_far(face)
    nears = [swap(tile, "gx", 1) for tile in [own] + side]
    early = [own, *side, *fars, *nears]
    count = len(early)
    field = (4 * width, C)
    columns = shape((9, 6 * width, C))

    hidden, slope, feature_cols, source, target = pl.pallas_call(
        functools.partial(hidden_kernel, sides, count),
        out_shape=(
            shape(field),
            shape(field, jnp.float32),
            columns,
            shape((8, LANES), jnp.float32),
            shape((9 * width, 2), jnp.float32),
        ),
        in_specs=[VMEM] * (count + 1),
        out_specs=(VMEM,) * 5,
        compiler_params=params(16),
        name="hidden",
    )(*early, first_weight)
    side_hidden = from_sides(hidden)

    grad, late_face, seed_cols = pl.pallas_call(
        functools.partial(grad_kernel, sides, count),
        out_shape=(shape(field), shape((2 * width, C)), columns),
        in_specs=[VMEM] * (count + 5),
        out_specs=(VMEM,) * 3,
        compiler_params=params(16),
        name="pre_grad",
    )(*early, second_weight, hidden, slope, source, target)
    side_grad = from_sides(grad)

    def terms(kernel, name, fields, cells):
        return pl.pallas_call(
            functools.partial(kernel, count, int(grouped)),
            out_shape=(
                shape((gx // 2, chunk, cols), jnp.float32),
                shape((gx // 2, chunk, cols)),
            ),
            in_specs=[VMEM] * (count + len(fields) + 3),
            out_specs=(VMEM, VMEM),
            scratch_shapes=[
                pltpu.VMEM((TAPS * C, cols), jnp.float32),
                pltpu.VMEM((9, 6 * width, cols if name == "second_terms" else C), jnp.bfloat16),
            ],
            compiler_params=params(24),
            name=name,
        )(*early, *fields, cells, source, target)

    members = 1 + grouped
    second = terms(second_terms_kernel, "second_terms", ([hidden] + side_hidden)[:members], seed_cols)
    first = terms(first_terms_kernel, "first_terms", ([grad] + side_grad)[:members], feature_cols)

    grad_scale = 1.0 / math.sqrt(64 * slots * gx * gy)

    def summed(keep, send):
        keep = keep.reshape(deeps, 2, chunk, cols)
        got = swap(send, "gx", 1).reshape(keep.shape)

        def part(i):
            return piece(keep, i, 1) + piece(got, i, 1).astype(jnp.float32)

        sent = part(1 - half).astype(jnp.bfloat16)
        total = part(half) + swap(sent, "gx", 2).astype(jnp.float32)
        if not grouped:
            total = total.reshape(deeps, chunk, gy, cols // gy)
            total = piece(total, iy, 2) + sum(
                swap(piece(total, iy ^ m, 2).astype(jnp.bfloat16), "gy", m).astype(jnp.float32)
                for m in range(1, gy)
            )
        total = piece(total, deep, 0) + sum(
            swap(piece(total, deep ^ m, 0).astype(jnp.bfloat16), "gx", 4 * m).astype(jnp.float32)
            for m in range(1, deeps)
        )
        return total * grad_scale

    second_grad = summed(*second)
    first_grad = summed(*first)

    late_fars = from_far(late_face)
    hidden_near = [swap(tile, "gx", 1) for tile in [hidden] + side_hidden]
    grad_near = [swap(tile, "gx", 1) for tile in [grad] + side_grad]
    late = [own, hidden, *side_hidden, grad, *side_grad, *late_fars, *hidden_near, *grad_near]
    late += [first_weight, second_weight, source, target]
    result = shape((slots, 64, C), jnp.float32)
    output, input_grad = pl.pallas_call(
        functools.partial(last_kernel, sides, len(late)),
        out_shape=(result, result),
        in_specs=[VMEM] * len(late),
        out_specs=(VMEM, VMEM),
        scratch_shapes=[pltpu.VMEM(columns.shape, jnp.bfloat16)] * 2,
        compiler_params=params(24),
        name="last_layer",
    )(*late)
    return (
        output.reshape(features.shape),
        input_grad.reshape(features.shape),
        first_grad,
        second_grad,
    )


def solution(mesh):
    placed = (
        P("gx", "gy", None, None, None),
        P("gx", "gy", None),
        P("gx", "gy"),
        P(),
        P(),
        P("gx", "gy", None, None, None),
    )
    return jax.shard_map(
        per_device,
        mesh=mesh,
        in_specs=placed,
        out_specs=(
            P("gx", "gy", None, None, None),
            P("gx", "gy", None, None, None),
            P("gx", "gy"),
            P("gx", "gy"),
        ),
        check_vma=False,
    )
```

time: 508 us -> 111 us (0.22); the launches traced: 500 us -> 109 us
  local copies, waits for them, and re-layouts: 380 us -> 19.5 us
  matrix products: 22.9 us -> 0 us
  Pallas kernels: 0 us -> 18.6 us
  between operations: 15.9 us -> 1.5 us
  starting transfers between devices: 47 us -> 35.5 us
  other arithmetic: 13.8 us -> 8.31 us
  waiting for transfers between devices: 20.6 us -> 26 us
    reshape x60 -> x0, local copies, waits for them, and re-layouts: 96 us -> none  [the longest x54 84.1 us: columns(): tap_list.append(piece.reshape(-1, chan_width))]
    concatenate x62 -> x0, local copies, waits for them, and re-layouts: 88.1 us -> none  [the longest x58 86.2 us: columns(): return jnp.concatenate(tap_list, axis=1)]
    unnamed x249 -> x60, local copies, waits for them, and re-layouts: 104 us -> 19.4 us
    gather x36 -> x0, local copies, waits for them, and re-layouts: 50.5 us -> none
    slice x16 -> x0, local copies, waits for them, and re-layouts: 34.5 us -> none  [the longest x8 27.6 us: columns(): cubes[:, shift_x:shift_x + 4, shift_y:shift_y + 4, shift_z:shift_z + 4, :]]
    dot_general x10 -> x0, matrix products: 22.9 us -> none  [the longest x2 8.12 us: contract_rows(): lax.dot_general(cols, rows, (((0,), (0,)), ((), ())), preferred_element_t...]
    pallas_call x0 -> x6, Pallas kernels: none -> 18.6 us  [the longest x2 7.45 us: terms(): pl.pallas_call(functools.partial(kernel, count, int(grouped)), out_shape=...]
    ppermute x16 -> x23, waiting for transfers between devices: 12.9 us -> 26 us  [the longest x16 13.4 us: swap(): lax.ppermute(cells, axis, [(i, i ^ bit) for i in range(lax.axis_size(axis...]
  transfers between devices with their start and end apart: 20 -> 23, of which waited for: 8 -> 8; matrix products, arithmetic and copies ran while one was open for 51% -> 7% of each run, Pallas kernels for 0% -> 11%
where the time goes in v2:
time: 111 us; the launch traced here: 109 us
  starting transfers between devices  35.5 us (32%)
  waiting for transfers between devices  26 us (23%)
  local copies, waits for them, and re-layouts  19.5 us (18%)
  Pallas kernels  18.6 us (17%)
  other arithmetic  8.31 us (7%)
  between operations  1.5 us (1%)
    unnamed x60, local copies, waits for them, and re-layouts  19.4 us
    ppermute x16, starting transfers between devices, swap(): lax.ppermute(cells, axis, [(i, i ^ bit) for i in range(lax.axis_size(axis...  15.9 us
    ppermute x16, waiting for transfers between devices, swap(): lax.ppermute(cells, axis, [(i, i ^ bit) for i in range(lax.axis_size(axis...  13.4 us
    ppermute x3, waiting for transfers between devices, from_sides(): lax.ppermute(cells, 'gy', step)  9.37 us
    ppermute x2, starting transfers between devices, from_far(): lax.ppermute(face, ('gx', 'gy'), [(a * gy + c, b * gy + d) for a, b in fa...  9.33 us
    pallas_call x2, Pallas kernels, terms(): pl.pallas_call(functools.partial(kernel, count, int(grouped)), out_shape=...  7.45 us
    pallas_call x1, Pallas kernels, per_device(): pl.pallas_call(functools.partial(last_kernel, sides, len(late)), out_shap...  6.39 us
    ppermute x2, starting transfers between devices, from_far(): far = lax.ppermute(face, 'gx', far_steps(gx))  5.56 us
  transfers between devices with their start and end apart: 23, of which 8 were waited for; matrix products, arithmetic and copies ran while one was open for 7% of the time, Pallas kernels for 11%

profile of v2, /device:TPU:8, one launch (start us, length us, event | category | flops | bytes accessed | tf_op | source)
XLA Modules:
  0.0 109.3 jit_solution(700314008296660939)
XLA Ops:
  1.3 0.9 copy-done.22
  2.2 0.9 copy-done.23
  3.1 0.7 copy-done.28
  4.3 1.6 %collective-permute-start = (bf16[400,256]{1,0:T(8,128)(2,1)S(1)}, bf16[400,256]{1,0:T(8,128)(2,1)S(1)}, u32[]{:S(2)}, u32[]{:S(2)}) collective-permute-start(bf16[400,256]{1,0:T(8,128)(2,1)S(1)} %get-tuple-element.20.refs_0_), channel_id=1, source_target_pairs={{0,1},{1,0},{2,3},{3,2},{4,5},{5,4},{6,7},{7,6},{8,9},{9,8},{10,11... | collective-permute-start | bytes 614408 | tf_op jit(solution)/shard_map/ppermute | solution.py:349
  5.9 5.3 %collective-permute-done.refs_1_ = bf16[400,256]{1,0:T(8,128)(2,1)S(1)} collective-permute-done((bf16[400,256]{1,0:T(8,128)(2,1)S(1)}, bf16[400,256]{1,0:T(8,128)(2,1)S(1)}, u32[]{:S(2)}, u32[]{:S(2)}) %collective-permute-start) | collective-permute-done | bytes 204832 | tf_op jit(solution)/shard_map/ppermute | solution.py:349
  11.2 3.6 %collective-permute-start.1 = (bf16[112,256]{1,0:T(8,128)(2,1)S(1)}, bf16[112,256]{1,0:T(8,128)(2,1)S(1)}, u32[]{:S(2)}, u32[]{:S(2)}) collective-permute-start(bf16[112,256]{1,0:T(8,128)(2,1)S(1)} %get-tuple-element.21), channel_id=1, source_target_pairs={{2,4},{6,8},{10,12},{14,16},{18,20},{22,24},{26,28},{4,2},{8,6},{1... | collective-permute-start | bytes 172040 | tf_op jit(solution)/shard_map/ppermute | solution.py:354
  14.9 4.0 %collective-permute-start.2 = (bf16[112,256]{1,0:T(8,128)(2,1)S(1)}, bf16[112,256]{1,0:T(8,128)(2,1)S(1)}, u32[]{:S(2)}, u32[]{:S(2)}) collective-permute-start(bf16[112,256]{1,0:T(8,128)(2,1)S(1)} %get-tuple-element.21), channel_id=1, source_target_pairs={{2,5},{3,4},{6,9},{7,8},{10,13},{11,12},{14,17},{15,16},{18,21},{1... | collective-permute-start | bytes 172040 | tf_op jit(solution)/shard_map/ppermute | solution.py:356
  18.9 3.3 %collective-permute-done.2.refs_3_ = bf16[112,256]{1,0:T(8,128)(2,1)S(1)} collective-permute-done((bf16[112,256]{1,0:T(8,128)(2,1)S(1)}, bf16[112,256]{1,0:T(8,128)(2,1)S(1)}, u32[]{:S(2)}, u32[]{:S(2)}) %collective-permute-start.2) | collective-permute-done | bytes 57376 | tf_op jit(solution)/shard_map/ppermute | solution.py:356
  22.2 2.0 %copy-done.1 = bf16[6912,256]{1,0:T(8,128)(2,1)S(1)} copy-done((bf16[6912,256]{1,0:T(8,128)(2,1)S(1)}, bf16[6912,256]{1,0:T(8,128)(2,1)}, u32[]{:S(2)}) %copy-start.1) | copy-done | bytes 3538968
  24.2 2.1 %hidden.1 = (bf16[192,256]{1,0:T(8,128)(2,1)S(1)}, f32[192,256]{1,0:T(8,128)S(1)}, bf16[9,288,256]{2,1,0:T(8,128)(2,1)S(1)}, f32[8,512]{1,0:T(8,128)S(1)}, f32[432,2]{1,0:T(8,128)S(1)}) custom-call(bf16[400,256]{1,0:T(8,128)(2,1)S(1)} %get-tuple-element.20.refs_0_, bf16[400,256]{1,0:T(8,128)(2,1)S(1)} %collective-permute-done.refs_1_, ...), custom_call_target="tpu_custom_call" | custom-call | tf_op jit(solution)/shard_map/hidden/pallas_call | solution.py:405
  26.3 1.6 %collective-permute-start.5 = (bf16[192,256]{1,0:T(8,128)(2,1)S(1)}, bf16[192,256]{1,0:T(8,128)(2,1)S(1)}, u32[]{:S(2)}, u32[]{:S(2)}) collective-permute-start(bf16[192,256]{1,0:T(8,128)(2,1)S(1)} %get-tuple-element.22.refs_7_.refs_1_.refs_6_), channel_id=1, source_target_pairs={{0,1},{1,0},{2,3},{3,2},{4,5},{5,4},{6,7},{7,6},{8,9},{9,8},{10,11... | collective-permute-start | bytes 294920 | tf_op jit(solution)/shard_map/ppermute | solution.py:349
  27.9 2.1 %pre_grad.1 = (bf16[192,256]{1,0:T(8,128)(2,1)S(1)}, bf16[96,256]{1,0:T(8,128)(2,1)S(1)}, bf16[9,288,256]{2,1,0:T(8,128)(2,1)S(1)}) custom-call(bf16[400,256]{1,0:T(8,128)(2,1)S(1)} %get-tuple-element.20.refs_0_, bf16[400,256]{1,0:T(8,128)(2,1)S(1)} %collective-permute-done.refs_1_, bf16[112,256]{1,0:T(8,128)(2,1)S(1)} %collective-permute-done.1.refs_2_, ...), custom_call_target="tpu_custom_call" | custom-call | tf_op jit(solution)/shard_map/pre_grad/pallas_call | solution.py:421
  31.0 3.4 %second_terms.1 = (f32[8,432,128]{2,1,0:T(8,128)S(1)}, bf16[8,432,128]{2,1,0:T(8,128)(2,1)}) custom-call(bf16[400,256]{1,0:T(8,128)(2,1)S(1)} %get-tuple-element.20.refs_0_, bf16[400,256]{1,0:T(8,128)(2,1)S(1)} %collective-permute-done.refs_1_, bf16[112,256]{1,0:T(8,128)(2,1)S(1)} %collective-permute-done.1.refs_2_, ...), custom_call_target="tpu_custom_call" | custom-call | tf_op jit(solution)/shard_map/second_terms/pallas_call | solution.py:432
  34.3 1.2 %copy-done.10 = f32[8,432,128]{2,1,0:T(8,128)} copy-done((f32[8,432,128]{2,1,0:T(8,128)}, f32[8,432,128]{2,1,0:T(8,128)S(1)}, u32[]{:S(2)}) %copy-start.10) | copy-done | bytes 1769496
  35.5 1.5 %collective-permute-start.6 = (bf16[192,256]{1,0:T(8,128)(2,1)S(1)}, bf16[192,256]{1,0:T(8,128)(2,1)S(1)}, u32[]{:S(2)}, u32[]{:S(2)}) collective-permute-start(bf16[192,256]{1,0:T(8,128)(2,1)S(1)} %get-tuple-element.26.refs_3_.refs_6_), channel_id=1, source_target_pairs={{0,1},{1,0},{2,3},{3,2},{4,5},{5,4},{6,7},{7,6},{8,9},{9,8},{10,11... | collective-permute-start | bytes 294920 | tf_op jit(solution)/shard_map/ppermute | solution.py:349
  37.1 3.7 %collective-permute-done.6.refs_4_.refs_7_ = bf16[192,256]{1,0:T(8,128)(2,1)S(1)} collective-permute-done((bf16[192,256]{1,0:T(8,128)(2,1)S(1)}, bf16[192,256]{1,0:T(8,128)(2,1)S(1)}, u32[]{:S(2)}, u32[]{:S(2)}) %collective-permute-start.6) | collective-permute-done | bytes 98336 | tf_op jit(solution)/shard_map/ppermute | solution.py:349
  40.8 4.1 %first_terms.1 = (f32[8,432,128]{2,1,0:T(8,128)S(1)}, bf16[8,432,128]{2,1,0:T(8,128)(2,1)}) custom-call(bf16[400,256]{1,0:T(8,128)(2,1)S(1)} %get-tuple-element.20.refs_0_, bf16[400,256]{1,0:T(8,128)(2,1)S(1)} %collective-permute-done.refs_1_, bf16[112,256]{1,0:T(8,128)(2,1)S(1)} %collective-permute-done.1.refs_2_, ...), custom_call_target="tpu_custom_call" | custom-call | tf_op jit(solution)/shard_map/first_terms/pallas_call | solution.py:432
  44.9 1.3 %copy-done.7 = f32[8,432,128]{2,1,0:T(8,128)} copy-done((f32[8,432,128]{2,1,0:T(8,128)}, f32[8,432,128]{2,1,0:T(8,128)S(1)}, u32[]{:S(2)}) %copy-start.7) | copy-done | bytes 1769496
  46.1 2.3 %fusion.7 = bf16[4,432,128]{2,1,0:T(8,128)(2,1)} fusion(f32[4,2,432,128]{3,2,1,0:T(8,128)} %bitcast.72, s32[]{:T(128)S(6)} %select_n.48, bf16[4,2,432,128]{3,2,1,0:T(8,128)(2,1)} %bitcast.11), kind=kLoop, calls=%fused_computation.11 | loop fusion | flops 663552 | bytes 1769476 | tf_op jit(solution)/shard_map/convert_element_type | solution.py:461
  48.9 1.9 %collective-permute-start.7 = (bf16[96,256]{1,0:T(8,128)(2,1)}, bf16[96,256]{1,0:T(8,128)(2,1)S(1)}, u32[]{:S(2)}, u32[]{:S(2)}) collective-permute-start(bf16[96,256]{1,0:T(8,128)(2,1)} %copy-done.29), channel_id=1, source_target_pairs={{2,4},{6,8},{10,12},{14,16},{18,20},{22,24},{26,28},{4,2},{8,6},{1... | collective-permute-start | bytes 147464 | tf_op jit(solution)/shard_map/ppermute | solution.py:354
  50.8 5.3 %collective-permute-start.8 = (bf16[96,256]{1,0:T(8,128)(2,1)}, bf16[96,256]{1,0:T(8,128)(2,1)S(1)}, u32[]{:S(2)}, u32[]{:S(2)}) collective-permute-start(bf16[96,256]{1,0:T(8,128)(2,1)} %copy-done.29), channel_id=1, source_target_pairs={{2,5},{3,4},{6,9},{7,8},{10,13},{11,12},{14,17},{15,16},{18,21},{1... | collective-permute-start | bytes 147464 | tf_op jit(solution)/shard_map/ppermute | solution.py:356
  56.8 6.4 %collective-permute-start.9 = (bf16[192,256]{1,0:T(8,128)(2,1)}, bf16[192,256]{1,0:T(8,128)(2,1)}, u32[]{:S(2)}, u32[]{:S(2)}) collective-permute-start(bf16[192,256]{1,0:T(8,128)(2,1)} %copy-done.12), channel_id=1, source_target_pairs={{0,2},{2,0},{4,6},{6,4},{8,10},{10,8},{12,14},{14,12},{16,18},{18,... | collective-permute-start | bytes 294920 | tf_op jit(solution)/shard_map/ppermute | solution.py:333
  63.8 0.9 collective-permute-start.12
  64.7 1.9 %fusion.6 = bf16[4,432,128]{2,1,0:T(8,128)(2,1)} fusion(f32[4,2,432,128]{3,2,1,0:T(8,128)S(1)} %bitcast.70, s32[]{:T(128)S(6)} %select_n.48, bf16[4,2,432,128]{3,2,1,0:T(8,128)(2,1)} %bitcast.3), kind=kLoop, calls=%fused_computation.10 | loop fusion | flops 663552 | bytes 1769476 | tf_op jit(solution)/shard_map/convert_element_type | solution.py:461
  66.6 0.7 copy-done.20
  67.2 1.0 collective-permute-start.14
  68.2 2.0 %copy-done.2 = bf16[6912,256]{1,0:T(8,128)(2,1)S(1)} copy-done((bf16[6912,256]{1,0:T(8,128)(2,1)S(1)}, bf16[6912,256]{1,0:T(8,128)(2,1)}, u32[]{:S(2)}) %copy-start.2) | copy-done | bytes 3538968
  70.2 0.9 copy-done.4
  71.2 0.9 copy-done.6
  72.1 0.9 copy-done.13
  73.0 0.9 copy-done.15
  73.9 0.9 copy-done.17
  74.8 0.9 copy-done.19
  75.7 0.9 copy-done.21
  76.6 0.8 copy-done.25
  77.4 0.8 copy-done.27
  78.2 6.4 %last_layer.1 = (f32[3,64,256]{2,1,0:T(8,128)}, f32[3,64,256]{2,1,0:T(8,128)}) custom-call(bf16[400,256]{1,0:T(8,128)(2,1)S(1)} %copy-done.4, bf16[192,256]{1,0:T(8,128)(2,1)S(1)} %copy-done.13, bf16[192,256]{1,0:T(8,128)(2,1)S(1)} %copy-done.15, bf16[192,256]{1,0:T(8,128)(2,1)S(1)} %copy-done.17, bf16[192,256]{1,0:T(8,128)(2,1)S(1)} %copy-done.19, ...), custom_call_target="tpu_custom_call" | custom-call | tf_op jit(solution)/shard_map/last_layer/pallas_call | solution.py:484
  84.6 1.4 %fusion.2 = f32[4,432,128]{2,1,0:T(8,128)S(1)} fusion(bf16[4,432,128]{2,1,0:T(8,128)(2,1)} %collective-permute-done.19, f32[4,2,432,128]{3,2,1,0:T(8,128)S(1)} %bitcast.73, s32[]{:T(128)S(6)} %select_n.47, bf16[4,2,432,128]{3,2,1,0:T(8,128)(2,1)} %bitcast.11), kind=kLoop, calls=%fused_computation.4 | loop fusion | flops 884736 | bytes 2654212 | tf_op jit(solution)/shard_map/add | solution.py:462
  86.3 2.8 %collective-permute-start.21 = (bf16[432,128]{1,0:T(8,128)(2,1)S(1)}, bf16[432,128]{1,0:T(8,128)(2,1)S(1)}, u32[]{:S(2)}, u32[]{:S(2)}) collective-permute-start(bf16[432,128]{1,0:T(8,128)(2,1)S(1)} %get-tuple-element.38), channel_id=1, source_target_pairs={{0,16},{2,18},{4,20},{6,22},{8,24},{10,26},{12,28},{14,30},{16,0},... | collective-permute-start | bytes 331784 | tf_op jit(solution)/shard_map/ppermute | solution.py:333
  89.6 1.3 %fusion.5 = f32[4,432,128]{2,1,0:T(8,128)S(1)} fusion(bf16[4,432,128]{2,1,0:T(8,128)(2,1)} %collective-permute-done.14, f32[4,2,432,128]{3,2,1,0:T(8,128)S(1)} %bitcast.71, s32[]{:T(128)S(6)} %select_n.47, bf16[4,2,432,128]{3,2,1,0:T(8,128)(2,1)} %bitcast.3), kind=kLoop, calls=%fused_computation.9 | loop fusion | flops 884736 | bytes 2654212 | tf_op jit(solution)/shard_map/add | solution.py:462
  90.9 1.2 %collective-permute-start.15 = (bf16[432,128]{1,0:T(8,128)(2,1)S(1)}, bf16[432,128]{1,0:T(8,128)(2,1)S(1)}, u32[]{:S(2)}, u32[]{:S(2)}) collective-permute-start(bf16[432,128]{1,0:T(8,128)(2,1)S(1)} %get-tuple-element.39), channel_id=1, source_target_pairs={{0,8},{2,10},{4,12},{6,14},{8,0},{10,2},{12,4},{14,6},{16,24},{18,... | collective-permute-start | bytes 331784 | tf_op jit(solution)/shard_map/ppermute | solution.py:333
  92.1 1.9 %collective-permute-start.16 = (bf16[432,128]{1,0:T(8,128)(2,1)S(1)}, bf16[432,128]{1,0:T(8,128)(2,1)S(1)}, u32[]{:S(2)}, u32[]{:S(2)}) collective-permute-start(bf16[432,128]{1,0:T(8,128)(2,1)S(1)} %get-tuple-element.41), channel_id=1, source_target_pairs={{0,16},{2,18},{4,20},{6,22},{8,24},{10,26},{12,28},{14,30},{16,0},... | collective-permute-start | bytes 331784 | tf_op jit(solution)/shard_map/ppermute | solution.py:333
  94.5 2.9 %collective-permute-done.21 = bf16[432,128]{1,0:T(8,128)(2,1)S(1)} collective-permute-done((bf16[432,128]{1,0:T(8,128)(2,1)S(1)}, bf16[432,128]{1,0:T(8,128)(2,1)S(1)}, u32[]{:S(2)}, u32[]{:S(2)}) %collective-permute-start.21) | collective-permute-done | bytes 110624 | tf_op jit(solution)/shard_map/ppermute | solution.py:333
  97.4 7.7 %collective-permute-done.22 = bf16[432,128]{1,0:T(8,128)(2,1)S(1)} collective-permute-done((bf16[432,128]{1,0:T(8,128)(2,1)S(1)}, bf16[432,128]{1,0:T(8,128)(2,1)S(1)}, u32[]{:S(2)}, u32[]{:S(2)}) %collective-permute-start.22) | collective-permute-done | bytes 110624 | tf_op jit(solution)/shard_map/ppermute | solution.py:333
  105.1 0.7 fusion.8
  105.9 0.7 collective-permute-done.16
  106.5 2.0 %collective-permute-done.17 = bf16[432,128]{1,0:T(8,128)(2,1)S(1)} collective-permute-done((bf16[432,128]{1,0:T(8,128)(2,1)S(1)}, bf16[432,128]{1,0:T(8,128)(2,1)S(1)}, u32[]{:S(2)}, u32[]{:S(2)}) %collective-permute-start.17) | collective-permute-done | bytes 110624 | tf_op jit(solution)/shard_map/ppermute | solution.py:333
  108.6 0.7 fusion.9
  (72 shorter events, 4.8 us)
Async XLA Ops:
  1.3 0.9 copy-start.22
  2.2 0.9 copy-start.23
  4.3 36.4 %copy-start.3 = (bf16[400,256]{1,0:T(8,128)(2,1)}, bf16[400,256]{1,0:T(8,128)(2,1)S(1)}, u32[]{:S(2)}) copy-start(bf16[400,256]{1,0:T(8,128)(2,1)S(1)} %get-tuple-element.20.refs_0_) | copy-start | bytes 614404
  4.3 6.9 %collective-permute-start = (bf16[400,256]{1,0:T(8,128)(2,1)S(1)}, bf16[400,256]{1,0:T(8,128)(2,1)S(1)}, u32[]{:S(2)}, u32[]{:S(2)}) collective-permute-start(bf16[400,256]{1,0:T(8,128)(2,1)S(1)} %get-tuple-element.20.refs_0_), channel_id=1, source_target_pairs={{0,1},{1,0},{2,3},{3,2},{4,5},{5,4},{6,7},{7,6},{8,9},{9,8},{10,11... | collective-permute-start | bytes 614408 | tf_op jit(solution)/shard_map/ppermute | solution.py:349
  5.9 16.3 %collective-permute-start.3 = (bf16[400,256]{1,0:T(8,128)(2,1)S(1)}, bf16[400,256]{1,0:T(8,128)(2,1)S(1)}, u32[]{:S(2)}, u32[]{:S(2)}) collective-permute-start(bf16[400,256]{1,0:T(8,128)(2,1)S(1)} %get-tuple-element.20.refs_0_), channel_id=1, source_target_pairs={{0,2},{2,0},{4,6},{6,4},{8,10},{10,8},{12,14},{14,12},{16,18},{18,... | collective-permute-start | bytes 614408 | tf_op jit(solution)/shard_map/ppermute | solution.py:333
  11.2 11.0 %collective-permute-start.4 = (bf16[400,256]{1,0:T(8,128)(2,1)S(1)}, bf16[400,256]{1,0:T(8,128)(2,1)S(1)}, u32[]{:S(2)}, u32[]{:S(2)}) collective-permute-start(bf16[400,256]{1,0:T(8,128)(2,1)S(1)} %collective-permute-done.refs_1_), channel_id=1, source_target_pairs={{0,2},{2,0},{4,6},{6,4},{8,10},{10,8},{12,14},{14,12},{16,18},{18,... | collective-permute-start | bytes 614408 | tf_op jit(solution)/shard_map/ppermute | solution.py:333
  11.2 16.7 %copy-start = (bf16[6912,256]{1,0:T(8,128)(2,1)S(1)}, bf16[6912,256]{1,0:T(8,128)(2,1)}, u32[]{:S(2)}) copy-start(bf16[6912,256]{1,0:T(8,128)(2,1)} %refs_12_.1) | copy-start | bytes 10616836
  11.2 7.7 %collective-permute-start.1 = (bf16[112,256]{1,0:T(8,128)(2,1)S(1)}, bf16[112,256]{1,0:T(8,128)(2,1)S(1)}, u32[]{:S(2)}, u32[]{:S(2)}) collective-permute-start(bf16[112,256]{1,0:T(8,128)(2,1)S(1)} %get-tuple-element.21), channel_id=1, source_target_pairs={{2,4},{6,8},{10,12},{14,16},{18,20},{22,24},{26,28},{4,2},{8,6},{1... | collective-permute-start | bytes 172040 | tf_op jit(solution)/shard_map/ppermute | solution.py:354
  14.9 7.3 %collective-permute-start.2 = (bf16[112,256]{1,0:T(8,128)(2,1)S(1)}, bf16[112,256]{1,0:T(8,128)(2,1)S(1)}, u32[]{:S(2)}, u32[]{:S(2)}) collective-permute-start(bf16[112,256]{1,0:T(8,128)(2,1)S(1)} %get-tuple-element.21), channel_id=1, source_target_pairs={{2,5},{3,4},{6,9},{7,8},{10,13},{11,12},{14,17},{15,16},{18,21},{1... | collective-permute-start | bytes 172040 | tf_op jit(solution)/shard_map/ppermute | solution.py:356
  22.2 2.0 %copy-start.1 = (bf16[6912,256]{1,0:T(8,128)(2,1)S(1)}, bf16[6912,256]{1,0:T(8,128)(2,1)}, u32[]{:S(2)}) copy-start(bf16[6912,256]{1,0:T(8,128)(2,1)} %refs_11_.1) | copy-start | bytes 10616836
  26.3 4.7 %copy-start.12 = (bf16[192,256]{1,0:T(8,128)(2,1)}, bf16[192,256]{1,0:T(8,128)(2,1)S(1)}, u32[]{:S(2)}) copy-start(bf16[192,256]{1,0:T(8,128)(2,1)S(1)} %get-tuple-element.22.refs_7_.refs_1_.refs_6_) | copy-start | bytes 294916
  26.3 14.5 %copy-start.5 = (f32[432,2]{1,0:T(8,128)}, f32[432,2]{1,0:T(8,128)S(1)}, u32[]{:S(2)}) copy-start(f32[432,2]{1,0:T(8,128)S(1)} %get-tuple-element.25.refs_10_.refs_14_) | copy-start | bytes 10372
  26.3 4.7 %collective-permute-start.5 = (bf16[192,256]{1,0:T(8,128)(2,1)S(1)}, bf16[192,256]{1,0:T(8,128)(2,1)S(1)}, u32[]{:S(2)}, u32[]{:S(2)}) collective-permute-start(bf16[192,256]{1,0:T(8,128)(2,1)S(1)} %get-tuple-element.22.refs_7_.refs_1_.refs_6_), channel_id=1, source_target_pairs={{0,1},{1,0},{2,3},{3,2},{4,5},{5,4},{6,7},{7,6},{8,9},{9,8},{10,11... | collective-permute-start | bytes 294920 | tf_op jit(solution)/shard_map/ppermute | solution.py:349
  30.6 14.3 %copy-start.16 = (bf16[192,256]{1,0:T(8,128)(2,1)}, bf16[192,256]{1,0:T(8,128)(2,1)S(1)}, u32[]{:S(2)}) copy-start(bf16[192,256]{1,0:T(8,128)(2,1)S(1)} %get-tuple-element.26.refs_3_.refs_6_) | copy-start | bytes 294916
  31.0 13.9 %copy-start.14 = (bf16[192,256]{1,0:T(8,128)(2,1)}, bf16[192,256]{1,0:T(8,128)(2,1)S(1)}, u32[]{:S(2)}) copy-start(bf16[192,256]{1,0:T(8,128)(2,1)S(1)} %collective-permute-done.5.refs_2_.refs_7_) | copy-start | bytes 294916
  34.3 1.2 %copy-start.10 = (f32[8,432,128]{2,1,0:T(8,128)}, f32[8,432,128]{2,1,0:T(8,128)S(1)}, u32[]{:S(2)}) copy-start(f32[8,432,128]{2,1,0:T(8,128)S(1)} %get-tuple-element.34) | copy-start | bytes 5308420
  35.5 10.6 %collective-permute-start.18 = (bf16[8,432,128]{2,1,0:T(8,128)(2,1)}, bf16[8,432,128]{2,1,0:T(8,128)(2,1)}, u32[]{:S(2)}, u32[]{:S(2)}) collective-permute-start(bf16[8,432,128]{2,1,0:T(8,128)(2,1)} %get-tuple-element.35), channel_id=1, source_target_pairs={{0,2},{2,0},{4,6},{6,4},{8,10},{10,8},{12,14},{14,12},{16,18},{18,... | collective-permute-start | bytes 2654216 | tf_op jit(solution)/shard_map/ppermute | solution.py:333
  35.5 5.2 %collective-permute-start.6 = (bf16[192,256]{1,0:T(8,128)(2,1)S(1)}, bf16[192,256]{1,0:T(8,128)(2,1)S(1)}, u32[]{:S(2)}, u32[]{:S(2)}) collective-permute-start(bf16[192,256]{1,0:T(8,128)(2,1)S(1)} %get-tuple-element.26.refs_3_.refs_6_), channel_id=1, source_target_pairs={{0,1},{1,0},{2,3},{3,2},{4,5},{5,4},{6,7},{7,6},{8,9},{9,8},{10,11... | collective-permute-start | bytes 294920 | tf_op jit(solution)/shard_map/ppermute | solution.py:349
  40.8 5.4 %copy-start.18 = (bf16[192,256]{1,0:T(8,128)(2,1)}, bf16[192,256]{1,0:T(8,128)(2,1)S(1)}, u32[]{:S(2)}) copy-start(bf16[192,256]{1,0:T(8,128)(2,1)S(1)} %collective-permute-done.6.refs_4_.refs_7_) | copy-start | bytes 294916
  44.9 1.3 %copy-start.7 = (f32[8,432,128]{2,1,0:T(8,128)}, f32[8,432,128]{2,1,0:T(8,128)S(1)}, u32[]{:S(2)}) copy-start(f32[8,432,128]{2,1,0:T(8,128)S(1)} %get-tuple-element.31) | copy-start | bytes 5308420
  46.1 18.6 %collective-permute-start.13 = (bf16[8,432,128]{2,1,0:T(8,128)(2,1)}, bf16[8,432,128]{2,1,0:T(8,128)(2,1)}, u32[]{:S(2)}, u32[]{:S(2)}) collective-permute-start(bf16[8,432,128]{2,1,0:T(8,128)(2,1)} %get-tuple-element.32), channel_id=1, source_target_pairs={{0,2},{2,0},{4,6},{6,4},{8,10},{10,8},{12,14},{14,12},{16,18},{18,... | collective-permute-start | bytes 2654216 | tf_op jit(solution)/shard_map/ppermute | solution.py:333
  46.1 18.6 %copy-start.8 = (f32[8,432,128]{2,1,0:T(8,128)S(1)}, f32[8,432,128]{2,1,0:T(8,128)}, u32[]{:S(2)}) copy-start(f32[8,432,128]{2,1,0:T(8,128)} %copy-done.7) | copy-start | bytes 5308420
  48.4 36.1 %collective-permute-start.19 = (bf16[4,432,128]{2,1,0:T(8,128)(2,1)}, bf16[4,432,128]{2,1,0:T(8,128)(2,1)}, u32[]{:S(2)}, u32[]{:S(2)}) collective-permute-start(bf16[4,432,128]{2,1,0:T(8,128)(2,1)} %fusion.7), channel_id=1, source_target_pairs={{0,4},{2,6},{4,0},{6,2},{8,12},{10,14},{12,8},{14,10},{16,20},{18,... | collective-permute-start | bytes 1327112 | tf_op jit(solution)/shard_map/ppermute | solution.py:333
  48.9 7.3 %collective-permute-start.7 = (bf16[96,256]{1,0:T(8,128)(2,1)}, bf16[96,256]{1,0:T(8,128)(2,1)S(1)}, u32[]{:S(2)}, u32[]{:S(2)}) collective-permute-start(bf16[96,256]{1,0:T(8,128)(2,1)} %copy-done.29), channel_id=1, source_target_pairs={{2,4},{6,8},{10,12},{14,16},{18,20},{22,24},{26,28},{4,2},{8,6},{1... | collective-permute-start | bytes 147464 | tf_op jit(solution)/shard_map/ppermute | solution.py:354
  50.8 12.4 %collective-permute-start.8 = (bf16[96,256]{1,0:T(8,128)(2,1)}, bf16[96,256]{1,0:T(8,128)(2,1)S(1)}, u32[]{:S(2)}, u32[]{:S(2)}) collective-permute-start(bf16[96,256]{1,0:T(8,128)(2,1)} %copy-done.29), channel_id=1, source_target_pairs={{2,5},{3,4},{6,9},{7,8},{10,13},{11,12},{14,17},{15,16},{18,21},{1... | collective-permute-start | bytes 147464 | tf_op jit(solution)/shard_map/ppermute | solution.py:356
  56.1 10.5 %collective-permute-start.11 = (bf16[192,256]{1,0:T(8,128)(2,1)}, bf16[192,256]{1,0:T(8,128)(2,1)S(1)}, u32[]{:S(2)}, u32[]{:S(2)}) collective-permute-start(bf16[192,256]{1,0:T(8,128)(2,1)} %copy-done.16), channel_id=1, source_target_pairs={{0,2},{2,0},{4,6},{6,4},{8,10},{10,8},{12,14},{14,12},{16,18},{18,... | collective-permute-start | bytes 294920 | tf_op jit(solution)/shard_map/ppermute | solution.py:333
  56.8 11.4 %collective-permute-start.9 = (bf16[192,256]{1,0:T(8,128)(2,1)}, bf16[192,256]{1,0:T(8,128)(2,1)}, u32[]{:S(2)}, u32[]{:S(2)}) collective-permute-start(bf16[192,256]{1,0:T(8,128)(2,1)} %copy-done.12), channel_id=1, source_target_pairs={{0,2},{2,0},{4,6},{6,4},{8,10},{10,8},{12,14},{14,12},{16,18},{18,... | collective-permute-start | bytes 294920 | tf_op jit(solution)/shard_map/ppermute | solution.py:333
  63.8 4.4 %collective-permute-start.12 = (bf16[192,256]{1,0:T(8,128)(2,1)}, bf16[192,256]{1,0:T(8,128)(2,1)}, u32[]{:S(2)}, u32[]{:S(2)}) collective-permute-start(bf16[192,256]{1,0:T(8,128)(2,1)} %copy-done.18), channel_id=1, source_target_pairs={{0,2},{2,0},{4,6},{6,4},{8,10},{10,8},{12,14},{14,12},{16,18},{18,... | collective-permute-start | bytes 294920 | tf_op jit(solution)/shard_map/ppermute | solution.py:333
  64.7 3.5 %collective-permute-start.10 = (bf16[192,256]{1,0:T(8,128)(2,1)}, bf16[192,256]{1,0:T(8,128)(2,1)}, u32[]{:S(2)}, u32[]{:S(2)}) collective-permute-start(bf16[192,256]{1,0:T(8,128)(2,1)} %copy-done.14), channel_id=1, source_target_pairs={{0,2},{2,0},{4,6},{6,4},{8,10},{10,8},{12,14},{14,12},{16,18},{18,... | collective-permute-start | bytes 294920 | tf_op jit(solution)/shard_map/ppermute | solution.py:333
  67.2 22.3 %collective-permute-start.14 = (bf16[4,432,128]{2,1,0:T(8,128)(2,1)}, bf16[4,432,128]{2,1,0:T(8,128)(2,1)}, u32[]{:S(2)}, u32[]{:S(2)}) collective-permute-start(bf16[4,432,128]{2,1,0:T(8,128)(2,1)} %fusion.6), channel_id=1, source_target_pairs={{0,4},{2,6},{4,0},{6,2},{8,12},{10,14},{12,8},{14,10},{16,20},{18,... | collective-permute-start | bytes 1327112 | tf_op jit(solution)/shard_map/ppermute | solution.py:333
  68.2 2.0 %copy-start.2 = (bf16[6912,256]{1,0:T(8,128)(2,1)S(1)}, bf16[6912,256]{1,0:T(8,128)(2,1)}, u32[]{:S(2)}) copy-start(bf16[6912,256]{1,0:T(8,128)(2,1)} %refs_11_.1) | copy-start | bytes 10616836
  70.2 0.9 copy-start.4
  71.1 0.9 copy-start.6
  72.1 0.9 copy-start.13
  73.0 0.9 copy-start.15
  73.9 0.9 copy-start.17
  74.8 0.9 copy-start.19
  75.7 0.9 copy-start.21
  76.5 0.8 copy-start.25
  77.3 0.8 copy-start.27
  78.1 6.4 %copy-start.11 = (f32[8,432,128]{2,1,0:T(8,128)S(1)}, f32[8,432,128]{2,1,0:T(8,128)}, u32[]{:S(2)}) copy-start(f32[8,432,128]{2,1,0:T(8,128)} %copy-done.10) | copy-start | bytes 5308420
  84.5 5.0 %copy-start.9 = (f32[8,432,128]{2,1,0:T(8,128)S(1)}, f32[8,432,128]{2,1,0:T(8,128)}, u32[]{:S(2)}) copy-start(f32[8,432,128]{2,1,0:T(8,128)} %copy-done.7) | copy-start | bytes 5308420
  86.0 8.0 %collective-permute-start.20 = (bf16[432,128]{1,0:T(8,128)(2,1)S(1)}, bf16[432,128]{1,0:T(8,128)(2,1)S(1)}, u32[]{:S(2)}, u32[]{:S(2)}) collective-permute-start(bf16[432,128]{1,0:T(8,128)(2,1)S(1)} %get-tuple-element.36), channel_id=1, source_target_pairs={{0,8},{2,10},{4,12},{6,14},{8,0},{10,2},{12,4},{14,6},{16,24},{18,... | collective-permute-start | bytes 331784 | tf_op jit(solution)/shard_map/ppermute | solution.py:333
  86.3 11.1 %collective-permute-start.21 = (bf16[432,128]{1,0:T(8,128)(2,1)S(1)}, bf16[432,128]{1,0:T(8,128)(2,1)S(1)}, u32[]{:S(2)}, u32[]{:S(2)}) collective-permute-start(bf16[432,128]{1,0:T(8,128)(2,1)S(1)} %get-tuple-element.38), channel_id=1, source_target_pairs={{0,16},{2,18},{4,20},{6,22},{8,24},{10,26},{12,28},{14,30},{16,0},... | collective-permute-start | bytes 331784 | tf_op jit(solution)/shard_map/ppermute | solution.py:333
  89.1 16.0 %collective-permute-start.22 = (bf16[432,128]{1,0:T(8,128)(2,1)S(1)}, bf16[432,128]{1,0:T(8,128)(2,1)S(1)}, u32[]{:S(2)}, u32[]{:S(2)}) collective-permute-start(bf16[432,128]{1,0:T(8,128)(2,1)S(1)} %get-tuple-element.37), channel_id=1, source_target_pairs={{0,24},{2,26},{4,28},{6,30},{8,16},{10,18},{12,20},{14,22},{16,8},... | collective-permute-start | bytes 331784 | tf_op jit(solution)/shard_map/ppermute | solution.py:333
  90.9 14.9 %collective-permute-start.15 = (bf16[432,128]{1,0:T(8,128)(2,1)S(1)}, bf16[432,128]{1,0:T(8,128)(2,1)S(1)}, u32[]{:S(2)}, u32[]{:S(2)}) collective-permute-start(bf16[432,128]{1,0:T(8,128)(2,1)S(1)} %get-tuple-element.39), channel_id=1, source_target_pairs={{0,8},{2,10},{4,12},{6,14},{8,0},{10,2},{12,4},{14,6},{16,24},{18,... | collective-permute-start | bytes 331784 | tf_op jit(solution)/shard_map/ppermute | solution.py:333
  92.1 14.4 %collective-permute-start.16 = (bf16[432,128]{1,0:T(8,128)(2,1)S(1)}, bf16[432,128]{1,0:T(8,128)(2,1)S(1)}, u32[]{:S(2)}, u32[]{:S(2)}) collective-permute-start(bf16[432,128]{1,0:T(8,128)(2,1)S(1)} %get-tuple-element.41), channel_id=1, source_target_pairs={{0,16},{2,18},{4,20},{6,22},{8,24},{10,26},{12,28},{14,30},{16,0},... | collective-permute-start | bytes 331784 | tf_op jit(solution)/shard_map/ppermute | solution.py:333
  94.0 14.5 %collective-permute-start.17 = (bf16[432,128]{1,0:T(8,128)(2,1)S(1)}, bf16[432,128]{1,0:T(8,128)(2,1)S(1)}, u32[]{:S(2)}, u32[]{:S(2)}) collective-permute-start(bf16[432,128]{1,0:T(8,128)(2,1)S(1)} %get-tuple-element.40), channel_id=1, source_target_pairs={{0,24},{2,26},{4,28},{6,30},{8,16},{10,18},{12,20},{14,22},{16,8},... | collective-permute-start | bytes 331784 | tf_op jit(solution)/shard_map/ppermute | solution.py:333
  (5 other events, 3.2 us)

commit v3 on v2

v3 whole, which is shorter than its diff:
```python
import functools
import math

import jax
import jax.numpy as jnp
from jax import lax
from jax.experimental import pallas as pl
from jax.experimental.pallas import tpu as pltpu
from jax.sharding import PartitionSpec as P

C = 256
TAPS = 27
PLANE = 16
META = 16
LANES = 512
STEP_Y = 64.0
STEP_X = 4096.0
NOWHERE = -1.0e7
VMEM = pl.BlockSpec(memory_space=pltpu.MemorySpace.VMEM)
HBM = pl.BlockSpec(memory_space=pltpu.MemorySpace.HBM)
ANY = pl.BlockSpec(memory_space=pl.ANY)


def params(mib):
    return pltpu.CompilerParams(vmem_limit_bytes=mib * 2**20)


def dot(lhs, rhs, dims=((1,), (0,))):
    return lax.dot_general(lhs, rhs, (dims, ((), ())), preferred_element_type=jnp.float32)


def iota(shape, dim):
    return lax.broadcasted_iota(jnp.int32, shape, dim)


def place_codes(meta, offset, absent=NOWHERE):
    rows = meta.astype(jnp.float32)
    parts = []
    for half in range(2):
        x, y, z, live = (rows[4 * half + i : 4 * half + i + 1] for i in range(4))
        parts.append(jnp.where(live > 0.5, x * STEP_X + y * STEP_Y + z + offset, absent))
    return jnp.concatenate(parts, axis=1)


def source_codes(metas, near, side_offsets, width):
    offsets = [0.0, *side_offsets, near, -near]
    for side_offset in side_offsets:
        offsets += [near + side_offset, side_offset - near]
    lane = iota((1, LANES), 1)
    total = jnp.full((1, LANES), NOWHERE, jnp.float32)
    for place, (meta, offset) in enumerate(zip(metas, offsets)):
        inside = (lane >= place * width) & (lane < (place + 1) * width)
        total = jnp.where(inside, place_codes(meta, offset), total)
    return total


def target_codes(meta, width):
    codes = place_codes(meta, 0.0, 3 * NOWHERE)
    own = iota((width, LANES), 0) == iota((width, LANES), 1)
    column = jnp.sum(jnp.where(own, codes, 0.0), axis=1, keepdims=True)
    return jnp.concatenate(
        [column + ((s // 3 - 1) * STEP_Y + (s % 3 - 1)) for s in range(9)], axis=0
    )


def selectors(source, target, sides, width):
    edge = source[:, : 3 * (1 + sides) * width]
    middle = source[:, : (1 + sides) * width]
    return tuple(
        (codes == target + step).astype(jnp.float32).astype(jnp.bfloat16)
        for codes, step in ((edge, -STEP_X), (middle, 0.0), (edge, STEP_X))
    )


def fill(cols_ref, tiles, faces, chosen, width, columns=slice(None)):
    def load(source, start):
        ref, first = source
        return ref[pl.ds(first + start, width), columns]

    for plane in range(6):
        if plane in (0, 5):
            near = 3 * width if plane == 0 else 0
            pieces = [load(tile, near) for tile in tiles] + [load(face, 0) for face in faces]
        else:
            pieces = [load(tile, (plane - 1) * width) for tile in tiles]
        select = chosen[0 if plane == 0 else 2 if plane == 5 else 1]
        moved = dot(select, jnp.concatenate(pieces, axis=0)).astype(jnp.bfloat16)
        for shift in range(9):
            cols_ref[shift, plane * width : (plane + 1) * width, :] = moved[
                shift * width : (shift + 1) * width
            ]


def tap_rows(cols_ref, tap, width, columns=slice(None)):
    start = tap // 9 * width
    return cols_ref[tap % 9, start : start + 4 * width, columns]


def conv(cols_ref, weight, width):
    total = None
    for tap in range(TAPS):
        term = dot(tap_rows(cols_ref, tap, width), weight.tap(tap))
        total = term if total is None else total + term
    return total


def conv_back(cols_ref, weight, width):
    total = None
    for tap in range(TAPS):
        term = dot(tap_rows(cols_ref, tap, width), weight.tap(26 - tap), ((1,), (1,)))
        total = term if total is None else total + term
    return total


def live_rows(meta, width):
    codes = place_codes(meta, 0.0)
    own = iota((width, LANES), 0) == iota((width, LANES), 1)
    column = jnp.sum(jnp.where(own, codes, 0.0), axis=1, keepdims=True)
    return jnp.concatenate([column] * 4, axis=0) > 0.5 * NOWHERE


def near_row(width, flip=0):
    core = lax.axis_index("gx") % 2
    return pl.multiple_of((1 - core if flip else core) * (3 * width), PLANE)


def side_offsets(sides):
    if sides == 2:
        return [-8 * STEP_Y, 8 * STEP_Y]
    return [(1 - 2 * lax.axis_index("gy")).astype(jnp.float32) * (8 * STEP_Y)]


def pack_kernel(features, cotangent, coords, counts, own_ref, face_ref, place_ref, live_ref, sems):
    slots = features.shape[2]
    width = slots * PLANE
    copies = [
        pltpu.make_async_copy(coords.at[0], place_ref, sems.at[0]),
        pltpu.make_async_copy(counts, live_ref, sems.at[1]),
    ]
    for field, ref in enumerate((features, cotangent)):
        for x in range(4):
            for slot in range(slots):
                start = field * 4 * width + x * width + slot * PLANE
                copies.append(
                    pltpu.make_async_copy(
                        ref.at[0, 0, slot, pl.ds(x * PLANE, PLANE)],
                        own_ref.at[pl.ds(start, PLANE)],
                        sems.at[len(copies)],
                    )
                )
    for copy in copies:
        copy.start()
    for copy in copies:
        copy.wait()
    lane = iota((1, LANES), 1)
    lane_slot = (lane // PLANE) % slots
    position = jnp.zeros((1, LANES), jnp.int32)
    for slot in range(slots):
        position = jnp.where(lane_slot == slot, place_ref[0, slot], position)
    values = [
        position // 16,
        4 * (position // 8 % 2) + lane % PLANE // 4,
        4 * (position % 8) + lane % 4,
        (lane_slot < live_ref[0, 0]).astype(jnp.int32),
    ]
    rows = [v[:, h * C : (h + 1) * C] for h in range(2) for v in values]
    rows.append(jnp.zeros((META - 8, C), jnp.int32))
    meta = jnp.concatenate(rows, axis=0).astype(jnp.float32).astype(jnp.bfloat16)
    own_ref[8 * width :, :] = meta
    at = near_row(width)
    face_ref[:width, :] = own_ref[pl.ds(at, width), :]
    face_ref[width : 2 * width, :] = own_ref[pl.ds(pl.multiple_of(4 * width + at, PLANE), width), :]
    face_ref[2 * width :, :] = meta


def relay_kernel(*refs):
    refs, relay_ref = refs[:-2], refs[-1]
    at = 0
    for ref in refs:
        relay_ref[at : at + ref.shape[0], :] = ref[...]
        at += ref.shape[0]


def placed(j_refs, sides, rows):
    width = rows // 8
    tiles, fars = [], []
    for (own, own_at), (relay, relay_at) in j_refs:
        tiles.append([(own, own_at)])
        tiles[-1] += [(relay, relay_at + s * (rows + META)) for s in range(sides)]
        start = relay_at + sides * (rows + META)
        fars.append([(relay, start + s * (2 * width + META)) for s in range(1 + sides)])
    return tiles, fars


class Around:
    def __init__(self, tiles, fars, sides, rows):
        self.tiles, self.fars, self.sides = tiles, fars, sides
        self.rows, self.width = rows, rows // 8

    def tile(self, j, s):
        return self.tiles[j][s]

    def far(self, j, s):
        return self.fars[j][s]

    def order(self, s):
        return [s] + [other for other in range(1 + self.sides) if other != s]

    def codes(self, j, s):
        def meta(source, start):
            ref, first = source
            return ref[first + start : first + start + 8, :]

        order = self.order(s)
        metas = [meta(self.tile(j, o), self.rows) for o in order]
        for o in order:
            metas.append(meta(self.tile(j ^ 1, o), self.rows))
            metas.append(meta(self.far(j, o), 2 * self.width))
        sign = (1 - 2 * (lax.axis_index("gx") % 2)).astype(jnp.float32) * (2 * STEP_X)
        offsets = side_offsets(self.sides)
        source = source_codes(
            metas, -sign if j % 2 else sign, [-o for o in offsets] if s else offsets, self.width
        )
        return source, target_codes(metas[0], self.width)

    def sources(self, j, s, field):
        top = field * 4 * self.width
        at = near_row(self.width, j % 2)
        order = self.order(s)
        tiles = [(ref, first + top) for ref, first in (self.tile(j, o) for o in order)]
        faces = []
        for o in order:
            ref, first = self.tile(j ^ 1, o)
            faces.append((ref, first + top + at))
            ref, first = self.far(j, o)
            faces.append((ref, first + field * self.width))
        return tiles, faces


class Weight:
    def __init__(self, hbm_ref, ref, sems):
        third = 9 * C
        self.ref = ref
        self.copies = [
            pltpu.make_async_copy(
                hbm_ref.at[pl.ds(i * third, third)], ref.at[pl.ds(i * third, third)], sems.at[i]
            )
            for i in range(3)
        ]

    def start(self, order=(0, 1, 2)):
        for i in order:
            self.copies[i].start()

    def tap(self, tap):
        if self.copies[tap // 9] is not None:
            self.copies[tap // 9].wait()
            self.copies[tap // 9] = None
        return self.ref[tap * C : (tap + 1) * C, :]


def layer_kernel(sides, *refs):
    own, relay, near, near_relay, first_hbm, second_hbm = refs[:6]
    both_ref, slim_ref, face_ref, feature_cols, seed_cols, source_ref, target_ref = refs[6:13]
    first_ref, second_ref, sems = refs[13:]
    first = Weight(first_hbm, first_ref, sems.at[0])
    second = Weight(second_hbm, second_ref, sems.at[1])
    first.start()
    second.start((2, 1, 0))
    rows = own.shape[0] - META
    width = rows // 8
    pairs = [((own, 0), (relay, 0)), ((near, 0), (near_relay, 0))]
    around = Around(*placed(pairs, sides, rows), sides, rows)
    source, target = around.codes(0, 0)
    source_ref[...] = source
    target_ref[...] = target
    chosen = selectors(source, target, sides, width)
    fill(feature_cols, *around.sources(0, 0, 0), chosen, width)
    fill(seed_cols, *around.sources(0, 0, 1), chosen, width)
    pre_first = conv(feature_cols, first, width)
    live = live_rows(own[rows : rows + 8, :], width)
    sigmoid = 1.0 / (1.0 + jnp.exp(-pre_first))
    hidden = jnp.where(live, pre_first * sigmoid, 0.0)
    both_ref[: 4 * width, :] = hidden.astype(jnp.bfloat16)
    slope = jnp.where(live, sigmoid * (1.0 + pre_first * (1.0 - sigmoid)), 0.0)
    hidden_grad = conv_back(seed_cols, second, width)
    both_ref[4 * width :, :] = (hidden_grad * slope).astype(jnp.bfloat16)
    store_face(both_ref, face_ref)
    if sides == 1:
        slim(both_ref, slim_ref)
    else:
        slim_ref[...] = jnp.zeros(slim_ref.shape, slim_ref.dtype)


def slim(both_ref, slim_ref):
    rows = both_ref.shape[0] // 2
    columns = my_columns(C // 2)
    slim_ref[:rows, :] = both_ref[:rows, :]
    slim_ref[rows:, : C // 2] = both_ref[rows : rows + rows // 2, columns]
    slim_ref[rows:, C // 2 :] = both_ref[rows + rows // 2 :, columns]


def gather_kernel(own_ref, relay_ref, both_ref, *refs):
    packed_ref, slim_ref = refs[-2:]
    packed_ref[: own_ref.shape[0], :] = own_ref[...]
    packed_ref[own_ref.shape[0] :, :] = relay_ref[...]
    slim(both_ref, slim_ref)


def store_face(both_ref, face_ref):
    width = both_ref.shape[0] // 8
    at = near_row(width)
    face_ref[:width, :] = both_ref[pl.ds(at, width), :]
    face_ref[width:, :] = both_ref[pl.ds(pl.multiple_of(4 * width + at, PLANE), width), :]


def my_columns(cols):
    if cols == C:
        return slice(None)
    return pl.ds(pl.multiple_of(lax.axis_index("gy") * cols, 128), cols)


def store_terms(keep_ref, send_ref, total_ref):
    core = lax.axis_index("gx") % 2
    pairs, rows = keep_ref.shape[0], keep_ref.shape[1]
    for i in range(pairs):
        keep_at = pl.multiple_of((2 * i + core) * rows, 8)
        send_at = pl.multiple_of((2 * i + 1 - core) * rows, 8)
        keep_ref[i] = total_ref[pl.ds(keep_at, rows), :]
        send_ref[i] = total_ref[pl.ds(send_at, rows), :].astype(jnp.bfloat16)


def second_terms_kernel(both_ref, cols_ref, keep_ref, send_ref, total_ref):
    rows = both_ref.shape[0] // 2
    hidden = both_ref[:rows, :].astype(jnp.float32).T.astype(jnp.bfloat16)
    for tap in range(TAPS):
        total_ref[tap * C : (tap + 1) * C, :] = dot(hidden, tap_rows(cols_ref, 26 - tap, rows // 4))
    store_terms(keep_ref, send_ref, total_ref)


def first_terms_kernel(both_ref, cols_ref, keep_ref, send_ref, total_ref):
    rows = both_ref.shape[0] // 2
    grad = both_ref[rows:, :]
    for tap in range(TAPS):
        total_ref[tap * C : (tap + 1) * C, :] = dot(
            tap_rows(cols_ref, tap, rows // 4), grad, ((0,), (0,))
        )
    store_terms(keep_ref, send_ref, total_ref)


def group_cols(around, members, feature_ref, seed_ref):
    columns = my_columns(seed_ref.shape[3])
    for index, (j, s) in enumerate(members):
        chosen = selectors(*around.codes(j, s), 1, around.width)
        fill(feature_ref.at[index], *around.sources(j, s, 0), chosen, around.width)
        fill(seed_ref.at[index], *around.sources(j, s, 1), chosen, around.width, columns)


CHIP_MEMBERS = ((0, 1), (1, 0), (1, 1))
OTHER_MEMBERS = ((2, 0), (2, 1), (3, 0), (3, 1))


def chip_cols_kernel(own, relay, near, near_relay, feature_ref, seed_ref):
    rows = own.shape[0] - META
    pairs = [((own, 0), (relay, 0)), ((near, 0), (near_relay, 0))]
    around = Around(*placed(pairs, 1, rows), 1, rows)
    group_cols(around, CHIP_MEMBERS, feature_ref, seed_ref)


def other_cols_kernel(packed, near_packed, feature_ref, seed_ref):
    width = feature_ref.shape[2] // 6
    rows = 8 * width
    pairs = [((ref, 0), (ref, rows + META)) for ref in (packed, near_packed)]
    tiles, fars = placed(pairs, 1, rows)
    around = Around([None, None] + tiles, [None, None] + fars, 1, rows)
    group_cols(around, OTHER_MEMBERS, feature_ref, seed_ref)


def group_terms(cols_of, fields, first, top, out_refs, total_ref):
    own_ref, send_refs = out_refs[0], out_refs[1:]
    chunk, cols = own_ref.shape[0] // 2, own_ref.shape[1]
    deep = lax.axis_index("gx") // 4
    row = lax.axis_index("gx") % 4
    taps = total_ref.shape[1] // C
    width = fields[0].shape[0] // 4
    starts = [((deep ^ m) * 4 + row) * chunk for m in range(1 + len(send_refs))]

    def rows(tap):
        tap = jnp.minimum(tap, TAPS - 1)
        tap = tap if first else TAPS - 1 - tap
        at = pl.multiple_of(tap // 9 * width, PLANE)
        return jnp.concatenate(
            [cols_of(i, tap % 9, pl.ds(at, 4 * width)) for i in range(len(fields))], axis=0
        )

    operand = jnp.concatenate(fields, axis=0).astype(jnp.float32).T.astype(jnp.bfloat16)
    wanted = [(m, i) for m in range(len(starts)) for i in range(taps)]
    if first:
        for m, i in wanted:
            result = dot(operand, rows(starts[m] // C + i))
            total_ref[m, i * C : (i + 1) * C, :] = result.T
    else:
        step = max(1, C // cols)
        for at in range(0, len(wanted), step):
            part = wanted[at : at + step]
            result = dot(
                operand, jnp.concatenate([rows(starts[m] // C + i) for m, i in part], axis=1)
            )
            for place, (m, i) in enumerate(part):
                total_ref[m, i * C : (i + 1) * C, :] = result[:, place * cols : (place + 1) * cols]
    for m, start in enumerate(starts):
        at = pl.multiple_of(start % C, 16)
        if m == 0:
            own_ref[top : top + chunk, :] = total_ref[m, pl.ds(at, chunk), :]
        else:
            send_refs[m - 1][top : top + chunk, :] = total_ref[m, pl.ds(at, chunk), :].astype(
                jnp.bfloat16
            )


def group_terms_kernel(*refs):
    both, slims, refs = refs[:4], refs[4:8], refs[8:]
    (feature_cols, seed_cols, *groups), refs = refs[:6], refs[6:]
    out_refs, total_ref = refs[:-1], refs[-1]
    rows = both[0].shape[0] // 2
    chunk = out_refs[0].shape[0] // 2
    columns = my_columns(out_refs[0].shape[1])

    def group(part, tile, shift, at):
        ref, index = (groups[part], tile - 1) if tile < 4 else (groups[2 + part], tile - 4)
        return ref[index, shift, at, :]

    def seeds_of(tile, shift, at):
        return seed_cols[shift, at, columns] if tile == 0 else group(1, tile, shift, at)

    def features_of(tile, shift, at):
        return feature_cols[shift, at, :] if tile == 0 else group(0, tile, shift, at)

    grads = [ref[rows:, columns] for ref in both]
    grads += [
        jnp.concatenate([ref[rows:, : C // 2], ref[rows:, C // 2 :]], axis=0) for ref in slims
    ]
    hiddens = [ref[:rows, :] for ref in (*both, *slims)]
    group_terms(features_of, grads, True, 0, out_refs, total_ref)
    group_terms(seeds_of, hiddens, False, chunk, out_refs, total_ref)


def last_kernel(sides, *refs):
    own_ref, refs = refs[0], refs[1:]
    tiles, refs = refs[: 1 + sides], refs[1 + sides :]
    nears, refs = refs[: 1 + sides], refs[1 + sides :]
    fars, refs = refs[: 1 + sides], refs[1 + sides :]
    first_hbm, second_hbm, source_ref, target_ref, _, output_ref, input_ref = refs[:7]
    hidden_cols_ref, grad_cols_ref, first_ref, second_ref, sems = refs[7:]
    first = Weight(first_hbm, first_ref, sems.at[0])
    second = Weight(second_hbm, second_ref, sems.at[1])
    second.start()
    first.start((2, 1, 0))
    width = tiles[0].shape[0] // 8
    slots = output_ref.shape[0]
    chosen = selectors(source_ref[...], target_ref[...], sides, width)
    live = live_rows(own_ref[8 * width : 8 * width + 8, :], width)
    at = near_row(width)

    def sources(field):
        top = field * 4 * width
        faces = []
        for near, far in zip(nears, fars):
            faces += [(near, top + at), (far, field * width)]
        return [(ref, top) for ref in tiles], faces

    def put(ref, total):
        total = jnp.where(live, total, 0.0)
        for x in range(4):
            for slot in range(slots):
                start = x * width + slot * PLANE
                ref[slot, x * PLANE : (x + 1) * PLANE, :] = total[start : start + PLANE]

    fill(hidden_cols_ref, *sources(0), chosen, width)
    fill(grad_cols_ref, *sources(1), chosen, width)
    put(output_ref, conv(hidden_cols_ref, second, width))
    put(input_ref, conv_back(grad_cols_ref, first, width))


def swap(cells, axis, bit):
    return lax.ppermute(cells, axis, [(i, i ^ bit) for i in range(lax.axis_size(axis))])


def side_steps(count):
    if count == 2:
        return [[(0, 1), (1, 0)]]
    ends = count - 1
    return [[(i, i + 1) for i in range(ends)], [(i + 1, i) for i in range(ends)]]


def far_steps(count):
    pairs = [(i, i + 1) for i in range(1, count - 1, 2)]
    return pairs + [(b, a) for a, b in pairs]


def from_sides(cells):
    return [lax.ppermute(cells, "gy", step) for step in side_steps(lax.axis_size("gy"))]


def from_far(face):
    far = lax.ppermute(face, "gx", far_steps(lax.axis_size("gx")))
    return [far, *from_sides(far)]


def piece(cells, index, axis):
    return lax.dynamic_index_in_dim(cells, index, axis, keepdims=False)


def per_device(features, block_coords, block_counts, first_weight, second_weight, cotangent):
    gx, gy = lax.axis_size("gx"), lax.axis_size("gy")
    iy, ix = lax.axis_index("gy"), lax.axis_index("gx")
    slots = features.shape[2]
    width = slots * PLANE
    rows = 8 * width
    half, deep = ix // 2 % 2, ix // 4
    deeps = gx // 4
    grouped = gy == 2
    sides = 1 if grouped else 2
    chunk = TAPS * C // gx

    def shape(dims, kind=jnp.bfloat16):
        return jax.ShapeDtypeStruct(dims, kind)

    def call(kernel, name, outs, args, mib, micros, scratch=(), specs=None):
        return pl.pallas_call(
            kernel,
            out_shape=outs,
            in_specs=specs or [VMEM] * len(args),
            out_specs=(VMEM,) * len(outs),
            scratch_shapes=list(scratch),
            compiler_params=params(mib),
            cost_estimate=pl.CostEstimate(
                flops=int(micros * 1.1e9), bytes_accessed=2**20, transcendentals=0
            ),
            name=name,
        )(*args)

    own, face = call(
        pack_kernel,
        "pack",
        (shape((rows + META, C)), shape((2 * width + META, C))),
        (features, cotangent, block_coords, block_counts),
        60,
        0.1,
        [
            pltpu.SMEM((1, slots), jnp.int32),
            pltpu.SMEM((1, 1), jnp.int32),
            pltpu.SemaphoreType.DMA((2 + 8 * slots,)),
        ],
        [HBM] * 4,
    )
    side = from_sides(own)
    fars = from_far(face)
    near = swap(own, "gx", 1)
    other = swap(own, "gx", 2) if grouped else own
    parts = [*side, *fars]
    (relay,) = call(
        relay_kernel,
        "relay",
        (shape((sum(cells.shape[0] for cells in parts), C)),),
        (*parts, other),
        8,
        0.1,
        specs=[VMEM] * len(parts) + [ANY],
    )
    near_relay = swap(relay, "gx", 1)
    columns = shape((9, 6 * width, C))
    weights = [pltpu.VMEM(first_weight.shape, jnp.bfloat16)] * 2
    weights.append(pltpu.SemaphoreType.DMA((2, 3)))
    both, thin, late_face, feature_cols, seed_cols, source, target = call(
        functools.partial(layer_kernel, sides),
        "layer",
        (
            shape((rows, C)),
            shape((6 * width, C)),
            shape((2 * width, C)),
            columns,
            columns,
            shape((1, LANES), jnp.float32),
            shape((9 * width, 1), jnp.float32),
        ),
        (own, relay, near, near_relay, first_weight, second_weight),
        58,
        4,
        weights,
        [VMEM] * 4 + [HBM] * 2,
    )
    late_fars = from_far(late_face)
    both_side = from_sides(both)
    both_near = [swap(cells, "gx", 1) for cells in [both] + both_side]
    grad_scale = 1.0 / math.sqrt(64 * slots * gx * gy)

    def over_z(own_part, sent):
        got = [swap(cells, "gx", 4 * m) for m, cells in enumerate(sent, 1)]
        return (own_part + sum(cells.astype(jnp.float32) for cells in got)) * grad_scale

    if grouped:
        cols = C // 2
        far_relay = swap(relay, "gx", 2)

        def group_shapes(count):
            return shape((count, *columns.shape)), shape((count, *columns.shape[:2], cols))

        chip_features, chip_seeds = call(
            chip_cols_kernel,
            "chip_cols",
            group_shapes(len(CHIP_MEMBERS)),
            (own, relay, near, near_relay),
            8,
            3,
        )
        packed, side_thin = call(
            gather_kernel,
            "gather",
            (shape((own.shape[0] + relay.shape[0], C)), shape(thin.shape)),
            (other, far_relay, both_side[0], chip_seeds, late_fars[0]),
            8,
            0.5,
            specs=[VMEM] * 3 + [ANY] * 2,
        )
        near_packed = swap(packed, "gx", 1)
        other_features, other_seeds = call(
            other_cols_kernel,
            "other_cols",
            group_shapes(len(OTHER_MEMBERS)),
            (packed, near_packed),
            8,
            4,
        )
        others = [swap(cells, "gx", 2) for cells in (thin, side_thin)]
        others += [swap(cells, "gx", 1) for cells in others]
        members = [both, both_side[0], *both_near, *others]
        taps = 2 + (chunk - 2) // C
        own_part, *sent = call(
            group_terms_kernel,
            "group_terms",
            (
                shape((2 * chunk, cols), jnp.float32),
                *[shape((2 * chunk, cols))] * (deeps - 1),
            ),
            (
                *members,
                feature_cols,
                seed_cols,
                chip_features,
                chip_seeds,
                other_features,
                other_seeds,
            ),
            12,
            3.5,
            [pltpu.VMEM((deeps, taps * C, cols), jnp.float32)],
        )
        token = sent[0]
        grads = over_z(own_part, sent)
        first_grad, second_grad = grads[:chunk], grads[chunk:]
    else:

        def summed(kernel, name, cells):
            keep, send = call(
                kernel,
                name,
                (
                    shape((gx // 2, chunk, C), jnp.float32),
                    shape((gx // 2, chunk, C)),
                ),
                (both, cells),
                24,
                4,
                [pltpu.VMEM((TAPS * C, C), jnp.float32)],
            )
            keep = keep.reshape(deeps, 2, chunk, C)
            got = swap(send, "gx", 1).reshape(keep.shape)

            def part(i):
                return piece(keep, i, 1) + piece(got, i, 1).astype(jnp.float32)

            total = part(half) + swap(part(1 - half).astype(jnp.bfloat16), "gx", 2).astype(
                jnp.float32
            )
            total = total.reshape(deeps, chunk, gy, C // gy)
            total = piece(total, iy, 2) + sum(
                swap(piece(total, iy ^ m, 2).astype(jnp.bfloat16), "gy", m).astype(jnp.float32)
                for m in range(1, gy)
            )
            total = over_z(
                piece(total, deep, 0),
                [piece(total, deep ^ m, 0).astype(jnp.bfloat16) for m in range(1, deeps)],
            )
            return total, send

        second_grad, token = summed(second_terms_kernel, "second_terms", seed_cols)
        first_grad, _ = summed(first_terms_kernel, "first_terms", feature_cols)

    late = [own, both, *both_side, *both_near, *late_fars]
    result = shape((slots, 64, C), jnp.float32)
    output, input_grad = call(
        functools.partial(last_kernel, sides),
        "last_layer",
        (result, result),
        (*late, first_weight, second_weight, source, target, token),
        58,
        0.1,
        [pltpu.VMEM(columns.shape, jnp.bfloat16)] * 2 + weights,
        [VMEM] * len(late) + [HBM, HBM, VMEM, VMEM, ANY],
    )
    return (
        output.reshape(features.shape),
        input_grad.reshape(features.shape),
        first_grad,
        second_grad,
    )


def solution(mesh):
    placed = (
        P("gx", "gy", None, None, None),
        P("gx", "gy", None),
        P("gx", "gy"),
        P(),
        P(),
        P("gx", "gy", None, None, None),
    )
    return jax.shard_map(
        per_device,
        mesh=mesh,
        in_specs=placed,
        out_specs=(
            P("gx", "gy", None, None, None),
            P("gx", "gy", None, None, None),
            P("gx", "gy"),
            P("gx", "gy"),
        ),
        check_vma=False,
    )
```

time: 111 us -> 79.3 us (0.71); the launches traced: 109 us -> 78.7 us
  starting transfers between devices: 35.5 us -> 17.9 us
  local copies, waits for them, and re-layouts: 19.5 us -> 5.7 us
  other arithmetic: 8.31 us -> 0.12 us
  Pallas kernels: 18.6 us -> 26.5 us
    unnamed x60 -> x34, local copies, waits for them, and re-layouts: 19.4 us -> 4.91 us
    ppermute x4 -> x2, starting transfers between devices: 14.9 us -> 4.13 us  [from_far(): far = lax.ppermute(face, 'gx', far_steps(lax.axis_size('gx')))]
    pallas_call x6 -> x8, Pallas kernels: 18.6 us -> 26.5 us  [call(): pl.pallas_call(kernel, out_shape=outs, in_specs=specs or [VMEM] * len(arg...]
    ppermute x16 -> x14, starting transfers between devices: 15.9 us -> 9.64 us  [swap(): lax.ppermute(cells, axis, [(i, i ^ bit) for i in range(lax.axis_size(axis...]
    convert_element_type x2 -> x0, other arithmetic: 4.16 us -> none  [summed(): sent = part(1 - half).astype(jnp.bfloat16)]
    ppermute x3 -> x4, waiting for transfers between devices: 9.37 us -> 6.25 us  [from_sides(): lax.ppermute(cells, 'gy', step)]
    ppermute x16 -> x14, waiting for transfers between devices: 13.4 us -> 16 us  [swap(): lax.ppermute(cells, axis, [(i, i ^ bit) for i in range(lax.axis_size(axis...]
    add x2 -> x0, other arithmetic: 2.66 us -> none  [summed(): total = part(half) + swap(sent, 'gx', 2).astype(jnp.float32)]
  transfers between devices with their start and end apart: 23 -> 20, of which waited for: 8 -> 8; matrix products, arithmetic and copies ran while one was open for 7% -> 0% of each run, Pallas kernels for 11% -> 28%
where the time goes in v3:
time: 79.3 us; the launch traced here: 78.7 us
  waiting for transfers between devices  27 us (34%)
  Pallas kernels  26.5 us (33%)
  starting transfers between devices  17.9 us (23%)
  local copies, waits for them, and re-layouts  5.7 us (7%)
  between operations  1.57 us (2%)
    pallas_call x8, Pallas kernels, call(): pl.pallas_call(kernel, out_shape=outs, in_specs=specs or [VMEM] * len(arg...  26.5 us
    ppermute x14, waiting for transfers between devices, swap(): lax.ppermute(cells, axis, [(i, i ^ bit) for i in range(lax.axis_size(axis...  16 us
    ppermute x14, starting transfers between devices, swap(): lax.ppermute(cells, axis, [(i, i ^ bit) for i in range(lax.axis_size(axis...  9.64 us
    ppermute x4, waiting for transfers between devices, from_sides(): lax.ppermute(cells, 'gy', step)  6.25 us
    unnamed x34, local copies, waits for them, and re-layouts  4.91 us
    ppermute x2, waiting for transfers between devices, from_far(): far = lax.ppermute(face, 'gx', far_steps(lax.axis_size('gx')))  4.68 us
    ppermute x2, starting transfers between devices, from_far(): far = lax.ppermute(face, 'gx', far_steps(lax.axis_size('gx')))  4.13 us
    ppermute x4, starting transfers between devices, from_sides(): lax.ppermute(cells, 'gy', step)  4.11 us
  transfers between devices with their start and end apart: 20, of which 8 were waited for; matrix products, arithmetic and copies ran while one was open for 0% of the time, Pallas kernels for 28%

profile of v3, /device:TPU:8, one launch (start us, length us, event | category | flops | bytes accessed | tf_op | source)
XLA Modules:
  0.0 78.7 jit_solution(16250578538094452237)
XLA Ops:
  1.3 1.9 %pack.1 = (bf16[400,256]{1,0:T(8,128)(2,1)}, bf16[112,256]{1,0:T(8,128)(2,1)}) custom-call(bf16[1,1,3,64,256]{4,3,2,1,0:T(8,128)(2,1)} %features.1, bf16[1,1,3,64,256]{4,3,2,1,0:T(8,128)(2,1)} %cotangent.1, s32[1,1,3]{2,1,0:T(1,128)} %coords.1, s32[1,1]{1,0:T(1,128)S(6)} %copy.10.counts), custom_call_target="tpu_custom_call" | custom-call | flops 110000000 | bytes 1048576 | tf_op jit(solution)/shard_map/pack/pallas_call | solution.py:530
  3.2 1.6 %collective-permute-start.3 = (bf16[400,256]{1,0:T(8,128)(2,1)}, bf16[400,256]{1,0:T(8,128)(2,1)S(1)}, u32[]{:S(2)}, u32[]{:S(2)}) collective-permute-start(bf16[400,256]{1,0:T(8,128)(2,1)} %get-tuple-element.25.refs_0_.own), channel_id=1, source_target_pairs={{0,4},{2,6},{4,0},{6,2},{8,12},{10,14},{12,8},{14,10},{16,20},{18,... | collective-permute-start | bytes 614408 | tf_op jit(solution)/shard_map/ppermute | solution.py:486
  4.7 1.5 %collective-permute-start = (bf16[400,256]{1,0:T(8,128)(2,1)}, bf16[400,256]{1,0:T(8,128)(2,1)S(1)}, u32[]{:S(2)}, u32[]{:S(2)}) collective-permute-start(bf16[400,256]{1,0:T(8,128)(2,1)} %get-tuple-element.25.refs_0_.own), channel_id=1, source_target_pairs={{0,1},{1,0},{2,3},{3,2},{4,5},{5,4},{6,7},{7,6},{8,9},{9,8},{10,11... | collective-permute-start | bytes 614408 | tf_op jit(solution)/shard_map/ppermute | solution.py:502
  6.2 1.9 %collective-permute-start.1 = (bf16[112,256]{1,0:T(8,128)(2,1)}, bf16[112,256]{1,0:T(8,128)(2,1)S(1)}, u32[]{:S(2)}, u32[]{:S(2)}) collective-permute-start(bf16[112,256]{1,0:T(8,128)(2,1)} %get-tuple-element.26), channel_id=1, source_target_pairs={{2,4},{6,8},{10,12},{14,16},{18,20},{22,24},{26,28},{4,2},{8,6},{1... | collective-permute-start | bytes 172040 | tf_op jit(solution)/shard_map/ppermute | solution.py:506
  8.1 4.7 %collective-permute-done.1.refs_1_ = bf16[112,256]{1,0:T(8,128)(2,1)S(1)} collective-permute-done((bf16[112,256]{1,0:T(8,128)(2,1)}, bf16[112,256]{1,0:T(8,128)(2,1)S(1)}, u32[]{:S(2)}, u32[]{:S(2)}) %collective-permute-start.1) | collective-permute-done | bytes 57376 | tf_op jit(solution)/shard_map/ppermute | solution.py:506
  12.8 0.5 collective-permute-start.2
  13.3 3.7 %collective-permute-done.2.refs_2_ = bf16[112,256]{1,0:T(8,128)(2,1)S(1)} collective-permute-done((bf16[112,256]{1,0:T(8,128)(2,1)S(1)}, bf16[112,256]{1,0:T(8,128)(2,1)S(1)}, u32[]{:S(2)}, u32[]{:S(2)}) %collective-permute-start.2) | collective-permute-done | bytes 57376 | tf_op jit(solution)/shard_map/ppermute | solution.py:502
  17.1 0.1 collective-permute-start.5
  17.1 0.5 collective-permute-start.4
  17.6 0.2 collective-permute-start.12
  17.8 1.4 %collective-permute-done.4.refs_2_.near = bf16[400,256]{1,0:T(8,128)(2,1)S(1)} collective-permute-done((bf16[400,256]{1,0:T(8,128)(2,1)}, bf16[400,256]{1,0:T(8,128)(2,1)S(1)}, u32[]{:S(2)}, u32[]{:S(2)}) %collective-permute-start.4) | collective-permute-done | bytes 204832 | tf_op jit(solution)/shard_map/ppermute | solution.py:486
  19.2 0.0 collective-permute-done.5.refs_3_.near_relay
  19.3 0.7 copy-done.13
  19.9 0.7 copy-done.11
  20.6 7.4 %layer.1 = (bf16[384,256]{1,0:T(8,128)(2,1)}, bf16[288,256]{1,0:T(8,128)(2,1)}, bf16[96,256]{1,0:T(8,128)(2,1)}, bf16[9,288,256]{2,1,0:T(8,128)(2,1)}, bf16[9,28...) custom-call(bf16[400,256]{1,0:T(8,128)(2,1)} %get-tuple-element.25.refs_0_.own, ...), custom_call_target="tpu_custom_call" | custom-call | flops 4400000000 | bytes 1048576 | tf_op jit(solution)/shard_map/layer/pallas_call | solution.py:530
  28.0 0.6 collective-permute-start.6
  28.6 2.2 %collective-permute-start.9 = (bf16[96,256]{1,0:T(8,128)(2,1)}, bf16[96,256]{1,0:T(8,128)(2,1)S(1)}, u32[]{:S(2)}, u32[]{:S(2)}) collective-permute-start(bf16[96,256]{1,0:T(8,128)(2,1)} %get-tuple-element.28), channel_id=1, source_target_pairs={{2,4},{6,8},{10,12},{14,16},{18,20},{22,24},{26,28},{4,2},{8,6},{1... | collective-permute-start | bytes 147464 | tf_op jit(solution)/shard_map/ppermute | solution.py:506
  30.9 1.0 %copy-done.7 = bf16[624,256]{1,0:T(8,128)(2,1)S(1)} copy-done((bf16[624,256]{1,0:T(8,128)(2,1)S(1)}, bf16[624,256]{1,0:T(8,128)(2,1)}, u32[]{:S(2)}) %copy-start.7) | copy-done | bytes 319512
  31.8 1.0 %copy-done.12 = bf16[624,256]{1,0:T(8,128)(2,1)S(1)} copy-done((bf16[624,256]{1,0:T(8,128)(2,1)S(1)}, bf16[624,256]{1,0:T(8,128)(2,1)}, u32[]{:S(2)}) %copy-start.12) | copy-done | bytes 319512
  32.8 0.9 %copy-done.14 = bf16[400,256]{1,0:T(8,128)(2,1)S(1)} copy-done((bf16[400,256]{1,0:T(8,128)(2,1)S(1)}, bf16[400,256]{1,0:T(8,128)(2,1)}, u32[]{:S(2)}) %copy-start.14) | copy-done | bytes 204824
  33.7 3.1 %chip_cols.1 = (bf16[3,9,288,256]{3,2,1,0:T(8,128)(2,1)S(1)}, bf16[3,9,288,128]{3,2,1,0:T(8,128)(2,1)S(1)}) custom-call(bf16[400,256]{1,0:T(8,128)(2,1)S(1)} %copy-done.9, bf16[624,256]{1,0:T(8,128)(2,1)S(1)} %copy-done.7, bf16[400,256]{1,0:T(8,128)(2,1)S(1)} %copy-done.14, bf16[624,256]{1,0:T(8,128)(2,1)S(1)} %copy-done.12), custom_call_target="tpu_custom_call" | custom-call | flops 3300000000 | bytes 1048576 | tf_op jit(solution)/shard_map/chip_cols/pallas_call | solution.py:530
  36.8 0.0 collective-permute-done.12.relay_ref
  36.9 0.0 collective-permute-done.6.both_ref.refs_1_.refs_2_
  36.9 0.1 gather.1
  36.9 1.1 %collective-permute-start.16 = (bf16[1024,256]{1,0:T(8,128)(2,1)S(1)}, bf16[1024,256]{1,0:T(8,128)(2,1)S(1)}, u32[]{:S(2)}, u32[]{:S(2)}) collective-permute-start(bf16[1024,256]{1,0:T(8,128)(2,1)S(1)} %get-tuple-element.37.packed), channel_id=1, source_target_pairs={{0,2},{2,0},{4,6},{6,4},{8,10},{10,8},{12,14},{14,12},{16,18},{18,... | collective-permute-start | bytes 1572872 | tf_op jit(solution)/shard_map/ppermute | solution.py:486
  38.0 2.1 %collective-permute-start.11 = (bf16[288,256]{1,0:T(8,128)(2,1)S(1)}, bf16[288,256]{1,0:T(8,128)(2,1)S(1)}, u32[]{:S(2)}, u32[]{:S(2)}) collective-permute-start(bf16[288,256]{1,0:T(8,128)(2,1)S(1)} %copy-done.16), channel_id=1, source_target_pairs={{0,4},{2,6},{4,0},{6,2},{8,12},{10,14},{12,8},{14,10},{16,20},{18,... | collective-permute-start | bytes 442376 | tf_op jit(solution)/shard_map/ppermute | solution.py:486
  40.2 0.1 collective-permute-start.13
  40.2 0.0 collective-permute-start.7
  40.2 4.5 %collective-permute-done.11.refs_4_ = bf16[288,256]{1,0:T(8,128)(2,1)S(1)} collective-permute-done((bf16[288,256]{1,0:T(8,128)(2,1)S(1)}, bf16[288,256]{1,0:T(8,128)(2,1)S(1)}, u32[]{:S(2)}, u32[]{:S(2)}) %collective-permute-start.11) | collective-permute-done | bytes 147488 | tf_op jit(solution)/shard_map/ppermute | solution.py:486
  44.8 0.5 collective-permute-start.8
  45.3 2.1 %collective-permute-done.13.refs_5_ = bf16[288,256]{1,0:T(8,128)(2,1)S(1)} collective-permute-done((bf16[288,256]{1,0:T(8,128)(2,1)S(1)}, bf16[288,256]{1,0:T(8,128)(2,1)S(1)}, u32[]{:S(2)}, u32[]{:S(2)}) %collective-permute-start.13) | collective-permute-done | bytes 147488 | tf_op jit(solution)/shard_map/ppermute | solution.py:486
  47.4 0.0 collective-permute-start.15
  47.4 0.0 collective-permute-done.16.near_packed
  47.4 4.0 %other_cols.1 = (bf16[4,9,288,256]{3,2,1,0:T(8,128)(2,1)S(1)}, bf16[4,9,288,128]{3,2,1,0:T(8,128)(2,1)S(1)}) custom-call(bf16[1024,256]{1,0:T(8,128)(2,1)S(1)} %get-tuple-element.37.packed, bf16[1024,256]{1,0:T(8,128)(2,1)S(1)} %collective-permute-done.16.near_packed), custom_call_target="tpu_custom_call" | custom-call | flops 4400000000 | bytes 1048576 | tf_op jit(solution)/shard_map/other_cols/pallas_call | solution.py:530
  51.5 0.0 collective-permute-done.14.refs_6_
  51.5 2.9 %group_terms.1 = (f32[864,128]{1,0:T(8,128)S(1)}, bf16[864,128]{1,0:T(8,128)(2,1)S(1)}, bf16[864,128]{1,0:T(8,128)(2,1)S(1)}, bf16[864,128]{1,0:T(8,128)(2,1)S(1)}) custom-call(bf16[384,256]{1,0:T(8,128)(2,1)S(1)} %copy-done.3, bf16[384,256]{1,0:T(8,128)(2,1)S(1)} %collective-permute-done.6.both_ref.refs_1_.refs_2_, ...), custom_call_target="tpu_custom_call" | custom-call | flops 3849999872 | bytes 1048576 | tf_op jit(solution)/shard_map/group_terms/pallas_call | solution.py:530
  54.4 0.0 copy-start.8
  54.4 0.5 collective-permute-start.17
  55.0 2.6 %collective-permute-start.18 = (bf16[864,128]{1,0:T(8,128)(2,1)S(1)}, bf16[864,128]{1,0:T(8,128)(2,1)S(1)}, u32[]{:S(2)}, u32[]{:S(2)}) collective-permute-start(bf16[864,128]{1,0:T(8,128)(2,1)S(1)} %get-tuple-element.44), channel_id=1, source_target_pairs={{0,16},{2,18},{4,20},{6,22},{8,24},{10,26},{12,28},{14,30},{16,0},... | collective-permute-start | bytes 663560 | tf_op jit(solution)/shard_map/ppermute | solution.py:486
  57.5 0.5 collective-permute-start.19
  58.0 1.5 %collective-permute-start.10 = (bf16[96,256]{1,0:T(8,128)(2,1)S(1)}, bf16[96,256]{1,0:T(8,128)(2,1)S(1)}, u32[]{:S(2)}, u32[]{:S(2)}) collective-permute-start(bf16[96,256]{1,0:T(8,128)(2,1)S(1)} %collective-permute-done.9.refs_1_.refs_5_), channel_id=1, source_target_pairs={{0,1},{1,0},{2,3},{3,2},{4,5},{5,4},{6,7},{7,6},{8,9},{9,8},{10,11... | collective-permute-start | bytes 147464 | tf_op jit(solution)/shard_map/ppermute | solution.py:502
  59.5 2.6 %collective-permute-done.10.refs_6_ = bf16[96,256]{1,0:T(8,128)(2,1)S(1)} collective-permute-done((bf16[96,256]{1,0:T(8,128)(2,1)S(1)}, bf16[96,256]{1,0:T(8,128)(2,1)S(1)}, u32[]{:S(2)}, u32[]{:S(2)}) %collective-permute-start.10) | collective-permute-done | bytes 49184 | tf_op jit(solution)/shard_map/ppermute | solution.py:502
  62.1 0.6 copy-done.15
  62.7 7.2 %last_layer.1 = (f32[3,64,256]{2,1,0:T(8,128)}, f32[3,64,256]{2,1,0:T(8,128)}) custom-call(bf16[400,256]{1,0:T(8,128)(2,1)} %get-tuple-element.25.refs_0_.own, bf16[384,256]{1,0:T(8,128)(2,1)} %get-tuple-element.27.refs_0_.refs_1_, bf16[384,256]{1,0:T(8,128)(2,1)} %copy-done, bf16[384,256]{1,0:T(8,128)(2,1)} %copy-done.4, bf16[384,256]{1,0:T(8,128)(2,1)} %copy-done.5, ...), custom_call_target="tpu_custom_call" | custom-call | flops 110000000 | bytes 1048576 | tf_op jit(solution)/shard_map/last_layer/pallas_call | solution.py:530
  69.9 2.9 %collective-permute-done.18 = bf16[864,128]{1,0:T(8,128)(2,1)S(1)} collective-permute-done((bf16[864,128]{1,0:T(8,128)(2,1)S(1)}, bf16[864,128]{1,0:T(8,128)(2,1)S(1)}, u32[]{:S(2)}, u32[]{:S(2)}) %collective-permute-start.18) | collective-permute-done | bytes 221216 | tf_op jit(solution)/shard_map/ppermute | solution.py:486
  72.8 5.0 %collective-permute-done.19 = bf16[864,128]{1,0:T(8,128)(2,1)S(1)} collective-permute-done((bf16[864,128]{1,0:T(8,128)(2,1)S(1)}, bf16[864,128]{1,0:T(8,128)(2,1)S(1)}, u32[]{:S(2)}, u32[]{:S(2)}) %collective-permute-start.19) | collective-permute-done | bytes 221216 | tf_op jit(solution)/shard_map/ppermute | solution.py:486
  77.8 0.1 add_multiply_fusion
  77.9 0.8 %fusion = (f32[432,128]{1,0:T(8,128)}, f32[432,128]{1,0:T(8,128)}) fusion(f32[864,128]{1,0:T(8,128)S(1)} %add_multiply_fusion), kind=kLoop, calls=%fused_computation.1 | loop fusion | bytes 884736 | tf_op jit(solution)/shard_map/slice | solution.py:661
  (36 shorter events, 0.1 us)
Async XLA Ops:
  3.2 13.9 %collective-permute-start.3 = (bf16[400,256]{1,0:T(8,128)(2,1)}, bf16[400,256]{1,0:T(8,128)(2,1)S(1)}, u32[]{:S(2)}, u32[]{:S(2)}) collective-permute-start(bf16[400,256]{1,0:T(8,128)(2,1)} %get-tuple-element.25.refs_0_.own), channel_id=1, source_target_pairs={{0,4},{2,6},{4,0},{6,2},{8,12},{10,14},{12,8},{14,10},{16,20},{18,... | collective-permute-start | bytes 614408 | tf_op jit(solution)/shard_map/ppermute | solution.py:486
  4.7 12.3 %collective-permute-start = (bf16[400,256]{1,0:T(8,128)(2,1)}, bf16[400,256]{1,0:T(8,128)(2,1)S(1)}, u32[]{:S(2)}, u32[]{:S(2)}) collective-permute-start(bf16[400,256]{1,0:T(8,128)(2,1)} %get-tuple-element.25.refs_0_.own), channel_id=1, source_target_pairs={{0,1},{1,0},{2,3},{3,2},{4,5},{5,4},{6,7},{7,6},{8,9},{9,8},{10,11... | collective-permute-start | bytes 614408 | tf_op jit(solution)/shard_map/ppermute | solution.py:502
  6.2 6.6 %collective-permute-start.1 = (bf16[112,256]{1,0:T(8,128)(2,1)}, bf16[112,256]{1,0:T(8,128)(2,1)S(1)}, u32[]{:S(2)}, u32[]{:S(2)}) collective-permute-start(bf16[112,256]{1,0:T(8,128)(2,1)} %get-tuple-element.26), channel_id=1, source_target_pairs={{2,4},{6,8},{10,12},{14,16},{18,20},{22,24},{26,28},{4,2},{8,6},{1... | collective-permute-start | bytes 172040 | tf_op jit(solution)/shard_map/ppermute | solution.py:506
  12.8 4.2 %collective-permute-start.2 = (bf16[112,256]{1,0:T(8,128)(2,1)S(1)}, bf16[112,256]{1,0:T(8,128)(2,1)S(1)}, u32[]{:S(2)}, u32[]{:S(2)}) collective-permute-start(bf16[112,256]{1,0:T(8,128)(2,1)S(1)} %collective-permute-done.1.refs_1_), channel_id=1, source_target_pairs={{0,1},{1,0},{2,3},{3,2},{4,5},{5,4},{6,7},{7,6},{8,9},{9,8},{10,11... | collective-permute-start | bytes 172040 | tf_op jit(solution)/shard_map/ppermute | solution.py:502
  17.0 2.2 %copy-start.6 = (bf16[624,256]{1,0:T(8,128)(2,1)}, bf16[624,256]{1,0:T(8,128)(2,1)S(1)}, u32[]{:S(2)}) copy-start(bf16[624,256]{1,0:T(8,128)(2,1)S(1)} %relay.1.refs_1_) | copy-start | bytes 958468
  17.0 13.8 %copy-start.9 = (bf16[400,256]{1,0:T(8,128)(2,1)S(1)}, bf16[400,256]{1,0:T(8,128)(2,1)}, u32[]{:S(2)}) copy-start(bf16[400,256]{1,0:T(8,128)(2,1)} %get-tuple-element.25.refs_0_.own) | copy-start | bytes 614404
  17.1 2.2 %collective-permute-start.5 = (bf16[624,256]{1,0:T(8,128)(2,1)S(1)}, bf16[624,256]{1,0:T(8,128)(2,1)S(1)}, u32[]{:S(2)}, u32[]{:S(2)}) collective-permute-start(bf16[624,256]{1,0:T(8,128)(2,1)S(1)} %relay.1.refs_1_), channel_id=1, source_target_pairs={{0,2},{2,0},{4,6},{6,4},{8,10},{10,8},{12,14},{14,12},{16,18},{18,... | collective-permute-start | bytes 958472 | tf_op jit(solution)/shard_map/ppermute | solution.py:486
  17.1 2.1 %collective-permute-start.4 = (bf16[400,256]{1,0:T(8,128)(2,1)}, bf16[400,256]{1,0:T(8,128)(2,1)S(1)}, u32[]{:S(2)}, u32[]{:S(2)}) collective-permute-start(bf16[400,256]{1,0:T(8,128)(2,1)} %get-tuple-element.25.refs_0_.own), channel_id=1, source_target_pairs={{0,2},{2,0},{4,6},{6,4},{8,10},{10,8},{12,14},{14,12},{16,18},{18,... | collective-permute-start | bytes 614408 | tf_op jit(solution)/shard_map/ppermute | solution.py:486
  17.6 19.2 %collective-permute-start.12 = (bf16[624,256]{1,0:T(8,128)(2,1)S(1)}, bf16[624,256]{1,0:T(8,128)(2,1)S(1)}, u32[]{:S(2)}, u32[]{:S(2)}) collective-permute-start(bf16[624,256]{1,0:T(8,128)(2,1)S(1)} %relay.1.refs_1_), channel_id=1, source_target_pairs={{0,4},{2,6},{4,0},{6,2},{8,12},{10,14},{12,8},{14,10},{16,20},{18,... | collective-permute-start | bytes 958472 | tf_op jit(solution)/shard_map/ppermute | solution.py:486
  19.2 0.7 copy-start.13
  19.9 0.7 copy-start.11
  28.0 8.8 %collective-permute-start.6 = (bf16[384,256]{1,0:T(8,128)(2,1)}, bf16[384,256]{1,0:T(8,128)(2,1)S(1)}, u32[]{:S(2)}, u32[]{:S(2)}) collective-permute-start(bf16[384,256]{1,0:T(8,128)(2,1)} %get-tuple-element.27.refs_0_.refs_1_), channel_id=1, source_target_pairs={{0,1},{1,0},{2,3},{3,2},{4,5},{5,4},{6,7},{7,6},{8,9},{9,8},{10,11... | collective-permute-start | bytes 589832 | tf_op jit(solution)/shard_map/ppermute | solution.py:502
  28.6 11.6 %copy-start.3 = (bf16[384,256]{1,0:T(8,128)(2,1)S(1)}, bf16[384,256]{1,0:T(8,128)(2,1)}, u32[]{:S(2)}) copy-start(bf16[384,256]{1,0:T(8,128)(2,1)} %get-tuple-element.27.refs_0_.refs_1_) | copy-start | bytes 589828
  28.6 8.2 %collective-permute-start.9 = (bf16[96,256]{1,0:T(8,128)(2,1)}, bf16[96,256]{1,0:T(8,128)(2,1)S(1)}, u32[]{:S(2)}, u32[]{:S(2)}) collective-permute-start(bf16[96,256]{1,0:T(8,128)(2,1)} %get-tuple-element.28), channel_id=1, source_target_pairs={{2,4},{6,8},{10,12},{14,16},{18,20},{22,24},{26,28},{4,2},{8,6},{1... | collective-permute-start | bytes 147464 | tf_op jit(solution)/shard_map/ppermute | solution.py:506
  30.9 1.0 %copy-start.7 = (bf16[624,256]{1,0:T(8,128)(2,1)S(1)}, bf16[624,256]{1,0:T(8,128)(2,1)}, u32[]{:S(2)}) copy-start(bf16[624,256]{1,0:T(8,128)(2,1)} %copy-done.6) | copy-start | bytes 958468
  31.8 1.0 %copy-start.12 = (bf16[624,256]{1,0:T(8,128)(2,1)S(1)}, bf16[624,256]{1,0:T(8,128)(2,1)}, u32[]{:S(2)}) copy-start(bf16[624,256]{1,0:T(8,128)(2,1)} %copy-done.11) | copy-start | bytes 958468
  32.8 0.9 %copy-start.14 = (bf16[400,256]{1,0:T(8,128)(2,1)S(1)}, bf16[400,256]{1,0:T(8,128)(2,1)}, u32[]{:S(2)}) copy-start(bf16[400,256]{1,0:T(8,128)(2,1)} %copy-done.13) | copy-start | bytes 614404
  33.7 4.3 %copy-start.16 = (bf16[288,256]{1,0:T(8,128)(2,1)S(1)}, bf16[288,256]{1,0:T(8,128)(2,1)}, u32[]{:S(2)}) copy-start(bf16[288,256]{1,0:T(8,128)(2,1)} %get-tuple-element.31) | copy-start | bytes 442372
  36.8 21.1 %copy-start.10 = (bf16[96,256]{1,0:T(8,128)(2,1)}, bf16[96,256]{1,0:T(8,128)(2,1)S(1)}, u32[]{:S(2)}) copy-start(bf16[96,256]{1,0:T(8,128)(2,1)S(1)} %collective-permute-done.9.refs_1_.refs_5_) | copy-start | bytes 147460
  36.9 14.6 %copy-start = (bf16[384,256]{1,0:T(8,128)(2,1)}, bf16[384,256]{1,0:T(8,128)(2,1)S(1)}, u32[]{:S(2)}) copy-start(bf16[384,256]{1,0:T(8,128)(2,1)S(1)} %collective-permute-done.6.both_ref.refs_1_.refs_2_) | copy-start | bytes 589828
  36.9 10.5 %collective-permute-start.16 = (bf16[1024,256]{1,0:T(8,128)(2,1)S(1)}, bf16[1024,256]{1,0:T(8,128)(2,1)S(1)}, u32[]{:S(2)}, u32[]{:S(2)}) collective-permute-start(bf16[1024,256]{1,0:T(8,128)(2,1)S(1)} %get-tuple-element.37.packed), channel_id=1, source_target_pairs={{0,2},{2,0},{4,6},{6,4},{8,10},{10,8},{12,14},{14,12},{16,18},{18,... | collective-permute-start | bytes 1572872 | tf_op jit(solution)/shard_map/ppermute | solution.py:486
  38.0 6.7 %collective-permute-start.11 = (bf16[288,256]{1,0:T(8,128)(2,1)S(1)}, bf16[288,256]{1,0:T(8,128)(2,1)S(1)}, u32[]{:S(2)}, u32[]{:S(2)}) collective-permute-start(bf16[288,256]{1,0:T(8,128)(2,1)S(1)} %copy-done.16), channel_id=1, source_target_pairs={{0,4},{2,6},{4,0},{6,2},{8,12},{10,14},{12,8},{14,10},{16,20},{18,... | collective-permute-start | bytes 442376 | tf_op jit(solution)/shard_map/ppermute | solution.py:486
  40.1 11.4 %copy-start.1 = (bf16[9,288,256]{2,1,0:T(8,128)(2,1)S(1)}, bf16[9,288,256]{2,1,0:T(8,128)(2,1)}, u32[]{:S(2)}) copy-start(bf16[9,288,256]{2,1,0:T(8,128)(2,1)} %get-tuple-element.34.refs_8_) | copy-start | bytes 3981316
  40.2 11.4 %copy-start.2 = (bf16[9,288,256]{2,1,0:T(8,128)(2,1)S(1)}, bf16[9,288,256]{2,1,0:T(8,128)(2,1)}, u32[]{:S(2)}) copy-start(bf16[9,288,256]{2,1,0:T(8,128)(2,1)} %get-tuple-element.35.refs_9_) | copy-start | bytes 3981316
  40.2 7.3 %collective-permute-start.13 = (bf16[288,256]{1,0:T(8,128)(2,1)S(1)}, bf16[288,256]{1,0:T(8,128)(2,1)S(1)}, u32[]{:S(2)}, u32[]{:S(2)}) collective-permute-start(bf16[288,256]{1,0:T(8,128)(2,1)S(1)} %get-tuple-element.33), channel_id=1, source_target_pairs={{0,4},{2,6},{4,0},{6,2},{8,12},{10,14},{12,8},{14,10},{16,20},{18,... | collective-permute-start | bytes 442376 | tf_op jit(solution)/shard_map/ppermute | solution.py:486
  40.2 11.2 %collective-permute-start.7 = (bf16[384,256]{1,0:T(8,128)(2,1)S(1)}, bf16[384,256]{1,0:T(8,128)(2,1)S(1)}, u32[]{:S(2)}, u32[]{:S(2)}) collective-permute-start(bf16[384,256]{1,0:T(8,128)(2,1)S(1)} %copy-done.3), channel_id=1, source_target_pairs={{0,2},{2,0},{4,6},{6,4},{8,10},{10,8},{12,14},{14,12},{16,18},{18,... | collective-permute-start | bytes 589832 | tf_op jit(solution)/shard_map/ppermute | solution.py:486
  44.8 6.7 %collective-permute-start.14 = (bf16[288,256]{1,0:T(8,128)(2,1)S(1)}, bf16[288,256]{1,0:T(8,128)(2,1)S(1)}, u32[]{:S(2)}, u32[]{:S(2)}) collective-permute-start(bf16[288,256]{1,0:T(8,128)(2,1)S(1)} %collective-permute-done.11.refs_4_), channel_id=1, source_target_pairs={{0,2},{2,0},{4,6},{6,4},{8,10},{10,8},{12,14},{14,12},{16,18},{18,... | collective-permute-start | bytes 442376 | tf_op jit(solution)/shard_map/ppermute | solution.py:486
  44.8 6.7 %collective-permute-start.8 = (bf16[384,256]{1,0:T(8,128)(2,1)S(1)}, bf16[384,256]{1,0:T(8,128)(2,1)S(1)}, u32[]{:S(2)}, u32[]{:S(2)}) collective-permute-start(bf16[384,256]{1,0:T(8,128)(2,1)S(1)} %collective-permute-done.6.both_ref.refs_1_.refs_2_), channel_id=1, source_target_pairs={{0,2},{2,0},{4,6},{6,4},{8,10},{10,8},{12,14},{14,12},{16,18},{18,... | collective-permute-start | bytes 589832 | tf_op jit(solution)/shard_map/ppermute | solution.py:486
  47.4 4.1 %collective-permute-start.15 = (bf16[288,256]{1,0:T(8,128)(2,1)S(1)}, bf16[288,256]{1,0:T(8,128)(2,1)S(1)}, u32[]{:S(2)}, u32[]{:S(2)}) collective-permute-start(bf16[288,256]{1,0:T(8,128)(2,1)S(1)} %collective-permute-done.13.refs_5_), channel_id=1, source_target_pairs={{0,2},{2,0},{4,6},{6,4},{8,10},{10,8},{12,14},{14,12},{16,18},{18,... | collective-permute-start | bytes 442376 | tf_op jit(solution)/shard_map/ppermute | solution.py:486
  51.4 3.0 %copy-start.4 = (bf16[384,256]{1,0:T(8,128)(2,1)}, bf16[384,256]{1,0:T(8,128)(2,1)S(1)}, u32[]{:S(2)}) copy-start(bf16[384,256]{1,0:T(8,128)(2,1)S(1)} %collective-permute-done.7.refs_2_.refs_3_) | copy-start | bytes 589828
  51.5 2.9 %copy-start.5 = (bf16[384,256]{1,0:T(8,128)(2,1)}, bf16[384,256]{1,0:T(8,128)(2,1)S(1)}, u32[]{:S(2)}) copy-start(bf16[384,256]{1,0:T(8,128)(2,1)S(1)} %collective-permute-done.8.refs_3_.refs_4_) | copy-start | bytes 589828
  54.4 7.7 %copy-start.8 = (bf16[864,128]{1,0:T(8,128)(2,1)}, bf16[864,128]{1,0:T(8,128)(2,1)S(1)}, u32[]{:S(2)}) copy-start(bf16[864,128]{1,0:T(8,128)(2,1)S(1)} %get-tuple-element.40.refs_11_) | copy-start | bytes 663556
  54.4 15.4 %collective-permute-start.17 = (bf16[864,128]{1,0:T(8,128)(2,1)S(1)}, bf16[864,128]{1,0:T(8,128)(2,1)S(1)}, u32[]{:S(2)}, u32[]{:S(2)}) collective-permute-start(bf16[864,128]{1,0:T(8,128)(2,1)S(1)} %get-tuple-element.40.refs_11_), channel_id=1, source_target_pairs={{0,8},{2,10},{4,12},{6,14},{8,0},{10,2},{12,4},{14,6},{16,24},{18,... | collective-permute-start | bytes 663560 | tf_op jit(solution)/shard_map/ppermute | solution.py:486
  55.0 17.9 %collective-permute-start.18 = (bf16[864,128]{1,0:T(8,128)(2,1)S(1)}, bf16[864,128]{1,0:T(8,128)(2,1)S(1)}, u32[]{:S(2)}, u32[]{:S(2)}) collective-permute-start(bf16[864,128]{1,0:T(8,128)(2,1)S(1)} %get-tuple-element.44), channel_id=1, source_target_pairs={{0,16},{2,18},{4,20},{6,22},{8,24},{10,26},{12,28},{14,30},{16,0},... | collective-permute-start | bytes 663560 | tf_op jit(solution)/shard_map/ppermute | solution.py:486
  57.5 20.3 %collective-permute-start.19 = (bf16[864,128]{1,0:T(8,128)(2,1)S(1)}, bf16[864,128]{1,0:T(8,128)(2,1)S(1)}, u32[]{:S(2)}, u32[]{:S(2)}) collective-permute-start(bf16[864,128]{1,0:T(8,128)(2,1)S(1)} %get-tuple-element.45), channel_id=1, source_target_pairs={{0,24},{2,26},{4,28},{6,30},{8,16},{10,18},{12,20},{14,22},{16,8},... | collective-permute-start | bytes 663560 | tf_op jit(solution)/shard_map/ppermute | solution.py:486
  58.0 4.1 %collective-permute-start.10 = (bf16[96,256]{1,0:T(8,128)(2,1)S(1)}, bf16[96,256]{1,0:T(8,128)(2,1)S(1)}, u32[]{:S(2)}, u32[]{:S(2)}) collective-permute-start(bf16[96,256]{1,0:T(8,128)(2,1)S(1)} %collective-permute-done.9.refs_1_.refs_5_), channel_id=1, source_target_pairs={{0,1},{1,0},{2,3},{3,2},{4,5},{5,4},{6,7},{7,6},{8,9},{9,8},{10,11... | collective-permute-start | bytes 147464 | tf_op jit(solution)/shard_map/ppermute | solution.py:502
  62.1 0.6 copy-start.15

commit v4 on v3

--- a/solution.py
+++ b/solution.py
@@ -42,10 +42,7 @@
     return jnp.concatenate(parts, axis=1)
 
 
-def source_codes(metas, near, side_offsets, width):
-    offsets = [0.0, *side_offsets, near, -near]
-    for side_offset in side_offsets:
-        offsets += [near + side_offset, side_offset - near]
+def source_codes(metas, offsets, width):
     lane = iota((1, LANES), 1)
     total = jnp.full((1, LANES), NOWHERE, jnp.float32)
     for place, (meta, offset) in enumerate(zip(metas, offsets)):
@@ -63,26 +60,35 @@
     )
 
 
-def selectors(source, target, sides, width):
-    edge = source[:, : 3 * (1 + sides) * width]
-    middle = source[:, : (1 + sides) * width]
+def selectors(before, after, target, sides, width):
+    middle = (1 + sides) * width
     return tuple(
         (codes == target + step).astype(jnp.float32).astype(jnp.bfloat16)
-        for codes, step in ((edge, -STEP_X), (middle, 0.0), (edge, STEP_X))
-    )
-
-
-def fill(cols_ref, tiles, faces, chosen, width, columns=slice(None)):
-    def load(source, start):
-        ref, first = source
-        return ref[pl.ds(first + start, width), columns]
+        for codes, step in (
+            (before[:, : 2 * middle], -STEP_X),
+            (before[:, :middle], 0.0),
+            (after[:, : 2 * middle], STEP_X),
+        )
+    )
+
+
+def fill(cols_ref, tiles, faces, odd, chosen, width, columns=slice(None)):
+    def load(source, plane):
+        ref, first, paired = source
+        if paired:
+            at = first + plane % 2 * width
+            return ref[at : at + width, plane // 2 * (C // 2) : (plane // 2 + 1) * (C // 2)]
+        return ref[first + plane * width : first + (plane + 1) * width, columns]
 
     for plane in range(6):
         if plane in (0, 5):
-            near = 3 * width if plane == 0 else 0
-            pieces = [load(tile, near) for tile in tiles] + [load(face, 0) for face in faces]
+            start = 3 if plane == 0 else 0
+            pieces = [load(tile, start) for tile in tiles]
+            for near, far in faces:
+                near, far = load(near, start), load(far, 0)
+                pieces.append(jnp.where(odd, near, far) if plane == 0 else jnp.where(odd, far, near))
         else:
-            pieces = [load(tile, (plane - 1) * width) for tile in tiles]
+            pieces = [load(tile, plane - 1) for tile in tiles]
         select = chosen[0 if plane == 0 else 2 if plane == 5 else 1]
         moved = dot(select, jnp.concatenate(pieces, axis=0)).astype(jnp.bfloat16)
         for shift in range(9):
@@ -96,18 +102,19 @@
     return cols_ref[tap % 9, start : start + 4 * width, columns]
 
 
-def conv(cols_ref, weight, width):
+def conv(cols_ref, weight_ref, width):
     total = None
     for tap in range(TAPS):
-        term = dot(tap_rows(cols_ref, tap, width), weight.tap(tap))
+        term = dot(tap_rows(cols_ref, tap, width), weight_ref[tap * C : (tap + 1) * C, :])
         total = term if total is None else total + term
     return total
 
 
-def conv_back(cols_ref, weight, width):
+def conv_back(cols_ref, weight_ref, width):
     total = None
     for tap in range(TAPS):
-        term = dot(tap_rows(cols_ref, tap, width), weight.tap(26 - tap), ((1,), (1,)))
+        weight = weight_ref[(26 - tap) * C : (27 - tap) * C, :]
+        term = dot(tap_rows(cols_ref, tap, width), weight, ((1,), (1,)))
         total = term if total is None else total + term
     return total
 
@@ -119,9 +126,8 @@
     return jnp.concatenate([column] * 4, axis=0) > 0.5 * NOWHERE
 
 
-def near_row(width, flip=0):
-    core = lax.axis_index("gx") % 2
-    return pl.multiple_of((1 - core if flip else core) * (3 * width), PLANE)
+def near_row(width):
+    return pl.multiple_of((lax.axis_index("gx") % 2) * (3 * width), PLANE)
 
 
 def side_offsets(sides):
@@ -130,7 +136,8 @@
     return [(1 - 2 * lax.axis_index("gy")).astype(jnp.float32) * (8 * STEP_Y)]
 
 
-def pack_kernel(features, cotangent, coords, counts, own_ref, face_ref, place_ref, live_ref, sems):
+def pack_kernel(features, cotangent, coords, counts, *refs):
+    own_ref, face_ref, thin_ref, cross_ref, place_ref, live_ref, sems = refs
     slots = features.shape[2]
     width = slots * PLANE
     copies = [
@@ -171,25 +178,17 @@
     face_ref[:width, :] = own_ref[pl.ds(at, width), :]
     face_ref[width : 2 * width, :] = own_ref[pl.ds(pl.multiple_of(4 * width + at, PLANE), width), :]
     face_ref[2 * width :, :] = meta
-
-
-def relay_kernel(*refs):
-    refs, relay_ref = refs[:-2], refs[-1]
-    at = 0
-    for ref in refs:
-        relay_ref[at : at + ref.shape[0], :] = ref[...]
-        at += ref.shape[0]
-
-
-def placed(j_refs, sides, rows):
-    width = rows // 8
-    tiles, fars = [], []
-    for (own, own_at), (relay, relay_at) in j_refs:
-        tiles.append([(own, own_at)])
-        tiles[-1] += [(relay, relay_at + s * (rows + META)) for s in range(sides)]
-        start = relay_at + sides * (rows + META)
-        fars.append([(relay, start + s * (2 * width + META)) for s in range(1 + sides)])
-    return tiles, fars
+    slim(own_ref, thin_ref, lax.axis_index("gy") % 2)
+    slim(own_ref, cross_ref, 1 - lax.axis_index("gy") % 2)
+
+
+def placed(relays, sides, rows):
+    face = rows // 4 + META
+    start = (1 + sides) * (rows + META)
+    return (
+        [[(relay, s * (rows + META), False) for s in range(1 + sides)] for relay in relays],
+        [[(relay, start + s * face) for s in range(1 + sides)] for relay in relays],
+    )
 
 
 class Around:
@@ -197,117 +196,109 @@
         self.tiles, self.fars, self.sides = tiles, fars, sides
         self.rows, self.width = rows, rows // 8
 
-    def tile(self, j, s):
-        return self.tiles[j][s]
-
-    def far(self, j, s):
-        return self.fars[j][s]
-
     def order(self, s):
         return [s] + [other for other in range(1 + self.sides) if other != s]
 
+    def odd(self, j):
+        return (lax.axis_index("gx") + j) % 2 == 1
+
     def codes(self, j, s):
-        def meta(source, start):
-            ref, first = source
-            return ref[first + start : first + start + 8, :]
+        def meta(ref, start):
+            return ref[start : start + 8, :]
+
+        def tile_meta(j, o):
+            ref, first, thin = self.tiles[j][o]
+            return meta(ref, first + (self.rows * 3 // 4 if thin else self.rows))
 
         order = self.order(s)
-        metas = [meta(self.tile(j, o), self.rows) for o in order]
+        metas = [tile_meta(j, o) for o in order]
+        offsets = side_offsets(self.sides)
+        offsets = [0.0] + ([-o for o in offsets] if s else offsets)
+        befores, afters = [], []
         for o in order:
-            metas.append(meta(self.tile(j ^ 1, o), self.rows))
-            metas.append(meta(self.far(j, o), 2 * self.width))
-        sign = (1 - 2 * (lax.axis_index("gx") % 2)).astype(jnp.float32) * (2 * STEP_X)
-        offsets = side_offsets(self.sides)
-        source = source_codes(
-            metas, -sign if j % 2 else sign, [-o for o in offsets] if s else offsets, self.width
+            near = tile_meta(j ^ 1, o)
+            ref, first = self.fars[j][o]
+            far = meta(ref, first + 2 * self.width)
+            befores.append(jnp.where(self.odd(j), near, far))
+            afters.append(jnp.where(self.odd(j), far, near))
+        before, after = (
+            source_codes(metas + beyond, offsets + [o + step for o in offsets], self.width)
+            for beyond, step in ((befores, -2 * STEP_X), (afters, 2 * STEP_X))
         )
-        return source, target_codes(metas[0], self.width)
+        return before, after, target_codes(metas[0], self.width)
 
     def sources(self, j, s, field):
-        top = field * 4 * self.width
-        at = near_row(self.width, j % 2)
+        def tile(j, o):
+            ref, first, thin = self.tiles[j][o]
+            return ref, first + field * 4 * self.width, thin and field == 1
+
         order = self.order(s)
-        tiles = [(ref, first + top) for ref, first in (self.tile(j, o) for o in order)]
         faces = []
         for o in order:
-            ref, first = self.tile(j ^ 1, o)
-            faces.append((ref, first + top + at))
-            ref, first = self.far(j, o)
-            faces.append((ref, first + field * self.width))
-        return tiles, faces
-
-
-class Weight:
-    def __init__(self, hbm_ref, ref, sems):
-        third = 9 * C
-        self.ref = ref
-        self.copies = [
-            pltpu.make_async_copy(
-                hbm_ref.at[pl.ds(i * third, third)], ref.at[pl.ds(i * third, third)], sems.at[i]
-            )
-            for i in range(3)
-        ]
-
-    def start(self, order=(0, 1, 2)):
-        for i in order:
-            self.copies[i].start()
-
-    def tap(self, tap):
-        if self.copies[tap // 9] is not None:
-            self.copies[tap // 9].wait()
-            self.copies[tap // 9] = None
-        return self.ref[tap * C : (tap + 1) * C, :]
+            ref, first = self.fars[j][o]
+            faces.append((tile(j ^ 1, o), (ref, first + field * self.width, False)))
+        return [tile(j, o) for o in order], faces, self.odd(j)
 
 
 def layer_kernel(sides, *refs):
-    own, relay, near, near_relay, first_hbm, second_hbm = refs[:6]
-    both_ref, slim_ref, face_ref, feature_cols, seed_cols, source_ref, target_ref = refs[6:13]
-    first_ref, second_ref, sems = refs[13:]
-    first = Weight(first_hbm, first_ref, sems.at[0])
-    second = Weight(second_hbm, second_ref, sems.at[1])
-    first.start()
-    second.start((2, 1, 0))
-    rows = own.shape[0] - META
+    relay, near_relay, first, second = refs[:4]
+    both_ref, slim_ref, cross_ref, feature_cols, seed_cols, source_ref, target_ref = refs[4:]
+    rows = both_ref.shape[0]
     width = rows // 8
-    pairs = [((own, 0), (relay, 0)), ((near, 0), (near_relay, 0))]
-    around = Around(*placed(pairs, sides, rows), sides, rows)
-    source, target = around.codes(0, 0)
-    source_ref[...] = source
+    around = Around(*placed([relay, near_relay], sides, rows), sides, rows)
+    before, after, target = around.codes(0, 0)
+    source_ref[0:1, :] = before
+    source_ref[1:2, :] = after
     target_ref[...] = target
-    chosen = selectors(source, target, sides, width)
+    chosen = selectors(before, after, target, sides, width)
     fill(feature_cols, *around.sources(0, 0, 0), chosen, width)
     fill(seed_cols, *around.sources(0, 0, 1), chosen, width)
     pre_first = conv(feature_cols, first, width)
-    live = live_rows(own[rows : rows + 8, :], width)
+    live = live_rows(relay[rows : rows + 8, :], width)
     sigmoid = 1.0 / (1.0 + jnp.exp(-pre_first))
     hidden = jnp.where(live, pre_first * sigmoid, 0.0)
     both_ref[: 4 * width, :] = hidden.astype(jnp.bfloat16)
     slope = jnp.where(live, sigmoid * (1.0 + pre_first * (1.0 - sigmoid)), 0.0)
     hidden_grad = conv_back(seed_cols, second, width)
     both_ref[4 * width :, :] = (hidden_grad * slope).astype(jnp.bfloat16)
-    store_face(both_ref, face_ref)
     if sides == 1:
-        slim(both_ref, slim_ref)
+        slim(both_ref, slim_ref, lax.axis_index("gy"))
+        slim(both_ref, cross_ref, 1 - lax.axis_index("gy"))
     else:
         slim_ref[...] = jnp.zeros(slim_ref.shape, slim_ref.dtype)
-
-
-def slim(both_ref, slim_ref):
-    rows = both_ref.shape[0] // 2
-    columns = my_columns(C // 2)
-    slim_ref[:rows, :] = both_ref[:rows, :]
-    slim_ref[rows:, : C // 2] = both_ref[rows : rows + rows // 2, columns]
-    slim_ref[rows:, C // 2 :] = both_ref[rows + rows // 2 :, columns]
-
-
-def gather_kernel(own_ref, relay_ref, both_ref, *refs):
-    packed_ref, slim_ref = refs[-2:]
-    packed_ref[: own_ref.shape[0], :] = own_ref[...]
-    packed_ref[own_ref.shape[0] :, :] = relay_ref[...]
-    slim(both_ref, slim_ref)
-
-
-def store_face(both_ref, face_ref):
+        cross_ref[...] = jnp.zeros(cross_ref.shape, cross_ref.dtype)
+
+
+def slim(tile_ref, slim_ref, half):
+    rows = tile_ref.shape[0] // (8 * PLANE) * 4 * PLANE
+    columns = pl.ds(pl.multiple_of(half * (C // 2), 128), C // 2)
+    slim_ref[:rows, :] = tile_ref[:rows, :]
+    slim_ref[rows : rows + rows // 2, : C // 2] = tile_ref[rows : rows + rows // 2, columns]
+    slim_ref[rows : rows + rows // 2, C // 2 :] = tile_ref[rows + rows // 2 : 2 * rows, columns]
+    if slim_ref.shape[0] > rows + rows // 2:
+        slim_ref[rows + rows // 2 :, :] = tile_ref[2 * rows :, :]
+
+
+def relay_kernel(count, *refs):
+    own_hbm, relay_ref, fars_ref, sem = refs[0], *refs[-3:]
+    size = own_hbm.shape[0]
+    copy = pltpu.make_async_copy(own_hbm, relay_ref.at[pl.ds(0, size)], sem)
+    copy.start()
+    gather_kernel(count - 1, *refs[1:count], relay_ref.at[pl.ds(size, relay_ref.shape[0] - size)])
+    gather_kernel(count // 2, *refs[count // 2 : count], fars_ref)
+    copy.wait()
+
+
+def gather_kernel(count, *refs):
+    packed_ref = refs[-1]
+    at = 0
+    for ref in refs[:count]:
+        packed_ref[at : at + ref.shape[0], :] = ref[...]
+        at += ref.shape[0]
+
+
+def face_kernel(both_ref, *refs):
+    face_ref = refs[-1]
     width = both_ref.shape[0] // 8
     at = near_row(width)
     face_ref[:width, :] = both_ref[pl.ds(at, width), :]
@@ -360,18 +351,18 @@
 OTHER_MEMBERS = ((2, 0), (2, 1), (3, 0), (3, 1))
 
 
-def chip_cols_kernel(own, relay, near, near_relay, feature_ref, seed_ref):
-    rows = own.shape[0] - META
-    pairs = [((own, 0), (relay, 0)), ((near, 0), (near_relay, 0))]
-    around = Around(*placed(pairs, 1, rows), 1, rows)
+def chip_cols_kernel(relay, near_relay, feature_ref, seed_ref):
+    rows = feature_ref.shape[2] // 6 * 8
+    around = Around(*placed([relay, near_relay], 1, rows), 1, rows)
     group_cols(around, CHIP_MEMBERS, feature_ref, seed_ref)
 
 
-def other_cols_kernel(packed, near_packed, feature_ref, seed_ref):
+def other_cols_kernel(packed, near_packed, _, feature_ref, seed_ref):
     width = feature_ref.shape[2] // 6
     rows = 8 * width
-    pairs = [((ref, 0), (ref, rows + META)) for ref in (packed, near_packed)]
-    tiles, fars = placed(pairs, 1, rows)
+    thin, face = 6 * width + META, 2 * width + META
+    tiles = [[(ref, s * thin, True) for s in range(2)] for ref in (packed, near_packed)]
+    fars = [[(ref, 2 * thin + s * face) for s in range(2)] for ref in (packed, near_packed)]
     around = Around([None, None] + tiles, [None, None] + fars, 1, rows)
     group_cols(around, OTHER_MEMBERS, feature_ref, seed_ref)
 
@@ -419,12 +410,16 @@
 
 
 def group_terms_kernel(*refs):
-    both, slims, refs = refs[:4], refs[4:8], refs[8:]
-    (feature_cols, seed_cols, *groups), refs = refs[:6], refs[6:]
+    both, thins, packed, refs = refs[:2], refs[2:4], refs[4], refs[5:]
+    (feature_cols, seed_cols, *groups), refs = refs[:6], refs[7:]
     out_refs, total_ref = refs[:-1], refs[-1]
     rows = both[0].shape[0] // 2
     chunk = out_refs[0].shape[0] // 2
     columns = my_columns(out_refs[0].shape[1])
+    thin_rows = thins[0].shape[0]
+    both = [(ref, 0) for ref in both]
+    both += [(packed, 2 * thin_rows), (packed, 2 * thin_rows + 2 * rows)]
+    thins = [(ref, 0) for ref in thins] + [(packed, 0), (packed, thin_rows)]
 
     def group(part, tile, shift, at):
         ref, index = (groups[part], tile - 1) if tile < 4 else (groups[2 + part], tile - 4)
@@ -436,11 +431,11 @@
     def features_of(tile, shift, at):
         return feature_cols[shift, at, :] if tile == 0 else group(0, tile, shift, at)
 
-    grads = [ref[rows:, columns] for ref in both]
-    grads += [
-        jnp.concatenate([ref[rows:, : C // 2], ref[rows:, C // 2 :]], axis=0) for ref in slims
-    ]
-    hiddens = [ref[:rows, :] for ref in (*both, *slims)]
+    grads = [ref[at + rows : at + 2 * rows, columns] for ref, at in both]
+    for ref, at in thins:
+        halves = ref[at + rows : at + rows + rows // 2, :]
+        grads.append(jnp.concatenate([halves[:, : C // 2], halves[:, C // 2 :]], axis=0))
+    hiddens = [ref[at : at + rows, :] for ref, at in (*both, *thins)]
     group_terms(features_of, grads, True, 0, out_refs, total_ref)
     group_terms(seeds_of, hiddens, False, chunk, out_refs, total_ref)
 
@@ -448,26 +443,27 @@
 def last_kernel(sides, *refs):
     own_ref, refs = refs[0], refs[1:]
     tiles, refs = refs[: 1 + sides], refs[1 + sides :]
-    nears, refs = refs[: 1 + sides], refs[1 + sides :]
+    count = 1 if sides == 1 else 1 + sides
+    nears, refs = refs[:count], refs[count:]
     fars, refs = refs[: 1 + sides], refs[1 + sides :]
-    first_hbm, second_hbm, source_ref, target_ref, _, output_ref, input_ref = refs[:7]
-    hidden_cols_ref, grad_cols_ref, first_ref, second_ref, sems = refs[7:]
-    first = Weight(first_hbm, first_ref, sems.at[0])
-    second = Weight(second_hbm, second_ref, sems.at[1])
-    second.start()
-    first.start((2, 1, 0))
+    first, second, source_ref, target_ref, _, output_ref, input_ref = refs[:7]
+    hidden_cols_ref, grad_cols_ref = refs[7:]
     width = tiles[0].shape[0] // 8
     slots = output_ref.shape[0]
-    chosen = selectors(source_ref[...], target_ref[...], sides, width)
+    chosen = selectors(source_ref[0:1, :], source_ref[1:2, :], target_ref[...], sides, width)
     live = live_rows(own_ref[8 * width : 8 * width + 8, :], width)
-    at = near_row(width)
-
-    def sources(field):
-        top = field * 4 * width
-        faces = []
-        for near, far in zip(nears, fars):
-            faces += [(near, top + at), (far, field * width)]
-        return [(ref, top) for ref in tiles], faces
+    rows = tiles[0].shape[0]
+    if sides == 1:
+        near_at = nears[0].shape[0] - 2 * rows
+        nears = [(nears[0], near_at, False), (nears[0], near_at + rows, False)]
+    else:
+        nears = [(ref, 0, False) for ref in nears]
+    around = Around(
+        [[(ref, 0, False) for ref in tiles], nears],
+        [[(ref, 0) for ref in fars]],
+        sides,
+        rows,
+    )
 
     def put(ref, total):
         total = jnp.where(live, total, 0.0)
@@ -476,8 +472,8 @@
                 start = x * width + slot * PLANE
                 ref[slot, x * PLANE : (x + 1) * PLANE, :] = total[start : start + PLANE]
 
-    fill(hidden_cols_ref, *sources(0), chosen, width)
-    fill(grad_cols_ref, *sources(1), chosen, width)
+    fill(hidden_cols_ref, *around.sources(0, 0, 0), chosen, width)
+    fill(grad_cols_ref, *around.sources(0, 0, 1), chosen, width)
     put(output_ref, conv(hidden_cols_ref, second, width))
     put(input_ref, conv_back(grad_cols_ref, first, width))
 
@@ -502,9 +498,19 @@
     return [lax.ppermute(cells, "gy", step) for step in side_steps(lax.axis_size("gy"))]
 
 
-def from_far(face):
-    far = lax.ppermute(face, "gx", far_steps(lax.axis_size("gx")))
-    return [far, *from_sides(far)]
+def across(face, gx_steps, gy_steps):
+    gy = lax.axis_size("gy")
+    return lax.ppermute(
+        face, ("gx", "gy"), [(a * gy + c, b * gy + d) for a, b in gx_steps for c, d in gy_steps]
+    )
+
+
+def from_far(face, late):
+    steps = far_steps(lax.axis_size("gx"))
+    far = lax.ppermute(face, "gx", steps)
+    if late:
+        return [far, *from_sides(far)]
+    return [far] + [across(face, steps, side) for side in side_steps(lax.axis_size("gy"))]
 
 
 def piece(cells, index, axis):
@@ -540,13 +546,18 @@
             name=name,
         )(*args)
 
-    own, face = call(
+    own, face, thin_own, cross_own = call(
         pack_kernel,
         "pack",
-        (shape((rows + META, C)), shape((2 * width + META, C))),
+        (
+            shape((rows + META, C)),
+            shape((2 * width + META, C)),
+            shape((6 * width + META, C)),
+            shape((6 * width + META, C)),
+        ),
         (features, cotangent, block_coords, block_counts),
         60,
-        0.1,
+        3,
         [
             pltpu.SMEM((1, slots), jnp.int32),
             pltpu.SMEM((1, 1), jnp.int32),
@@ -555,44 +566,56 @@
         [HBM] * 4,
     )
     side = from_sides(own)
-    fars = from_far(face)
-    near = swap(own, "gx", 1)
-    other = swap(own, "gx", 2) if grouped else own
-    parts = [*side, *fars]
-    (relay,) = call(
-        relay_kernel,
+    fars = from_far(face, False)
+    others = []
+    if grouped:
+        beside = [(i, i ^ 2) for i in range(gx)]
+        others = [swap(thin_own, "gx", 2), across(cross_own, beside, side_steps(gy)[0])]
+    parts = [own, *side, *fars]
+    relay, far_faces = call(
+        functools.partial(relay_kernel, len(parts)),
         "relay",
-        (shape((sum(cells.shape[0] for cells in parts), C)),),
-        (*parts, other),
+        (
+            shape((sum(cells.shape[0] for cells in parts), C)),
+            shape((sum(cells.shape[0] for cells in fars), C)),
+        ),
+        (*parts, *others),
         8,
-        0.1,
-        specs=[VMEM] * len(parts) + [ANY],
+        3,
+        [pltpu.SemaphoreType.DMA],
+        [ANY] + [VMEM] * (len(parts) - 1) + [ANY] * len(others),
     )
     near_relay = swap(relay, "gx", 1)
     columns = shape((9, 6 * width, C))
-    weights = [pltpu.VMEM(first_weight.shape, jnp.bfloat16)] * 2
-    weights.append(pltpu.SemaphoreType.DMA((2, 3)))
-    both, thin, late_face, feature_cols, seed_cols, source, target = call(
+    both, thin, cross, feature_cols, seed_cols, source, target = call(
         functools.partial(layer_kernel, sides),
         "layer",
         (
             shape((rows, C)),
             shape((6 * width, C)),
-            shape((2 * width, C)),
+            shape((6 * width, C)),
             columns,
             columns,
-            shape((1, LANES), jnp.float32),
+            shape((2, LANES), jnp.float32),
             shape((9 * width, 1), jnp.float32),
         ),
-        (own, relay, near, near_relay, first_weight, second_weight),
-        58,
+        (relay, near_relay, first_weight, second_weight),
+        12,
         4,
-        weights,
-        [VMEM] * 4 + [HBM] * 2,
-    )
-    late_fars = from_far(late_face)
+    )
     both_side = from_sides(both)
-    both_near = [swap(cells, "gx", 1) for cells in [both] + both_side]
+
+    def faced(*after):
+        return call(
+            face_kernel,
+            "face",
+            (shape((2 * width, C)),),
+            (both, *after),
+            8,
+            0.3,
+            specs=[VMEM] + [ANY] * len(after),
+        )[0]
+
     grad_scale = 1.0 / math.sqrt(64 * slots * gx * gy)
 
     def over_z(own_part, sent):
@@ -601,40 +624,46 @@
 
     if grouped:
         cols = C // 2
-        far_relay = swap(relay, "gx", 2)
+
+        def gathered(name, cells, after):
+            return call(
+                functools.partial(gather_kernel, len(cells)),
+                name,
+                (shape((sum(part.shape[0] for part in cells), C)),),
+                (*cells, *after),
+                8,
+                0.5,
+                specs=[VMEM] * len(cells) + [ANY] * len(after),
+            )[0]
 
         def group_shapes(count):
             return shape((count, *columns.shape)), shape((count, *columns.shape[:2], cols))
 
+        early = gathered("gather_early", (*others, swap(far_faces, "gx", 2)), (both,))
+        near_early = swap(early, "gx", 1)
         chip_features, chip_seeds = call(
-            chip_cols_kernel,
-            "chip_cols",
-            group_shapes(len(CHIP_MEMBERS)),
-            (own, relay, near, near_relay),
-            8,
-            3,
+            chip_cols_kernel, "chip_cols", group_shapes(len(CHIP_MEMBERS)), (relay, near_relay), 8, 2.5
         )
-        packed, side_thin = call(
-            gather_kernel,
-            "gather",
-            (shape((own.shape[0] + relay.shape[0], C)), shape(thin.shape)),
-            (other, far_relay, both_side[0], chip_seeds, late_fars[0]),
-            8,
-            0.5,
-            specs=[VMEM] * 3 + [ANY] * 2,
+        late_fars = from_far(faced(chip_seeds), True)
+        thin_other = swap(thin, "gx", 2)
+        cross_other = across(cross, beside, side_steps(gy)[0])
+        packed = gathered(
+            "gather_late",
+            (thin_other, cross_other, both, both_side[0]),
+            (chip_seeds, late_fars[0]),
         )
         near_packed = swap(packed, "gx", 1)
+        nears = [near_packed]
         other_features, other_seeds = call(
             other_cols_kernel,
             "other_cols",
             group_shapes(len(OTHER_MEMBERS)),
-            (packed, near_packed),
+            (early, near_early, packed),
             8,
-            4,
+            3,
+            specs=[VMEM] * 2 + [ANY],
         )
-        others = [swap(cells, "gx", 2) for cells in (thin, side_thin)]
-        others += [swap(cells, "gx", 1) for cells in others]
-        members = [both, both_side[0], *both_near, *others]
+        members = [both, both_side[0], thin_other, cross_other, near_packed]
         taps = 2 + (chunk - 2) // C
         own_part, *sent = call(
             group_terms_kernel,
@@ -651,15 +680,19 @@
                 chip_seeds,
                 other_features,
                 other_seeds,
+                late_fars[0],
             ),
             12,
             3.5,
             [pltpu.VMEM((deeps, taps * C, cols), jnp.float32)],
+            [VMEM] * (len(members) + 6) + [ANY],
         )
         token = sent[0]
         grads = over_z(own_part, sent)
         first_grad, second_grad = grads[:chunk], grads[chunk:]
     else:
+        nears = [swap(cells, "gx", 1) for cells in (both, *both_side)]
+        late_fars = from_far(faced(), True)
 
         def summed(kernel, name, cells):
             keep, send = call(
@@ -697,17 +730,17 @@
         second_grad, token = summed(second_terms_kernel, "second_terms", seed_cols)
         first_grad, _ = summed(first_terms_kernel, "first_terms", feature_cols)
 
-    late = [own, both, *both_side, *both_near, *late_fars]
+    late = [own, both, *both_side, *nears, *late_fars]
     result = shape((slots, 64, C), jnp.float32)
     output, input_grad = call(
         functools.partial(last_kernel, sides),
         "last_layer",
         (result, result),
         (*late, first_weight, second_weight, source, target, token),
-        58,
+        12,
         0.1,
-        [pltpu.VMEM(columns.shape, jnp.bfloat16)] * 2 + weights,
-        [VMEM] * len(late) + [HBM, HBM, VMEM, VMEM, ANY],
+        [pltpu.VMEM(columns.shape, jnp.bfloat16)] * 2,
+        [VMEM] * (len(late) + 4) + [ANY],
     )
     return (
         output.reshape(features.shape),

time: 79.3 us -> 66.9 us (0.84)
  Pallas kernels: 26.5 us -> 17.3 us
  starting transfers between devices: 17.9 us -> 26.8 us
  waiting for transfers between devices: 27 us -> 19.3 us
  local copies, waits for them, and re-layouts: 5.7 us -> 1.73 us
    pallas_call x8 -> x10, Pallas kernels: 26.5 us -> 17.3 us  [call(): pl.pallas_call(kernel, out_shape=outs, in_specs=specs or [VMEM] * len(arg...]
    ppermute x2 -> x5, starting transfers between devices: 4.13 us -> 11.2 us  [the longest x3 6.27 us: across(): lax.ppermute(face, ('gx', 'gy'), [(a * gy + c, b * gy + d) for a, b in gx...]
    unnamed x34 -> x8, local copies, waits for them, and re-layouts: 4.91 us -> 0.94 us
    ppermute x14 -> x9, waiting for transfers between devices: 16 us -> 12.1 us  [swap(): lax.ppermute(cells, axis, [(i, i ^ bit) for i in range(lax.axis_size(axis...]
    ppermute x4 -> x3, waiting for transfers between devices: 6.25 us -> 2.57 us  [from_sides(): lax.ppermute(cells, 'gy', step)]
    ppermute x14 -> x9, starting transfers between devices: 9.64 us -> 10.9 us  [swap(): lax.ppermute(cells, axis, [(i, i ^ bit) for i in range(lax.axis_size(axis...]
    ppermute x4 -> x3, starting transfers between devices: 4.11 us -> 4.7 us  [from_sides(): lax.ppermute(cells, 'gy', step)]
    ppermute x2 -> x5, waiting for transfers between devices: 4.68 us -> 4.56 us  [the longest x2 2.44 us: from_far(): far = lax.ppermute(face, 'gx', steps)]
  transfers between devices with their start and end apart: 20 -> 17, of which waited for: 8 -> 5; matrix products, arithmetic and copies ran while one was open for 0% -> 0% of each run, Pallas kernels for 28% -> 18%
where the time goes in v4:
time: 66.9 us; the launch traced here: 66.7 us
  starting transfers between devices  26.8 us (40%)
  waiting for transfers between devices  19.3 us (29%)
  Pallas kernels  17.3 us (26%)
  local copies, waits for them, and re-layouts  1.73 us (3%)
  between operations  1.45 us (2%)
    pallas_call x10, Pallas kernels, call(): pl.pallas_call(kernel, out_shape=outs, in_specs=specs or [VMEM] * len(arg...  17.3 us
    ppermute x9, waiting for transfers between devices, swap(): lax.ppermute(cells, axis, [(i, i ^ bit) for i in range(lax.axis_size(axis...  12.1 us
    ppermute x9, starting transfers between devices, swap(): lax.ppermute(cells, axis, [(i, i ^ bit) for i in range(lax.axis_size(axis...  10.9 us
    ppermute x3, starting transfers between devices, across(): lax.ppermute(face, ('gx', 'gy'), [(a * gy + c, b * gy + d) for a, b in gx...  6.27 us
    ppermute x2, starting transfers between devices, from_far(): far = lax.ppermute(face, 'gx', steps)  4.94 us
    ppermute x3, starting transfers between devices, from_sides(): lax.ppermute(cells, 'gy', step)  4.7 us
    ppermute x3, waiting for transfers between devices, from_sides(): lax.ppermute(cells, 'gy', step)  2.57 us
    ppermute x2, waiting for transfers between devices, from_far(): far = lax.ppermute(face, 'gx', steps)  2.44 us
  transfers between devices with their start and end apart: 17, of which 5 were waited for; matrix products, arithmetic and copies ran while one was open for 0% of the time, Pallas kernels for 18%

profile of v4, /device:TPU:8, one launch (start us, length us, event | category | flops | bytes accessed | tf_op | source)
XLA Modules:
  0.0 66.7 jit_solution(5210988423877348365)
XLA Ops:
  1.3 2.0 %pack.1 = (bf16[400,256]{1,0:T(8,128)(2,1)}, bf16[112,256]{1,0:T(8,128)(2,1)}, bf16[304,256]{1,0:T(8,128)(2,1)}, bf16[304,256]{1,0:T(8,128)(2,1)}) custom-call(bf16[1,1,3,64,256]{4,3,2,1,0:T(8,128)(2,1)} %features.1, bf16[1,1,3,64,256]{4,3,2,1,0:T(8,128)(2,1)} %cotangent.1, s32[1,1,3]{2,1,0:T(1,128)} %coords.1, s32[1,1]{1,0:T(1,128)S(6)} %copy.10.counts), custom_call_target="tpu_custom_call" | custom-call | flops 3300000000 | bytes 1048576 | tf_op jit(solution)/shard_map/pack/pallas_call | solution.py:536
  3.3 1.6 %collective-permute-start = (bf16[400,256]{1,0:T(8,128)(2,1)}, bf16[400,256]{1,0:T(8,128)(2,1)S(1)}, u32[]{:S(2)}, u32[]{:S(2)}) collective-permute-start(bf16[400,256]{1,0:T(8,128)(2,1)} %get-tuple-element.27.refs_0_), channel_id=1, source_target_pairs={{0,1},{1,0},{2,3},{3,2},{4,5},{5,4},{6,7},{7,6},{8,9},{9,8},{10,11... | collective-permute-start | bytes 614408 | tf_op jit(solution)/shard_map/ppermute | solution.py:498
  4.9 1.5 %collective-permute-start.3 = (bf16[304,256]{1,0:T(8,128)(2,1)}, bf16[304,256]{1,0:T(8,128)(2,1)S(1)}, u32[]{:S(2)}, u32[]{:S(2)}) collective-permute-start(bf16[304,256]{1,0:T(8,128)(2,1)} %get-tuple-element.29), channel_id=1, source_target_pairs={{0,4},{2,6},{4,0},{6,2},{8,12},{10,14},{12,8},{14,10},{16,20},{18,... | collective-permute-start | bytes 466952 | tf_op jit(solution)/shard_map/ppermute | solution.py:482
  6.4 0.5 collective-permute-start.4
  6.8 2.3 %collective-permute-start.1 = (bf16[112,256]{1,0:T(8,128)(2,1)}, bf16[112,256]{1,0:T(8,128)(2,1)S(1)}, u32[]{:S(2)}, u32[]{:S(2)}) collective-permute-start(bf16[112,256]{1,0:T(8,128)(2,1)} %get-tuple-element.28), channel_id=1, source_target_pairs={{2,4},{6,8},{10,12},{14,16},{18,20},{22,24},{26,28},{4,2},{8,6},{1... | collective-permute-start | bytes 172040 | tf_op jit(solution)/shard_map/ppermute | solution.py:510
  9.1 5.4 %collective-permute-start.2 = (bf16[112,256]{1,0:T(8,128)(2,1)}, bf16[112,256]{1,0:T(8,128)(2,1)S(1)}, u32[]{:S(2)}, u32[]{:S(2)}) collective-permute-start(bf16[112,256]{1,0:T(8,128)(2,1)} %get-tuple-element.28), channel_id=1, source_target_pairs={{2,5},{3,4},{6,9},{7,8},{10,13},{11,12},{14,17},{15,16},{18,21},{1... | collective-permute-start | bytes 172040 | tf_op jit(solution)/shard_map/ppermute | solution.py:503
  14.5 0.0 collective-permute-done.1.refs_2_
  14.5 2.1 %collective-permute-done.2.refs_3_ = bf16[112,256]{1,0:T(8,128)(2,1)S(1)} collective-permute-done((bf16[112,256]{1,0:T(8,128)(2,1)}, bf16[112,256]{1,0:T(8,128)(2,1)S(1)}, u32[]{:S(2)}, u32[]{:S(2)}) %collective-permute-start.2) | collective-permute-done | bytes 57376 | tf_op jit(solution)/shard_map/ppermute | solution.py:503
  16.6 0.0 collective-permute-done.3.refs_4_.refs_0_
  16.7 0.0 collective-permute-done.4.refs_5_.refs_1_
  16.7 0.0 collective-permute-done.refs_1_
  16.7 0.0 copy-start.2
  16.7 0.9 %copy-done.2 = bf16[400,256]{1,0:T(8,128)(2,1)S(1)} copy-done((bf16[400,256]{1,0:T(8,128)(2,1)S(1)}, bf16[400,256]{1,0:T(8,128)(2,1)}, u32[]{:S(2)}) %copy-start.2) | copy-done | bytes 204824
  17.6 0.3 relay.1
  17.9 0.6 collective-permute-start.5
  18.5 2.4 %collective-permute-start.12 = (bf16[224,256]{1,0:T(8,128)(2,1)S(1)}, bf16[224,256]{1,0:T(8,128)(2,1)S(1)}, u32[]{:S(2)}, u32[]{:S(2)}) collective-permute-start(bf16[224,256]{1,0:T(8,128)(2,1)S(1)} %get-tuple-element.41), channel_id=1, source_target_pairs={{0,4},{2,6},{4,0},{6,2},{8,12},{10,14},{12,8},{14,10},{16,20},{18,... | collective-permute-start | bytes 344072 | tf_op jit(solution)/shard_map/ppermute | solution.py:482
  20.9 0.0 collective-permute-done.5.refs_1_.near_relay
  21.0 0.0 copy-done
  21.0 0.0 copy-done.1
  21.0 3.0 %layer.1 = (bf16[384,256]{1,0:T(8,128)(2,1)S(1)}, bf16[288,256]{1,0:T(8,128)(2,1)S(1)}, bf16[288,256]{1,0:T(8,128)(2,1)S(1)}, bf16[9,288,256]{2,1,0:T(8,128)(2,1...) custom-call(bf16[1024,256]{1,0:T(8,128)(2,1)S(1)} %get-tuple-element.31.refs_0_.relay, ...), custom_call_target="tpu_custom_call" | custom-call | flops 4400000000 | bytes 1048576 | tf_op jit(solution)/shard_map/layer/pallas_call | solution.py:536
  24.0 1.6 %collective-permute-start.6 = (bf16[384,256]{1,0:T(8,128)(2,1)S(1)}, bf16[384,256]{1,0:T(8,128)(2,1)S(1)}, u32[]{:S(2)}, u32[]{:S(2)}) collective-permute-start(bf16[384,256]{1,0:T(8,128)(2,1)S(1)} %get-tuple-element.32.both_ref.refs_2_.refs_3_.refs_0_.refs_1_), channel_id=1, source_target_pairs={{0,1},{1,0},{2,3},{3,2},{4,5},{5,4},{6,7},{7,6},{8,9},{9,8},{10,11... | collective-permute-start | bytes 589832 | tf_op jit(solution)/shard_map/ppermute | solution.py:498
  25.6 1.5 %collective-permute-start.7 = (bf16[288,256]{1,0:T(8,128)(2,1)S(1)}, bf16[288,256]{1,0:T(8,128)(2,1)S(1)}, u32[]{:S(2)}, u32[]{:S(2)}) collective-permute-start(bf16[288,256]{1,0:T(8,128)(2,1)S(1)} %get-tuple-element.33), channel_id=1, source_target_pairs={{0,4},{2,6},{4,0},{6,2},{8,12},{10,14},{12,8},{14,10},{16,20},{18,... | collective-permute-start | bytes 442376 | tf_op jit(solution)/shard_map/ppermute | solution.py:482
  27.1 0.4 collective-permute-start.8
  27.5 2.4 %chip_cols.1 = (bf16[3,9,288,256]{3,2,1,0:T(8,128)(2,1)S(1)}, bf16[3,9,288,128]{3,2,1,0:T(8,128)(2,1)S(1)}) custom-call(bf16[1024,256]{1,0:T(8,128)(2,1)S(1)} %get-tuple-element.31.refs_0_.relay, bf16[1024,256]{1,0:T(8,128)(2,1)S(1)} %collective-permute-done.5.refs_1_.near_relay), custom_call_target="tpu_custom_call" | custom-call | flops 2750000128 | bytes 1048576 | tf_op jit(solution)/shard_map/chip_cols/pallas_call | solution.py:536
  29.9 2.6 %collective-permute-start.9 = (bf16[96,256]{1,0:T(8,128)(2,1)S(1)}, bf16[96,256]{1,0:T(8,128)(2,1)S(1)}, u32[]{:S(2)}, u32[]{:S(2)}) collective-permute-start(bf16[96,256]{1,0:T(8,128)(2,1)S(1)} %face.1), channel_id=1, source_target_pairs={{2,4},{6,8},{10,12},{14,16},{18,20},{22,24},{26,28},{4,2},{8,6},{1... | collective-permute-start | bytes 147464 | tf_op jit(solution)/shard_map/ppermute | solution.py:510
  32.6 0.0 collective-permute-done.12.refs_2_
  32.6 1.2 %collective-permute-start.13 = (bf16[832,256]{1,0:T(8,128)(2,1)S(1)}, bf16[832,256]{1,0:T(8,128)(2,1)S(1)}, u32[]{:S(2)}, u32[]{:S(2)}) collective-permute-start(bf16[832,256]{1,0:T(8,128)(2,1)S(1)} %gather_early.1.packed), channel_id=1, source_target_pairs={{0,2},{2,0},{4,6},{6,4},{8,10},{10,8},{12,14},{14,12},{16,18},{18,... | collective-permute-start | bytes 1277960 | tf_op jit(solution)/shard_map/ppermute | solution.py:482
  33.8 2.4 %collective-permute-done.9.refs_5_.refs_11_.refs_4_ = bf16[96,256]{1,0:T(8,128)(2,1)S(1)} collective-permute-done((bf16[96,256]{1,0:T(8,128)(2,1)S(1)}, bf16[96,256]{1,0:T(8,128)(2,1)S(1)}, u32[]{:S(2)}, u32[]{:S(2)}) %collective-permute-start.9) | collective-permute-done | bytes 49184 | tf_op jit(solution)/shard_map/ppermute | solution.py:510
  36.2 0.0 collective-permute-done.7.refs_0_.refs_2_
  36.2 0.0 collective-permute-done.8.refs_1_.refs_3_
  36.2 0.0 collective-permute-done.6.refs_3_.refs_1_.refs_2_
  36.3 0.1 collective-permute-start.10
  36.4 0.0 collective-permute-done.13.near_packed
  36.4 3.1 %other_cols.1 = (bf16[4,9,288,256]{3,2,1,0:T(8,128)(2,1)S(1)}, bf16[4,9,288,128]{3,2,1,0:T(8,128)(2,1)S(1)}) custom-call(bf16[832,256]{1,0:T(8,128)(2,1)S(1)} %gather_early.1.packed, bf16[832,256]{1,0:T(8,128)(2,1)S(1)} %collective-permute-done.13.near_packed, bf16[1344,256]{1,0:T(8,128)(2,1)S(1)} %gather_late.1._), custom_call_target="tpu_custom_call" | custom-call | flops 3300000000 | bytes 1048576 | tf_op jit(solution)/shard_map/other_cols/pallas_call | solution.py:536
  39.5 0.0 collective-permute-done.10.refs_4_.refs_3_
  39.5 0.0 copy-start.3
  39.5 2.9 %group_terms.1 = (f32[864,128]{1,0:T(8,128)S(1)}, bf16[864,128]{1,0:T(8,128)(2,1)S(1)}, bf16[864,128]{1,0:T(8,128)(2,1)S(1)}, bf16[864,128]{1,0:T(8,128)(2,1)S(1)}) custom-call(bf16[384,256]{1,0:T(8,128)(2,1)S(1)} %get-tuple-element.32.both_ref.refs_2_.refs_3_.refs_0_.refs_1_, bf16[384,256]{1,0:T(8,128)(2,1)S(1)} %collective-permute-done.6.refs_3_.refs_1_.refs_2_, ...), custom_call_target="tpu_custom_call" | custom-call | flops 3849999872 | bytes 1048576 | tf_op jit(solution)/shard_map/group_terms/pallas_call | solution.py:536
  42.4 0.1 collective-permute-start.14
  42.5 3.0 %collective-permute-start.15 = (bf16[864,128]{1,0:T(8,128)(2,1)S(1)}, bf16[864,128]{1,0:T(8,128)(2,1)S(1)}, u32[]{:S(2)}, u32[]{:S(2)}) collective-permute-start(bf16[864,128]{1,0:T(8,128)(2,1)S(1)} %get-tuple-element.48), channel_id=1, source_target_pairs={{0,16},{2,18},{4,20},{6,22},{8,24},{10,26},{12,28},{14,30},{16,0},... | collective-permute-start | bytes 663560 | tf_op jit(solution)/shard_map/ppermute | solution.py:482
  45.5 0.5 collective-permute-start.16
  46.0 1.5 %collective-permute-start.11 = (bf16[96,256]{1,0:T(8,128)(2,1)S(1)}, bf16[96,256]{1,0:T(8,128)(2,1)S(1)}, u32[]{:S(2)}, u32[]{:S(2)}) collective-permute-start(bf16[96,256]{1,0:T(8,128)(2,1)S(1)} %collective-permute-done.9.refs_5_.refs_11_.refs_4_), channel_id=1, source_target_pairs={{0,1},{1,0},{2,3},{3,2},{4,5},{5,4},{6,7},{7,6},{8,9},{9,8},{10,11... | collective-permute-start | bytes 147464 | tf_op jit(solution)/shard_map/ppermute | solution.py:498
  47.5 2.6 %collective-permute-done.11.refs_5_ = bf16[96,256]{1,0:T(8,128)(2,1)S(1)} collective-permute-done((bf16[96,256]{1,0:T(8,128)(2,1)S(1)}, bf16[96,256]{1,0:T(8,128)(2,1)S(1)}, u32[]{:S(2)}, u32[]{:S(2)}) %collective-permute-start.11) | collective-permute-done | bytes 49184 | tf_op jit(solution)/shard_map/ppermute | solution.py:498
  50.1 3.6 %last_layer.1 = (f32[3,64,256]{2,1,0:T(8,128)}, f32[3,64,256]{2,1,0:T(8,128)}) custom-call(bf16[400,256]{1,0:T(8,128)(2,1)S(1)} %copy-done.3, bf16[384,256]{1,0:T(8,128)(2,1)S(1)} %get-tuple-element.32.both_ref.refs_2_.refs_3_.refs_0_.refs_1_, bf16[384,256]{1,0:T(8,128)(2,1)S(1)} %collective-permute-done.6.refs_3_.refs_1_.refs_2_, ...), custom_call_target="tpu_custom_call" | custom-call | flops 110000000 | bytes 1048576 | tf_op jit(solution)/shard_map/last_layer/pallas_call | solution.py:536
  53.6 0.0 collective-permute-done.14
  53.6 7.2 %collective-permute-done.15 = bf16[864,128]{1,0:T(8,128)(2,1)S(1)} collective-permute-done((bf16[864,128]{1,0:T(8,128)(2,1)S(1)}, bf16[864,128]{1,0:T(8,128)(2,1)S(1)}, u32[]{:S(2)}, u32[]{:S(2)}) %collective-permute-start.15) | collective-permute-done | bytes 221216 | tf_op jit(solution)/shard_map/ppermute | solution.py:482
  60.8 5.0 %collective-permute-done.16 = bf16[864,128]{1,0:T(8,128)(2,1)S(1)} collective-permute-done((bf16[864,128]{1,0:T(8,128)(2,1)S(1)}, bf16[864,128]{1,0:T(8,128)(2,1)S(1)}, u32[]{:S(2)}, u32[]{:S(2)}) %collective-permute-start.16) | collective-permute-done | bytes 221216 | tf_op jit(solution)/shard_map/ppermute | solution.py:482
  65.8 0.1 add_multiply_fusion
  65.9 0.8 %fusion = (f32[432,128]{1,0:T(8,128)}, f32[432,128]{1,0:T(8,128)}) fusion(f32[864,128]{1,0:T(8,128)S(1)} %add_multiply_fusion), kind=kLoop, calls=%fused_computation.1 | loop fusion | bytes 884736 | tf_op jit(solution)/shard_map/slice | solution.py:692
  (6 shorter events, 0.1 us)
Async XLA Ops:
  3.3 13.4 %collective-permute-start = (bf16[400,256]{1,0:T(8,128)(2,1)}, bf16[400,256]{1,0:T(8,128)(2,1)S(1)}, u32[]{:S(2)}, u32[]{:S(2)}) collective-permute-start(bf16[400,256]{1,0:T(8,128)(2,1)} %get-tuple-element.27.refs_0_), channel_id=1, source_target_pairs={{0,1},{1,0},{2,3},{3,2},{4,5},{5,4},{6,7},{7,6},{8,9},{9,8},{10,11... | collective-permute-start | bytes 614408 | tf_op jit(solution)/shard_map/ppermute | solution.py:498
  4.9 11.8 %collective-permute-start.3 = (bf16[304,256]{1,0:T(8,128)(2,1)}, bf16[304,256]{1,0:T(8,128)(2,1)S(1)}, u32[]{:S(2)}, u32[]{:S(2)}) collective-permute-start(bf16[304,256]{1,0:T(8,128)(2,1)} %get-tuple-element.29), channel_id=1, source_target_pairs={{0,4},{2,6},{4,0},{6,2},{8,12},{10,14},{12,8},{14,10},{16,20},{18,... | collective-permute-start | bytes 466952 | tf_op jit(solution)/shard_map/ppermute | solution.py:482
  6.4 10.3 %collective-permute-start.4 = (bf16[304,256]{1,0:T(8,128)(2,1)}, bf16[304,256]{1,0:T(8,128)(2,1)S(1)}, u32[]{:S(2)}, u32[]{:S(2)}) collective-permute-start(bf16[304,256]{1,0:T(8,128)(2,1)} %get-tuple-element.30), channel_id=1, source_target_pairs={{0,5},{1,4},{2,7},{3,6},{4,1},{5,0},{6,3},{7,2},{8,13},{9,12},{10,... | collective-permute-start | bytes 466952 | tf_op jit(solution)/shard_map/ppermute | solution.py:503
  6.8 14.1 %copy-start = (bf16[6912,256]{1,0:T(8,128)(2,1)S(1)}, bf16[6912,256]{1,0:T(8,128)(2,1)}, u32[]{:S(2)}) copy-start(bf16[6912,256]{1,0:T(8,128)(2,1)} %refs_6_.1) | copy-start | bytes 10616836
  6.8 14.1 %copy-start.1 = (bf16[6912,256]{1,0:T(8,128)(2,1)S(1)}, bf16[6912,256]{1,0:T(8,128)(2,1)}, u32[]{:S(2)}) copy-start(bf16[6912,256]{1,0:T(8,128)(2,1)} %refs_7_.1) | copy-start | bytes 10616836
  6.8 7.7 %collective-permute-start.1 = (bf16[112,256]{1,0:T(8,128)(2,1)}, bf16[112,256]{1,0:T(8,128)(2,1)S(1)}, u32[]{:S(2)}, u32[]{:S(2)}) collective-permute-start(bf16[112,256]{1,0:T(8,128)(2,1)} %get-tuple-element.28), channel_id=1, source_target_pairs={{2,4},{6,8},{10,12},{14,16},{18,20},{22,24},{26,28},{4,2},{8,6},{1... | collective-permute-start | bytes 172040 | tf_op jit(solution)/shard_map/ppermute | solution.py:510
  9.1 7.5 %collective-permute-start.2 = (bf16[112,256]{1,0:T(8,128)(2,1)}, bf16[112,256]{1,0:T(8,128)(2,1)S(1)}, u32[]{:S(2)}, u32[]{:S(2)}) collective-permute-start(bf16[112,256]{1,0:T(8,128)(2,1)} %get-tuple-element.28), channel_id=1, source_target_pairs={{2,5},{3,4},{6,9},{7,8},{10,13},{11,12},{14,17},{15,16},{18,21},{1... | collective-permute-start | bytes 172040 | tf_op jit(solution)/shard_map/ppermute | solution.py:503
  16.7 0.9 %copy-start.2 = (bf16[400,256]{1,0:T(8,128)(2,1)S(1)}, bf16[400,256]{1,0:T(8,128)(2,1)}, u32[]{:S(2)}) copy-start(bf16[400,256]{1,0:T(8,128)(2,1)} %get-tuple-element.27.refs_0_) | copy-start | bytes 614404
  17.9 3.1 %collective-permute-start.5 = (bf16[1024,256]{1,0:T(8,128)(2,1)S(1)}, bf16[1024,256]{1,0:T(8,128)(2,1)S(1)}, u32[]{:S(2)}, u32[]{:S(2)}) collective-permute-start(bf16[1024,256]{1,0:T(8,128)(2,1)S(1)} %get-tuple-element.31.refs_0_.relay), channel_id=1, source_target_pairs={{0,2},{2,0},{4,6},{6,4},{8,10},{10,8},{12,14},{14,12},{16,18},{18,... | collective-permute-start | bytes 1572872 | tf_op jit(solution)/shard_map/ppermute | solution.py:482
  18.5 14.1 %collective-permute-start.12 = (bf16[224,256]{1,0:T(8,128)(2,1)S(1)}, bf16[224,256]{1,0:T(8,128)(2,1)S(1)}, u32[]{:S(2)}, u32[]{:S(2)}) collective-permute-start(bf16[224,256]{1,0:T(8,128)(2,1)S(1)} %get-tuple-element.41), channel_id=1, source_target_pairs={{0,4},{2,6},{4,0},{6,2},{8,12},{10,14},{12,8},{14,10},{16,20},{18,... | collective-permute-start | bytes 344072 | tf_op jit(solution)/shard_map/ppermute | solution.py:482
  24.0 12.3 %collective-permute-start.6 = (bf16[384,256]{1,0:T(8,128)(2,1)S(1)}, bf16[384,256]{1,0:T(8,128)(2,1)S(1)}, u32[]{:S(2)}, u32[]{:S(2)}) collective-permute-start(bf16[384,256]{1,0:T(8,128)(2,1)S(1)} %get-tuple-element.32.both_ref.refs_2_.refs_3_.refs_0_.refs_1_), channel_id=1, source_target_pairs={{0,1},{1,0},{2,3},{3,2},{4,5},{5,4},{6,7},{7,6},{8,9},{9,8},{10,11... | collective-permute-start | bytes 589832 | tf_op jit(solution)/shard_map/ppermute | solution.py:498
  25.6 10.7 %collective-permute-start.7 = (bf16[288,256]{1,0:T(8,128)(2,1)S(1)}, bf16[288,256]{1,0:T(8,128)(2,1)S(1)}, u32[]{:S(2)}, u32[]{:S(2)}) collective-permute-start(bf16[288,256]{1,0:T(8,128)(2,1)S(1)} %get-tuple-element.33), channel_id=1, source_target_pairs={{0,4},{2,6},{4,0},{6,2},{8,12},{10,14},{12,8},{14,10},{16,20},{18,... | collective-permute-start | bytes 442376 | tf_op jit(solution)/shard_map/ppermute | solution.py:482
  27.1 9.1 %collective-permute-start.8 = (bf16[288,256]{1,0:T(8,128)(2,1)S(1)}, bf16[288,256]{1,0:T(8,128)(2,1)S(1)}, u32[]{:S(2)}, u32[]{:S(2)}) collective-permute-start(bf16[288,256]{1,0:T(8,128)(2,1)S(1)} %get-tuple-element.34), channel_id=1, source_target_pairs={{0,5},{1,4},{2,7},{3,6},{4,1},{5,0},{6,3},{7,2},{8,13},{9,12},{10,... | collective-permute-start | bytes 442376 | tf_op jit(solution)/shard_map/ppermute | solution.py:503
  29.9 6.3 %collective-permute-start.9 = (bf16[96,256]{1,0:T(8,128)(2,1)S(1)}, bf16[96,256]{1,0:T(8,128)(2,1)S(1)}, u32[]{:S(2)}, u32[]{:S(2)}) collective-permute-start(bf16[96,256]{1,0:T(8,128)(2,1)S(1)} %face.1), channel_id=1, source_target_pairs={{2,4},{6,8},{10,12},{14,16},{18,20},{22,24},{26,28},{4,2},{8,6},{1... | collective-permute-start | bytes 147464 | tf_op jit(solution)/shard_map/ppermute | solution.py:510
  32.6 3.8 %collective-permute-start.13 = (bf16[832,256]{1,0:T(8,128)(2,1)S(1)}, bf16[832,256]{1,0:T(8,128)(2,1)S(1)}, u32[]{:S(2)}, u32[]{:S(2)}) collective-permute-start(bf16[832,256]{1,0:T(8,128)(2,1)S(1)} %gather_early.1.packed), channel_id=1, source_target_pairs={{0,2},{2,0},{4,6},{6,4},{8,10},{10,8},{12,14},{14,12},{16,18},{18,... | collective-permute-start | bytes 1277960 | tf_op jit(solution)/shard_map/ppermute | solution.py:482
  36.3 3.2 %collective-permute-start.10 = (bf16[1344,256]{1,0:T(8,128)(2,1)S(1)}, bf16[1344,256]{1,0:T(8,128)(2,1)S(1)}, u32[]{:S(2)}, u32[]{:S(2)}) collective-permute-start(bf16[1344,256]{1,0:T(8,128)(2,1)S(1)} %gather_late.1._), channel_id=1, source_target_pairs={{0,2},{2,0},{4,6},{6,4},{8,10},{10,8},{12,14},{14,12},{16,18},{18,... | collective-permute-start | bytes 2064392 | tf_op jit(solution)/shard_map/ppermute | solution.py:482
  39.5 10.6 %copy-start.3 = (bf16[400,256]{1,0:T(8,128)(2,1)S(1)}, bf16[400,256]{1,0:T(8,128)(2,1)}, u32[]{:S(2)}) copy-start(bf16[400,256]{1,0:T(8,128)(2,1)} %get-tuple-element.27.refs_0_) | copy-start | bytes 614404
  42.4 11.2 %collective-permute-start.14 = (bf16[864,128]{1,0:T(8,128)(2,1)S(1)}, bf16[864,128]{1,0:T(8,128)(2,1)S(1)}, u32[]{:S(2)}, u32[]{:S(2)}) collective-permute-start(bf16[864,128]{1,0:T(8,128)(2,1)S(1)} %get-tuple-element.44.refs_10_), channel_id=1, source_target_pairs={{0,8},{2,10},{4,12},{6,14},{8,0},{10,2},{12,4},{14,6},{16,24},{18,... | collective-permute-start | bytes 663560 | tf_op jit(solution)/shard_map/ppermute | solution.py:482
  42.5 18.3 %collective-permute-start.15 = (bf16[864,128]{1,0:T(8,128)(2,1)S(1)}, bf16[864,128]{1,0:T(8,128)(2,1)S(1)}, u32[]{:S(2)}, u32[]{:S(2)}) collective-permute-start(bf16[864,128]{1,0:T(8,128)(2,1)S(1)} %get-tuple-element.48), channel_id=1, source_target_pairs={{0,16},{2,18},{4,20},{6,22},{8,24},{10,26},{12,28},{14,30},{16,0},... | collective-permute-start | bytes 663560 | tf_op jit(solution)/shard_map/ppermute | solution.py:482
  45.5 20.3 %collective-permute-start.16 = (bf16[864,128]{1,0:T(8,128)(2,1)S(1)}, bf16[864,128]{1,0:T(8,128)(2,1)S(1)}, u32[]{:S(2)}, u32[]{:S(2)}) collective-permute-start(bf16[864,128]{1,0:T(8,128)(2,1)S(1)} %get-tuple-element.49), channel_id=1, source_target_pairs={{0,24},{2,26},{4,28},{6,30},{8,16},{10,18},{12,20},{14,22},{16,8},... | collective-permute-start | bytes 663560 | tf_op jit(solution)/shard_map/ppermute | solution.py:482
  46.0 4.1 %collective-permute-start.11 = (bf16[96,256]{1,0:T(8,128)(2,1)S(1)}, bf16[96,256]{1,0:T(8,128)(2,1)S(1)}, u32[]{:S(2)}, u32[]{:S(2)}) collective-permute-start(bf16[96,256]{1,0:T(8,128)(2,1)S(1)} %collective-permute-done.9.refs_5_.refs_11_.refs_4_), channel_id=1, source_target_pairs={{0,1},{1,0},{2,3},{3,2},{4,5},{5,4},{6,7},{7,6},{8,9},{9,8},{10,11... | collective-permute-start | bytes 147464 | tf_op jit(solution)/shard_map/ppermute | solution.py:498

commit v5 on v4

--- a/solution.py
+++ b/solution.py
@@ -85,6 +85,9 @@
             start = 3 if plane == 0 else 0
             pieces = [load(tile, start) for tile in tiles]
             for near, far in faces:
+                if far is None:
+                    pieces.append(load(near, start))
+                    continue
                 near, far = load(near, start), load(far, 0)
                 pieces.append(jnp.where(odd, near, far) if plane == 0 else jnp.where(odd, far, near))
         else:
@@ -137,7 +140,7 @@
 
 
 def pack_kernel(features, cotangent, coords, counts, *refs):
-    own_ref, face_ref, thin_ref, cross_ref, place_ref, live_ref, sems = refs
+    own_ref, face_ref, place_ref, live_ref, sems = refs
     slots = features.shape[2]
     width = slots * PLANE
     copies = [
@@ -178,17 +181,6 @@
     face_ref[:width, :] = own_ref[pl.ds(at, width), :]
     face_ref[width : 2 * width, :] = own_ref[pl.ds(pl.multiple_of(4 * width + at, PLANE), width), :]
     face_ref[2 * width :, :] = meta
-    slim(own_ref, thin_ref, lax.axis_index("gy") % 2)
-    slim(own_ref, cross_ref, 1 - lax.axis_index("gy") % 2)
-
-
-def placed(relays, sides, rows):
-    face = rows // 4 + META
-    start = (1 + sides) * (rows + META)
-    return (
-        [[(relay, s * (rows + META), False) for s in range(1 + sides)] for relay in relays],
-        [[(relay, start + s * face) for s in range(1 + sides)] for relay in relays],
-    )
 
 
 class Around:
@@ -217,8 +209,11 @@
         befores, afters = [], []
         for o in order:
             near = tile_meta(j ^ 1, o)
-            ref, first = self.fars[j][o]
-            far = meta(ref, first + 2 * self.width)
+            if self.fars is None:
+                far = jnp.zeros_like(near)
+            else:
+                ref, first = self.fars[j][o]
+                far = meta(ref, first + 2 * self.width)
             befores.append(jnp.where(self.odd(j), near, far))
             afters.append(jnp.where(self.odd(j), far, near))
         before, after = (
@@ -235,38 +230,96 @@
         order = self.order(s)
         faces = []
         for o in order:
-            ref, first = self.fars[j][o]
-            faces.append((tile(j ^ 1, o), (ref, first + field * self.width, False)))
+            far = None
+            if self.fars is not None:
+                ref, first = self.fars[j][o]
+                far = (ref, first + field * self.width, False)
+            faces.append((tile(j ^ 1, o), far))
         return [tile(j, o) for o in order], faces, self.odd(j)
 
 
+def chip_places(refs, sides, rows):
+    return [[(ref, s * (rows + META), False) for s in range(1 + sides)] for ref in refs]
+
+
+def main_kernel(sides, *refs):
+    tiles, refs = refs[:2], refs[2:]
+    first, second, pre_ref, back_ref, feature_cols, seed_cols = refs
+    rows = 2 * pre_ref.shape[0]
+    width = rows // 8
+    around = Around(chip_places(tiles, sides, rows), None, sides, rows)
+    chosen = selectors(*around.codes(0, 0), sides, width)
+    fill(feature_cols, *around.sources(0, 0, 0), chosen, width)
+    fill(seed_cols, *around.sources(0, 0, 1), chosen, width)
+    pre_ref[...] = conv(feature_cols, first, width)
+    back_ref[...] = conv_back(seed_cols, second, width)
+
+
 def layer_kernel(sides, *refs):
-    relay, near_relay, first, second = refs[:4]
-    both_ref, slim_ref, cross_ref, feature_cols, seed_cols, source_ref, target_ref = refs[4:]
+    tiles, refs = refs[:2], refs[2:]
+    fars, refs = refs[: 1 + sides], refs[1 + sides :]
+    first, second, pre_main, back_main = refs[:4]
+    both_ref, slim_ref, cross_ref, source_ref, target_ref, pre_ref, back_ref = refs[-7:]
     rows = both_ref.shape[0]
     width = rows // 8
-    around = Around(*placed([relay, near_relay], sides, rows), sides, rows)
+    around = Around(chip_places(tiles, sides, rows), [[(ref, 0) for ref in fars]], sides, rows)
     before, after, target = around.codes(0, 0)
     source_ref[0:1, :] = before
     source_ref[1:2, :] = after
     target_ref[...] = target
-    chosen = selectors(before, after, target, sides, width)
-    fill(feature_cols, *around.sources(0, 0, 0), chosen, width)
-    fill(seed_cols, *around.sources(0, 0, 1), chosen, width)
-    pre_first = conv(feature_cols, first, width)
-    live = live_rows(relay[rows : rows + 8, :], width)
+    odd = around.odd(0)
+    codes = jnp.where(odd, after, before)[:, : 2 * (1 + sides) * width]
+    chosen = (codes == target + jnp.where(odd, STEP_X, -STEP_X)).astype(jnp.float32)
+    chosen = chosen.astype(jnp.bfloat16)
+    nothing = jnp.zeros(((1 + sides) * width, C), jnp.bfloat16)
+    at = near_row(width)
+
+    def add(total_ref, main_ref, field, weight):
+        pieces = [nothing] + [ref[field * width : (field + 1) * width, :] for ref in fars]
+        moved = dot(chosen, jnp.concatenate(pieces, axis=0)).astype(jnp.bfloat16)
+        more = sum(weight(shift, moved[shift * width : (shift + 1) * width]) for shift in range(9))
+        total_ref[...] = main_ref[...]
+        total_ref[pl.ds(at, width), :] = total_ref[pl.ds(at, width), :] + more
+
+    def tap(weight_ref, index):
+        return weight_ref[pl.ds(pl.multiple_of(index * C, C), C), :]
+
+    add(
+        pre_ref,
+        pre_main,
+        0,
+        lambda shift, cells: dot(cells, tap(first, jnp.where(odd, 18, 0) + shift)),
+    )
+    add(
+        back_ref,
+        back_main,
+        1,
+        lambda shift, cells: dot(cells, tap(second, jnp.where(odd, 8, 26) - shift), ((1,), (1,))),
+    )
+    pre_first = pre_ref[...]
+    live = live_rows(tiles[0][rows : rows + 8, :], width)
     sigmoid = 1.0 / (1.0 + jnp.exp(-pre_first))
     hidden = jnp.where(live, pre_first * sigmoid, 0.0)
     both_ref[: 4 * width, :] = hidden.astype(jnp.bfloat16)
     slope = jnp.where(live, sigmoid * (1.0 + pre_first * (1.0 - sigmoid)), 0.0)
-    hidden_grad = conv_back(seed_cols, second, width)
-    both_ref[4 * width :, :] = (hidden_grad * slope).astype(jnp.bfloat16)
+    both_ref[4 * width :, :] = (back_ref[...] * slope).astype(jnp.bfloat16)
     if sides == 1:
         slim(both_ref, slim_ref, lax.axis_index("gy"))
         slim(both_ref, cross_ref, 1 - lax.axis_index("gy"))
     else:
         slim_ref[...] = jnp.zeros(slim_ref.shape, slim_ref.dtype)
         cross_ref[...] = jnp.zeros(cross_ref.shape, cross_ref.dtype)
+
+
+def join_kernel(count, *refs):
+    joined_ref, slim_ref = refs[-2:]
+    gather_kernel(count, *refs[:count], joined_ref)
+    if count == 2:
+        size = slim_ref.shape[0] // 2
+        for i in range(2):
+            slim(refs[i], slim_ref.at[pl.ds(i * size, size)], lax.axis_index("gy"))
+    else:
+        slim_ref[...] = jnp.zeros(slim_ref.shape, slim_ref.dtype)
 
 
 def slim(tile_ref, slim_ref, half):
@@ -279,16 +332,6 @@
         slim_ref[rows + rows // 2 :, :] = tile_ref[2 * rows :, :]
 
 
-def relay_kernel(count, *refs):
-    own_hbm, relay_ref, fars_ref, sem = refs[0], *refs[-3:]
-    size = own_hbm.shape[0]
-    copy = pltpu.make_async_copy(own_hbm, relay_ref.at[pl.ds(0, size)], sem)
-    copy.start()
-    gather_kernel(count - 1, *refs[1:count], relay_ref.at[pl.ds(size, relay_ref.shape[0] - size)])
-    gather_kernel(count // 2, *refs[count // 2 : count], fars_ref)
-    copy.wait()
-
-
 def gather_kernel(count, *refs):
     packed_ref = refs[-1]
     at = 0
@@ -318,7 +361,7 @@
         keep_at = pl.multiple_of((2 * i + core) * rows, 8)
         send_at = pl.multiple_of((2 * i + 1 - core) * rows, 8)
         keep_ref[i] = total_ref[pl.ds(keep_at, rows), :]
-        send_ref[i] = total_ref[pl.ds(send_at, rows), :].astype(jnp.bfloat16)
+        send_ref[i] = total_ref[pl.ds(send_at, rows), :]
 
 
 def second_terms_kernel(both_ref, cols_ref, keep_ref, send_ref, total_ref):
@@ -342,19 +385,22 @@
 def group_cols(around, members, feature_ref, seed_ref):
     columns = my_columns(seed_ref.shape[3])
     for index, (j, s) in enumerate(members):
-        chosen = selectors(*around.codes(j, s), 1, around.width)
+        chosen = selectors(*around.codes(j, s), around.sides, around.width)
         fill(feature_ref.at[index], *around.sources(j, s, 0), chosen, around.width)
         fill(seed_ref.at[index], *around.sources(j, s, 1), chosen, around.width, columns)
 
 
-CHIP_MEMBERS = ((0, 1), (1, 0), (1, 1))
+CHIP_MEMBERS = (((0, 0), (0, 1)), ((1, 0), (1, 1)))
 OTHER_MEMBERS = ((2, 0), (2, 1), (3, 0), (3, 1))
 
 
-def chip_cols_kernel(relay, near_relay, feature_ref, seed_ref):
+def chip_cols_kernel(sides, members, *refs):
+    tiles, (far, near_far), (feature_ref, seed_ref) = refs[:2], refs[2:4], refs[-2:]
     rows = feature_ref.shape[2] // 6 * 8
-    around = Around(*placed([relay, near_relay], 1, rows), 1, rows)
-    group_cols(around, CHIP_MEMBERS, feature_ref, seed_ref)
+    face = rows // 4 + META
+    fars = [[(ref, s * face) for s in range(1 + sides)] for ref in (far, near_far)]
+    around = Around(chip_places(tiles, sides, rows), fars, sides, rows)
+    group_cols(around, members, feature_ref, seed_ref)
 
 
 def other_cols_kernel(packed, near_packed, _, feature_ref, seed_ref):
@@ -411,7 +457,7 @@
 
 def group_terms_kernel(*refs):
     both, thins, packed, refs = refs[:2], refs[2:4], refs[4], refs[5:]
-    (feature_cols, seed_cols, *groups), refs = refs[:6], refs[7:]
+    groups, refs = refs[:6], refs[6:]
     out_refs, total_ref = refs[:-1], refs[-1]
     rows = both[0].shape[0] // 2
     chunk = out_refs[0].shape[0] // 2
@@ -422,15 +468,10 @@
     thins = [(ref, 0) for ref in thins] + [(packed, 0), (packed, thin_rows)]
 
     def group(part, tile, shift, at):
-        ref, index = (groups[part], tile - 1) if tile < 4 else (groups[2 + part], tile - 4)
-        return ref[index, shift, at, :]
-
-    def seeds_of(tile, shift, at):
-        return seed_cols[shift, at, columns] if tile == 0 else group(1, tile, shift, at)
-
-    def features_of(tile, shift, at):
-        return feature_cols[shift, at, :] if tile == 0 else group(0, tile, shift, at)
-
+        place, index = (tile // 2, tile % 2) if tile < 4 else (2, tile - 4)
+        return groups[part + 2 * place][index, shift, at, :]
+
+    features_of, seeds_of = functools.partial(group, 0), functools.partial(group, 1)
     grads = [ref[at + rows : at + 2 * rows, columns] for ref, at in both]
     for ref, at in thins:
         halves = ref[at + rows : at + rows + rows // 2, :]
@@ -505,12 +546,9 @@
     )
 
 
-def from_far(face, late):
-    steps = far_steps(lax.axis_size("gx"))
-    far = lax.ppermute(face, "gx", steps)
-    if late:
-        return [far, *from_sides(far)]
-    return [far] + [across(face, steps, side) for side in side_steps(lax.axis_size("gy"))]
+def from_far(face):
+    far = lax.ppermute(face, "gx", far_steps(lax.axis_size("gx")))
+    return [far, *from_sides(far)]
 
 
 def piece(cells, index, axis):
@@ -546,14 +584,12 @@
             name=name,
         )(*args)
 
-    own, face, thin_own, cross_own = call(
+    own, face = call(
         pack_kernel,
         "pack",
         (
             shape((rows + META, C)),
             shape((2 * width + META, C)),
-            shape((6 * width + META, C)),
-            shape((6 * width + META, C)),
         ),
         (features, cotangent, block_coords, block_counts),
         60,
@@ -566,47 +602,62 @@
         [HBM] * 4,
     )
     side = from_sides(own)
-    fars = from_far(face, False)
-    others = []
-    if grouped:
-        beside = [(i, i ^ 2) for i in range(gx)]
-        others = [swap(thin_own, "gx", 2), across(cross_own, beside, side_steps(gy)[0])]
-    parts = [own, *side, *fars]
-    relay, far_faces = call(
-        functools.partial(relay_kernel, len(parts)),
-        "relay",
+    field = (4 * width, C)
+    fars = from_far(face)
+    def gathered(name, cells, after, micros=0.5):
+        return call(
+            functools.partial(gather_kernel, len(cells)),
+            name,
+            (shape((sum(part.shape[0] for part in cells), C)),),
+            (*cells, *after),
+            8,
+            micros,
+            specs=[VMEM] * len(cells) + [ANY] * len(after),
+        )[0]
+
+    parts = [own, *side]
+    chip, thins = call(
+        functools.partial(join_kernel, len(parts)),
+        "join",
         (
-            shape((sum(cells.shape[0] for cells in parts), C)),
-            shape((sum(cells.shape[0] for cells in fars), C)),
+            shape((len(parts) * (rows + META), C)),
+            shape((2 * (6 * width + META), C)),
         ),
-        (*parts, *others),
+        (*parts, fars[0]),
         8,
         3,
-        [pltpu.SemaphoreType.DMA],
-        [ANY] + [VMEM] * (len(parts) - 1) + [ANY] * len(others),
-    )
-    near_relay = swap(relay, "gx", 1)
+        specs=[VMEM] * len(parts) + [ANY],
+    )
+    chip = [chip, swap(chip, "gx", 1)]
     columns = shape((9, 6 * width, C))
-    both, thin, cross, feature_cols, seed_cols, source, target = call(
+    main = call(
+        functools.partial(main_kernel, sides),
+        "first_convs",
+        (shape(field, jnp.float32),) * 2,
+        (*chip, first_weight, second_weight),
+        12,
+        3,
+        [pltpu.VMEM(columns.shape, jnp.bfloat16)] * 2,
+    )
+    both, thin, cross, source, target = call(
         functools.partial(layer_kernel, sides),
         "layer",
         (
             shape((rows, C)),
             shape((6 * width, C)),
             shape((6 * width, C)),
-            columns,
-            columns,
             shape((2, LANES), jnp.float32),
             shape((9 * width, 1), jnp.float32),
         ),
-        (relay, near_relay, first_weight, second_weight),
-        12,
-        4,
+        (*chip, *fars, first_weight, second_weight, *main),
+        8,
+        1,
+        [pltpu.VMEM(field, jnp.float32)] * 2,
     )
     both_side = from_sides(both)
 
-    def faced(*after):
-        return call(
+    def late_far(after):
+        (late_face,) = call(
             face_kernel,
             "face",
             (shape((2 * width, C)),),
@@ -614,7 +665,8 @@
             8,
             0.3,
             specs=[VMEM] + [ANY] * len(after),
-        )[0]
+        )
+        return from_far(late_face)
 
     grad_scale = 1.0 / math.sqrt(64 * slots * gx * gy)
 
@@ -625,32 +677,33 @@
     if grouped:
         cols = C // 2
 
-        def gathered(name, cells, after):
-            return call(
-                functools.partial(gather_kernel, len(cells)),
-                name,
-                (shape((sum(part.shape[0] for part in cells), C)),),
-                (*cells, *after),
-                8,
-                0.5,
-                specs=[VMEM] * len(cells) + [ANY] * len(after),
-            )[0]
-
         def group_shapes(count):
             return shape((count, *columns.shape)), shape((count, *columns.shape[:2], cols))
 
-        early = gathered("gather_early", (*others, swap(far_faces, "gx", 2)), (both,))
+        far_faces = gathered("far_faces", fars, main[:1])
+        near_faces = swap(far_faces, "gx", 1)
+        beside = [swap(thins, "gx", 2), swap(far_faces, "gx", 2)]
+        early = gathered("gather_early", beside, (both,))
         near_early = swap(early, "gx", 1)
-        chip_features, chip_seeds = call(
-            chip_cols_kernel, "chip_cols", group_shapes(len(CHIP_MEMBERS)), (relay, near_relay), 8, 2.5
-        )
-        late_fars = from_far(faced(chip_seeds), True)
+        chip_cols = [
+            call(
+                functools.partial(chip_cols_kernel, 1, members),
+                "chip_cols",
+                group_shapes(len(members)),
+                (*chip, far_faces, near_faces, *after),
+                8,
+                1.6,
+                specs=[VMEM] * 4 + [ANY] * len(after),
+            )
+            for members, after in zip(CHIP_MEMBERS, ((), beside))
+        ]
+        late_fars = late_far(chip_cols[0][1:])
         thin_other = swap(thin, "gx", 2)
-        cross_other = across(cross, beside, side_steps(gy)[0])
+        cross_other = across(cross, [(i, i ^ 2) for i in range(gx)], side_steps(gy)[0])
         packed = gathered(
             "gather_late",
             (thin_other, cross_other, both, both_side[0]),
-            (chip_seeds, late_fars[0]),
+            (chip_cols[1][1], late_fars[0]),
         )
         near_packed = swap(packed, "gx", 1)
         nears = [near_packed]
@@ -674,25 +727,22 @@
             ),
             (
                 *members,
-                feature_cols,
-                seed_cols,
-                chip_features,
-                chip_seeds,
+                *chip_cols[0],
+                *chip_cols[1],
                 other_features,
                 other_seeds,
-                late_fars[0],
             ),
             12,
             3.5,
             [pltpu.VMEM((deeps, taps * C, cols), jnp.float32)],
-            [VMEM] * (len(members) + 6) + [ANY],
         )
         token = sent[0]
         grads = over_z(own_part, sent)
         first_grad, second_grad = grads[:chunk], grads[chunk:]
     else:
+        far_faces = jnp.concatenate(fars, axis=0)
         nears = [swap(cells, "gx", 1) for cells in (both, *both_side)]
-        late_fars = from_far(faced(), True)
+        late_fars = late_far(())
 
         def summed(kernel, name, cells):
             keep, send = call(
@@ -700,7 +750,7 @@
                 name,
                 (
                     shape((gx // 2, chunk, C), jnp.float32),
-                    shape((gx // 2, chunk, C)),
+                    shape((gx // 2, chunk, C), jnp.float32),
                 ),
                 (both, cells),
                 24,
@@ -711,7 +761,7 @@
             got = swap(send, "gx", 1).reshape(keep.shape)
 
             def part(i):
-                return piece(keep, i, 1) + piece(got, i, 1).astype(jnp.float32)
+                return piece(keep, i, 1) + piece(got, i, 1)
 
             total = part(half) + swap(part(1 - half).astype(jnp.bfloat16), "gx", 2).astype(
                 jnp.float32
@@ -727,10 +777,19 @@
             )
             return total, send
 
+        feature_cols, seed_cols = call(
+            functools.partial(chip_cols_kernel, sides, ((0, 0),)),
+            "own_cols",
+            (shape((1, *columns.shape)),) * 2,
+            (*chip, far_faces, far_faces),
+            8,
+            1,
+        )
+        feature_cols, seed_cols = feature_cols[0], seed_cols[0]
         second_grad, token = summed(second_terms_kernel, "second_terms", seed_cols)
         first_grad, _ = summed(first_terms_kernel, "first_terms", feature_cols)
 
-    late = [own, both, *both_side, *nears, *late_fars]
+    late = [chip[0], both, *both_side, *nears, *late_fars]
     result = shape((slots, 64, C), jnp.float32)
     output, input_grad = call(
         functools.partial(last_kernel, sides),

time: 66.9 us -> 63.5 us (0.949)
  starting transfers between devices: 26.8 us -> 18.8 us
  waiting for transfers between devices: 19.3 us -> 22 us
  Pallas kernels: 17.3 us -> 19.3 us
    ppermute x3 -> x1, starting transfers between devices: 6.27 us -> 1.1 us  [across(): lax.ppermute(face, ('gx', 'gy'), [(a * gy + c, b * gy + d) for a, b in gx...]
    ppermute x9 -> x10, starting transfers between devices: 10.9 us -> 8.35 us  [swap(): lax.ppermute(cells, axis, [(i, i ^ bit) for i in range(lax.axis_size(axis...]
    pallas_call x10 -> x13, Pallas kernels: 17.3 us -> 19.3 us  [call(): pl.pallas_call(kernel, out_shape=outs, in_specs=specs or [VMEM] * len(arg...]
    ppermute x2, waiting for transfers between devices: 2.44 us -> 4.02 us  [from_far(): far = lax.ppermute(face, 'gx', far_steps(lax.axis_size('gx')))]
    ppermute x3 -> x4, waiting for transfers between devices: 2.57 us -> 3.21 us  [from_sides(): lax.ppermute(cells, 'gy', step)]
    ppermute x3 -> x1, waiting for transfers between devices: 2.13 us -> 2.57 us  [across(): lax.ppermute(face, ('gx', 'gy'), [(a * gy + c, b * gy + d) for a, b in gx...]
    ppermute x3 -> x4, starting transfers between devices: 4.7 us -> 4.4 us  [from_sides(): lax.ppermute(cells, 'gy', step)]
    ppermute x9 -> x10, waiting for transfers between devices: 12.1 us -> 12.1 us  [swap(): lax.ppermute(cells, axis, [(i, i ^ bit) for i in range(lax.axis_size(axis...]
  transfers between devices with their start and end apart: 17 -> 17, of which waited for: 5 -> 5; matrix products, arithmetic and copies ran while one was open for 0% -> 0% of each run, Pallas kernels for 18% -> 23%
where the time goes in v5:
time: 63.5 us; the launch traced here: 63.3 us
  waiting for transfers between devices  22 us (35%)
  Pallas kernels  19.3 us (30%)
  starting transfers between devices  18.8 us (30%)
  local copies, waits for them, and re-layouts  1.73 us (3%)
  between operations  1.46 us (2%)
    pallas_call x13, Pallas kernels, call(): pl.pallas_call(kernel, out_shape=outs, in_specs=specs or [VMEM] * len(arg...  19.3 us
    ppermute x10, waiting for transfers between devices, swap(): lax.ppermute(cells, axis, [(i, i ^ bit) for i in range(lax.axis_size(axis...  12.1 us
    ppermute x10, starting transfers between devices, swap(): lax.ppermute(cells, axis, [(i, i ^ bit) for i in range(lax.axis_size(axis...  8.35 us
    ppermute x2, starting transfers between devices, from_far(): far = lax.ppermute(face, 'gx', far_steps(lax.axis_size('gx')))  4.93 us
    ppermute x4, starting transfers between devices, from_sides(): lax.ppermute(cells, 'gy', step)  4.4 us
    ppermute x2, waiting for transfers between devices, from_far(): far = lax.ppermute(face, 'gx', far_steps(lax.axis_size('gx')))  4.02 us
    ppermute x4, waiting for transfers between devices, from_sides(): lax.ppermute(cells, 'gy', step)  3.21 us
    ppermute x1, waiting for transfers between devices, across(): lax.ppermute(face, ('gx', 'gy'), [(a * gy + c, b * gy + d) for a, b in gx...  2.57 us
  transfers between devices with their start and end apart: 17, of which 5 were waited for; matrix products, arithmetic and copies ran while one was open for 0% of the time, Pallas kernels for 23%

profile of v5, /device:TPU:8, one launch (start us, length us, event | category | flops | bytes accessed | tf_op | source)
XLA Modules:
  0.0 63.3 jit_solution(9953993731822589278)
XLA Ops:
  1.3 1.9 %pack.1 = (bf16[400,256]{1,0:T(8,128)(2,1)}, bf16[112,256]{1,0:T(8,128)(2,1)}) custom-call(bf16[1,1,3,64,256]{4,3,2,1,0:T(8,128)(2,1)} %features.1, bf16[1,1,3,64,256]{4,3,2,1,0:T(8,128)(2,1)} %cotangent.1, s32[1,1,3]{2,1,0:T(1,128)} %coords.1, s32[1,1]{1,0:T(1,128)S(6)} %copy.10.counts), custom_call_target="tpu_custom_call" | custom-call | flops 3300000000 | bytes 1048576 | tf_op jit(solution)/shard_map/pack/pallas_call | solution.py:574
  3.2 1.6 %collective-permute-start = (bf16[400,256]{1,0:T(8,128)(2,1)}, bf16[400,256]{1,0:T(8,128)(2,1)S(1)}, u32[]{:S(2)}, u32[]{:S(2)}) collective-permute-start(bf16[400,256]{1,0:T(8,128)(2,1)} %get-tuple-element.27.refs_0_), channel_id=1, source_target_pairs={{0,1},{1,0},{2,3},{3,2},{4,5},{5,4},{6,7},{7,6},{8,9},{9,8},{10,11... | collective-permute-start | bytes 614408 | tf_op jit(solution)/shard_map/ppermute | solution.py:539
  4.7 2.8 %collective-permute-start.1 = (bf16[112,256]{1,0:T(8,128)(2,1)}, bf16[112,256]{1,0:T(8,128)(2,1)S(1)}, u32[]{:S(2)}, u32[]{:S(2)}) collective-permute-start(bf16[112,256]{1,0:T(8,128)(2,1)} %get-tuple-element.28), channel_id=1, source_target_pairs={{2,4},{6,8},{10,12},{14,16},{18,20},{22,24},{26,28},{4,2},{8,6},{1... | collective-permute-start | bytes 172040 | tf_op jit(solution)/shard_map/ppermute | solution.py:550
  7.6 4.0 %collective-permute-done.1.refs_2_.refs_0_ = bf16[112,256]{1,0:T(8,128)(2,1)S(1)} collective-permute-done((bf16[112,256]{1,0:T(8,128)(2,1)}, bf16[112,256]{1,0:T(8,128)(2,1)S(1)}, u32[]{:S(2)}, u32[]{:S(2)}) %collective-permute-start.1) | collective-permute-done | bytes 57376 | tf_op jit(solution)/shard_map/ppermute | solution.py:550
  11.6 0.0 collective-permute-done.refs_1_
  11.6 0.9 %copy-done.2 = bf16[400,256]{1,0:T(8,128)(2,1)S(1)} copy-done((bf16[400,256]{1,0:T(8,128)(2,1)S(1)}, bf16[400,256]{1,0:T(8,128)(2,1)}, u32[]{:S(2)}) %copy-start.2) | copy-done | bytes 204824
  12.5 0.1 join.1
  12.6 0.1 collective-permute-start.2
  12.7 0.6 collective-permute-start.3
  13.2 1.1 %collective-permute-start.8 = (bf16[608,256]{1,0:T(8,128)(2,1)S(1)}, bf16[608,256]{1,0:T(8,128)(2,1)S(1)}, u32[]{:S(2)}, u32[]{:S(2)}) collective-permute-start(bf16[608,256]{1,0:T(8,128)(2,1)S(1)} %get-tuple-element.35), channel_id=1, source_target_pairs={{0,4},{2,6},{4,0},{6,2},{8,12},{10,14},{12,8},{14,10},{16,20},{18,... | collective-permute-start | bytes 933896 | tf_op jit(solution)/shard_map/ppermute | solution.py:523
  14.4 0.0 collective-permute-done.2.refs_1_
  14.4 0.0 copy-done
  14.4 0.0 copy-done.1
  14.4 3.0 %first_convs.1 = (f32[192,256]{1,0:T(8,128)S(1)}, f32[192,256]{1,0:T(8,128)S(1)}) custom-call(bf16[800,256]{1,0:T(8,128)(2,1)S(1)} %get-tuple-element.29.refs_0_, bf16[800,256]{1,0:T(8,128)(2,1)S(1)} %collective-permute-done.2.refs_1_, bf16[6912,256]{1,0:T(8,128)(2,1)S(1)} %copy-done, bf16[6912,256]{1,0:T(8,128)(2,1)S(1)} %copy-done.1), custom_call_target="tpu_custom_call" | custom-call | flops 3300000000 | bytes 1048576 | tf_op jit(solution)/shard_map/first_convs/pallas_call | solution.py:574
  17.4 0.0 collective-permute-done.3.refs_3_.refs_1_
  17.4 0.2 collective-permute-start.7
  17.6 1.0 %collective-permute-start.9 = (bf16[224,256]{1,0:T(8,128)(2,1)S(1)}, bf16[224,256]{1,0:T(8,128)(2,1)S(1)}, u32[]{:S(2)}, u32[]{:S(2)}) collective-permute-start(bf16[224,256]{1,0:T(8,128)(2,1)S(1)} %far_faces.1.refs_2_), channel_id=1, source_target_pairs={{0,4},{2,6},{4,0},{6,2},{8,12},{10,14},{12,8},{14,10},{16,20},{18,... | collective-permute-start | bytes 344072 | tf_op jit(solution)/shard_map/ppermute | solution.py:523
  18.7 1.4 %layer.1 = (bf16[384,256]{1,0:T(8,128)(2,1)S(1)}, bf16[288,256]{1,0:T(8,128)(2,1)S(1)}, bf16[288,256]{1,0:T(8,128)(2,1)S(1)}, f32[2,512]{1,0:T(2,128)S(1)}, f32[432,1]{1,0:T(8,128)S(1)}) custom-call(bf16[800,256]{1,0:T(8,128)(2,1)S(1)} %get-tuple-element.29.refs_0_, bf16[800,256]{1,0:T(8,128)(2,1)S(1)} %collective-permute-done.2.refs_1_, ...), custom_call_target="tpu_custom_call" | custom-call | flops 1100000000 | bytes 1048576 | tf_op jit(solution)/shard_map/layer/pallas_call | solution.py:574
  20.1 1.4 %collective-permute-start.4 = (bf16[384,256]{1,0:T(8,128)(2,1)S(1)}, bf16[384,256]{1,0:T(8,128)(2,1)S(1)}, u32[]{:S(2)}, u32[]{:S(2)}) collective-permute-start(bf16[384,256]{1,0:T(8,128)(2,1)S(1)} %get-tuple-element.32.both_ref.refs_2_.refs_0_.refs_1_), channel_id=1, source_target_pairs={{0,1},{1,0},{2,3},{3,2},{4,5},{5,4},{6,7},{7,6},{8,9},{9,8},{10,11... | collective-permute-start | bytes 589832 | tf_op jit(solution)/shard_map/ppermute | solution.py:539
  21.4 1.1 %collective-permute-start.5 = (bf16[288,256]{1,0:T(8,128)(2,1)S(1)}, bf16[288,256]{1,0:T(8,128)(2,1)S(1)}, u32[]{:S(2)}, u32[]{:S(2)}) collective-permute-start(bf16[288,256]{1,0:T(8,128)(2,1)S(1)} %get-tuple-element.33), channel_id=1, source_target_pairs={{0,4},{2,6},{4,0},{6,2},{8,12},{10,14},{12,8},{14,10},{16,20},{18,... | collective-permute-start | bytes 442376 | tf_op jit(solution)/shard_map/ppermute | solution.py:523
  22.5 0.0 collective-permute-done.7.refs_3_
  22.5 1.1 %collective-permute-start.6 = (bf16[288,256]{1,0:T(8,128)(2,1)S(1)}, bf16[288,256]{1,0:T(8,128)(2,1)S(1)}, u32[]{:S(2)}, u32[]{:S(2)}) collective-permute-start(bf16[288,256]{1,0:T(8,128)(2,1)S(1)} %get-tuple-element.34), channel_id=1, source_target_pairs={{0,5},{1,4},{2,7},{3,6},{4,1},{5,0},{6,3},{7,2},{8,13},{9,12},{10,... | collective-permute-start | bytes 442376 | tf_op jit(solution)/shard_map/ppermute | solution.py:544
  23.6 1.7 %chip_cols.3 = (bf16[2,9,288,256]{3,2,1,0:T(8,128)(2,1)S(1)}, bf16[2,9,288,128]{3,2,1,0:T(8,128)(2,1)S(1)}) custom-call(bf16[800,256]{1,0:T(8,128)(2,1)S(1)} %get-tuple-element.29.refs_0_, bf16[800,256]{1,0:T(8,128)(2,1)S(1)} %collective-permute-done.2.refs_1_, bf16[224,256]{1,0:T(8,128)(2,1)S(1)} %far_faces.1.refs_2_, ...), custom_call_target="tpu_custom_call" | custom-call | flops 1760000000 | bytes 1048576 | tf_op jit(solution)/shard_map/chip_cols/pallas_call | solution.py:574
  25.3 0.0 collective-permute-done.8.refs_4_.refs_0_
  25.3 2.1 %collective-permute-start.10 = (bf16[96,256]{1,0:T(8,128)(2,1)S(1)}, bf16[96,256]{1,0:T(8,128)(2,1)S(1)}, u32[]{:S(2)}, u32[]{:S(2)}) collective-permute-start(bf16[96,256]{1,0:T(8,128)(2,1)S(1)} %face.1), channel_id=1, source_target_pairs={{2,4},{6,8},{10,12},{14,16},{18,20},{22,24},{26,28},{4,2},{8,6},{1... | collective-permute-start | bytes 147464 | tf_op jit(solution)/shard_map/ppermute | solution.py:550
  27.4 0.0 collective-permute-done.9.refs_5_.refs_1_
  27.5 1.2 %collective-permute-start.13 = (bf16[832,256]{1,0:T(8,128)(2,1)S(1)}, bf16[832,256]{1,0:T(8,128)(2,1)S(1)}, u32[]{:S(2)}, u32[]{:S(2)}) collective-permute-start(bf16[832,256]{1,0:T(8,128)(2,1)S(1)} %gather_early.1.packed), channel_id=1, source_target_pairs={{0,2},{2,0},{4,6},{6,4},{8,10},{10,8},{12,14},{14,12},{16,18},{18,... | collective-permute-start | bytes 1277960 | tf_op jit(solution)/shard_map/ppermute | solution.py:523
  28.7 1.7 %chip_cols.2 = (bf16[2,9,288,256]{3,2,1,0:T(8,128)(2,1)S(1)}, bf16[2,9,288,128]{3,2,1,0:T(8,128)(2,1)S(1)}) custom-call(bf16[800,256]{1,0:T(8,128)(2,1)S(1)} %get-tuple-element.29.refs_0_, bf16[800,256]{1,0:T(8,128)(2,1)S(1)} %collective-permute-done.2.refs_1_, bf16[224,256]{1,0:T(8,128)(2,1)S(1)} %far_faces.1.refs_2_, ...), custom_call_target="tpu_custom_call" | custom-call | flops 1760000000 | bytes 1048576 | tf_op jit(solution)/shard_map/chip_cols/pallas_call | solution.py:574
  30.4 0.0 collective-permute-done.5.refs_0_.refs_2_
  30.4 2.6 %collective-permute-done.6.refs_1_.refs_3_ = bf16[288,256]{1,0:T(8,128)(2,1)S(1)} collective-permute-done((bf16[288,256]{1,0:T(8,128)(2,1)S(1)}, bf16[288,256]{1,0:T(8,128)(2,1)S(1)}, u32[]{:S(2)}, u32[]{:S(2)}) %collective-permute-start.6) | collective-permute-done | bytes 147488 | tf_op jit(solution)/shard_map/ppermute | solution.py:544
  32.9 0.0 collective-permute-done.10.refs_5_.refs_4_
  32.9 0.0 collective-permute-done.4.refs_3_.refs_1_.refs_2_
  33.0 0.1 collective-permute-start.11
  33.1 0.0 collective-permute-done.13.near_packed
  33.1 3.1 %other_cols.1 = (bf16[4,9,288,256]{3,2,1,0:T(8,128)(2,1)S(1)}, bf16[4,9,288,128]{3,2,1,0:T(8,128)(2,1)S(1)}) custom-call(bf16[832,256]{1,0:T(8,128)(2,1)S(1)} %gather_early.1.packed, bf16[832,256]{1,0:T(8,128)(2,1)S(1)} %collective-permute-done.13.near_packed, bf16[1344,256]{1,0:T(8,128)(2,1)S(1)} %gather_late.1._), custom_call_target="tpu_custom_call" | custom-call | flops 3300000000 | bytes 1048576 | tf_op jit(solution)/shard_map/other_cols/pallas_call | solution.py:574
  36.2 0.0 collective-permute-done.11.refs_4_.refs_3_
  36.2 2.9 %group_terms.1 = (f32[864,128]{1,0:T(8,128)S(1)}, bf16[864,128]{1,0:T(8,128)(2,1)S(1)}, bf16[864,128]{1,0:T(8,128)(2,1)S(1)}, bf16[864,128]{1,0:T(8,128)(2,1)S(1)}) custom-call(bf16[384,256]{1,0:T(8,128)(2,1)S(1)} %get-tuple-element.32.both_ref.refs_2_.refs_0_.refs_1_, bf16[384,256]{1,0:T(8,128)(2,1)S(1)} %collective-permute-done.4.refs_3_.refs_1_.refs_2_, ...), custom_call_target="tpu_custom_call" | custom-call | flops 3849999872 | bytes 1048576 | tf_op jit(solution)/shard_map/group_terms/pallas_call | solution.py:574
  39.1 0.1 collective-permute-start.14
  39.1 3.0 %collective-permute-start.15 = (bf16[864,128]{1,0:T(8,128)(2,1)S(1)}, bf16[864,128]{1,0:T(8,128)(2,1)S(1)}, u32[]{:S(2)}, u32[]{:S(2)}) collective-permute-start(bf16[864,128]{1,0:T(8,128)(2,1)S(1)} %get-tuple-element.48), channel_id=1, source_target_pairs={{0,16},{2,18},{4,20},{6,22},{8,24},{10,26},{12,28},{14,30},{16,0},... | collective-permute-start | bytes 663560 | tf_op jit(solution)/shard_map/ppermute | solution.py:523
  42.1 0.5 collective-permute-start.16
  42.6 0.9 %collective-permute-start.12 = (bf16[96,256]{1,0:T(8,128)(2,1)S(1)}, bf16[96,256]{1,0:T(8,128)(2,1)S(1)}, u32[]{:S(2)}, u32[]{:S(2)}) collective-permute-start(bf16[96,256]{1,0:T(8,128)(2,1)S(1)} %collective-permute-done.10.refs_5_.refs_4_), channel_id=1, source_target_pairs={{0,1},{1,0},{2,3},{3,2},{4,5},{5,4},{6,7},{7,6},{8,9},{9,8},{10,11... | collective-permute-start | bytes 147464 | tf_op jit(solution)/shard_map/ppermute | solution.py:539
  43.5 3.2 %collective-permute-done.12.refs_5_ = bf16[96,256]{1,0:T(8,128)(2,1)S(1)} collective-permute-done((bf16[96,256]{1,0:T(8,128)(2,1)S(1)}, bf16[96,256]{1,0:T(8,128)(2,1)S(1)}, u32[]{:S(2)}, u32[]{:S(2)}) %collective-permute-start.12) | collective-permute-done | bytes 49184 | tf_op jit(solution)/shard_map/ppermute | solution.py:539
  46.7 3.6 %last_layer.1 = (f32[3,64,256]{2,1,0:T(8,128)}, f32[3,64,256]{2,1,0:T(8,128)}) custom-call(bf16[800,256]{1,0:T(8,128)(2,1)S(1)} %get-tuple-element.29.refs_0_, bf16[384,256]{1,0:T(8,128)(2,1)S(1)} %get-tuple-element.32.both_ref.refs_2_.refs_0_.refs_1_, bf16[384,256]{1,0:T(8,128)(2,1)S(1)} %collective-permute-done.4.refs_3_.refs_1_.refs_2_, ...), custom_call_target="tpu_custom_call" | custom-call | flops 110000000 | bytes 1048576 | tf_op jit(solution)/shard_map/last_layer/pallas_call | solution.py:574
  50.3 0.0 collective-permute-done.14
  50.3 7.1 %collective-permute-done.15 = bf16[864,128]{1,0:T(8,128)(2,1)S(1)} collective-permute-done((bf16[864,128]{1,0:T(8,128)(2,1)S(1)}, bf16[864,128]{1,0:T(8,128)(2,1)S(1)}, u32[]{:S(2)}, u32[]{:S(2)}) %collective-permute-start.15) | collective-permute-done | bytes 221216 | tf_op jit(solution)/shard_map/ppermute | solution.py:523
  57.4 5.0 %collective-permute-done.16 = bf16[864,128]{1,0:T(8,128)(2,1)S(1)} collective-permute-done((bf16[864,128]{1,0:T(8,128)(2,1)S(1)}, bf16[864,128]{1,0:T(8,128)(2,1)S(1)}, u32[]{:S(2)}, u32[]{:S(2)}) %collective-permute-start.16) | collective-permute-done | bytes 221216 | tf_op jit(solution)/shard_map/ppermute | solution.py:523
  62.4 0.1 add_multiply_fusion
  62.5 0.8 %fusion = (f32[432,128]{1,0:T(8,128)}, f32[432,128]{1,0:T(8,128)}) fusion(f32[864,128]{1,0:T(8,128)S(1)} %add_multiply_fusion), kind=kLoop, calls=%fused_computation.1 | loop fusion | bytes 884736 | tf_op jit(solution)/shard_map/slice | solution.py:741
  (7 shorter events, 0.1 us)
Async XLA Ops:
  3.2 8.4 %collective-permute-start = (bf16[400,256]{1,0:T(8,128)(2,1)}, bf16[400,256]{1,0:T(8,128)(2,1)S(1)}, u32[]{:S(2)}, u32[]{:S(2)}) collective-permute-start(bf16[400,256]{1,0:T(8,128)(2,1)} %get-tuple-element.27.refs_0_), channel_id=1, source_target_pairs={{0,1},{1,0},{2,3},{3,2},{4,5},{5,4},{6,7},{7,6},{8,9},{9,8},{10,11... | collective-permute-start | bytes 614408 | tf_op jit(solution)/shard_map/ppermute | solution.py:539
  4.7 9.7 %copy-start = (bf16[6912,256]{1,0:T(8,128)(2,1)S(1)}, bf16[6912,256]{1,0:T(8,128)(2,1)}, u32[]{:S(2)}) copy-start(bf16[6912,256]{1,0:T(8,128)(2,1)} %refs_6_.1) | copy-start | bytes 10616836
  4.7 9.7 %copy-start.1 = (bf16[6912,256]{1,0:T(8,128)(2,1)S(1)}, bf16[6912,256]{1,0:T(8,128)(2,1)}, u32[]{:S(2)}) copy-start(bf16[6912,256]{1,0:T(8,128)(2,1)} %refs_7_.1) | copy-start | bytes 10616836
  4.7 6.9 %collective-permute-start.1 = (bf16[112,256]{1,0:T(8,128)(2,1)}, bf16[112,256]{1,0:T(8,128)(2,1)S(1)}, u32[]{:S(2)}, u32[]{:S(2)}) collective-permute-start(bf16[112,256]{1,0:T(8,128)(2,1)} %get-tuple-element.28), channel_id=1, source_target_pairs={{2,4},{6,8},{10,12},{14,16},{18,20},{22,24},{26,28},{4,2},{8,6},{1... | collective-permute-start | bytes 172040 | tf_op jit(solution)/shard_map/ppermute | solution.py:550
  11.6 0.9 %copy-start.2 = (bf16[400,256]{1,0:T(8,128)(2,1)S(1)}, bf16[400,256]{1,0:T(8,128)(2,1)}, u32[]{:S(2)}) copy-start(bf16[400,256]{1,0:T(8,128)(2,1)} %get-tuple-element.27.refs_0_) | copy-start | bytes 614404
  12.6 1.8 %collective-permute-start.2 = (bf16[800,256]{1,0:T(8,128)(2,1)S(1)}, bf16[800,256]{1,0:T(8,128)(2,1)S(1)}, u32[]{:S(2)}, u32[]{:S(2)}) collective-permute-start(bf16[800,256]{1,0:T(8,128)(2,1)S(1)} %get-tuple-element.29.refs_0_), channel_id=1, source_target_pairs={{0,2},{2,0},{4,6},{6,4},{8,10},{10,8},{12,14},{14,12},{16,18},{18,... | collective-permute-start | bytes 1228808 | tf_op jit(solution)/shard_map/ppermute | solution.py:523
  12.7 4.7 %collective-permute-start.3 = (bf16[112,256]{1,0:T(8,128)(2,1)S(1)}, bf16[112,256]{1,0:T(8,128)(2,1)S(1)}, u32[]{:S(2)}, u32[]{:S(2)}) collective-permute-start(bf16[112,256]{1,0:T(8,128)(2,1)S(1)} %collective-permute-done.1.refs_2_.refs_0_), channel_id=1, source_target_pairs={{0,1},{1,0},{2,3},{3,2},{4,5},{5,4},{6,7},{7,6},{8,9},{9,8},{10,11... | collective-permute-start | bytes 172040 | tf_op jit(solution)/shard_map/ppermute | solution.py:539
  13.2 12.1 %collective-permute-start.8 = (bf16[608,256]{1,0:T(8,128)(2,1)S(1)}, bf16[608,256]{1,0:T(8,128)(2,1)S(1)}, u32[]{:S(2)}, u32[]{:S(2)}) collective-permute-start(bf16[608,256]{1,0:T(8,128)(2,1)S(1)} %get-tuple-element.35), channel_id=1, source_target_pairs={{0,4},{2,6},{4,0},{6,2},{8,12},{10,14},{12,8},{14,10},{16,20},{18,... | collective-permute-start | bytes 933896 | tf_op jit(solution)/shard_map/ppermute | solution.py:523
  17.4 5.1 %collective-permute-start.7 = (bf16[224,256]{1,0:T(8,128)(2,1)S(1)}, bf16[224,256]{1,0:T(8,128)(2,1)S(1)}, u32[]{:S(2)}, u32[]{:S(2)}) collective-permute-start(bf16[224,256]{1,0:T(8,128)(2,1)S(1)} %far_faces.1.refs_2_), channel_id=1, source_target_pairs={{0,2},{2,0},{4,6},{6,4},{8,10},{10,8},{12,14},{14,12},{16,18},{18,... | collective-permute-start | bytes 344072 | tf_op jit(solution)/shard_map/ppermute | solution.py:523
  17.6 9.8 %collective-permute-start.9 = (bf16[224,256]{1,0:T(8,128)(2,1)S(1)}, bf16[224,256]{1,0:T(8,128)(2,1)S(1)}, u32[]{:S(2)}, u32[]{:S(2)}) collective-permute-start(bf16[224,256]{1,0:T(8,128)(2,1)S(1)} %far_faces.1.refs_2_), channel_id=1, source_target_pairs={{0,4},{2,6},{4,0},{6,2},{8,12},{10,14},{12,8},{14,10},{16,20},{18,... | collective-permute-start | bytes 344072 | tf_op jit(solution)/shard_map/ppermute | solution.py:523
  20.1 12.9 %collective-permute-start.4 = (bf16[384,256]{1,0:T(8,128)(2,1)S(1)}, bf16[384,256]{1,0:T(8,128)(2,1)S(1)}, u32[]{:S(2)}, u32[]{:S(2)}) collective-permute-start(bf16[384,256]{1,0:T(8,128)(2,1)S(1)} %get-tuple-element.32.both_ref.refs_2_.refs_0_.refs_1_), channel_id=1, source_target_pairs={{0,1},{1,0},{2,3},{3,2},{4,5},{5,4},{6,7},{7,6},{8,9},{9,8},{10,11... | collective-permute-start | bytes 589832 | tf_op jit(solution)/shard_map/ppermute | solution.py:539
  21.4 8.9 %collective-permute-start.5 = (bf16[288,256]{1,0:T(8,128)(2,1)S(1)}, bf16[288,256]{1,0:T(8,128)(2,1)S(1)}, u32[]{:S(2)}, u32[]{:S(2)}) collective-permute-start(bf16[288,256]{1,0:T(8,128)(2,1)S(1)} %get-tuple-element.33), channel_id=1, source_target_pairs={{0,4},{2,6},{4,0},{6,2},{8,12},{10,14},{12,8},{14,10},{16,20},{18,... | collective-permute-start | bytes 442376 | tf_op jit(solution)/shard_map/ppermute | solution.py:523
  22.5 10.4 %collective-permute-start.6 = (bf16[288,256]{1,0:T(8,128)(2,1)S(1)}, bf16[288,256]{1,0:T(8,128)(2,1)S(1)}, u32[]{:S(2)}, u32[]{:S(2)}) collective-permute-start(bf16[288,256]{1,0:T(8,128)(2,1)S(1)} %get-tuple-element.34), channel_id=1, source_target_pairs={{0,5},{1,4},{2,7},{3,6},{4,1},{5,0},{6,3},{7,2},{8,13},{9,12},{10,... | collective-permute-start | bytes 442376 | tf_op jit(solution)/shard_map/ppermute | solution.py:544
  25.3 7.6 %collective-permute-start.10 = (bf16[96,256]{1,0:T(8,128)(2,1)S(1)}, bf16[96,256]{1,0:T(8,128)(2,1)S(1)}, u32[]{:S(2)}, u32[]{:S(2)}) collective-permute-start(bf16[96,256]{1,0:T(8,128)(2,1)S(1)} %face.1), channel_id=1, source_target_pairs={{2,4},{6,8},{10,12},{14,16},{18,20},{22,24},{26,28},{4,2},{8,6},{1... | collective-permute-start | bytes 147464 | tf_op jit(solution)/shard_map/ppermute | solution.py:550
  27.5 5.6 %collective-permute-start.13 = (bf16[832,256]{1,0:T(8,128)(2,1)S(1)}, bf16[832,256]{1,0:T(8,128)(2,1)S(1)}, u32[]{:S(2)}, u32[]{:S(2)}) collective-permute-start(bf16[832,256]{1,0:T(8,128)(2,1)S(1)} %gather_early.1.packed), channel_id=1, source_target_pairs={{0,2},{2,0},{4,6},{6,4},{8,10},{10,8},{12,14},{14,12},{16,18},{18,... | collective-permute-start | bytes 1277960 | tf_op jit(solution)/shard_map/ppermute | solution.py:523
  33.0 3.2 %collective-permute-start.11 = (bf16[1344,256]{1,0:T(8,128)(2,1)S(1)}, bf16[1344,256]{1,0:T(8,128)(2,1)S(1)}, u32[]{:S(2)}, u32[]{:S(2)}) collective-permute-start(bf16[1344,256]{1,0:T(8,128)(2,1)S(1)} %gather_late.1._), channel_id=1, source_target_pairs={{0,2},{2,0},{4,6},{6,4},{8,10},{10,8},{12,14},{14,12},{16,18},{18,... | collective-permute-start | bytes 2064392 | tf_op jit(solution)/shard_map/ppermute | solution.py:523
  39.1 11.2 %collective-permute-start.14 = (bf16[864,128]{1,0:T(8,128)(2,1)S(1)}, bf16[864,128]{1,0:T(8,128)(2,1)S(1)}, u32[]{:S(2)}, u32[]{:S(2)}) collective-permute-start(bf16[864,128]{1,0:T(8,128)(2,1)S(1)} %get-tuple-element.44.refs_10_), channel_id=1, source_target_pairs={{0,8},{2,10},{4,12},{6,14},{8,0},{10,2},{12,4},{14,6},{16,24},{18,... | collective-permute-start | bytes 663560 | tf_op jit(solution)/shard_map/ppermute | solution.py:523
  39.1 18.3 %collective-permute-start.15 = (bf16[864,128]{1,0:T(8,128)(2,1)S(1)}, bf16[864,128]{1,0:T(8,128)(2,1)S(1)}, u32[]{:S(2)}, u32[]{:S(2)}) collective-permute-start(bf16[864,128]{1,0:T(8,128)(2,1)S(1)} %get-tuple-element.48), channel_id=1, source_target_pairs={{0,16},{2,18},{4,20},{6,22},{8,24},{10,26},{12,28},{14,30},{16,0},... | collective-permute-start | bytes 663560 | tf_op jit(solution)/shard_map/ppermute | solution.py:523
  42.1 20.3 %collective-permute-start.16 = (bf16[864,128]{1,0:T(8,128)(2,1)S(1)}, bf16[864,128]{1,0:T(8,128)(2,1)S(1)}, u32[]{:S(2)}, u32[]{:S(2)}) collective-permute-start(bf16[864,128]{1,0:T(8,128)(2,1)S(1)} %get-tuple-element.49), channel_id=1, source_target_pairs={{0,24},{2,26},{4,28},{6,30},{8,16},{10,18},{12,20},{14,22},{16,8},... | collective-permute-start | bytes 663560 | tf_op jit(solution)/shard_map/ppermute | solution.py:523
  42.6 4.1 %collective-permute-start.12 = (bf16[96,256]{1,0:T(8,128)(2,1)S(1)}, bf16[96,256]{1,0:T(8,128)(2,1)S(1)}, u32[]{:S(2)}, u32[]{:S(2)}) collective-permute-start(bf16[96,256]{1,0:T(8,128)(2,1)S(1)} %collective-permute-done.10.refs_5_.refs_4_), channel_id=1, source_target_pairs={{0,1},{1,0},{2,3},{3,2},{4,5},{5,4},{6,7},{7,6},{8,9},{9,8},{10,11... | collective-permute-start | bytes 147464 | tf_op jit(solution)/shard_map/ppermute | solution.py:539

commit v6 on v5

--- a/solution.py
+++ b/solution.py
@@ -148,16 +148,15 @@
         pltpu.make_async_copy(counts, live_ref, sems.at[1]),
     ]
     for field, ref in enumerate((features, cotangent)):
-        for x in range(4):
-            for slot in range(slots):
-                start = field * 4 * width + x * width + slot * PLANE
-                copies.append(
-                    pltpu.make_async_copy(
-                        ref.at[0, 0, slot, pl.ds(x * PLANE, PLANE)],
-                        own_ref.at[pl.ds(start, PLANE)],
-                        sems.at[len(copies)],
-                    )
+        planes = own_ref.at[pl.ds(field * 4 * width, 4 * width)].reshape(4, slots, PLANE, C)
+        for slot in range(slots):
+            copies.append(
+                pltpu.make_async_copy(
+                    ref.at[0, 0, slot].reshape(4, PLANE, C),
+                    planes.at[:, slot],
+                    sems.at[len(copies)],
                 )
+            )
     for copy in copies:
         copy.start()
     for copy in copies:
@@ -597,7 +596,7 @@
         [
             pltpu.SMEM((1, slots), jnp.int32),
             pltpu.SMEM((1, 1), jnp.int32),
-            pltpu.SemaphoreType.DMA((2 + 8 * slots,)),
+            pltpu.SemaphoreType.DMA((2 + 2 * slots,)),
         ],
         [HBM] * 4,
     )

time: 63.5 us -> 63.3 us (level)
  no operation moved by 1% of the time
where the time goes in v6:
time: 63.3 us; the launch traced here: 63.1 us
  waiting for transfers between devices  22 us (35%)
  Pallas kernels  19.1 us (30%)
  starting transfers between devices  18.8 us (30%)
  local copies, waits for them, and re-layouts  1.73 us (3%)
  between operations  1.46 us (2%)
    pallas_call x13, Pallas kernels, call(): pl.pallas_call(kernel, out_shape=outs, in_specs=specs or [VMEM] * len(arg...  19.1 us
    ppermute x10, waiting for transfers between devices, swap(): lax.ppermute(cells, axis, [(i, i ^ bit) for i in range(lax.axis_size(axis...  12.2 us
    ppermute x10, starting transfers between devices, swap(): lax.ppermute(cells, axis, [(i, i ^ bit) for i in range(lax.axis_size(axis...  8.34 us
    ppermute x2, starting transfers between devices, from_far(): far = lax.ppermute(face, 'gx', far_steps(lax.axis_size('gx')))  4.93 us
    ppermute x4, starting transfers between devices, from_sides(): lax.ppermute(cells, 'gy', step)  4.4 us
    ppermute x2, waiting for transfers between devices, from_far(): far = lax.ppermute(face, 'gx', far_steps(lax.axis_size('gx')))  4.02 us
    ppermute x4, waiting for transfers between devices, from_sides(): lax.ppermute(cells, 'gy', step)  3.21 us
    ppermute x1, waiting for transfers between devices, across(): lax.ppermute(face, ('gx', 'gy'), [(a * gy + c, b * gy + d) for a, b in gx...  2.58 us
  transfers between devices with their start and end apart: 17, of which 5 were waited for; matrix products, arithmetic and copies ran while one was open for 0% of the time, Pallas kernels for 23%

profile of v6, /device:TPU:8, one launch (start us, length us, event | category | flops | bytes accessed | tf_op | source)
XLA Modules:
  0.0 63.1 jit_solution(10532794234237358757)
XLA Ops:
  1.3 1.7 %pack.1 = (bf16[400,256]{1,0:T(8,128)(2,1)}, bf16[112,256]{1,0:T(8,128)(2,1)}) custom-call(bf16[1,1,3,64,256]{4,3,2,1,0:T(8,128)(2,1)} %features.1, bf16[1,1,3,64,256]{4,3,2,1,0:T(8,128)(2,1)} %cotangent.1, s32[1,1,3]{2,1,0:T(1,128)} %coords.1, s32[1,1]{1,0:T(1,128)S(6)} %copy.10.counts), custom_call_target="tpu_custom_call" | custom-call | flops 3300000000 | bytes 1048576 | tf_op jit(solution)/shard_map/pack/pallas_call | solution.py:573
  2.9 1.6 %collective-permute-start = (bf16[400,256]{1,0:T(8,128)(2,1)}, bf16[400,256]{1,0:T(8,128)(2,1)S(1)}, u32[]{:S(2)}, u32[]{:S(2)}) collective-permute-start(bf16[400,256]{1,0:T(8,128)(2,1)} %get-tuple-element.27.refs_0_), channel_id=1, source_target_pairs={{0,1},{1,0},{2,3},{3,2},{4,5},{5,4},{6,7},{7,6},{8,9},{9,8},{10,11... | collective-permute-start | bytes 614408 | tf_op jit(solution)/shard_map/ppermute | solution.py:538
  4.5 2.8 %collective-permute-start.1 = (bf16[112,256]{1,0:T(8,128)(2,1)}, bf16[112,256]{1,0:T(8,128)(2,1)S(1)}, u32[]{:S(2)}, u32[]{:S(2)}) collective-permute-start(bf16[112,256]{1,0:T(8,128)(2,1)} %get-tuple-element.28), channel_id=1, source_target_pairs={{2,4},{6,8},{10,12},{14,16},{18,20},{22,24},{26,28},{4,2},{8,6},{1... | collective-permute-start | bytes 172040 | tf_op jit(solution)/shard_map/ppermute | solution.py:549
  7.4 4.0 %collective-permute-done.1.refs_2_.refs_0_ = bf16[112,256]{1,0:T(8,128)(2,1)S(1)} collective-permute-done((bf16[112,256]{1,0:T(8,128)(2,1)}, bf16[112,256]{1,0:T(8,128)(2,1)S(1)}, u32[]{:S(2)}, u32[]{:S(2)}) %collective-permute-start.1) | collective-permute-done | bytes 57376 | tf_op jit(solution)/shard_map/ppermute | solution.py:549
  11.4 0.0 collective-permute-done.refs_1_
  11.4 0.9 %copy-done.2 = bf16[400,256]{1,0:T(8,128)(2,1)S(1)} copy-done((bf16[400,256]{1,0:T(8,128)(2,1)S(1)}, bf16[400,256]{1,0:T(8,128)(2,1)}, u32[]{:S(2)}) %copy-start.2) | copy-done | bytes 204824
  12.3 0.1 join.1
  12.4 0.1 collective-permute-start.2
  12.5 0.6 collective-permute-start.3
  13.0 1.1 %collective-permute-start.8 = (bf16[608,256]{1,0:T(8,128)(2,1)S(1)}, bf16[608,256]{1,0:T(8,128)(2,1)S(1)}, u32[]{:S(2)}, u32[]{:S(2)}) collective-permute-start(bf16[608,256]{1,0:T(8,128)(2,1)S(1)} %get-tuple-element.35), channel_id=1, source_target_pairs={{0,4},{2,6},{4,0},{6,2},{8,12},{10,14},{12,8},{14,10},{16,20},{18,... | collective-permute-start | bytes 933896 | tf_op jit(solution)/shard_map/ppermute | solution.py:522
  14.2 0.0 collective-permute-done.2.refs_1_
  14.2 0.0 copy-done
  14.2 0.0 copy-done.1
  14.2 3.0 %first_convs.1 = (f32[192,256]{1,0:T(8,128)S(1)}, f32[192,256]{1,0:T(8,128)S(1)}) custom-call(bf16[800,256]{1,0:T(8,128)(2,1)S(1)} %get-tuple-element.29.refs_0_, bf16[800,256]{1,0:T(8,128)(2,1)S(1)} %collective-permute-done.2.refs_1_, bf16[6912,256]{1,0:T(8,128)(2,1)S(1)} %copy-done, bf16[6912,256]{1,0:T(8,128)(2,1)S(1)} %copy-done.1), custom_call_target="tpu_custom_call" | custom-call | flops 3300000000 | bytes 1048576 | tf_op jit(solution)/shard_map/first_convs/pallas_call | solution.py:573
  17.2 0.0 collective-permute-done.3.refs_3_.refs_1_
  17.2 0.2 collective-permute-start.7
  17.4 1.0 %collective-permute-start.9 = (bf16[224,256]{1,0:T(8,128)(2,1)S(1)}, bf16[224,256]{1,0:T(8,128)(2,1)S(1)}, u32[]{:S(2)}, u32[]{:S(2)}) collective-permute-start(bf16[224,256]{1,0:T(8,128)(2,1)S(1)} %far_faces.1.refs_2_), channel_id=1, source_target_pairs={{0,4},{2,6},{4,0},{6,2},{8,12},{10,14},{12,8},{14,10},{16,20},{18,... | collective-permute-start | bytes 344072 | tf_op jit(solution)/shard_map/ppermute | solution.py:522
  18.5 1.4 %layer.1 = (bf16[384,256]{1,0:T(8,128)(2,1)S(1)}, bf16[288,256]{1,0:T(8,128)(2,1)S(1)}, bf16[288,256]{1,0:T(8,128)(2,1)S(1)}, f32[2,512]{1,0:T(2,128)S(1)}, f32[432,1]{1,0:T(8,128)S(1)}) custom-call(bf16[800,256]{1,0:T(8,128)(2,1)S(1)} %get-tuple-element.29.refs_0_, bf16[800,256]{1,0:T(8,128)(2,1)S(1)} %collective-permute-done.2.refs_1_, ...), custom_call_target="tpu_custom_call" | custom-call | flops 1100000000 | bytes 1048576 | tf_op jit(solution)/shard_map/layer/pallas_call | solution.py:573
  19.8 1.4 %collective-permute-start.4 = (bf16[384,256]{1,0:T(8,128)(2,1)S(1)}, bf16[384,256]{1,0:T(8,128)(2,1)S(1)}, u32[]{:S(2)}, u32[]{:S(2)}) collective-permute-start(bf16[384,256]{1,0:T(8,128)(2,1)S(1)} %get-tuple-element.32.both_ref.refs_2_.refs_0_.refs_1_), channel_id=1, source_target_pairs={{0,1},{1,0},{2,3},{3,2},{4,5},{5,4},{6,7},{7,6},{8,9},{9,8},{10,11... | collective-permute-start | bytes 589832 | tf_op jit(solution)/shard_map/ppermute | solution.py:538
  21.2 1.1 %collective-permute-start.5 = (bf16[288,256]{1,0:T(8,128)(2,1)S(1)}, bf16[288,256]{1,0:T(8,128)(2,1)S(1)}, u32[]{:S(2)}, u32[]{:S(2)}) collective-permute-start(bf16[288,256]{1,0:T(8,128)(2,1)S(1)} %get-tuple-element.33), channel_id=1, source_target_pairs={{0,4},{2,6},{4,0},{6,2},{8,12},{10,14},{12,8},{14,10},{16,20},{18,... | collective-permute-start | bytes 442376 | tf_op jit(solution)/shard_map/ppermute | solution.py:522
  22.3 0.0 collective-permute-done.7.refs_3_
  22.3 1.1 %collective-permute-start.6 = (bf16[288,256]{1,0:T(8,128)(2,1)S(1)}, bf16[288,256]{1,0:T(8,128)(2,1)S(1)}, u32[]{:S(2)}, u32[]{:S(2)}) collective-permute-start(bf16[288,256]{1,0:T(8,128)(2,1)S(1)} %get-tuple-element.34), channel_id=1, source_target_pairs={{0,5},{1,4},{2,7},{3,6},{4,1},{5,0},{6,3},{7,2},{8,13},{9,12},{10,... | collective-permute-start | bytes 442376 | tf_op jit(solution)/shard_map/ppermute | solution.py:543
  23.4 1.7 %chip_cols.3 = (bf16[2,9,288,256]{3,2,1,0:T(8,128)(2,1)S(1)}, bf16[2,9,288,128]{3,2,1,0:T(8,128)(2,1)S(1)}) custom-call(bf16[800,256]{1,0:T(8,128)(2,1)S(1)} %get-tuple-element.29.refs_0_, bf16[800,256]{1,0:T(8,128)(2,1)S(1)} %collective-permute-done.2.refs_1_, bf16[224,256]{1,0:T(8,128)(2,1)S(1)} %far_faces.1.refs_2_, ...), custom_call_target="tpu_custom_call" | custom-call | flops 1760000000 | bytes 1048576 | tf_op jit(solution)/shard_map/chip_cols/pallas_call | solution.py:573
  25.1 0.0 collective-permute-done.8.refs_4_.refs_0_
  25.1 2.1 %collective-permute-start.10 = (bf16[96,256]{1,0:T(8,128)(2,1)S(1)}, bf16[96,256]{1,0:T(8,128)(2,1)S(1)}, u32[]{:S(2)}, u32[]{:S(2)}) collective-permute-start(bf16[96,256]{1,0:T(8,128)(2,1)S(1)} %face.1), channel_id=1, source_target_pairs={{2,4},{6,8},{10,12},{14,16},{18,20},{22,24},{26,28},{4,2},{8,6},{1... | collective-permute-start | bytes 147464 | tf_op jit(solution)/shard_map/ppermute | solution.py:549
  27.2 0.0 collective-permute-done.9.refs_5_.refs_1_
  27.3 1.2 %collective-permute-start.13 = (bf16[832,256]{1,0:T(8,128)(2,1)S(1)}, bf16[832,256]{1,0:T(8,128)(2,1)S(1)}, u32[]{:S(2)}, u32[]{:S(2)}) collective-permute-start(bf16[832,256]{1,0:T(8,128)(2,1)S(1)} %gather_early.1.packed), channel_id=1, source_target_pairs={{0,2},{2,0},{4,6},{6,4},{8,10},{10,8},{12,14},{14,12},{16,18},{18,... | collective-permute-start | bytes 1277960 | tf_op jit(solution)/shard_map/ppermute | solution.py:522
  28.4 1.7 %chip_cols.2 = (bf16[2,9,288,256]{3,2,1,0:T(8,128)(2,1)S(1)}, bf16[2,9,288,128]{3,2,1,0:T(8,128)(2,1)S(1)}) custom-call(bf16[800,256]{1,0:T(8,128)(2,1)S(1)} %get-tuple-element.29.refs_0_, bf16[800,256]{1,0:T(8,128)(2,1)S(1)} %collective-permute-done.2.refs_1_, bf16[224,256]{1,0:T(8,128)(2,1)S(1)} %far_faces.1.refs_2_, ...), custom_call_target="tpu_custom_call" | custom-call | flops 1760000000 | bytes 1048576 | tf_op jit(solution)/shard_map/chip_cols/pallas_call | solution.py:573
  30.1 0.0 collective-permute-done.5.refs_0_.refs_2_
  30.1 2.6 %collective-permute-done.6.refs_1_.refs_3_ = bf16[288,256]{1,0:T(8,128)(2,1)S(1)} collective-permute-done((bf16[288,256]{1,0:T(8,128)(2,1)S(1)}, bf16[288,256]{1,0:T(8,128)(2,1)S(1)}, u32[]{:S(2)}, u32[]{:S(2)}) %collective-permute-start.6) | collective-permute-done | bytes 147488 | tf_op jit(solution)/shard_map/ppermute | solution.py:543
  32.7 0.0 collective-permute-done.10.refs_5_.refs_4_
  32.7 0.0 collective-permute-done.4.refs_3_.refs_1_.refs_2_
  32.8 0.1 collective-permute-start.11
  32.9 0.0 collective-permute-done.13.near_packed
  32.9 3.1 %other_cols.1 = (bf16[4,9,288,256]{3,2,1,0:T(8,128)(2,1)S(1)}, bf16[4,9,288,128]{3,2,1,0:T(8,128)(2,1)S(1)}) custom-call(bf16[832,256]{1,0:T(8,128)(2,1)S(1)} %gather_early.1.packed, bf16[832,256]{1,0:T(8,128)(2,1)S(1)} %collective-permute-done.13.near_packed, bf16[1344,256]{1,0:T(8,128)(2,1)S(1)} %gather_late.1._), custom_call_target="tpu_custom_call" | custom-call | flops 3300000000 | bytes 1048576 | tf_op jit(solution)/shard_map/other_cols/pallas_call | solution.py:573
  35.9 0.0 collective-permute-done.11.refs_4_.refs_3_
  36.0 2.9 %group_terms.1 = (f32[864,128]{1,0:T(8,128)S(1)}, bf16[864,128]{1,0:T(8,128)(2,1)S(1)}, bf16[864,128]{1,0:T(8,128)(2,1)S(1)}, bf16[864,128]{1,0:T(8,128)(2,1)S(1)}) custom-call(bf16[384,256]{1,0:T(8,128)(2,1)S(1)} %get-tuple-element.32.both_ref.refs_2_.refs_0_.refs_1_, bf16[384,256]{1,0:T(8,128)(2,1)S(1)} %collective-permute-done.4.refs_3_.refs_1_.refs_2_, ...), custom_call_target="tpu_custom_call" | custom-call | flops 3849999872 | bytes 1048576 | tf_op jit(solution)/shard_map/group_terms/pallas_call | solution.py:573
  38.8 0.1 collective-permute-start.14
  38.9 3.0 %collective-permute-start.15 = (bf16[864,128]{1,0:T(8,128)(2,1)S(1)}, bf16[864,128]{1,0:T(8,128)(2,1)S(1)}, u32[]{:S(2)}, u32[]{:S(2)}) collective-permute-start(bf16[864,128]{1,0:T(8,128)(2,1)S(1)} %get-tuple-element.48), channel_id=1, source_target_pairs={{0,16},{2,18},{4,20},{6,22},{8,24},{10,26},{12,28},{14,30},{16,0},... | collective-permute-start | bytes 663560 | tf_op jit(solution)/shard_map/ppermute | solution.py:522
  41.9 0.5 collective-permute-start.16
  42.4 0.9 %collective-permute-start.12 = (bf16[96,256]{1,0:T(8,128)(2,1)S(1)}, bf16[96,256]{1,0:T(8,128)(2,1)S(1)}, u32[]{:S(2)}, u32[]{:S(2)}) collective-permute-start(bf16[96,256]{1,0:T(8,128)(2,1)S(1)} %collective-permute-done.10.refs_5_.refs_4_), channel_id=1, source_target_pairs={{0,1},{1,0},{2,3},{3,2},{4,5},{5,4},{6,7},{7,6},{8,9},{9,8},{10,11... | collective-permute-start | bytes 147464 | tf_op jit(solution)/shard_map/ppermute | solution.py:538
  43.3 3.2 %collective-permute-done.12.refs_5_ = bf16[96,256]{1,0:T(8,128)(2,1)S(1)} collective-permute-done((bf16[96,256]{1,0:T(8,128)(2,1)S(1)}, bf16[96,256]{1,0:T(8,128)(2,1)S(1)}, u32[]{:S(2)}, u32[]{:S(2)}) %collective-permute-start.12) | collective-permute-done | bytes 49184 | tf_op jit(solution)/shard_map/ppermute | solution.py:538
  46.5 3.6 %last_layer.1 = (f32[3,64,256]{2,1,0:T(8,128)}, f32[3,64,256]{2,1,0:T(8,128)}) custom-call(bf16[800,256]{1,0:T(8,128)(2,1)S(1)} %get-tuple-element.29.refs_0_, bf16[384,256]{1,0:T(8,128)(2,1)S(1)} %get-tuple-element.32.both_ref.refs_2_.refs_0_.refs_1_, bf16[384,256]{1,0:T(8,128)(2,1)S(1)} %collective-permute-done.4.refs_3_.refs_1_.refs_2_, ...), custom_call_target="tpu_custom_call" | custom-call | flops 110000000 | bytes 1048576 | tf_op jit(solution)/shard_map/last_layer/pallas_call | solution.py:573
  50.1 0.0 collective-permute-done.14
  50.1 7.2 %collective-permute-done.15 = bf16[864,128]{1,0:T(8,128)(2,1)S(1)} collective-permute-done((bf16[864,128]{1,0:T(8,128)(2,1)S(1)}, bf16[864,128]{1,0:T(8,128)(2,1)S(1)}, u32[]{:S(2)}, u32[]{:S(2)}) %collective-permute-start.15) | collective-permute-done | bytes 221216 | tf_op jit(solution)/shard_map/ppermute | solution.py:522
  57.2 5.0 %collective-permute-done.16 = bf16[864,128]{1,0:T(8,128)(2,1)S(1)} collective-permute-done((bf16[864,128]{1,0:T(8,128)(2,1)S(1)}, bf16[864,128]{1,0:T(8,128)(2,1)S(1)}, u32[]{:S(2)}, u32[]{:S(2)}) %collective-permute-start.16) | collective-permute-done | bytes 221216 | tf_op jit(solution)/shard_map/ppermute | solution.py:522
  62.2 0.1 add_multiply_fusion
  62.3 0.8 %fusion = (f32[432,128]{1,0:T(8,128)}, f32[432,128]{1,0:T(8,128)}) fusion(f32[864,128]{1,0:T(8,128)S(1)} %add_multiply_fusion), kind=kLoop, calls=%fused_computation.1 | loop fusion | bytes 884736 | tf_op jit(solution)/shard_map/slice | solution.py:740
  (7 shorter events, 0.1 us)
Async XLA Ops:
  2.9 8.4 %collective-permute-start = (bf16[400,256]{1,0:T(8,128)(2,1)}, bf16[400,256]{1,0:T(8,128)(2,1)S(1)}, u32[]{:S(2)}, u32[]{:S(2)}) collective-permute-start(bf16[400,256]{1,0:T(8,128)(2,1)} %get-tuple-element.27.refs_0_), channel_id=1, source_target_pairs={{0,1},{1,0},{2,3},{3,2},{4,5},{5,4},{6,7},{7,6},{8,9},{9,8},{10,11... | collective-permute-start | bytes 614408 | tf_op jit(solution)/shard_map/ppermute | solution.py:538
  4.5 9.7 %copy-start = (bf16[6912,256]{1,0:T(8,128)(2,1)S(1)}, bf16[6912,256]{1,0:T(8,128)(2,1)}, u32[]{:S(2)}) copy-start(bf16[6912,256]{1,0:T(8,128)(2,1)} %refs_6_.1) | copy-start | bytes 10616836
  4.5 9.7 %copy-start.1 = (bf16[6912,256]{1,0:T(8,128)(2,1)S(1)}, bf16[6912,256]{1,0:T(8,128)(2,1)}, u32[]{:S(2)}) copy-start(bf16[6912,256]{1,0:T(8,128)(2,1)} %refs_7_.1) | copy-start | bytes 10616836
  4.5 6.9 %collective-permute-start.1 = (bf16[112,256]{1,0:T(8,128)(2,1)}, bf16[112,256]{1,0:T(8,128)(2,1)S(1)}, u32[]{:S(2)}, u32[]{:S(2)}) collective-permute-start(bf16[112,256]{1,0:T(8,128)(2,1)} %get-tuple-element.28), channel_id=1, source_target_pairs={{2,4},{6,8},{10,12},{14,16},{18,20},{22,24},{26,28},{4,2},{8,6},{1... | collective-permute-start | bytes 172040 | tf_op jit(solution)/shard_map/ppermute | solution.py:549
  11.4 0.9 %copy-start.2 = (bf16[400,256]{1,0:T(8,128)(2,1)S(1)}, bf16[400,256]{1,0:T(8,128)(2,1)}, u32[]{:S(2)}) copy-start(bf16[400,256]{1,0:T(8,128)(2,1)} %get-tuple-element.27.refs_0_) | copy-start | bytes 614404
  12.4 1.8 %collective-permute-start.2 = (bf16[800,256]{1,0:T(8,128)(2,1)S(1)}, bf16[800,256]{1,0:T(8,128)(2,1)S(1)}, u32[]{:S(2)}, u32[]{:S(2)}) collective-permute-start(bf16[800,256]{1,0:T(8,128)(2,1)S(1)} %get-tuple-element.29.refs_0_), channel_id=1, source_target_pairs={{0,2},{2,0},{4,6},{6,4},{8,10},{10,8},{12,14},{14,12},{16,18},{18,... | collective-permute-start | bytes 1228808 | tf_op jit(solution)/shard_map/ppermute | solution.py:522
  12.5 4.7 %collective-permute-start.3 = (bf16[112,256]{1,0:T(8,128)(2,1)S(1)}, bf16[112,256]{1,0:T(8,128)(2,1)S(1)}, u32[]{:S(2)}, u32[]{:S(2)}) collective-permute-start(bf16[112,256]{1,0:T(8,128)(2,1)S(1)} %collective-permute-done.1.refs_2_.refs_0_), channel_id=1, source_target_pairs={{0,1},{1,0},{2,3},{3,2},{4,5},{5,4},{6,7},{7,6},{8,9},{9,8},{10,11... | collective-permute-start | bytes 172040 | tf_op jit(solution)/shard_map/ppermute | solution.py:538
  13.0 12.1 %collective-permute-start.8 = (bf16[608,256]{1,0:T(8,128)(2,1)S(1)}, bf16[608,256]{1,0:T(8,128)(2,1)S(1)}, u32[]{:S(2)}, u32[]{:S(2)}) collective-permute-start(bf16[608,256]{1,0:T(8,128)(2,1)S(1)} %get-tuple-element.35), channel_id=1, source_target_pairs={{0,4},{2,6},{4,0},{6,2},{8,12},{10,14},{12,8},{14,10},{16,20},{18,... | collective-permute-start | bytes 933896 | tf_op jit(solution)/shard_map/ppermute | solution.py:522
  17.2 5.1 %collective-permute-start.7 = (bf16[224,256]{1,0:T(8,128)(2,1)S(1)}, bf16[224,256]{1,0:T(8,128)(2,1)S(1)}, u32[]{:S(2)}, u32[]{:S(2)}) collective-permute-start(bf16[224,256]{1,0:T(8,128)(2,1)S(1)} %far_faces.1.refs_2_), channel_id=1, source_target_pairs={{0,2},{2,0},{4,6},{6,4},{8,10},{10,8},{12,14},{14,12},{16,18},{18,... | collective-permute-start | bytes 344072 | tf_op jit(solution)/shard_map/ppermute | solution.py:522
  17.4 9.8 %collective-permute-start.9 = (bf16[224,256]{1,0:T(8,128)(2,1)S(1)}, bf16[224,256]{1,0:T(8,128)(2,1)S(1)}, u32[]{:S(2)}, u32[]{:S(2)}) collective-permute-start(bf16[224,256]{1,0:T(8,128)(2,1)S(1)} %far_faces.1.refs_2_), channel_id=1, source_target_pairs={{0,4},{2,6},{4,0},{6,2},{8,12},{10,14},{12,8},{14,10},{16,20},{18,... | collective-permute-start | bytes 344072 | tf_op jit(solution)/shard_map/ppermute | solution.py:522
  19.8 12.9 %collective-permute-start.4 = (bf16[384,256]{1,0:T(8,128)(2,1)S(1)}, bf16[384,256]{1,0:T(8,128)(2,1)S(1)}, u32[]{:S(2)}, u32[]{:S(2)}) collective-permute-start(bf16[384,256]{1,0:T(8,128)(2,1)S(1)} %get-tuple-element.32.both_ref.refs_2_.refs_0_.refs_1_), channel_id=1, source_target_pairs={{0,1},{1,0},{2,3},{3,2},{4,5},{5,4},{6,7},{7,6},{8,9},{9,8},{10,11... | collective-permute-start | bytes 589832 | tf_op jit(solution)/shard_map/ppermute | solution.py:538
  21.2 8.9 %collective-permute-start.5 = (bf16[288,256]{1,0:T(8,128)(2,1)S(1)}, bf16[288,256]{1,0:T(8,128)(2,1)S(1)}, u32[]{:S(2)}, u32[]{:S(2)}) collective-permute-start(bf16[288,256]{1,0:T(8,128)(2,1)S(1)} %get-tuple-element.33), channel_id=1, source_target_pairs={{0,4},{2,6},{4,0},{6,2},{8,12},{10,14},{12,8},{14,10},{16,20},{18,... | collective-permute-start | bytes 442376 | tf_op jit(solution)/shard_map/ppermute | solution.py:522
  22.3 10.4 %collective-permute-start.6 = (bf16[288,256]{1,0:T(8,128)(2,1)S(1)}, bf16[288,256]{1,0:T(8,128)(2,1)S(1)}, u32[]{:S(2)}, u32[]{:S(2)}) collective-permute-start(bf16[288,256]{1,0:T(8,128)(2,1)S(1)} %get-tuple-element.34), channel_id=1, source_target_pairs={{0,5},{1,4},{2,7},{3,6},{4,1},{5,0},{6,3},{7,2},{8,13},{9,12},{10,... | collective-permute-start | bytes 442376 | tf_op jit(solution)/shard_map/ppermute | solution.py:543
  25.1 7.6 %collective-permute-start.10 = (bf16[96,256]{1,0:T(8,128)(2,1)S(1)}, bf16[96,256]{1,0:T(8,128)(2,1)S(1)}, u32[]{:S(2)}, u32[]{:S(2)}) collective-permute-start(bf16[96,256]{1,0:T(8,128)(2,1)S(1)} %face.1), channel_id=1, source_target_pairs={{2,4},{6,8},{10,12},{14,16},{18,20},{22,24},{26,28},{4,2},{8,6},{1... | collective-permute-start | bytes 147464 | tf_op jit(solution)/shard_map/ppermute | solution.py:549
  27.3 5.6 %collective-permute-start.13 = (bf16[832,256]{1,0:T(8,128)(2,1)S(1)}, bf16[832,256]{1,0:T(8,128)(2,1)S(1)}, u32[]{:S(2)}, u32[]{:S(2)}) collective-permute-start(bf16[832,256]{1,0:T(8,128)(2,1)S(1)} %gather_early.1.packed), channel_id=1, source_target_pairs={{0,2},{2,0},{4,6},{6,4},{8,10},{10,8},{12,14},{14,12},{16,18},{18,... | collective-permute-start | bytes 1277960 | tf_op jit(solution)/shard_map/ppermute | solution.py:522
  32.8 3.2 %collective-permute-start.11 = (bf16[1344,256]{1,0:T(8,128)(2,1)S(1)}, bf16[1344,256]{1,0:T(8,128)(2,1)S(1)}, u32[]{:S(2)}, u32[]{:S(2)}) collective-permute-start(bf16[1344,256]{1,0:T(8,128)(2,1)S(1)} %gather_late.1._), channel_id=1, source_target_pairs={{0,2},{2,0},{4,6},{6,4},{8,10},{10,8},{12,14},{14,12},{16,18},{18,... | collective-permute-start | bytes 2064392 | tf_op jit(solution)/shard_map/ppermute | solution.py:522
  38.8 11.2 %collective-permute-start.14 = (bf16[864,128]{1,0:T(8,128)(2,1)S(1)}, bf16[864,128]{1,0:T(8,128)(2,1)S(1)}, u32[]{:S(2)}, u32[]{:S(2)}) collective-permute-start(bf16[864,128]{1,0:T(8,128)(2,1)S(1)} %get-tuple-element.44.refs_10_), channel_id=1, source_target_pairs={{0,8},{2,10},{4,12},{6,14},{8,0},{10,2},{12,4},{14,6},{16,24},{18,... | collective-permute-start | bytes 663560 | tf_op jit(solution)/shard_map/ppermute | solution.py:522
  38.9 18.3 %collective-permute-start.15 = (bf16[864,128]{1,0:T(8,128)(2,1)S(1)}, bf16[864,128]{1,0:T(8,128)(2,1)S(1)}, u32[]{:S(2)}, u32[]{:S(2)}) collective-permute-start(bf16[864,128]{1,0:T(8,128)(2,1)S(1)} %get-tuple-element.48), channel_id=1, source_target_pairs={{0,16},{2,18},{4,20},{6,22},{8,24},{10,26},{12,28},{14,30},{16,0},... | collective-permute-start | bytes 663560 | tf_op jit(solution)/shard_map/ppermute | solution.py:522
  41.9 20.3 %collective-permute-start.16 = (bf16[864,128]{1,0:T(8,128)(2,1)S(1)}, bf16[864,128]{1,0:T(8,128)(2,1)S(1)}, u32[]{:S(2)}, u32[]{:S(2)}) collective-permute-start(bf16[864,128]{1,0:T(8,128)(2,1)S(1)} %get-tuple-element.49), channel_id=1, source_target_pairs={{0,24},{2,26},{4,28},{6,30},{8,16},{10,18},{12,20},{14,22},{16,8},... | collective-permute-start | bytes 663560 | tf_op jit(solution)/shard_map/ppermute | solution.py:522
  42.4 4.1 %collective-permute-start.12 = (bf16[96,256]{1,0:T(8,128)(2,1)S(1)}, bf16[96,256]{1,0:T(8,128)(2,1)S(1)}, u32[]{:S(2)}, u32[]{:S(2)}) collective-permute-start(bf16[96,256]{1,0:T(8,128)(2,1)S(1)} %collective-permute-done.10.refs_5_.refs_4_), channel_id=1, source_target_pairs={{0,1},{1,0},{2,3},{3,2},{4,5},{5,4},{6,7},{7,6},{8,9},{9,8},{10,11... | collective-permute-start | bytes 147464 | tf_op jit(solution)/shard_map/ppermute | solution.py:538

commit v7 on v6

--- a/solution.py
+++ b/solution.py
@@ -74,7 +74,7 @@
 
 def fill(cols_ref, tiles, faces, odd, chosen, width, columns=slice(None)):
     def load(source, plane):
-        ref, first, paired = source
+        ref, first, paired = source[:3]
         if paired:
             at = first + plane % 2 * width
             return ref[at : at + width, plane // 2 * (C // 2) : (plane // 2 + 1) * (C // 2)]
@@ -88,7 +88,7 @@
                 if far is None:
                     pieces.append(load(near, start))
                     continue
-                near, far = load(near, start), load(far, 0)
+                near, far = load(near, start), load(far, far[3])
                 pieces.append(jnp.where(odd, near, far) if plane == 0 else jnp.where(odd, far, near))
         else:
             pieces = [load(tile, plane - 1) for tile in tiles]
@@ -211,8 +211,9 @@
             if self.fars is None:
                 far = jnp.zeros_like(near)
             else:
-                ref, first = self.fars[j][o]
-                far = meta(ref, first + 2 * self.width)
+                ref, first, *side = self.fars[j][o]
+                places = 3 * self.width + side[0] * META if side else 2 * self.width
+                far = meta(ref, first + places)
             befores.append(jnp.where(self.odd(j), near, far))
             afters.append(jnp.where(self.odd(j), far, near))
         before, after = (
@@ -231,8 +232,12 @@
         for o in order:
             far = None
             if self.fars is not None:
-                ref, first = self.fars[j][o]
-                far = (ref, first + field * self.width, False)
+                ref, first, *side = self.fars[j][o]
+                far = (ref, first + field * self.width, False, 0)
+                if side and field:
+                    far = (ref, first + 2 * self.width, True, 2 * side[0])
+                elif side:
+                    far = (ref, first + side[0] * self.width, False, 0)
             faces.append((tile(j ^ 1, o), far))
         return [tile(j, o) for o in order], faces, self.odd(j)
 
@@ -331,6 +336,18 @@
         slim_ref[rows + rows // 2 :, :] = tile_ref[2 * rows :, :]
 
 
+def slim_faces_kernel(far, side_far, _, slim_ref):
+    width = (far.shape[0] - META) // 2
+    columns = my_columns(C // 2)
+    for s, ref in enumerate((far, side_far)):
+        slim_ref[s * width : (s + 1) * width, :] = ref[:width, :]
+        slim_ref[2 * width : 3 * width, s * (C // 2) : (s + 1) * (C // 2)] = ref[
+            width : 2 * width, columns
+        ]
+        at = 3 * width + s * META
+        slim_ref[at : at + META, :] = ref[2 * width :, :]
+
+
 def gather_kernel(count, *refs):
     packed_ref = refs[-1]
     at = 0
@@ -405,9 +422,9 @@
 def other_cols_kernel(packed, near_packed, _, feature_ref, seed_ref):
     width = feature_ref.shape[2] // 6
     rows = 8 * width
-    thin, face = 6 * width + META, 2 * width + META
+    thin = 6 * width + META
     tiles = [[(ref, s * thin, True) for s in range(2)] for ref in (packed, near_packed)]
-    fars = [[(ref, 2 * thin + s * face) for s in range(2)] for ref in (packed, near_packed)]
+    fars = [[(ref, 2 * thin, s) for s in range(2)] for ref in (packed, near_packed)]
     around = Around([None, None] + tiles, [None, None] + fars, 1, rows)
     group_cols(around, OTHER_MEMBERS, feature_ref, seed_ref)
 
@@ -681,9 +698,16 @@
 
         far_faces = gathered("far_faces", fars, main[:1])
         near_faces = swap(far_faces, "gx", 1)
-        beside = [swap(thins, "gx", 2), swap(far_faces, "gx", 2)]
-        early = gathered("gather_early", beside, (both,))
-        near_early = swap(early, "gx", 1)
+        (slim_faces,) = call(
+            slim_faces_kernel,
+            "slim_faces",
+            (shape((3 * width + 2 * META, C)),),
+            (*fars, main[0]),
+            8,
+            0.5,
+            specs=[VMEM] * 2 + [ANY],
+        )
+        beside = [swap(cells, "gx", 2) for cells in (thins, slim_faces)]
         chip_cols = [
             call(
                 functools.partial(chip_cols_kernel, 1, members),
@@ -697,6 +721,8 @@
             for members, after in zip(CHIP_MEMBERS, ((), beside))
         ]
         late_fars = late_far(chip_cols[0][1:])
+        early = gathered("gather_early", beside, chip_cols[0][1:])
+        near_early = swap(early, "gx", 1)
         thin_other = swap(thin, "gx", 2)
         cross_other = across(cross, [(i, i ^ 2) for i in range(gx)], side_steps(gy)[0])
         packed = gathered(

time: 63.3 us -> 62.4 us (0.986)
  waiting for transfers between devices: 22 us -> 20.4 us
    ppermute x10, starting transfers between devices: 8.34 us -> 7.35 us  [swap(): lax.ppermute(cells, axis, [(i, i ^ bit) for i in range(lax.axis_size(axis...]
    ppermute x1, waiting for transfers between devices: 2.58 us -> 1.61 us  [across(): lax.ppermute(face, ('gx', 'gy'), [(a * gy + c, b * gy + d) for a, b in gx...]
    ppermute x2, starting transfers between devices: 4.93 us -> 5.85 us  [from_far(): far = lax.ppermute(face, 'gx', far_steps(lax.axis_size('gx')))]
    pallas_call x13 -> x14, Pallas kernels: 19.1 us -> 19.1 us  [call(): pl.pallas_call(kernel, out_shape=outs, in_specs=specs or [VMEM] * len(arg...]
  transfers between devices with their start and end apart: 17 -> 17, of which waited for: 5 -> 6; matrix products, arithmetic and copies ran while one was open for 0% -> 0% of each run, Pallas kernels for 23% -> 23%
where the time goes in v7:
time: 62.4 us; the launch traced here: 62.1 us
  waiting for transfers between devices  20.4 us (33%)
  starting transfers between devices  19.3 us (31%)
  Pallas kernels  19.1 us (31%)
  local copies, waits for them, and re-layouts  1.73 us (3%)
  between operations  1.46 us (2%)
    pallas_call x14, Pallas kernels, call(): pl.pallas_call(kernel, out_shape=outs, in_specs=specs or [VMEM] * len(arg...  19.1 us
    ppermute x10, waiting for transfers between devices, swap(): lax.ppermute(cells, axis, [(i, i ^ bit) for i in range(lax.axis_size(axis...  12.1 us
    ppermute x10, starting transfers between devices, swap(): lax.ppermute(cells, axis, [(i, i ^ bit) for i in range(lax.axis_size(axis...  7.35 us
    ppermute x2, starting transfers between devices, from_far(): far = lax.ppermute(face, 'gx', far_steps(lax.axis_size('gx')))  5.85 us
    ppermute x4, starting transfers between devices, from_sides(): lax.ppermute(cells, 'gy', step)  4.93 us
    ppermute x2, waiting for transfers between devices, from_far(): far = lax.ppermute(face, 'gx', far_steps(lax.axis_size('gx')))  4.1 us
    ppermute x4, waiting for transfers between devices, from_sides(): lax.ppermute(cells, 'gy', step)  2.62 us
    ppermute x1, waiting for transfers between devices, across(): lax.ppermute(face, ('gx', 'gy'), [(a * gy + c, b * gy + d) for a, b in gx...  1.61 us
  transfers between devices with their start and end apart: 17, of which 6 were waited for; matrix products, arithmetic and copies ran while one was open for 0% of the time, Pallas kernels for 23%

profile of v7, /device:TPU:8, one launch (start us, length us, event | category | flops | bytes accessed | tf_op | source)
XLA Modules:
  0.0 62.1 jit_solution(4420295127007307213)
XLA Ops:
  1.3 1.7 %pack.1 = (bf16[400,256]{1,0:T(8,128)(2,1)}, bf16[112,256]{1,0:T(8,128)(2,1)}) custom-call(bf16[1,1,3,64,256]{4,3,2,1,0:T(8,128)(2,1)} %features.1, bf16[1,1,3,64,256]{4,3,2,1,0:T(8,128)(2,1)} %cotangent.1, s32[1,1,3]{2,1,0:T(1,128)} %coords.1, s32[1,1]{1,0:T(1,128)S(6)} %copy.10.counts), custom_call_target="tpu_custom_call" | custom-call | flops 3300000000 | bytes 1048576 | tf_op jit(solution)/shard_map/pack/pallas_call | solution.py:590
  2.9 1.6 %collective-permute-start = (bf16[400,256]{1,0:T(8,128)(2,1)}, bf16[400,256]{1,0:T(8,128)(2,1)S(1)}, u32[]{:S(2)}, u32[]{:S(2)}) collective-permute-start(bf16[400,256]{1,0:T(8,128)(2,1)} %get-tuple-element.27.refs_0_), channel_id=1, source_target_pairs={{0,1},{1,0},{2,3},{3,2},{4,5},{5,4},{6,7},{7,6},{8,9},{9,8},{10,11... | collective-permute-start | bytes 614408 | tf_op jit(solution)/shard_map/ppermute | solution.py:555
  4.5 2.8 %collective-permute-start.1 = (bf16[112,256]{1,0:T(8,128)(2,1)}, bf16[112,256]{1,0:T(8,128)(2,1)S(1)}, u32[]{:S(2)}, u32[]{:S(2)}) collective-permute-start(bf16[112,256]{1,0:T(8,128)(2,1)} %get-tuple-element.28), channel_id=1, source_target_pairs={{2,4},{6,8},{10,12},{14,16},{18,20},{22,24},{26,28},{4,2},{8,6},{1... | collective-permute-start | bytes 172040 | tf_op jit(solution)/shard_map/ppermute | solution.py:566
  7.4 4.0 %collective-permute-done.1.refs_2_.refs_0_.far = bf16[112,256]{1,0:T(8,128)(2,1)S(1)} collective-permute-done((bf16[112,256]{1,0:T(8,128)(2,1)}, bf16[112,256]{1,0:T(8,128)(2,1)S(1)}, u32[]{:S(2)}, u32[]{:S(2)}) %collective-permute-start.1) | collective-permute-done | bytes 57376 | tf_op jit(solution)/shard_map/ppermute | solution.py:566
  11.4 0.0 collective-permute-done.refs_1_
  11.4 0.9 %copy-done.2 = bf16[400,256]{1,0:T(8,128)(2,1)S(1)} copy-done((bf16[400,256]{1,0:T(8,128)(2,1)S(1)}, bf16[400,256]{1,0:T(8,128)(2,1)}, u32[]{:S(2)}) %copy-start.2) | copy-done | bytes 204824
  12.3 0.1 join.1
  12.4 0.1 collective-permute-start.2
  12.5 0.6 collective-permute-start.3
  13.0 1.1 %collective-permute-start.8 = (bf16[608,256]{1,0:T(8,128)(2,1)S(1)}, bf16[608,256]{1,0:T(8,128)(2,1)S(1)}, u32[]{:S(2)}, u32[]{:S(2)}) collective-permute-start(bf16[608,256]{1,0:T(8,128)(2,1)S(1)} %get-tuple-element.35), channel_id=1, source_target_pairs={{0,4},{2,6},{4,0},{6,2},{8,12},{10,14},{12,8},{14,10},{16,20},{18,... | collective-permute-start | bytes 933896 | tf_op jit(solution)/shard_map/ppermute | solution.py:539
  14.2 0.0 collective-permute-done.2.refs_1_
  14.2 0.0 copy-done
  14.2 0.0 copy-done.1
  14.2 3.0 %first_convs.1 = (f32[192,256]{1,0:T(8,128)S(1)}, f32[192,256]{1,0:T(8,128)S(1)}) custom-call(bf16[800,256]{1,0:T(8,128)(2,1)S(1)} %get-tuple-element.29.refs_0_, bf16[800,256]{1,0:T(8,128)(2,1)S(1)} %collective-permute-done.2.refs_1_, bf16[6912,256]{1,0:T(8,128)(2,1)S(1)} %copy-done, bf16[6912,256]{1,0:T(8,128)(2,1)S(1)} %copy-done.1), custom_call_target="tpu_custom_call" | custom-call | flops 3300000000 | bytes 1048576 | tf_op jit(solution)/shard_map/first_convs/pallas_call | solution.py:590
  17.2 0.0 collective-permute-done.3.refs_3_.refs_1_.side_far
  17.2 0.2 collective-permute-start.7
  17.4 1.1 %collective-permute-start.9 = (bf16[176,256]{1,0:T(8,128)(2,1)S(1)}, bf16[176,256]{1,0:T(8,128)(2,1)S(1)}, u32[]{:S(2)}, u32[]{:S(2)}) collective-permute-start(bf16[176,256]{1,0:T(8,128)(2,1)S(1)} %slim_faces.1), channel_id=1, source_target_pairs={{0,4},{2,6},{4,0},{6,2},{8,12},{10,14},{12,8},{14,10},{16,20},{18,... | collective-permute-start | bytes 270344 | tf_op jit(solution)/shard_map/ppermute | solution.py:539
  18.5 1.4 %layer.1 = (bf16[384,256]{1,0:T(8,128)(2,1)S(1)}, bf16[288,256]{1,0:T(8,128)(2,1)S(1)}, bf16[288,256]{1,0:T(8,128)(2,1)S(1)}, f32[2,512]{1,0:T(2,128)S(1)}, f32[432,1]{1,0:T(8,128)S(1)}) custom-call(bf16[800,256]{1,0:T(8,128)(2,1)S(1)} %get-tuple-element.29.refs_0_, bf16[800,256]{1,0:T(8,128)(2,1)S(1)} %collective-permute-done.2.refs_1_, ...), custom_call_target="tpu_custom_call" | custom-call | flops 1100000000 | bytes 1048576 | tf_op jit(solution)/shard_map/layer/pallas_call | solution.py:590
  19.9 1.3 %collective-permute-start.4 = (bf16[384,256]{1,0:T(8,128)(2,1)S(1)}, bf16[384,256]{1,0:T(8,128)(2,1)S(1)}, u32[]{:S(2)}, u32[]{:S(2)}) collective-permute-start(bf16[384,256]{1,0:T(8,128)(2,1)S(1)} %get-tuple-element.32.both_ref.refs_2_.refs_0_.refs_1_), channel_id=1, source_target_pairs={{0,1},{1,0},{2,3},{3,2},{4,5},{5,4},{6,7},{7,6},{8,9},{9,8},{10,11... | collective-permute-start | bytes 589832 | tf_op jit(solution)/shard_map/ppermute | solution.py:555
  21.2 1.1 %collective-permute-start.5 = (bf16[288,256]{1,0:T(8,128)(2,1)S(1)}, bf16[288,256]{1,0:T(8,128)(2,1)S(1)}, u32[]{:S(2)}, u32[]{:S(2)}) collective-permute-start(bf16[288,256]{1,0:T(8,128)(2,1)S(1)} %get-tuple-element.33), channel_id=1, source_target_pairs={{0,4},{2,6},{4,0},{6,2},{8,12},{10,14},{12,8},{14,10},{16,20},{18,... | collective-permute-start | bytes 442376 | tf_op jit(solution)/shard_map/ppermute | solution.py:539
  22.3 0.0 collective-permute-done.7.refs_3_
  22.3 1.2 %collective-permute-start.6 = (bf16[288,256]{1,0:T(8,128)(2,1)S(1)}, bf16[288,256]{1,0:T(8,128)(2,1)S(1)}, u32[]{:S(2)}, u32[]{:S(2)}) collective-permute-start(bf16[288,256]{1,0:T(8,128)(2,1)S(1)} %get-tuple-element.34), channel_id=1, source_target_pairs={{0,5},{1,4},{2,7},{3,6},{4,1},{5,0},{6,3},{7,2},{8,13},{9,12},{10,... | collective-permute-start | bytes 442376 | tf_op jit(solution)/shard_map/ppermute | solution.py:560
  23.5 1.7 %chip_cols.3 = (bf16[2,9,288,256]{3,2,1,0:T(8,128)(2,1)S(1)}, bf16[2,9,288,128]{3,2,1,0:T(8,128)(2,1)S(1)}) custom-call(bf16[800,256]{1,0:T(8,128)(2,1)S(1)} %get-tuple-element.29.refs_0_, bf16[800,256]{1,0:T(8,128)(2,1)S(1)} %collective-permute-done.2.refs_1_, bf16[224,256]{1,0:T(8,128)(2,1)S(1)} %far_faces.1.refs_2_, ...), custom_call_target="tpu_custom_call" | custom-call | flops 1760000000 | bytes 1048576 | tf_op jit(solution)/shard_map/chip_cols/pallas_call | solution.py:590
  25.2 0.0 collective-permute-done.8.refs_4_.refs_0_
  25.2 0.0 collective-permute-done.9.refs_5_.refs_1_
  25.2 0.1 collective-permute-start.13
  25.3 3.0 %collective-permute-start.10 = (bf16[96,256]{1,0:T(8,128)(2,1)S(1)}, bf16[96,256]{1,0:T(8,128)(2,1)S(1)}, u32[]{:S(2)}, u32[]{:S(2)}) collective-permute-start(bf16[96,256]{1,0:T(8,128)(2,1)S(1)} %face.1), channel_id=1, source_target_pairs={{2,4},{6,8},{10,12},{14,16},{18,20},{22,24},{26,28},{4,2},{8,6},{1... | collective-permute-start | bytes 147464 | tf_op jit(solution)/shard_map/ppermute | solution.py:566
  28.4 1.7 %chip_cols.2 = (bf16[2,9,288,256]{3,2,1,0:T(8,128)(2,1)S(1)}, bf16[2,9,288,128]{3,2,1,0:T(8,128)(2,1)S(1)}) custom-call(bf16[800,256]{1,0:T(8,128)(2,1)S(1)} %get-tuple-element.29.refs_0_, bf16[800,256]{1,0:T(8,128)(2,1)S(1)} %collective-permute-done.2.refs_1_, bf16[224,256]{1,0:T(8,128)(2,1)S(1)} %far_faces.1.refs_2_, ...), custom_call_target="tpu_custom_call" | custom-call | flops 1760000000 | bytes 1048576 | tf_op jit(solution)/shard_map/chip_cols/pallas_call | solution.py:590
  30.0 0.0 collective-permute-done.5.refs_0_.refs_2_
  30.1 1.6 %collective-permute-done.6.refs_1_.refs_3_ = bf16[288,256]{1,0:T(8,128)(2,1)S(1)} collective-permute-done((bf16[288,256]{1,0:T(8,128)(2,1)S(1)}, bf16[288,256]{1,0:T(8,128)(2,1)S(1)}, u32[]{:S(2)}, u32[]{:S(2)}) %collective-permute-start.6) | collective-permute-done | bytes 147488 | tf_op jit(solution)/shard_map/ppermute | solution.py:560
  31.7 0.1 collective-permute-done.10.refs_5_.refs_4_
  31.7 0.0 collective-permute-done.4.refs_3_.refs_1_.refs_2_
  31.8 0.1 collective-permute-start.11
  31.9 0.0 collective-permute-done.13.near_packed
  31.9 3.1 %other_cols.1 = (bf16[4,9,288,256]{3,2,1,0:T(8,128)(2,1)S(1)}, bf16[4,9,288,128]{3,2,1,0:T(8,128)(2,1)S(1)}) custom-call(bf16[784,256]{1,0:T(8,128)(2,1)S(1)} %gather_early.1.packed, bf16[784,256]{1,0:T(8,128)(2,1)S(1)} %collective-permute-done.13.near_packed, bf16[1344,256]{1,0:T(8,128)(2,1)S(1)} %gather_late.1._), custom_call_target="tpu_custom_call" | custom-call | flops 3300000000 | bytes 1048576 | tf_op jit(solution)/shard_map/other_cols/pallas_call | solution.py:590
  35.0 0.0 collective-permute-done.11.refs_4_.refs_3_
  35.0 2.9 %group_terms.1 = (f32[864,128]{1,0:T(8,128)S(1)}, bf16[864,128]{1,0:T(8,128)(2,1)S(1)}, bf16[864,128]{1,0:T(8,128)(2,1)S(1)}, bf16[864,128]{1,0:T(8,128)(2,1)S(1)}) custom-call(bf16[384,256]{1,0:T(8,128)(2,1)S(1)} %get-tuple-element.32.both_ref.refs_2_.refs_0_.refs_1_, bf16[384,256]{1,0:T(8,128)(2,1)S(1)} %collective-permute-done.4.refs_3_.refs_1_.refs_2_, ...), custom_call_target="tpu_custom_call" | custom-call | flops 3849999872 | bytes 1048576 | tf_op jit(solution)/shard_map/group_terms/pallas_call | solution.py:590
  37.9 0.1 collective-permute-start.14
  38.0 3.0 %collective-permute-start.15 = (bf16[864,128]{1,0:T(8,128)(2,1)S(1)}, bf16[864,128]{1,0:T(8,128)(2,1)S(1)}, u32[]{:S(2)}, u32[]{:S(2)}) collective-permute-start(bf16[864,128]{1,0:T(8,128)(2,1)S(1)} %get-tuple-element.48), channel_id=1, source_target_pairs={{0,16},{2,18},{4,20},{6,22},{8,24},{10,26},{12,28},{14,30},{16,0},... | collective-permute-start | bytes 663560 | tf_op jit(solution)/shard_map/ppermute | solution.py:539
  41.0 0.5 collective-permute-start.16
  41.4 1.5 %collective-permute-start.12 = (bf16[96,256]{1,0:T(8,128)(2,1)S(1)}, bf16[96,256]{1,0:T(8,128)(2,1)S(1)}, u32[]{:S(2)}, u32[]{:S(2)}) collective-permute-start(bf16[96,256]{1,0:T(8,128)(2,1)S(1)} %collective-permute-done.10.refs_5_.refs_4_), channel_id=1, source_target_pairs={{0,1},{1,0},{2,3},{3,2},{4,5},{5,4},{6,7},{7,6},{8,9},{9,8},{10,11... | collective-permute-start | bytes 147464 | tf_op jit(solution)/shard_map/ppermute | solution.py:555
  42.9 2.6 %collective-permute-done.12.refs_5_ = bf16[96,256]{1,0:T(8,128)(2,1)S(1)} collective-permute-done((bf16[96,256]{1,0:T(8,128)(2,1)S(1)}, bf16[96,256]{1,0:T(8,128)(2,1)S(1)}, u32[]{:S(2)}, u32[]{:S(2)}) %collective-permute-start.12) | collective-permute-done | bytes 49184 | tf_op jit(solution)/shard_map/ppermute | solution.py:555
  45.5 3.6 %last_layer.1 = (f32[3,64,256]{2,1,0:T(8,128)}, f32[3,64,256]{2,1,0:T(8,128)}) custom-call(bf16[800,256]{1,0:T(8,128)(2,1)S(1)} %get-tuple-element.29.refs_0_, bf16[384,256]{1,0:T(8,128)(2,1)S(1)} %get-tuple-element.32.both_ref.refs_2_.refs_0_.refs_1_, bf16[384,256]{1,0:T(8,128)(2,1)S(1)} %collective-permute-done.4.refs_3_.refs_1_.refs_2_, ...), custom_call_target="tpu_custom_call" | custom-call | flops 110000000 | bytes 1048576 | tf_op jit(solution)/shard_map/last_layer/pallas_call | solution.py:590
  49.1 0.0 collective-permute-done.14
  49.1 7.2 %collective-permute-done.15 = bf16[864,128]{1,0:T(8,128)(2,1)S(1)} collective-permute-done((bf16[864,128]{1,0:T(8,128)(2,1)S(1)}, bf16[864,128]{1,0:T(8,128)(2,1)S(1)}, u32[]{:S(2)}, u32[]{:S(2)}) %collective-permute-start.15) | collective-permute-done | bytes 221216 | tf_op jit(solution)/shard_map/ppermute | solution.py:539
  56.3 4.9 %collective-permute-done.16 = bf16[864,128]{1,0:T(8,128)(2,1)S(1)} collective-permute-done((bf16[864,128]{1,0:T(8,128)(2,1)S(1)}, bf16[864,128]{1,0:T(8,128)(2,1)S(1)}, u32[]{:S(2)}, u32[]{:S(2)}) %collective-permute-start.16) | collective-permute-done | bytes 221216 | tf_op jit(solution)/shard_map/ppermute | solution.py:539
  61.2 0.1 add_multiply_fusion
  61.3 0.8 %fusion = (f32[432,128]{1,0:T(8,128)}, f32[432,128]{1,0:T(8,128)}) fusion(f32[864,128]{1,0:T(8,128)S(1)} %add_multiply_fusion), kind=kLoop, calls=%fused_computation.1 | loop fusion | bytes 884736 | tf_op jit(solution)/shard_map/slice | solution.py:766
  (8 shorter events, 0.1 us)
Async XLA Ops:
  2.9 8.4 %collective-permute-start = (bf16[400,256]{1,0:T(8,128)(2,1)}, bf16[400,256]{1,0:T(8,128)(2,1)S(1)}, u32[]{:S(2)}, u32[]{:S(2)}) collective-permute-start(bf16[400,256]{1,0:T(8,128)(2,1)} %get-tuple-element.27.refs_0_), channel_id=1, source_target_pairs={{0,1},{1,0},{2,3},{3,2},{4,5},{5,4},{6,7},{7,6},{8,9},{9,8},{10,11... | collective-permute-start | bytes 614408 | tf_op jit(solution)/shard_map/ppermute | solution.py:555
  4.5 9.7 %copy-start = (bf16[6912,256]{1,0:T(8,128)(2,1)S(1)}, bf16[6912,256]{1,0:T(8,128)(2,1)}, u32[]{:S(2)}) copy-start(bf16[6912,256]{1,0:T(8,128)(2,1)} %refs_6_.1) | copy-start | bytes 10616836
  4.5 9.7 %copy-start.1 = (bf16[6912,256]{1,0:T(8,128)(2,1)S(1)}, bf16[6912,256]{1,0:T(8,128)(2,1)}, u32[]{:S(2)}) copy-start(bf16[6912,256]{1,0:T(8,128)(2,1)} %refs_7_.1) | copy-start | bytes 10616836
  4.5 6.9 %collective-permute-start.1 = (bf16[112,256]{1,0:T(8,128)(2,1)}, bf16[112,256]{1,0:T(8,128)(2,1)S(1)}, u32[]{:S(2)}, u32[]{:S(2)}) collective-permute-start(bf16[112,256]{1,0:T(8,128)(2,1)} %get-tuple-element.28), channel_id=1, source_target_pairs={{2,4},{6,8},{10,12},{14,16},{18,20},{22,24},{26,28},{4,2},{8,6},{1... | collective-permute-start | bytes 172040 | tf_op jit(solution)/shard_map/ppermute | solution.py:566
  11.4 0.9 %copy-start.2 = (bf16[400,256]{1,0:T(8,128)(2,1)S(1)}, bf16[400,256]{1,0:T(8,128)(2,1)}, u32[]{:S(2)}) copy-start(bf16[400,256]{1,0:T(8,128)(2,1)} %get-tuple-element.27.refs_0_) | copy-start | bytes 614404
  12.4 1.8 %collective-permute-start.2 = (bf16[800,256]{1,0:T(8,128)(2,1)S(1)}, bf16[800,256]{1,0:T(8,128)(2,1)S(1)}, u32[]{:S(2)}, u32[]{:S(2)}) collective-permute-start(bf16[800,256]{1,0:T(8,128)(2,1)S(1)} %get-tuple-element.29.refs_0_), channel_id=1, source_target_pairs={{0,2},{2,0},{4,6},{6,4},{8,10},{10,8},{12,14},{14,12},{16,18},{18,... | collective-permute-start | bytes 1228808 | tf_op jit(solution)/shard_map/ppermute | solution.py:539
  12.5 4.7 %collective-permute-start.3 = (bf16[112,256]{1,0:T(8,128)(2,1)S(1)}, bf16[112,256]{1,0:T(8,128)(2,1)S(1)}, u32[]{:S(2)}, u32[]{:S(2)}) collective-permute-start(bf16[112,256]{1,0:T(8,128)(2,1)S(1)} %collective-permute-done.1.refs_2_.refs_0_.far), channel_id=1, source_target_pairs={{0,1},{1,0},{2,3},{3,2},{4,5},{5,4},{6,7},{7,6},{8,9},{9,8},{10,11... | collective-permute-start | bytes 172040 | tf_op jit(solution)/shard_map/ppermute | solution.py:555
  13.0 12.1 %collective-permute-start.8 = (bf16[608,256]{1,0:T(8,128)(2,1)S(1)}, bf16[608,256]{1,0:T(8,128)(2,1)S(1)}, u32[]{:S(2)}, u32[]{:S(2)}) collective-permute-start(bf16[608,256]{1,0:T(8,128)(2,1)S(1)} %get-tuple-element.35), channel_id=1, source_target_pairs={{0,4},{2,6},{4,0},{6,2},{8,12},{10,14},{12,8},{14,10},{16,20},{18,... | collective-permute-start | bytes 933896 | tf_op jit(solution)/shard_map/ppermute | solution.py:539
  17.2 5.1 %collective-permute-start.7 = (bf16[224,256]{1,0:T(8,128)(2,1)S(1)}, bf16[224,256]{1,0:T(8,128)(2,1)S(1)}, u32[]{:S(2)}, u32[]{:S(2)}) collective-permute-start(bf16[224,256]{1,0:T(8,128)(2,1)S(1)} %far_faces.1.refs_2_), channel_id=1, source_target_pairs={{0,2},{2,0},{4,6},{6,4},{8,10},{10,8},{12,14},{14,12},{16,18},{18,... | collective-permute-start | bytes 344072 | tf_op jit(solution)/shard_map/ppermute | solution.py:539
  17.4 7.8 %collective-permute-start.9 = (bf16[176,256]{1,0:T(8,128)(2,1)S(1)}, bf16[176,256]{1,0:T(8,128)(2,1)S(1)}, u32[]{:S(2)}, u32[]{:S(2)}) collective-permute-start(bf16[176,256]{1,0:T(8,128)(2,1)S(1)} %slim_faces.1), channel_id=1, source_target_pairs={{0,4},{2,6},{4,0},{6,2},{8,12},{10,14},{12,8},{14,10},{16,20},{18,... | collective-permute-start | bytes 270344 | tf_op jit(solution)/shard_map/ppermute | solution.py:539
  19.9 11.8 %collective-permute-start.4 = (bf16[384,256]{1,0:T(8,128)(2,1)S(1)}, bf16[384,256]{1,0:T(8,128)(2,1)S(1)}, u32[]{:S(2)}, u32[]{:S(2)}) collective-permute-start(bf16[384,256]{1,0:T(8,128)(2,1)S(1)} %get-tuple-element.32.both_ref.refs_2_.refs_0_.refs_1_), channel_id=1, source_target_pairs={{0,1},{1,0},{2,3},{3,2},{4,5},{5,4},{6,7},{7,6},{8,9},{9,8},{10,11... | collective-permute-start | bytes 589832 | tf_op jit(solution)/shard_map/ppermute | solution.py:555
  21.2 8.8 %collective-permute-start.5 = (bf16[288,256]{1,0:T(8,128)(2,1)S(1)}, bf16[288,256]{1,0:T(8,128)(2,1)S(1)}, u32[]{:S(2)}, u32[]{:S(2)}) collective-permute-start(bf16[288,256]{1,0:T(8,128)(2,1)S(1)} %get-tuple-element.33), channel_id=1, source_target_pairs={{0,4},{2,6},{4,0},{6,2},{8,12},{10,14},{12,8},{14,10},{16,20},{18,... | collective-permute-start | bytes 442376 | tf_op jit(solution)/shard_map/ppermute | solution.py:539
  22.3 9.3 %collective-permute-start.6 = (bf16[288,256]{1,0:T(8,128)(2,1)S(1)}, bf16[288,256]{1,0:T(8,128)(2,1)S(1)}, u32[]{:S(2)}, u32[]{:S(2)}) collective-permute-start(bf16[288,256]{1,0:T(8,128)(2,1)S(1)} %get-tuple-element.34), channel_id=1, source_target_pairs={{0,5},{1,4},{2,7},{3,6},{4,1},{5,0},{6,3},{7,2},{8,13},{9,12},{10,... | collective-permute-start | bytes 442376 | tf_op jit(solution)/shard_map/ppermute | solution.py:560
  25.2 6.7 %collective-permute-start.13 = (bf16[784,256]{1,0:T(8,128)(2,1)S(1)}, bf16[784,256]{1,0:T(8,128)(2,1)S(1)}, u32[]{:S(2)}, u32[]{:S(2)}) collective-permute-start(bf16[784,256]{1,0:T(8,128)(2,1)S(1)} %gather_early.1.packed), channel_id=1, source_target_pairs={{0,2},{2,0},{4,6},{6,4},{8,10},{10,8},{12,14},{14,12},{16,18},{18,... | collective-permute-start | bytes 1204232 | tf_op jit(solution)/shard_map/ppermute | solution.py:539
  25.3 6.4 %collective-permute-start.10 = (bf16[96,256]{1,0:T(8,128)(2,1)S(1)}, bf16[96,256]{1,0:T(8,128)(2,1)S(1)}, u32[]{:S(2)}, u32[]{:S(2)}) collective-permute-start(bf16[96,256]{1,0:T(8,128)(2,1)S(1)} %face.1), channel_id=1, source_target_pairs={{2,4},{6,8},{10,12},{14,16},{18,20},{22,24},{26,28},{4,2},{8,6},{1... | collective-permute-start | bytes 147464 | tf_op jit(solution)/shard_map/ppermute | solution.py:566
  31.8 3.2 %collective-permute-start.11 = (bf16[1344,256]{1,0:T(8,128)(2,1)S(1)}, bf16[1344,256]{1,0:T(8,128)(2,1)S(1)}, u32[]{:S(2)}, u32[]{:S(2)}) collective-permute-start(bf16[1344,256]{1,0:T(8,128)(2,1)S(1)} %gather_late.1._), channel_id=1, source_target_pairs={{0,2},{2,0},{4,6},{6,4},{8,10},{10,8},{12,14},{14,12},{16,18},{18,... | collective-permute-start | bytes 2064392 | tf_op jit(solution)/shard_map/ppermute | solution.py:539
  37.9 11.2 %collective-permute-start.14 = (bf16[864,128]{1,0:T(8,128)(2,1)S(1)}, bf16[864,128]{1,0:T(8,128)(2,1)S(1)}, u32[]{:S(2)}, u32[]{:S(2)}) collective-permute-start(bf16[864,128]{1,0:T(8,128)(2,1)S(1)} %get-tuple-element.44.refs_10_), channel_id=1, source_target_pairs={{0,8},{2,10},{4,12},{6,14},{8,0},{10,2},{12,4},{14,6},{16,24},{18,... | collective-permute-start | bytes 663560 | tf_op jit(solution)/shard_map/ppermute | solution.py:539
  38.0 18.3 %collective-permute-start.15 = (bf16[864,128]{1,0:T(8,128)(2,1)S(1)}, bf16[864,128]{1,0:T(8,128)(2,1)S(1)}, u32[]{:S(2)}, u32[]{:S(2)}) collective-permute-start(bf16[864,128]{1,0:T(8,128)(2,1)S(1)} %get-tuple-element.48), channel_id=1, source_target_pairs={{0,16},{2,18},{4,20},{6,22},{8,24},{10,26},{12,28},{14,30},{16,0},... | collective-permute-start | bytes 663560 | tf_op jit(solution)/shard_map/ppermute | solution.py:539
  41.0 20.2 %collective-permute-start.16 = (bf16[864,128]{1,0:T(8,128)(2,1)S(1)}, bf16[864,128]{1,0:T(8,128)(2,1)S(1)}, u32[]{:S(2)}, u32[]{:S(2)}) collective-permute-start(bf16[864,128]{1,0:T(8,128)(2,1)S(1)} %get-tuple-element.49), channel_id=1, source_target_pairs={{0,24},{2,26},{4,28},{6,30},{8,16},{10,18},{12,20},{14,22},{16,8},... | collective-permute-start | bytes 663560 | tf_op jit(solution)/shard_map/ppermute | solution.py:539
  41.4 4.1 %collective-permute-start.12 = (bf16[96,256]{1,0:T(8,128)(2,1)S(1)}, bf16[96,256]{1,0:T(8,128)(2,1)S(1)}, u32[]{:S(2)}, u32[]{:S(2)}) collective-permute-start(bf16[96,256]{1,0:T(8,128)(2,1)S(1)} %collective-permute-done.10.refs_5_.refs_4_), channel_id=1, source_target_pairs={{0,1},{1,0},{2,3},{3,2},{4,5},{5,4},{6,7},{7,6},{8,9},{9,8},{10,11... | collective-permute-start | bytes 147464 | tf_op jit(solution)/shard_map/ppermute | solution.py:555

commit v8 on v7

--- a/solution.py
+++ b/solution.py
@@ -336,7 +336,8 @@
         slim_ref[rows + rows // 2 :, :] = tile_ref[2 * rows :, :]
 
 
-def slim_faces_kernel(far, side_far, _, slim_ref):
+def faces_kernel(far, side_far, _, faces_ref, slim_ref):
+    gather_kernel(2, far, side_far, faces_ref)
     width = (far.shape[0] - META) // 2
     columns = my_columns(C // 2)
     for s, ref in enumerate((far, side_far)):
@@ -696,17 +697,16 @@
         def group_shapes(count):
             return shape((count, *columns.shape)), shape((count, *columns.shape[:2], cols))
 
-        far_faces = gathered("far_faces", fars, main[:1])
-        near_faces = swap(far_faces, "gx", 1)
-        (slim_faces,) = call(
-            slim_faces_kernel,
-            "slim_faces",
-            (shape((3 * width + 2 * META, C)),),
+        far_faces, slim_faces = call(
+            faces_kernel,
+            "far_faces",
+            (shape((2 * (2 * width + META), C)), shape((3 * width + 2 * META, C))),
             (*fars, main[0]),
             8,
             0.5,
             specs=[VMEM] * 2 + [ANY],
         )
+        near_faces = swap(far_faces, "gx", 1)
         beside = [swap(cells, "gx", 2) for cells in (thins, slim_faces)]
         chip_cols = [
             call(

time: 62.4 us -> 62.3 us (level)
    pallas_call x14 -> x13, Pallas kernels: 19.1 us -> 19.1 us  [call(): pl.pallas_call(kernel, out_shape=outs, in_specs=specs or [VMEM] * len(arg...]
  transfers between devices with their start and end apart: 17 -> 17, of which waited for: 6 -> 5; matrix products, arithmetic and copies ran while one was open for 0% -> 0% of each run, Pallas kernels for 23% -> 23%
where the time goes in v8:
time: 62.3 us; the launch traced here: 62.1 us
  waiting for transfers between devices  20.3 us (33%)
  starting transfers between devices  19.4 us (31%)
  Pallas kernels  19.1 us (31%)
  local copies, waits for them, and re-layouts  1.73 us (3%)
  between operations  1.46 us (2%)
    pallas_call x13, Pallas kernels, call(): pl.pallas_call(kernel, out_shape=outs, in_specs=specs or [VMEM] * len(arg...  19.1 us
    ppermute x10, waiting for transfers between devices, swap(): lax.ppermute(cells, axis, [(i, i ^ bit) for i in range(lax.axis_size(axis...  12.1 us
    ppermute x10, starting transfers between devices, swap(): lax.ppermute(cells, axis, [(i, i ^ bit) for i in range(lax.axis_size(axis...  7.35 us
    ppermute x2, starting transfers between devices, from_far(): far = lax.ppermute(face, 'gx', far_steps(lax.axis_size('gx')))  5.98 us
    ppermute x4, starting transfers between devices, from_sides(): lax.ppermute(cells, 'gy', step)  4.99 us
    ppermute x2, waiting for transfers between devices, from_far(): far = lax.ppermute(face, 'gx', far_steps(lax.axis_size('gx')))  4.03 us
    ppermute x4, waiting for transfers between devices, from_sides(): lax.ppermute(cells, 'gy', step)  2.62 us
    ppermute x1, waiting for transfers between devices, across(): lax.ppermute(face, ('gx', 'gy'), [(a * gy + c, b * gy + d) for a, b in gx...  1.55 us
  transfers between devices with their start and end apart: 17, of which 5 were waited for; matrix products, arithmetic and copies ran while one was open for 0% of the time, Pallas kernels for 23%

profile of v8, /device:TPU:8, one launch (start us, length us, event | category | flops | bytes accessed | tf_op | source)
XLA Modules:
  0.0 62.1 jit_solution(17987726386200468846)
XLA Ops:
  1.3 1.7 %pack.1 = (bf16[400,256]{1,0:T(8,128)(2,1)}, bf16[112,256]{1,0:T(8,128)(2,1)}) custom-call(bf16[1,1,3,64,256]{4,3,2,1,0:T(8,128)(2,1)} %features.1, bf16[1,1,3,64,256]{4,3,2,1,0:T(8,128)(2,1)} %cotangent.1, s32[1,1,3]{2,1,0:T(1,128)} %coords.1, s32[1,1]{1,0:T(1,128)S(6)} %copy.10.counts), custom_call_target="tpu_custom_call" | custom-call | flops 3300000000 | bytes 1048576 | tf_op jit(solution)/shard_map/pack/pallas_call | solution.py:591
  2.9 1.6 %collective-permute-start = (bf16[400,256]{1,0:T(8,128)(2,1)}, bf16[400,256]{1,0:T(8,128)(2,1)S(1)}, u32[]{:S(2)}, u32[]{:S(2)}) collective-permute-start(bf16[400,256]{1,0:T(8,128)(2,1)} %get-tuple-element.29.refs_0_), channel_id=1, source_target_pairs={{0,1},{1,0},{2,3},{3,2},{4,5},{5,4},{6,7},{7,6},{8,9},{9,8},{10,11... | collective-permute-start | bytes 614408 | tf_op jit(solution)/shard_map/ppermute | solution.py:556
  4.5 2.8 %collective-permute-start.1 = (bf16[112,256]{1,0:T(8,128)(2,1)}, bf16[112,256]{1,0:T(8,128)(2,1)S(1)}, u32[]{:S(2)}, u32[]{:S(2)}) collective-permute-start(bf16[112,256]{1,0:T(8,128)(2,1)} %get-tuple-element.30), channel_id=1, source_target_pairs={{2,4},{6,8},{10,12},{14,16},{18,20},{22,24},{26,28},{4,2},{8,6},{1... | collective-permute-start | bytes 172040 | tf_op jit(solution)/shard_map/ppermute | solution.py:567
  7.4 4.0 %collective-permute-done.1.refs_2_.far = bf16[112,256]{1,0:T(8,128)(2,1)S(1)} collective-permute-done((bf16[112,256]{1,0:T(8,128)(2,1)}, bf16[112,256]{1,0:T(8,128)(2,1)S(1)}, u32[]{:S(2)}, u32[]{:S(2)}) %collective-permute-start.1) | collective-permute-done | bytes 57376 | tf_op jit(solution)/shard_map/ppermute | solution.py:567
  11.4 0.0 collective-permute-done.refs_1_
  11.4 0.9 %copy-done.2 = bf16[400,256]{1,0:T(8,128)(2,1)S(1)} copy-done((bf16[400,256]{1,0:T(8,128)(2,1)S(1)}, bf16[400,256]{1,0:T(8,128)(2,1)}, u32[]{:S(2)}) %copy-start.2) | copy-done | bytes 204824
  12.3 0.1 join.1
  12.4 0.1 collective-permute-start.2
  12.5 0.6 collective-permute-start.3
  13.0 1.1 %collective-permute-start.8 = (bf16[608,256]{1,0:T(8,128)(2,1)S(1)}, bf16[608,256]{1,0:T(8,128)(2,1)S(1)}, u32[]{:S(2)}, u32[]{:S(2)}) collective-permute-start(bf16[608,256]{1,0:T(8,128)(2,1)S(1)} %get-tuple-element.38), channel_id=1, source_target_pairs={{0,4},{2,6},{4,0},{6,2},{8,12},{10,14},{12,8},{14,10},{16,20},{18,... | collective-permute-start | bytes 933896 | tf_op jit(solution)/shard_map/ppermute | solution.py:540
  14.2 0.0 collective-permute-done.2.refs_1_
  14.2 0.0 copy-done
  14.2 0.0 copy-done.1
  14.2 3.0 %first_convs.1 = (f32[192,256]{1,0:T(8,128)S(1)}, f32[192,256]{1,0:T(8,128)S(1)}) custom-call(bf16[800,256]{1,0:T(8,128)(2,1)S(1)} %get-tuple-element.31.refs_0_, bf16[800,256]{1,0:T(8,128)(2,1)S(1)} %collective-permute-done.2.refs_1_, bf16[6912,256]{1,0:T(8,128)(2,1)S(1)} %copy-done, bf16[6912,256]{1,0:T(8,128)(2,1)S(1)} %copy-done.1), custom_call_target="tpu_custom_call" | custom-call | flops 3300000000 | bytes 1048576 | tf_op jit(solution)/shard_map/first_convs/pallas_call | solution.py:591
  17.2 0.0 collective-permute-done.3.refs_3_.side_far
  17.2 0.2 collective-permute-start.7
  17.4 1.0 %collective-permute-start.9 = (bf16[176,256]{1,0:T(8,128)(2,1)S(1)}, bf16[176,256]{1,0:T(8,128)(2,1)S(1)}, u32[]{:S(2)}, u32[]{:S(2)}) collective-permute-start(bf16[176,256]{1,0:T(8,128)(2,1)S(1)} %get-tuple-element.39), channel_id=1, source_target_pairs={{0,4},{2,6},{4,0},{6,2},{8,12},{10,14},{12,8},{14,10},{16,20},{18,... | collective-permute-start | bytes 270344 | tf_op jit(solution)/shard_map/ppermute | solution.py:540
  18.5 1.4 %layer.1 = (bf16[384,256]{1,0:T(8,128)(2,1)S(1)}, bf16[288,256]{1,0:T(8,128)(2,1)S(1)}, bf16[288,256]{1,0:T(8,128)(2,1)S(1)}, f32[2,512]{1,0:T(2,128)S(1)}, f32[432,1]{1,0:T(8,128)S(1)}) custom-call(bf16[800,256]{1,0:T(8,128)(2,1)S(1)} %get-tuple-element.31.refs_0_, bf16[800,256]{1,0:T(8,128)(2,1)S(1)} %collective-permute-done.2.refs_1_, ...), custom_call_target="tpu_custom_call" | custom-call | flops 1100000000 | bytes 1048576 | tf_op jit(solution)/shard_map/layer/pallas_call | solution.py:591
  19.8 1.4 %collective-permute-start.4 = (bf16[384,256]{1,0:T(8,128)(2,1)S(1)}, bf16[384,256]{1,0:T(8,128)(2,1)S(1)}, u32[]{:S(2)}, u32[]{:S(2)}) collective-permute-start(bf16[384,256]{1,0:T(8,128)(2,1)S(1)} %get-tuple-element.34.both_ref.refs_2_.refs_0_.refs_1_), channel_id=1, source_target_pairs={{0,1},{1,0},{2,3},{3,2},{4,5},{5,4},{6,7},{7,6},{8,9},{9,8},{10,11... | collective-permute-start | bytes 589832 | tf_op jit(solution)/shard_map/ppermute | solution.py:556
  21.2 1.1 %collective-permute-start.5 = (bf16[288,256]{1,0:T(8,128)(2,1)S(1)}, bf16[288,256]{1,0:T(8,128)(2,1)S(1)}, u32[]{:S(2)}, u32[]{:S(2)}) collective-permute-start(bf16[288,256]{1,0:T(8,128)(2,1)S(1)} %get-tuple-element.35), channel_id=1, source_target_pairs={{0,4},{2,6},{4,0},{6,2},{8,12},{10,14},{12,8},{14,10},{16,20},{18,... | collective-permute-start | bytes 442376 | tf_op jit(solution)/shard_map/ppermute | solution.py:540
  22.3 0.0 collective-permute-done.7.refs_3_
  22.3 1.1 %collective-permute-start.6 = (bf16[288,256]{1,0:T(8,128)(2,1)S(1)}, bf16[288,256]{1,0:T(8,128)(2,1)S(1)}, u32[]{:S(2)}, u32[]{:S(2)}) collective-permute-start(bf16[288,256]{1,0:T(8,128)(2,1)S(1)} %get-tuple-element.36), channel_id=1, source_target_pairs={{0,5},{1,4},{2,7},{3,6},{4,1},{5,0},{6,3},{7,2},{8,13},{9,12},{10,... | collective-permute-start | bytes 442376 | tf_op jit(solution)/shard_map/ppermute | solution.py:561
  23.4 1.7 %chip_cols.3 = (bf16[2,9,288,256]{3,2,1,0:T(8,128)(2,1)S(1)}, bf16[2,9,288,128]{3,2,1,0:T(8,128)(2,1)S(1)}) custom-call(bf16[800,256]{1,0:T(8,128)(2,1)S(1)} %get-tuple-element.31.refs_0_, bf16[800,256]{1,0:T(8,128)(2,1)S(1)} %collective-permute-done.2.refs_1_, bf16[224,256]{1,0:T(8,128)(2,1)S(1)} %get-tuple-element.37.refs_2_, ...), custom_call_target="tpu_custom_call" | custom-call | flops 1760000000 | bytes 1048576 | tf_op jit(solution)/shard_map/chip_cols/pallas_call | solution.py:591
  25.1 0.0 collective-permute-done.8.refs_4_.refs_0_
  25.1 0.0 collective-permute-done.9.refs_5_.refs_1_
  25.1 0.1 collective-permute-start.13
  25.3 3.2 %collective-permute-start.10 = (bf16[96,256]{1,0:T(8,128)(2,1)S(1)}, bf16[96,256]{1,0:T(8,128)(2,1)S(1)}, u32[]{:S(2)}, u32[]{:S(2)}) collective-permute-start(bf16[96,256]{1,0:T(8,128)(2,1)S(1)} %face.1), channel_id=1, source_target_pairs={{2,4},{6,8},{10,12},{14,16},{18,20},{22,24},{26,28},{4,2},{8,6},{1... | collective-permute-start | bytes 147464 | tf_op jit(solution)/shard_map/ppermute | solution.py:567
  28.4 1.7 %chip_cols.2 = (bf16[2,9,288,256]{3,2,1,0:T(8,128)(2,1)S(1)}, bf16[2,9,288,128]{3,2,1,0:T(8,128)(2,1)S(1)}) custom-call(bf16[800,256]{1,0:T(8,128)(2,1)S(1)} %get-tuple-element.31.refs_0_, bf16[800,256]{1,0:T(8,128)(2,1)S(1)} %collective-permute-done.2.refs_1_, bf16[224,256]{1,0:T(8,128)(2,1)S(1)} %get-tuple-element.37.refs_2_, ...), custom_call_target="tpu_custom_call" | custom-call | flops 1760000000 | bytes 1048576 | tf_op jit(solution)/shard_map/chip_cols/pallas_call | solution.py:591
  30.1 0.0 collective-permute-done.5.refs_0_.refs_2_
  30.1 1.6 %collective-permute-done.6.refs_1_.refs_3_ = bf16[288,256]{1,0:T(8,128)(2,1)S(1)} collective-permute-done((bf16[288,256]{1,0:T(8,128)(2,1)S(1)}, bf16[288,256]{1,0:T(8,128)(2,1)S(1)}, u32[]{:S(2)}, u32[]{:S(2)}) %collective-permute-start.6) | collective-permute-done | bytes 147488 | tf_op jit(solution)/shard_map/ppermute | solution.py:561
  31.7 0.0 collective-permute-done.10.refs_5_.refs_4_
  31.7 0.0 collective-permute-done.4.refs_3_.refs_1_.refs_2_
  31.7 0.2 collective-permute-start.11
  31.9 0.0 collective-permute-done.13.near_packed
  31.9 3.1 %other_cols.1 = (bf16[4,9,288,256]{3,2,1,0:T(8,128)(2,1)S(1)}, bf16[4,9,288,128]{3,2,1,0:T(8,128)(2,1)S(1)}) custom-call(bf16[784,256]{1,0:T(8,128)(2,1)S(1)} %gather_early.1.packed, bf16[784,256]{1,0:T(8,128)(2,1)S(1)} %collective-permute-done.13.near_packed, bf16[1344,256]{1,0:T(8,128)(2,1)S(1)} %gather_late.1._), custom_call_target="tpu_custom_call" | custom-call | flops 3300000000 | bytes 1048576 | tf_op jit(solution)/shard_map/other_cols/pallas_call | solution.py:591
  35.0 0.0 collective-permute-done.11.refs_4_.refs_3_
  35.0 2.9 %group_terms.1 = (f32[864,128]{1,0:T(8,128)S(1)}, bf16[864,128]{1,0:T(8,128)(2,1)S(1)}, bf16[864,128]{1,0:T(8,128)(2,1)S(1)}, bf16[864,128]{1,0:T(8,128)(2,1)S(1)}) custom-call(bf16[384,256]{1,0:T(8,128)(2,1)S(1)} %get-tuple-element.34.both_ref.refs_2_.refs_0_.refs_1_, bf16[384,256]{1,0:T(8,128)(2,1)S(1)} %collective-permute-done.4.refs_3_.refs_1_.refs_2_, ...), custom_call_target="tpu_custom_call" | custom-call | flops 3849999872 | bytes 1048576 | tf_op jit(solution)/shard_map/group_terms/pallas_call | solution.py:591
  37.9 0.1 collective-permute-start.14
  38.0 3.0 %collective-permute-start.15 = (bf16[864,128]{1,0:T(8,128)(2,1)S(1)}, bf16[864,128]{1,0:T(8,128)(2,1)S(1)}, u32[]{:S(2)}, u32[]{:S(2)}) collective-permute-start(bf16[864,128]{1,0:T(8,128)(2,1)S(1)} %get-tuple-element.52), channel_id=1, source_target_pairs={{0,16},{2,18},{4,20},{6,22},{8,24},{10,26},{12,28},{14,30},{16,0},... | collective-permute-start | bytes 663560 | tf_op jit(solution)/shard_map/ppermute | solution.py:540
  41.0 0.5 collective-permute-start.16
  41.4 1.5 %collective-permute-start.12 = (bf16[96,256]{1,0:T(8,128)(2,1)S(1)}, bf16[96,256]{1,0:T(8,128)(2,1)S(1)}, u32[]{:S(2)}, u32[]{:S(2)}) collective-permute-start(bf16[96,256]{1,0:T(8,128)(2,1)S(1)} %collective-permute-done.10.refs_5_.refs_4_), channel_id=1, source_target_pairs={{0,1},{1,0},{2,3},{3,2},{4,5},{5,4},{6,7},{7,6},{8,9},{9,8},{10,11... | collective-permute-start | bytes 147464 | tf_op jit(solution)/shard_map/ppermute | solution.py:556
  42.9 2.6 %collective-permute-done.12.refs_5_ = bf16[96,256]{1,0:T(8,128)(2,1)S(1)} collective-permute-done((bf16[96,256]{1,0:T(8,128)(2,1)S(1)}, bf16[96,256]{1,0:T(8,128)(2,1)S(1)}, u32[]{:S(2)}, u32[]{:S(2)}) %collective-permute-start.12) | collective-permute-done | bytes 49184 | tf_op jit(solution)/shard_map/ppermute | solution.py:556
  45.5 3.6 %last_layer.1 = (f32[3,64,256]{2,1,0:T(8,128)}, f32[3,64,256]{2,1,0:T(8,128)}) custom-call(bf16[800,256]{1,0:T(8,128)(2,1)S(1)} %get-tuple-element.31.refs_0_, bf16[384,256]{1,0:T(8,128)(2,1)S(1)} %get-tuple-element.34.both_ref.refs_2_.refs_0_.refs_1_, bf16[384,256]{1,0:T(8,128)(2,1)S(1)} %collective-permute-done.4.refs_3_.refs_1_.refs_2_, ...), custom_call_target="tpu_custom_call" | custom-call | flops 110000000 | bytes 1048576 | tf_op jit(solution)/shard_map/last_layer/pallas_call | solution.py:591
  49.1 0.0 collective-permute-done.14
  49.1 7.2 %collective-permute-done.15 = bf16[864,128]{1,0:T(8,128)(2,1)S(1)} collective-permute-done((bf16[864,128]{1,0:T(8,128)(2,1)S(1)}, bf16[864,128]{1,0:T(8,128)(2,1)S(1)}, u32[]{:S(2)}, u32[]{:S(2)}) %collective-permute-start.15) | collective-permute-done | bytes 221216 | tf_op jit(solution)/shard_map/ppermute | solution.py:540
  56.3 4.9 %collective-permute-done.16 = bf16[864,128]{1,0:T(8,128)(2,1)S(1)} collective-permute-done((bf16[864,128]{1,0:T(8,128)(2,1)S(1)}, bf16[864,128]{1,0:T(8,128)(2,1)S(1)}, u32[]{:S(2)}, u32[]{:S(2)}) %collective-permute-start.16) | collective-permute-done | bytes 221216 | tf_op jit(solution)/shard_map/ppermute | solution.py:540
  61.2 0.1 add_multiply_fusion
  61.3 0.8 %fusion = (f32[432,128]{1,0:T(8,128)}, f32[432,128]{1,0:T(8,128)}) fusion(f32[864,128]{1,0:T(8,128)S(1)} %add_multiply_fusion), kind=kLoop, calls=%fused_computation.1 | loop fusion | bytes 884736 | tf_op jit(solution)/shard_map/slice | solution.py:766
  (7 shorter events, 0.1 us)
Async XLA Ops:
  2.9 8.4 %collective-permute-start = (bf16[400,256]{1,0:T(8,128)(2,1)}, bf16[400,256]{1,0:T(8,128)(2,1)S(1)}, u32[]{:S(2)}, u32[]{:S(2)}) collective-permute-start(bf16[400,256]{1,0:T(8,128)(2,1)} %get-tuple-element.29.refs_0_), channel_id=1, source_target_pairs={{0,1},{1,0},{2,3},{3,2},{4,5},{5,4},{6,7},{7,6},{8,9},{9,8},{10,11... | collective-permute-start | bytes 614408 | tf_op jit(solution)/shard_map/ppermute | solution.py:556
  4.5 9.7 %copy-start = (bf16[6912,256]{1,0:T(8,128)(2,1)S(1)}, bf16[6912,256]{1,0:T(8,128)(2,1)}, u32[]{:S(2)}) copy-start(bf16[6912,256]{1,0:T(8,128)(2,1)} %refs_6_.1) | copy-start | bytes 10616836
  4.5 9.7 %copy-start.1 = (bf16[6912,256]{1,0:T(8,128)(2,1)S(1)}, bf16[6912,256]{1,0:T(8,128)(2,1)}, u32[]{:S(2)}) copy-start(bf16[6912,256]{1,0:T(8,128)(2,1)} %refs_7_.1) | copy-start | bytes 10616836
  4.5 6.9 %collective-permute-start.1 = (bf16[112,256]{1,0:T(8,128)(2,1)}, bf16[112,256]{1,0:T(8,128)(2,1)S(1)}, u32[]{:S(2)}, u32[]{:S(2)}) collective-permute-start(bf16[112,256]{1,0:T(8,128)(2,1)} %get-tuple-element.30), channel_id=1, source_target_pairs={{2,4},{6,8},{10,12},{14,16},{18,20},{22,24},{26,28},{4,2},{8,6},{1... | collective-permute-start | bytes 172040 | tf_op jit(solution)/shard_map/ppermute | solution.py:567
  11.4 0.9 %copy-start.2 = (bf16[400,256]{1,0:T(8,128)(2,1)S(1)}, bf16[400,256]{1,0:T(8,128)(2,1)}, u32[]{:S(2)}) copy-start(bf16[400,256]{1,0:T(8,128)(2,1)} %get-tuple-element.29.refs_0_) | copy-start | bytes 614404
  12.4 1.8 %collective-permute-start.2 = (bf16[800,256]{1,0:T(8,128)(2,1)S(1)}, bf16[800,256]{1,0:T(8,128)(2,1)S(1)}, u32[]{:S(2)}, u32[]{:S(2)}) collective-permute-start(bf16[800,256]{1,0:T(8,128)(2,1)S(1)} %get-tuple-element.31.refs_0_), channel_id=1, source_target_pairs={{0,2},{2,0},{4,6},{6,4},{8,10},{10,8},{12,14},{14,12},{16,18},{18,... | collective-permute-start | bytes 1228808 | tf_op jit(solution)/shard_map/ppermute | solution.py:540
  12.5 4.7 %collective-permute-start.3 = (bf16[112,256]{1,0:T(8,128)(2,1)S(1)}, bf16[112,256]{1,0:T(8,128)(2,1)S(1)}, u32[]{:S(2)}, u32[]{:S(2)}) collective-permute-start(bf16[112,256]{1,0:T(8,128)(2,1)S(1)} %collective-permute-done.1.refs_2_.far), channel_id=1, source_target_pairs={{0,1},{1,0},{2,3},{3,2},{4,5},{5,4},{6,7},{7,6},{8,9},{9,8},{10,11... | collective-permute-start | bytes 172040 | tf_op jit(solution)/shard_map/ppermute | solution.py:556
  13.0 12.1 %collective-permute-start.8 = (bf16[608,256]{1,0:T(8,128)(2,1)S(1)}, bf16[608,256]{1,0:T(8,128)(2,1)S(1)}, u32[]{:S(2)}, u32[]{:S(2)}) collective-permute-start(bf16[608,256]{1,0:T(8,128)(2,1)S(1)} %get-tuple-element.38), channel_id=1, source_target_pairs={{0,4},{2,6},{4,0},{6,2},{8,12},{10,14},{12,8},{14,10},{16,20},{18,... | collective-permute-start | bytes 933896 | tf_op jit(solution)/shard_map/ppermute | solution.py:540
  17.2 5.1 %collective-permute-start.7 = (bf16[224,256]{1,0:T(8,128)(2,1)S(1)}, bf16[224,256]{1,0:T(8,128)(2,1)S(1)}, u32[]{:S(2)}, u32[]{:S(2)}) collective-permute-start(bf16[224,256]{1,0:T(8,128)(2,1)S(1)} %get-tuple-element.37.refs_2_), channel_id=1, source_target_pairs={{0,2},{2,0},{4,6},{6,4},{8,10},{10,8},{12,14},{14,12},{16,18},{18,... | collective-permute-start | bytes 344072 | tf_op jit(solution)/shard_map/ppermute | solution.py:540
  17.4 7.7 %collective-permute-start.9 = (bf16[176,256]{1,0:T(8,128)(2,1)S(1)}, bf16[176,256]{1,0:T(8,128)(2,1)S(1)}, u32[]{:S(2)}, u32[]{:S(2)}) collective-permute-start(bf16[176,256]{1,0:T(8,128)(2,1)S(1)} %get-tuple-element.39), channel_id=1, source_target_pairs={{0,4},{2,6},{4,0},{6,2},{8,12},{10,14},{12,8},{14,10},{16,20},{18,... | collective-permute-start | bytes 270344 | tf_op jit(solution)/shard_map/ppermute | solution.py:540
  19.8 11.8 %collective-permute-start.4 = (bf16[384,256]{1,0:T(8,128)(2,1)S(1)}, bf16[384,256]{1,0:T(8,128)(2,1)S(1)}, u32[]{:S(2)}, u32[]{:S(2)}) collective-permute-start(bf16[384,256]{1,0:T(8,128)(2,1)S(1)} %get-tuple-element.34.both_ref.refs_2_.refs_0_.refs_1_), channel_id=1, source_target_pairs={{0,1},{1,0},{2,3},{3,2},{4,5},{5,4},{6,7},{7,6},{8,9},{9,8},{10,11... | collective-permute-start | bytes 589832 | tf_op jit(solution)/shard_map/ppermute | solution.py:556
  21.2 8.9 %collective-permute-start.5 = (bf16[288,256]{1,0:T(8,128)(2,1)S(1)}, bf16[288,256]{1,0:T(8,128)(2,1)S(1)}, u32[]{:S(2)}, u32[]{:S(2)}) collective-permute-start(bf16[288,256]{1,0:T(8,128)(2,1)S(1)} %get-tuple-element.35), channel_id=1, source_target_pairs={{0,4},{2,6},{4,0},{6,2},{8,12},{10,14},{12,8},{14,10},{16,20},{18,... | collective-permute-start | bytes 442376 | tf_op jit(solution)/shard_map/ppermute | solution.py:540
  22.3 9.4 %collective-permute-start.6 = (bf16[288,256]{1,0:T(8,128)(2,1)S(1)}, bf16[288,256]{1,0:T(8,128)(2,1)S(1)}, u32[]{:S(2)}, u32[]{:S(2)}) collective-permute-start(bf16[288,256]{1,0:T(8,128)(2,1)S(1)} %get-tuple-element.36), channel_id=1, source_target_pairs={{0,5},{1,4},{2,7},{3,6},{4,1},{5,0},{6,3},{7,2},{8,13},{9,12},{10,... | collective-permute-start | bytes 442376 | tf_op jit(solution)/shard_map/ppermute | solution.py:561
  25.1 6.8 %collective-permute-start.13 = (bf16[784,256]{1,0:T(8,128)(2,1)S(1)}, bf16[784,256]{1,0:T(8,128)(2,1)S(1)}, u32[]{:S(2)}, u32[]{:S(2)}) collective-permute-start(bf16[784,256]{1,0:T(8,128)(2,1)S(1)} %gather_early.1.packed), channel_id=1, source_target_pairs={{0,2},{2,0},{4,6},{6,4},{8,10},{10,8},{12,14},{14,12},{16,18},{18,... | collective-permute-start | bytes 1204232 | tf_op jit(solution)/shard_map/ppermute | solution.py:540
  25.3 6.4 %collective-permute-start.10 = (bf16[96,256]{1,0:T(8,128)(2,1)S(1)}, bf16[96,256]{1,0:T(8,128)(2,1)S(1)}, u32[]{:S(2)}, u32[]{:S(2)}) collective-permute-start(bf16[96,256]{1,0:T(8,128)(2,1)S(1)} %face.1), channel_id=1, source_target_pairs={{2,4},{6,8},{10,12},{14,16},{18,20},{22,24},{26,28},{4,2},{8,6},{1... | collective-permute-start | bytes 147464 | tf_op jit(solution)/shard_map/ppermute | solution.py:567
  31.7 3.3 %collective-permute-start.11 = (bf16[1344,256]{1,0:T(8,128)(2,1)S(1)}, bf16[1344,256]{1,0:T(8,128)(2,1)S(1)}, u32[]{:S(2)}, u32[]{:S(2)}) collective-permute-start(bf16[1344,256]{1,0:T(8,128)(2,1)S(1)} %gather_late.1._), channel_id=1, source_target_pairs={{0,2},{2,0},{4,6},{6,4},{8,10},{10,8},{12,14},{14,12},{16,18},{18,... | collective-permute-start | bytes 2064392 | tf_op jit(solution)/shard_map/ppermute | solution.py:540
  37.9 11.2 %collective-permute-start.14 = (bf16[864,128]{1,0:T(8,128)(2,1)S(1)}, bf16[864,128]{1,0:T(8,128)(2,1)S(1)}, u32[]{:S(2)}, u32[]{:S(2)}) collective-permute-start(bf16[864,128]{1,0:T(8,128)(2,1)S(1)} %get-tuple-element.48.refs_10_), channel_id=1, source_target_pairs={{0,8},{2,10},{4,12},{6,14},{8,0},{10,2},{12,4},{14,6},{16,24},{18,... | collective-permute-start | bytes 663560 | tf_op jit(solution)/shard_map/ppermute | solution.py:540
  38.0 18.3 %collective-permute-start.15 = (bf16[864,128]{1,0:T(8,128)(2,1)S(1)}, bf16[864,128]{1,0:T(8,128)(2,1)S(1)}, u32[]{:S(2)}, u32[]{:S(2)}) collective-permute-start(bf16[864,128]{1,0:T(8,128)(2,1)S(1)} %get-tuple-element.52), channel_id=1, source_target_pairs={{0,16},{2,18},{4,20},{6,22},{8,24},{10,26},{12,28},{14,30},{16,0},... | collective-permute-start | bytes 663560 | tf_op jit(solution)/shard_map/ppermute | solution.py:540
  41.0 20.2 %collective-permute-start.16 = (bf16[864,128]{1,0:T(8,128)(2,1)S(1)}, bf16[864,128]{1,0:T(8,128)(2,1)S(1)}, u32[]{:S(2)}, u32[]{:S(2)}) collective-permute-start(bf16[864,128]{1,0:T(8,128)(2,1)S(1)} %get-tuple-element.53), channel_id=1, source_target_pairs={{0,24},{2,26},{4,28},{6,30},{8,16},{10,18},{12,20},{14,22},{16,8},... | collective-permute-start | bytes 663560 | tf_op jit(solution)/shard_map/ppermute | solution.py:540
  41.4 4.1 %collective-permute-start.12 = (bf16[96,256]{1,0:T(8,128)(2,1)S(1)}, bf16[96,256]{1,0:T(8,128)(2,1)S(1)}, u32[]{:S(2)}, u32[]{:S(2)}) collective-permute-start(bf16[96,256]{1,0:T(8,128)(2,1)S(1)} %collective-permute-done.10.refs_5_.refs_4_), channel_id=1, source_target_pairs={{0,1},{1,0},{2,3},{3,2},{4,5},{5,4},{6,7},{7,6},{8,9},{9,8},{10,11... | collective-permute-start | bytes 147464 | tf_op jit(solution)/shard_map/ppermute | solution.py:556
